TPU v7x, 256 devices: a whole 4x4x8 slice. The times are simulated.
256 devices in a mesh: dp: 8 (over z), ctx: 32 (over x, y, core).
Axes of the slice: x: 4, y: 4, z: 8, core: 2. Of those that a mesh axis runs over, the one named last changes fastest.
Arguments:
- conv_input: bfloat16 [8, 4096, 5120], P('dp', 'ctx'), may hold values from -11 to 11
- conv_weight: float32 [4, 5120], replicated, may hold values from 0.2 to 0.6
- step_raw: float32 [8, 64, 4096], P('dp', None, 'ctx'), may hold values from -7 to -4.8
- decay_log: float32 [64], replicated, may hold values from -7 to 2.5
- skip_gain: float32 [64], replicated, may hold values from 0.25 to 1.75
- cotangent: bfloat16 [8, 4096, 4096], P('dp', 'ctx'), may hold values from -6 to 6
Outputs:
- layer_out: bfloat16 [8, 4096, 4096], P('dp', 'ctx')
- grad_input: bfloat16 [8, 4096, 5120], P('dp', 'ctx')
- grad_step: float32 [8, 64, 4096], P('dp', None, 'ctx')
- grad_conv: float32 [4, 5120], replicated
- grad_decay_log: float32 [64], replicated
- grad_skip: float32 [64], replicated
All inputs are finite; a program needn't handle non-finite values.
Results may differ from a plain program's by a relative error of at most 0.0059.
Values may be sent and summed in bfloat16 or wider, within the bound.
No kernel may reach another device: no remote copies, remote signals or barrier semaphores. Data moves between devices by JAX's collectives and lax.ppermute only.
A program may use at most 320 MiB of HBM per device.

v0:
```python
import jax
import jax.numpy as jnp
from jax import lax
from jax.sharding import PartitionSpec as P

HEAD_DIM = 64
GROUPS = 4
STATE = 128
SPAN = 128


split_mode = lax.Precision.HIGH


def shifted(value, axis, steps):
    count = lax.axis_size(axis)
    first, last = (max(0, -steps), min(count, count - steps))
    return lax.ppermute(value, axis, [(source, source + steps) for source in range(first, last)])


def prefix(value, axis, join, neutral, backward):
    count, mine = (lax.axis_size(axis), lax.axis_index(axis))
    pieces = jax.tree.map(lambda part: lax.all_gather(part, axis), value)
    if backward:
        pieces = jax.tree.map(lambda part: part[::-1], pieces)
        mine = count - 1 - mine
    so_far = jax.tree.map(
        lambda part, zero: jnp.full_like(part, 0) + jnp.asarray(zero, part.dtype), value, neutral
    )

    def step(position, so_far):
        longer = join(so_far, jax.tree.map(lambda part: part[position], pieces))
        return jax.tree.map(lambda new, old: jnp.where(position < mine, new, old), longer, so_far)

    return lax.fori_loop(0, count - 1, step, so_far)


def group_core(x_group, b_group, c_group, rate_group, decay_group, block_len):
    total_len, heads_here, head_dim = x_group.shape
    state_dim = b_group.shape[1]
    blocks = total_len // block_len
    x_blocks = x_group.reshape(blocks, block_len, heads_here, head_dim)
    b_blocks = b_group.reshape(blocks, block_len, state_dim)
    c_blocks = c_group.reshape(blocks, block_len, state_dim)
    rate_blocks = rate_group.reshape(heads_here, blocks, block_len).transpose(1, 0, 2)
    row_ids = lax.broadcasted_iota(jnp.int32, (block_len, block_len), 0)
    col_ids = lax.broadcasted_iota(jnp.int32, (block_len, block_len), 1)
    lower_mask = row_ids >= col_ids

    def advance(state_now, pieces):
        x_part, b_part, c_part, rate_part = pieces
        segment = jnp.cumsum(rate_part * decay_group[:, None], axis=1)
        spread = segment[:, :, None] - segment[:, None, :]
        kernel = (
            jnp.where(lower_mask, jnp.exp(jnp.where(lower_mask, spread, 0.0)), 0.0)
            * rate_part[:, None, :]
        )
        scores = jnp.dot(c_part, b_part.T, precision=split_mode)
        inner_out = jnp.einsum("hts,shp->thp", kernel * scores[None], x_part, precision=split_mode)
        from_state = (
            jnp.einsum("tn,hpn->thp", c_part, state_now, precision=split_mode)
            * jnp.exp(segment).T[:, :, None]
        )
        weights = jnp.exp(segment[:, -1:] - segment) * rate_part
        fresh_state = jnp.einsum(
            "shp,sn->hpn", x_part * weights.T[:, :, None], b_part, precision=split_mode
        )
        next_state = jnp.exp(segment[:, -1])[:, None, None] * state_now + fresh_state
        return (next_state, inner_out + from_state)

    zero_state = jnp.zeros((heads_here, head_dim, state_dim), jnp.float32)
    final_state, outputs = lax.scan(
        jax.checkpoint(advance), zero_state, (x_blocks, b_blocks, c_blocks, rate_blocks)
    )
    totals = jnp.exp(decay_group * jnp.sum(rate_group, axis=1))
    return (outputs.reshape(total_len, heads_here, head_dim), final_state, totals)


def ssd_core(x_all, b_all, c_all, step_rates, decay_rate):
    groups_here = b_all.shape[1]
    per_group = x_all.shape[1] // groups_here
    outputs = []
    states = []
    totals = []
    for member in range(groups_here):
        first_head = member * per_group
        last_head = first_head + per_group
        result = group_core(
            x_all[:, first_head:last_head],
            b_all[:, member],
            c_all[:, member],
            step_rates[first_head:last_head],
            decay_rate[first_head:last_head],
            SPAN,
        )
        outputs.append(result[0])
        states.append(result[1])
        totals.append(result[2])
    return (
        jnp.concatenate(outputs, axis=1),
        jnp.concatenate(states, axis=0),
        jnp.concatenate(totals, axis=0),
    )


def combine_chain(earlier, later):
    early_decay, early_state = earlier
    late_decay, late_state = later
    return (early_decay * late_decay, late_decay[:, None, None] * early_state + late_state)


def silu_slope(values):
    sigmoid_v = jax.nn.sigmoid(values)
    return sigmoid_v * (1.0 + values * (1.0 - sigmoid_v))


def local(conv_input, conv_weight, step_raw, decay_log, skip_gain, cotangent):
    tokens_in = conv_input[0]
    tok_count, channels = tokens_in.shape
    tap_count = conv_weight.shape[0]
    head_count = decay_log.shape[0]
    head_dim = HEAD_DIM
    state_dim = STATE
    groups = GROUPS
    width_x = head_count * head_dim
    width_b = groups * state_dim
    previous = shifted(tokens_in[tok_count - (tap_count - 1) :], "ctx", 1)
    padded = jnp.concatenate([previous, tokens_in], axis=0)
    pre_conv = conv_weight[0] * padded[0:tok_count]
    for offset in range(1, tap_count):
        pre_conv = pre_conv + conv_weight[offset] * padded[offset : offset + tok_count]
    mixed_in = jax.nn.silu(pre_conv).astype(jnp.bfloat16)
    raw_rates = step_raw[0]
    step_rates = jax.nn.softplus(raw_rates)
    decay_rate = -jnp.exp(decay_log)
    per_group = head_count // groups
    x_here = mixed_in[:, :width_x].astype(jnp.float32).reshape(tok_count, head_count, head_dim)
    b_here = (
        mixed_in[:, width_x : width_x + width_b]
        .astype(jnp.float32)
        .reshape(tok_count, groups, state_dim)
    )
    c_here = (
        mixed_in[:, width_x + width_b :].astype(jnp.float32).reshape(tok_count, groups, state_dim)
    )
    grad_out = cotangent[0].astype(jnp.float32).reshape(tok_count, head_count, head_dim)
    (own_out, own_state, own_decay), pull_own = jax.vjp(
        ssd_core, x_here, b_here, c_here, step_rates, decay_rate
    )
    growth = jnp.exp(jnp.cumsum(step_rates * decay_rate[:, None], axis=1)).T
    scaled_grad = (grad_out * growth[:, :, None]).reshape(tok_count, groups, per_group, head_dim)
    entry_grad = jnp.einsum("tghp,tgn->ghpn", scaled_grad, c_here, precision=split_mode).reshape(
        head_count, head_dim, state_dim
    )
    identity = (jnp.ones_like(own_decay), jnp.zeros_like(own_state))
    _, entry_state = prefix((own_decay, own_state), "ctx", combine_chain, identity, False)
    _, exit_grad = prefix((own_decay, entry_grad), "ctx", combine_chain, identity, True)

    def entry_part(c_part, rate_part, decay_part):
        rise_rates = jnp.exp(jnp.cumsum(rate_part * decay_part[:, None], axis=1)).T
        reached = jnp.einsum(
            "tgn,ghpn->tghp",
            c_part,
            entry_state.reshape(groups, per_group, head_dim, state_dim),
            precision=split_mode,
        )
        return reached.reshape(tok_count, head_count, head_dim) * rise_rates[:, :, None]

    from_entry, pull_entry = jax.vjp(entry_part, c_here, step_rates, decay_rate)
    mixer_out = own_out + from_entry + skip_gain[None, :, None] * x_here
    out_tokens = mixer_out.astype(jnp.bfloat16).reshape(tok_count, width_x)
    link_grad = jnp.sum(exit_grad * entry_state, axis=(1, 2))
    grad_xpart, grad_bpart, grad_cpart, grad_rates, grad_decay = pull_own(
        (grad_out, exit_grad, link_grad)
    )
    more_c, more_rates, more_decay = pull_entry(grad_out)
    grad_xpart = grad_xpart + skip_gain[None, :, None] * grad_out
    grad_cpart = grad_cpart + more_c
    grad_rates = grad_rates + more_rates
    grad_decay = grad_decay + more_decay
    grad_skip = jnp.sum(grad_out * x_here, axis=(0, 2))
    grad_mixed = jnp.concatenate(
        [
            grad_xpart.reshape(tok_count, width_x),
            grad_bpart.reshape(tok_count, width_b),
            grad_cpart.reshape(tok_count, width_b),
        ],
        axis=1,
    ).astype(jnp.bfloat16)
    grad_pre = grad_mixed.astype(jnp.float32) * silu_slope(pre_conv)
    following = shifted(grad_pre[: tap_count - 1].astype(jnp.bfloat16), "ctx", -1).astype(
        jnp.float32
    )
    extended = jnp.concatenate([grad_pre, following], axis=0)
    grad_tokens = conv_weight[0] * extended[tap_count - 1 : tap_count - 1 + tok_count]
    for offset in range(1, tap_count):
        start_row = tap_count - 1 - offset
        grad_tokens = (
            grad_tokens + conv_weight[offset] * extended[start_row : start_row + tok_count]
        )
    conv_terms = jnp.stack(
        [
            jnp.sum(grad_pre * padded[offset : offset + tok_count], axis=0)
            for offset in range(tap_count)
        ]
    )
    grad_dt = grad_rates * jax.nn.sigmoid(raw_rates)
    conv_total, decay_total, skip_total = lax.psum(
        (conv_terms, grad_decay * decay_rate, grad_skip), ("dp", "ctx")
    )
    return (
        out_tokens[None],
        grad_tokens.astype(jnp.bfloat16)[None],
        grad_dt[None],
        conv_total,
        decay_total,
        skip_total,
    )


def solution(mesh):
    in_specs = (P("dp", "ctx", None), P(), P("dp", None, "ctx"), P(), P(), P("dp", "ctx", None))
    out_specs = (P("dp", "ctx", None), P("dp", "ctx", None), P("dp", None, "ctx"), P(), P(), P())
    return jax.shard_map(local, mesh=mesh, in_specs=in_specs, out_specs=out_specs, check_vma=False)
```

profile of v0, /device:TPU:2, one launch (start us, length us, event | category | flops | bytes accessed | tf_op | source)
XLA Modules:
  0.0 1085.8 jit_solution(7420171384837330508)
XLA Ops:
  21.5 6.7 multiply_convert_fusion
  38.0 59.5 %all-reduce.28 = f32[2048]{0:T(1024)S(1)} all-reduce(f32[2048]{0:T(1024)S(1)} %maximum_dynamic-update-slice_fusion), channel_id=2, replica_groups=mesh['dp'=8,'ctx'=32] {'ctx'}, use_global_device_ids=true, to_apply=%add.28 | all-reduce | flops 2048 | bytes 16384
  97.9 145.9 %all-gather.7.cloned.1.call-done = f32[2048,64,128]{2,1,0:T(8,128)} async-done(((f32[64,64,128]{2,1,0:T(8,128)}), f32[2048,64,128]{2,1,0:T(8,128)}) %all-gather.7.cloned.1.call-update) | async-done | bytes 67108880 | tf_op jit(solution)/shard_map/all_gather | solution.py:23
  243.8 65.9 %while.26 = (s32[]{:T(128)}, f32[64,64,128]{2,1,0:T(8,128)S(1)}, s32[]{:T(128)}, f32[32,64]{1,0:T(8,128)S(1)}, f32[32,64,64,128]{3,2,1,0:T(8,128)}, /*index=5*/s32[]{:T(128)}, s32[]{:T(128)}) while((s32[]{:T(128)}, f32[64,64,128]{2,1,0:T(8,128)S(1)}, s32[]{:T(128)}, f32[32,64]{1,0:T(8,128)S(1)}, f32[32,64,64,128]{3,2,1,0:T(8,128)}, ...), condition=%wide.region_9.10_spmd.clone, body=%wide.region_8.9_spmd.clone.sunk | while | flops 2097156 | bytes 6292337 | solution.py:35
  309.7 3.9 fusion.24
  339.8 181.9 %all-gather.5.cloned.1.call-done = f32[32,64,64,128]{3,2,1,0:T(8,128)} async-done(((f32[1,64,64,128]{3,2,1,0:T(8,128)}), f32[32,64,64,128]{3,2,1,0:T(8,128)}) %all-gather.5.cloned.1.call-update) | async-done | bytes 67108880 | tf_op jit(solution)/shard_map/all_gather | solution.py:23
  521.7 43.6 %rev.7 = f32[32,64,64,128]{3,2,1,0:T(8,128)} reverse(f32[32,64,64,128]{3,2,1,0:T(8,128)} %all-gather.5.cloned.1.call-done), dimensions={0} | reverse | bytes 134217728 | tf_op jit(solution)/shard_map/rev | solution.py:25
  565.3 142.7 %while.27 = (s32[]{:T(128)}, f32[64,64,128]{2,1,0:T(8,128)}, s32[]{:T(128)}, f32[32,64]{1,0:T(8,128)}, f32[32,64,64,128]{3,2,1,0:T(8,128)}, /*index=5*/s32[]{:T(128)}, s32[]{:T(128)}) while((s32[]{:T(128)}, f32[64,64,128]{2,1,0:T(8,128)}, s32[]{:T(128)}, f32[32,64]{1,0:T(8,128)}, f32[32,64,64,128]{3,2,1,0:T(8,128)}, ...), condition=%wide.region_12.13_spmd.clone, body=%wide.region_11.12_spmd.clone.sunk | while | flops 2097156 | bytes 6292337 | solution.py:35
  566.0 3.3 fusion.375
  570.0 3.9 fusion.375
  574.6 3.9 fusion.375
  579.2 3.9 fusion.375
  583.8 3.9 fusion.375
  588.5 3.9 fusion.375
  593.1 3.9 fusion.375
  597.7 3.9 fusion.375
  602.3 3.9 fusion.375
  606.9 3.9 fusion.375
  611.6 3.9 fusion.375
  616.2 3.9 fusion.375
  620.8 3.9 fusion.375
  625.4 3.9 fusion.375
  630.0 3.9 fusion.375
  634.6 3.9 fusion.375
  639.2 3.9 fusion.375
  643.9 3.9 fusion.375
  648.5 3.9 fusion.375
  653.1 3.9 fusion.375
  657.7 3.9 fusion.375
  662.3 3.9 fusion.375
  666.9 3.9 fusion.375
  671.6 3.9 fusion.375
  676.2 3.9 fusion.375
  680.8 3.9 fusion.375
  685.4 3.9 fusion.375
  690.0 3.9 fusion.375
  694.6 3.9 fusion.375
  699.3 3.9 fusion.375
  703.9 3.9 fusion.375
  733.3 3.6 fusion.109
  750.2 3.6 fusion.107
  784.6 3.6 fusion.105
  800.0 3.6 fusion.103
  824.7 9.6 fusion.5
  836.6 3.0 collective-permute-start.1
  841.6 75.3 %all-reduce.29 = (f32[64]{0:T(128)}, f32[64]{0:T(128)}) all-reduce(f32[64]{0:T(128)S(1)} %add_multiply_fusion, f32[64]{0:T(128)S(1)} %copy-done.167), channel_id=1, replica_groups=mesh['dp'=8,'ctx'=32] {'dp','ctx'}, use_global_device_ids=true, to_apply=%region_66.67 | all-reduce | flops 128 | bytes 1024 | tf_op jit(solution)/shard_map/psum | solution.py:208
  918.9 13.6 %fusion.30 = bf16[1,128,5120]{1,2,0:T(8,128)(2,1)S(1)} fusion(f32[128,5120]{0,1:T(8,128)} %copy-done.7, f32[5120]{0:T(1024)S(1)} %bitcast.567, f32[3,5120]{0,1:T(8,128)} %copy.112, f32[5120]{0:T(1024)S(1)} %bitcast.569, f32[5120]{0:T(1024)S(1)} %bitcast.565, f32[5120]{0:T(1024)S(1)} %bitcast.563), kind=kLoop, calls=%fused_computation.63 | loop fusion | flops 7208960 | bytes 4075520 | tf_op jit(solution)/shard_map/broadcast_in_dim | solution.py:213
  933.9 143.6 %all-reduce.32.cloned.1.call-done = f32[4,5120]{1,0:T(4,128)} async-done(((f32[4,5120]{1,0:T(4,128)}), f32[4,5120]{1,0:T(4,128)}) %all-reduce.32.cloned.1.call-update) | async-done | bytes 81936 | tf_op jit(solution)/shard_map/psum | solution.py:208
  (605 shorter events, 244.6 us)
Async XLA Ops:
  7.2 236.6 %all-gather.7.cloned.1.call-start = ((), (), s32[]{:S(2)}) async-start(), calls=%async_computation.2 | async-start | bytes 69206016 | tf_op jit(solution)/shard_map/all_gather | solution.py:23
  8.1 12.8 %collective-permute-start = (bf16[3,5120]{1,0:T(4,128)(2,1)S(1)}, bf16[3,5120]{1,0:T(4,128)(2,1)S(1)}, u32[]{:S(2)}, u32[]{:S(2)}) collective-permute-start(bf16[3,5120]{1,0:T(4,128)(2,1)S(1)} %slice_bitcast_fusion.8), channel_id=1, source_target_pairs={{0,1},{1,2},{2,3},{3,4},{4,5},{5,6},{6,7},{7,8},{8,9},{9,10},{10,1... | collective-permute-start | bytes 92168 | tf_op jit(solution)/shard_map/ppermute | solution.py:18
  10.7 7.9 copy-start.81
  10.8 6.0 copy-start.147
  10.8 6.0 copy-start.148
  14.1 310.8 %copy-start.39 = (f32[16,128]{1,0:T(8,128)}, f32[16,128]{1,0:T(8,128)S(1)}, u32[]{:S(2)}) copy-start(f32[16,128]{1,0:T(8,128)S(1)} %get-tuple-element.796) | copy-start | bytes 24580
  14.1 311.8 %copy-start.44 = (f32[16,128]{1,0:T(8,128)}, f32[16,128]{1,0:T(8,128)S(1)}, u32[]{:S(2)}) copy-start(f32[16,128]{1,0:T(8,128)S(1)} %get-tuple-element.803) | copy-start | bytes 24580
  18.6 9.6 copy-start.61
  18.6 9.6 copy-start.63
  18.6 9.6 copy-start.65
  18.6 9.6 copy-start.67
  20.9 7.3 copy-start.3
  21.5 6.7 copy-start.8
  32.7 489.0 %all-gather.5.cloned.1.call-start = ((), (), s32[]{:S(2)}) async-start(), calls=%async_computation | async-start | bytes 69206016 | tf_op jit(solution)/shard_map/all_gather | solution.py:23
  37.3 206.5 %copy-start.133 = (f32[16]{0:T(128)}, f32[16]{0:T(128)S(1)}, u32[]{:S(2)}) copy-start(f32[16]{0:T(128)S(1)} %get-tuple-element.1017) | copy-start | bytes 196
  37.3 206.5 %copy-start.135 = (f32[16]{0:T(128)}, f32[16]{0:T(128)S(1)}, u32[]{:S(2)}) copy-start(f32[16]{0:T(128)S(1)} %get-tuple-element.1018) | copy-start | bytes 196
  37.3 206.5 %copy-start.137 = (f32[16]{0:T(128)}, f32[16]{0:T(128)S(1)}, u32[]{:S(2)}) copy-start(f32[16]{0:T(128)S(1)} %get-tuple-element.1019) | copy-start | bytes 196
  316.4 761.1 %all-reduce.32.cloned.1.call-start = ((), (), s32[]{:S(2)}) async-start(), calls=%async_computation.1 | async-start | bytes 163840 | tf_op jit(solution)/shard_map/psum | solution.py:208
  318.0 7.9 copy-start.129
  724.0 6.4 copy-start.52
  724.0 6.4 copy-start.119
  724.0 7.2 copy-start.41
  724.0 7.2 copy-start.46
  724.0 7.2 copy-start.49
  726.5 5.4 copy-start.74
  775.2 6.2 copy-start.58
  775.2 6.2 copy-start.120
  775.2 7.0 copy-start.55
  777.6 5.7 copy-start.76
  806.8 5.8 copy-start.23
  806.8 5.9 copy-start.32
  806.8 5.9 copy-start.35
  806.8 6.1 copy-start.24
  806.9 6.3 copy-start.15
  806.9 6.3 copy-start.18
  806.9 6.3 copy-start.102
  806.9 7.0 copy-start.33
  806.9 7.0 copy-start.36
  809.1 5.2 copy-start.14
  809.1 5.2 copy-start.17
  809.1 5.2 copy-start.103
  836.0 5.5 copy-start.172
  836.0 5.6 copy-start.167
  836.1 82.7 %copy-start.62 = (f32[1,5120]{1,0:T(1,128)S(1)}, f32[1,5120]{1,0:T(1,128)}, u32[]{:S(2)}) copy-start(f32[1,5120]{1,0:T(1,128)} %copy-done.61) | copy-start | bytes 61444
  836.1 82.7 %copy-start.64 = (f32[1,5120]{1,0:T(1,128)S(1)}, f32[1,5120]{1,0:T(1,128)}, u32[]{:S(2)}) copy-start(f32[1,5120]{1,0:T(1,128)} %copy-done.63) | copy-start | bytes 61444
  836.2 82.7 %copy-start.66 = (f32[1,5120]{1,0:T(1,128)S(1)}, f32[1,5120]{1,0:T(1,128)}, u32[]{:S(2)}) copy-start(f32[1,5120]{1,0:T(1,128)} %copy-done.65) | copy-start | bytes 61444
  836.2 82.7 %copy-start.68 = (f32[1,5120]{1,0:T(1,128)S(1)}, f32[1,5120]{1,0:T(1,128)}, u32[]{:S(2)}) copy-start(f32[1,5120]{1,0:T(1,128)} %copy-done.67) | copy-start | bytes 61444
  836.6 80.2 %collective-permute-start.1 = (bf16[3,5120]{1,0:T(4,128)(2,1)S(1)}, bf16[3,5120]{1,0:T(4,128)(2,1)S(1)}, u32[]{:S(2)}, u32[]{:S(2)}) collective-permute-start(bf16[3,5120]{1,0:T(4,128)(2,1)S(1)} %copy.111), channel_id=1, source_target_pairs={{1,0},{2,1},{3,2},{4,3},{5,4},{6,5},{7,6},{8,7},{9,8},{10,9},{11,1... | collective-permute-start | bytes 92168 | tf_op jit(solution)/shard_map/ppermute | solution.py:18
  (131 other events, 377.6 us)
Sparse Core Ops, SparseCore 0:
  32.8 210.9 all-gather.6
  316.5 205.1 all-gather.4
  840.5 236.9 all-reduce.31
where the time goes:
time: 1100 us; the launch traced here: 1090 us
  waiting for transfers between devices  471 us (43%)
  other arithmetic  280 us (25%)
  blocking collectives  135 us (12%)
  local copies, waits for them, and re-layouts  108 us (10%)
  matrix products  68.3 us (6%)
  between operations  17.2 us (2%)
    all_gather x2, waiting for transfers between devices, prefix(): pieces = jax.tree.map(lambda part: lax.all_gather(part, axis), value)  328 us
    select_n x62, other arithmetic, step(): jnp.where(position < mine, new, old)  186 us
    psum x1, waiting for transfers between devices, local(): lax.psum((conv_terms, grad_decay * decay_rate, grad_skip), ('dp', 'ctx'))  144 us
    psum x1, blocking collectives, local(): lax.psum((conv_terms, grad_decay * decay_rate, grad_skip), ('dp', 'ctx'))  75.3 us
    unnamed x1, blocking collectives  59.5 us
    rev x2, local copies, waits for them, and re-layouts, prefix(): pieces = jax.tree.map(lambda part: part[::-1], pieces)  44.2 us
  transfers between devices with their start and end apart: 5, of which 3 were waited for; matrix products, arithmetic and copies ran while one was open for 5% of the time, Pallas kernels for 0%

commit v1 on v0

v1 whole, which is shorter than its diff:
```python
import functools

import jax
import jax.numpy as jnp
from jax import lax
from jax.experimental import pallas as pl
from jax.experimental.pallas import tpu as pltpu
from jax.sharding import Mesh
from jax.sharding import PartitionSpec as P

HEADS = 64
HEAD_DIM = 64
GROUPS = 4
STATE = 128
TAPS = 4
T = 128
LANES = 128
WIDTH_X = HEADS * HEAD_DIM
GROUP_X = WIDTH_X // GROUPS
PAIRS = HEADS // 2
GROUP_PAIRS = PAIRS // GROUPS
GROUP_HEADS = HEADS // GROUPS
HALF_PAIRS = PAIRS // 2
F32 = jnp.float32
BF16 = jnp.bfloat16
EXACT = lax.Precision.HIGHEST
NT = (((1,), (1,)), ((), ()))
TN = (((0,), (0,)), ((), ()))


def dot(a, b, dims=None):
    if dims is None:
        dims = (((1,), (0,)), ((), ()))
    return lax.dot_general(a, b, dims, preferred_element_type=F32)


def exact_dot(a, b):
    return lax.dot_general(
        a, b, (((1,), (0,)), ((), ())), precision=EXACT, preferred_element_type=F32
    )


def iota(shape, dim):
    return lax.broadcasted_iota(jnp.int32, shape, dim)


def sigmoid(v):
    return 1.0 / (1.0 + jnp.exp(-v))


def split_two(v):
    high = v.astype(BF16)
    return high, (v - high.astype(F32)).astype(BF16)


def rates_kernel(raw_ref, head_ref, dt_ref, seg_ref, cols_ref, rise_ref, keep_ref, tot_ref, skip_ref, decay_ref):
    raw = raw_ref[...]
    dt = jnp.log1p(jnp.exp(raw))
    decay = -jnp.exp(head_ref[:, 0:1])
    upper = (iota((T, T), 0) <= iota((T, T), 1)).astype(F32)
    seg = exact_dot(dt * decay, upper)
    total = seg[:, T - 1 : T]
    dt_ref[...] = dt
    seg_ref[...] = seg
    cols_ref[...] = jnp.transpose(jnp.concatenate([seg, dt], axis=0))

    def stacked(v):
        high = v.astype(BF16).astype(F32)
        return jnp.transpose(jnp.concatenate([high, v - high], axis=0)).astype(BF16)

    rise_ref[...] = stacked(jnp.exp(seg))
    keep_ref[...] = stacked(jnp.exp(total - seg) * dt)
    first = iota((PAIRS, LANES), 1) < HEAD_DIM
    even = (iota((PAIRS, HEADS), 1) == 2 * iota((PAIRS, HEADS), 0)).astype(F32)
    odd = (iota((PAIRS, HEADS), 1) == 2 * iota((PAIRS, HEADS), 0) + 1).astype(F32)

    def paired(col):
        wide = jnp.broadcast_to(col, (HEADS, LANES))
        return jnp.where(first, exact_dot(even, wide), exact_dot(odd, wide))

    tot_ref[...] = paired(total)
    skip_ref[...] = paired(head_ref[:, 1:2])
    decay_ref[...] = jnp.broadcast_to(decay, (HEADS, LANES))


def run_rates(raw, head_cols):
    shapes = [
        ((HEADS, T), F32),
        ((HEADS, T), F32),
        ((T, 2 * HEADS), F32),
        ((T, 2 * HEADS), BF16),
        ((T, 2 * HEADS), BF16),
        ((PAIRS, LANES), F32),
        ((PAIRS, LANES), F32),
        ((HEADS, LANES), F32),
    ]
    return pl.pallas_call(
        rates_kernel,
        out_shape=[jax.ShapeDtypeStruct(s, d) for s, d in shapes],
        name="rates",
    )(raw, head_cols)


def fill_window(tok_ref, halo_ref, win_ref):
    width = tok_ref.shape[1]
    win_ref[5:8, :width] = halo_ref[...].astype(F32)
    win_ref[8 : 8 + T, :width] = tok_ref[...].astype(F32)


def pre_conv(win_ref, weight_ref, lo, width):
    acc = weight_ref[0:1, lo : lo + width] * win_ref[5 : 5 + T, lo : lo + width]
    for k in range(1, TAPS):
        acc = acc + weight_ref[k : k + 1, lo : lo + width] * win_ref[5 + k : 5 + k + T, lo : lo + width]
    return acc


def expander(pair):
    rows = iota((2 * HEADS, LANES), 0) % HEADS
    return (rows == 2 * pair + iota((2 * HEADS, LANES), 1) // HEAD_DIM).astype(F32).astype(BF16)


def enter_kernel(core_ref, tx_ref, tb_ref, tc_ref, hx_ref, hb_ref, hc_ref, wx_ref, wb_ref, wc_ref,
                 g_ref, rise_ref, keep_ref, x_ref, b_ref, c_ref, own_ref, out_ref, win_ref):
    j = pl.program_id(0)

    def mixed(tok_ref, halo_ref, weight_ref, dst_ref):
        fill_window(tok_ref, halo_ref, win_ref)
        width = tok_ref.shape[1]
        for lo in range(0, width, LANES):
            pre = pre_conv(win_ref, weight_ref, lo, LANES)
            dst_ref[:, lo : lo + LANES] = (pre * sigmoid(pre)).astype(BF16)

    mixed(tb_ref, hb_ref, wb_ref, b_ref)
    mixed(tc_ref, hc_ref, wc_ref, c_ref)
    mixed(tx_ref, hx_ref, wx_ref, x_ref)
    b_flip = jnp.transpose(b_ref[...].astype(F32)).astype(BF16)
    c_flip = jnp.transpose(c_ref[...].astype(F32)).astype(BF16)
    rise = rise_ref[...]
    keep = keep_ref[...]
    mine = (j // 2) == core_ref[0]

    def fill(dst_ref):
        for i in range(GROUP_PAIRS):
            cols = slice(i * LANES, (i + 1) * LANES)
            spread = expander(j * GROUP_PAIRS + i)
            xw = (x_ref[:, cols].astype(F32) * dot(keep, spread)).astype(BF16)
            gw = (g_ref[:, cols].astype(F32) * dot(rise, spread)).astype(BF16)
            dst_ref[0, i] = dot(b_flip, xw).astype(BF16)
            dst_ref[1, i] = dot(c_flip, gw).astype(BF16)

    @pl.when(mine)
    def _():
        fill(own_ref)

    @pl.when(jnp.logical_not(mine))
    def _():
        fill(out_ref)


def group_specs(rows, width_rows=None):
    del width_rows
    return [
        pl.BlockSpec((rows, GROUP_X), lambda j, c: (0, j)),
        pl.BlockSpec((rows, STATE), lambda j, c: (0, WIDTH_X // STATE + j)),
        pl.BlockSpec((rows, STATE), lambda j, c: (0, WIDTH_X // STATE + GROUPS + j)),
    ]


def whole(shape):
    return pl.BlockSpec(shape, lambda j, c: (0,) * len(shape))


def params(mib=48):
    return pltpu.CompilerParams(vmem_limit_bytes=mib << 20)


def run_enter(core, tokens, halo, weight, cot, rise, keep):
    half = (2, HALF_PAIRS, STATE, LANES)
    half_block = (2, GROUP_PAIRS, STATE, LANES)
    return pl.pallas_call(
        enter_kernel,
        grid_spec=pltpu.PrefetchScalarGridSpec(
            num_scalar_prefetch=1,
            grid=(GROUPS,),
            in_specs=group_specs(T) + group_specs(TAPS - 1) + group_specs(TAPS)
            + [pl.BlockSpec((T, GROUP_X), lambda j, c: (0, j)), whole((T, LANES)), whole((T, LANES))],
            out_specs=[
                pl.BlockSpec((T, GROUP_X), lambda j, c: (0, j)),
                pl.BlockSpec((T, STATE), lambda j, c: (0, j)),
                pl.BlockSpec((T, STATE), lambda j, c: (0, j)),
                pl.BlockSpec(half_block, lambda j, c: (0, jnp.clip(j - 2 * c[0], 0, 1), 0, 0)),
                pl.BlockSpec(half_block, lambda j, c: (0, jnp.clip(j - 2 * (1 - c[0]), 0, 1), 0, 0)),
            ],
            scratch_shapes=[pltpu.VMEM((8 + T, GROUP_X), F32)],
        ),
        out_shape=[
            jax.ShapeDtypeStruct((T, WIDTH_X), BF16),
            jax.ShapeDtypeStruct((T, GROUPS * STATE), BF16),
            jax.ShapeDtypeStruct((T, GROUPS * STATE), BF16),
            jax.ShapeDtypeStruct(half, BF16),
            jax.ShapeDtypeStruct(half, BF16),
        ],
        compiler_params=params(),
        name="enter",
    )(core, tokens, tokens, tokens, halo, halo, halo, weight, weight, weight, cot, rise, keep)


STEP_PAIRS = 4
PACK_ROWS = 2 * STATE + 16


def pack_kernel(core_ref, own_ref, got_ref, tot_ref, other_ref, out_ref):
    second = core_ref[0] == 1
    start = core_ref[0] * HALF_PAIRS + pl.program_id(0) * STEP_PAIRS
    for i in range(STEP_PAIRS):
        tot = tot_ref[pl.ds(start + i, 1), :]
        other = other_ref[pl.ds(start + i, 1), :]
        one = jnp.ones_like(tot)
        by_own = jnp.exp(tot)
        by_other = jnp.exp(other)
        state = (
            jnp.where(second, one, by_other) * own_ref[0, i].astype(F32)
            + jnp.where(second, by_own, one) * got_ref[0, i].astype(F32)
        )
        grad = (
            jnp.where(second, by_other, one) * own_ref[1, i].astype(F32)
            + jnp.where(second, one, by_own) * got_ref[1, i].astype(F32)
        )
        out_ref[i, 0:STATE, :] = state.astype(BF16)
        out_ref[i, STATE : 2 * STATE, :] = grad.astype(BF16)
        both = tot + other
        high = both.astype(BF16).astype(F32)
        mid = (both - high).astype(BF16).astype(F32)
        low = both - high - mid
        row = iota((16, LANES), 0)
        wide = jnp.where(row == 0, high, jnp.where(row == 1, mid, jnp.where(row == 2, low, 0.0)))
        out_ref[i, 2 * STATE : PACK_ROWS, :] = wide.astype(BF16)


def run_pack(core, own, got, tot, other):
    block = pl.BlockSpec((2, STEP_PAIRS, STATE, LANES), lambda j, c: (0, j, 0, 0))
    return pl.pallas_call(
        pack_kernel,
        grid_spec=pltpu.PrefetchScalarGridSpec(
            num_scalar_prefetch=1,
            grid=(HALF_PAIRS // STEP_PAIRS,),
            in_specs=[block, block, whole((PAIRS, LANES)), whole((PAIRS, LANES))],
            out_specs=pl.BlockSpec((STEP_PAIRS, PACK_ROWS, LANES), lambda j, c: (j, 0, 0)),
        ),
        out_shape=jax.ShapeDtypeStruct((HALF_PAIRS, PACK_ROWS, LANES), BF16),
        compiler_params=params(),
        name="pack",
    )(core, own, got, tot, other)


def chain_kernel(chips, per, in_ref, out_ref):
    for q in range(per):
        def decay(k):
            rows = in_ref[k * per + q, 2 * STATE : PACK_ROWS, :].astype(F32)
            return jnp.exp(rows[0:1] + rows[1:2] + rows[2:3])

        carry = jnp.zeros((STATE, LANES), F32)
        for k in range(chips):
            out_ref[k * per + q, 0:STATE, :] = carry.astype(BF16)
            if k < chips - 1:
                carry = decay(k) * carry + in_ref[k * per + q, 0:STATE, :].astype(F32)
        carry = jnp.zeros((STATE, LANES), F32)
        for k in reversed(range(chips)):
            out_ref[k * per + q, STATE : 2 * STATE, :] = carry.astype(BF16)
            if k > 0:
                carry = decay(k) * carry + in_ref[k * per + q, STATE : 2 * STATE, :].astype(F32)


def run_chain(chips, packed):
    return pl.pallas_call(
        functools.partial(chain_kernel, chips, HALF_PAIRS // chips),
        out_shape=jax.ShapeDtypeStruct((HALF_PAIRS, 2 * STATE, LANES), BF16),
        compiler_params=params(),
        name="chain",
    )(packed)


def unpack_kernel(core_ref, back_ref, own_ref, got_ref, tot_ref, other_ref, mine_ref, send_ref):
    second = core_ref[0] == 1
    start = core_ref[0] * HALF_PAIRS + pl.program_id(0) * STEP_PAIRS
    for i in range(STEP_PAIRS):
        tot = tot_ref[pl.ds(start + i, 1), :]
        other = other_ref[pl.ds(start + i, 1), :]
        decay_zero = jnp.exp(jnp.where(second, other, tot))
        decay_one = jnp.exp(jnp.where(second, tot, other))
        state_zero = back_ref[i, 0:STATE, :].astype(F32)
        grad_one = back_ref[i, STATE : 2 * STATE, :].astype(F32)
        left = jnp.where(second, got_ref[0, i].astype(F32), own_ref[0, i].astype(F32))
        right = jnp.where(second, own_ref[1, i].astype(F32), got_ref[1, i].astype(F32))
        state_one = decay_zero * state_zero + left
        grad_zero = decay_one * grad_one + right
        mine_ref[0, i] = jnp.where(second, state_one, state_zero).astype(BF16)
        mine_ref[1, i] = jnp.where(second, grad_one, grad_zero).astype(BF16)
        send_ref[0, i] = jnp.where(second, state_zero, state_one).astype(BF16)
        send_ref[1, i] = jnp.where(second, grad_zero, grad_one).astype(BF16)


def run_unpack(core, back, own, got, tot, other):
    block = pl.BlockSpec((2, STEP_PAIRS, STATE, LANES), lambda j, c: (0, j, 0, 0))
    half = jax.ShapeDtypeStruct((2, HALF_PAIRS, STATE, LANES), BF16)
    return pl.pallas_call(
        unpack_kernel,
        grid_spec=pltpu.PrefetchScalarGridSpec(
            num_scalar_prefetch=1,
            grid=(HALF_PAIRS // STEP_PAIRS,),
            in_specs=[
                pl.BlockSpec((STEP_PAIRS, 2 * STATE, LANES), lambda j, c: (j, 0, 0)),
                block,
                block,
                whole((PAIRS, LANES)),
                whole((PAIRS, LANES)),
            ],
            out_specs=[block, block],
        ),
        out_shape=[half, half],
        compiler_params=params(),
        name="unpack",
    )(core, back, own, got, tot, other)


def by_lane_half(v):
    first = iota(v.shape, 1) < HEAD_DIM
    wide = v.astype(F32)
    return jnp.concatenate(
        [jnp.where(first, wide, 0.0).astype(BF16), jnp.where(first, 0.0, wide).astype(BF16)], axis=0
    )


def inner_kernel(core_ref, x_ref, b_ref, c_ref, g_ref, seg_ref, dt_ref, cols_ref, y_ref, gb_ref, gc_ref):
    j = pl.program_id(0)
    b = b_ref[...]
    c = c_ref[...]
    scores = dot(c, b, NT)
    lower = iota((T, T), 0) >= iota((T, T), 1)
    cols = pltpu.roll(cols_ref[...], (LANES - j * GROUP_HEADS) % LANES, 1)
    total = jnp.zeros((T, T), F32)
    for i in range(GROUP_PAIRS):
        lanes = slice(i * LANES, (i + 1) * LANES)
        x = x_ref[:, lanes]
        g_two = by_lane_half(g_ref[:, lanes])
        inner = dot(g_two, x, NT)
        weights = []
        for k in range(2):
            h = 2 * i + k
            spread = cols[:, h : h + 1] - seg_ref[h : h + 1, :]
            kernel = jnp.exp(jnp.where(lower, spread, -1e30)) * dt_ref[h : h + 1, :]
            total = total + kernel * inner[k * T : (k + 1) * T]
            weights.append((kernel * scores).astype(BF16))
        y_ref[:, lanes] = dot(jnp.concatenate(weights, axis=1), by_lane_half(x))
    total = total.astype(BF16)
    gc_ref[...] = dot(total, b)
    gb_ref[...] = dot(jnp.transpose(total.astype(F32)).astype(BF16), c)


def run_inner(core, x, b, c, cot, seg, dt, cols):
    wide = pl.BlockSpec((T, GROUP_X), lambda j, c: (0, j))
    slim = pl.BlockSpec((T, STATE), lambda j, c: (0, j))
    heads = pl.BlockSpec((GROUP_HEADS, T), lambda j, c: (j, 0))
    return pl.pallas_call(
        inner_kernel,
        grid_spec=pltpu.PrefetchScalarGridSpec(
            num_scalar_prefetch=1,
            grid=(GROUPS,),
            in_specs=[wide, slim, slim, wide, heads, heads, whole((T, 2 * HEADS))],
            out_specs=[wide, slim, slim],
        ),
        out_shape=[
            jax.ShapeDtypeStruct((T, WIDTH_X), F32),
            jax.ShapeDtypeStruct((T, GROUPS * STATE), F32),
            jax.ShapeDtypeStruct((T, GROUPS * STATE), F32),
        ],
        compiler_params=params(),
        name="inner",
    )(core, x, b, c, cot, seg, dt, cols)


def slopes_kernel(core_ref, b_ref, c_ref, g_ref, seg_ref, dt_ref, cols_ref, tx_ref, tb_ref, tc_ref,
                  hx_ref, hb_ref, hc_ref, wx_ref, wb_ref, wc_ref, gx_ref, sx_ref, sb_ref, sc_ref, win_ref):
    j = pl.program_id(0)
    scores = jnp.transpose(dot(c_ref[...], b_ref[...], NT))
    upper = iota((T, T), 0) <= iota((T, T), 1)
    rolled = pltpu.roll(cols_ref[...], (LANES - j * GROUP_HEADS) % LANES, 1)
    for i in range(GROUP_PAIRS):
        lanes = slice(i * LANES, (i + 1) * LANES)
        weights = []
        for k in range(2):
            h = 2 * i + k
            spread = seg_ref[h : h + 1, :] - rolled[:, h : h + 1]
            kernel = jnp.exp(jnp.where(upper, spread, -1e30)) * rolled[:, HEADS + h : HEADS + h + 1]
            weights.append((kernel * scores).astype(BF16))
        gx_ref[:, lanes] = dot(jnp.concatenate(weights, axis=1), by_lane_half(g_ref[:, lanes]))

    def slope(tok_ref, halo_ref, weight_ref, dst_ref):
        fill_window(tok_ref, halo_ref, win_ref)
        for lo in range(0, tok_ref.shape[1], LANES):
            pre = pre_conv(win_ref, weight_ref, lo, LANES)
            s = sigmoid(pre)
            dst_ref[:, lo : lo + LANES] = s * (1.0 + pre * (1.0 - s))

    slope(tx_ref, hx_ref, wx_ref, sx_ref)
    slope(tb_ref, hb_ref, wb_ref, sb_ref)
    slope(tc_ref, hc_ref, wc_ref, sc_ref)


def run_slopes(core, b, c, cot, seg, dt, cols, tokens, halo, weight):
    wide = pl.BlockSpec((T, GROUP_X), lambda j, c: (0, j))
    slim = pl.BlockSpec((T, STATE), lambda j, c: (0, j))
    heads = pl.BlockSpec((GROUP_HEADS, T), lambda j, c: (j, 0))
    return pl.pallas_call(
        slopes_kernel,
        grid_spec=pltpu.PrefetchScalarGridSpec(
            num_scalar_prefetch=1,
            grid=(GROUPS,),
            in_specs=[slim, slim, wide, heads, heads, whole((T, 2 * HEADS))]
            + group_specs(T) + group_specs(TAPS - 1) + group_specs(TAPS),
            out_specs=[wide, wide, slim, slim],
            scratch_shapes=[pltpu.VMEM((8 + T, GROUP_X), F32)],
        ),
        out_shape=[
            jax.ShapeDtypeStruct((T, WIDTH_X), F32),
            jax.ShapeDtypeStruct((T, WIDTH_X), F32),
            jax.ShapeDtypeStruct((T, GROUPS * STATE), F32),
            jax.ShapeDtypeStruct((T, GROUPS * STATE), F32),
        ],
        compiler_params=params(),
        name="slopes",
    )(core, b, c, cot, seg, dt, cols, tokens, tokens, tokens, halo, halo, halo, weight, weight, weight)


SUM_ROWS = 256


def leave_kernel(core_ref, x_ref, b_ref, c_ref, g_ref, y_ref, gx_ref, gb_ref, gc_ref, sx_ref, sb_ref, sc_ref,
                 tx_ref, tb_ref, tc_ref, hx_ref, hb_ref, hc_ref, mine_ref, got_ref, rise_ref, keep_ref,
                 tot_ref, skip_ref, dt_ref, raw_ref, decay_ref,
                 out_ref, px_ref, pbc_ref, step_ref, sum_ref, win_ref):
    j = pl.program_id(0)
    mine = (j // 2) == core_ref[0]
    b = b_ref[...]
    c = c_ref[...]
    rise_all = rise_ref[...]
    keep_all = keep_ref[...]
    grad_b = gb_ref[...]
    grad_c = gc_ref[...]
    seg_grad = jnp.zeros((GROUP_HEADS, T), F32)
    dt_grad = jnp.zeros((GROUP_HEADS, T), F32)
    last = iota((T, LANES), 0) == T - 1
    skips = []
    terms = []
    fill_window(tx_ref, hx_ref, win_ref)

    def tap_sums(grad_pre, lo):
        return [
            jnp.sum(grad_pre * win_ref[5 + k : 5 + k + T, lo : lo + LANES], axis=0, keepdims=True)
            for k in range(TAPS)
        ]

    for i in range(GROUP_PAIRS):
        lanes = slice(i * LANES, (i + 1) * LANES)
        spread = expander(j * GROUP_PAIRS + i)
        rise = dot(rise_all, spread)
        keep = dot(keep_all, spread)
        state = jnp.where(mine, mine_ref[0, i].astype(F32), got_ref[0, i].astype(F32))
        exits = jnp.where(mine, mine_ref[1, i].astype(F32), got_ref[1, i].astype(F32))
        state_b = state.astype(BF16)
        exits_b = exits.astype(BF16)
        x = x_ref[:, lanes].astype(F32)
        g = g_ref[:, lanes].astype(F32)
        skip = skip_ref[i : i + 1, :]
        y = y_ref[:, lanes] + rise * dot(c, state_b)
        through = keep * dot(b, exits_b)
        gx = gx_ref[:, lanes] + through
        grad_c = grad_c + dot((g * rise).astype(BF16), state_b, NT)
        grad_b = grad_b + dot((x * keep).astype(BF16), exits_b, NT)
        out_ref[:, lanes] = (y + skip * x).astype(BF16)
        grad_pre = (gx + skip * g) * sx_ref[:, lanes]
        px_ref[:, lanes] = grad_pre
        terms += tap_sums(grad_pre, i * LANES)
        skips.append(jnp.sum(g * x, axis=0, keepdims=True))
        x_gx = x * gx
        end = jnp.sum(x * through, axis=0, keepdims=True) + jnp.exp(tot_ref[i : i + 1, :]) * jnp.sum(
            exits * state, axis=0, keepdims=True
        )
        moved = g * y - x_gx + jnp.where(last, end, 0.0)
        pick = (
            iota((GROUP_HEADS, LANES), 0) == 2 * i + iota((GROUP_HEADS, LANES), 1) // HEAD_DIM
        ).astype(F32).astype(BF16)
        for high_low in split_two(moved):
            seg_grad = seg_grad + dot(pick, high_low, NT)
        for high_low in split_two(x_gx):
            dt_grad = dt_grad + dot(pick, high_low, NT)

    sum_ref[pl.ds(pl.multiple_of(j * 32, 32), 32), :] = jnp.concatenate(terms, axis=0)
    terms = []
    for grad, slope_ref, tok_ref, halo_ref, base in (
        (grad_b, sb_ref, tb_ref, hb_ref, 0),
        (grad_c, sc_ref, tc_ref, hc_ref, GROUPS * STATE),
    ):
        fill_window(tok_ref, halo_ref, win_ref)
        grad_pre = grad * slope_ref[...]
        pbc_ref[:, pl.ds(pl.multiple_of(base + j * STATE, STATE), STATE)] = grad_pre
        terms += tap_sums(grad_pre, 0)
    sum_ref[pl.ds(pl.multiple_of(128 + j * 8, 8), 8), :] = jnp.concatenate(terms, axis=0)
    sum_ref[pl.ds(pl.multiple_of(160 + j * 8, 8), 8), :] = jnp.concatenate(skips, axis=0)

    lower = (iota((T, T), 0) >= iota((T, T), 1)).astype(F32)
    behind = exact_dot(seg_grad, lower)
    dt = dt_ref[...]
    decay = decay_ref[...]
    step_ref[...] = (dt_grad / dt + decay * behind) * sigmoid(raw_ref[...])
    sum_ref[pl.ds(pl.multiple_of(192 + j * 16, 16), 16), :] = dt * behind * decay


def run_leave(core, x, b, c, cot, y, gx, gb, gc, sx, sb, sc, tokens, halo, mine, got, rise, keep, tot, skip, dt, raw, decay):
    wide = pl.BlockSpec((T, GROUP_X), lambda j, c: (0, j))
    slim = pl.BlockSpec((T, STATE), lambda j, c: (0, j))
    heads = pl.BlockSpec((GROUP_HEADS, T), lambda j, c: (j, 0))
    pairs = pl.BlockSpec((GROUP_PAIRS, LANES), lambda j, c: (j, 0))
    half_block = (2, GROUP_PAIRS, STATE, LANES)
    return pl.pallas_call(
        leave_kernel,
        grid_spec=pltpu.PrefetchScalarGridSpec(
            num_scalar_prefetch=1,
            grid=(GROUPS,),
            in_specs=[wide, slim, slim, wide, wide, wide, slim, slim, wide, slim, slim]
            + group_specs(T) + group_specs(TAPS - 1)
            + [
                pl.BlockSpec(half_block, lambda j, c: (0, jnp.clip(j - 2 * c[0], 0, 1), 0, 0)),
                pl.BlockSpec(half_block, lambda j, c: (0, jnp.clip(j - 2 * (1 - c[0]), 0, 1), 0, 0)),
                whole((T, 2 * HEADS)),
                whole((T, 2 * HEADS)),
                pairs,
                pairs,
                heads,
                heads,
                heads,
            ],
            out_specs=[
                wide,
                wide,
                whole((T, 2 * GROUPS * STATE)),
                heads,
                whole((SUM_ROWS, LANES)),
            ],
            scratch_shapes=[pltpu.VMEM((8 + T, GROUP_X), F32)],
        ),
        out_shape=[
            jax.ShapeDtypeStruct((T, WIDTH_X), BF16),
            jax.ShapeDtypeStruct((T, WIDTH_X), F32),
            jax.ShapeDtypeStruct((T, 2 * GROUPS * STATE), F32),
            jax.ShapeDtypeStruct((HEADS, T), F32),
            jax.ShapeDtypeStruct((SUM_ROWS, LANES), F32),
        ],
        compiler_params=params(),
        name="leave",
    )(core, x, b, c, cot, y, gx, gb, gc, sx, sb, sc, tokens, tokens, tokens, halo, halo, halo,
      mine, got, rise, keep, tot, skip, dt, raw, decay)


def spread_kernel(px_ref, pbc_ref, halo_ref, weight_ref, out_ref, win_ref):
    is_x = pl.program_id(0) < GROUPS

    @pl.when(is_x)
    def _():
        win_ref[0:T, :] = px_ref[...]

    @pl.when(jnp.logical_not(is_x))
    def _():
        win_ref[0:T, :] = pbc_ref[...]

    win_ref[T : T + 3, :] = halo_ref[...].astype(F32)
    for lo in range(0, GROUP_X, LANES):
        cols = slice(lo, lo + LANES)
        acc = weight_ref[0:1, cols] * win_ref[3 : 3 + T, cols]
        for k in range(1, TAPS):
            acc = acc + weight_ref[k : k + 1, cols] * win_ref[3 - k : 3 - k + T, cols]
        out_ref[:, cols] = acc.astype(BF16)


def run_spread(px, pbc, halo, weight):
    return pl.pallas_call(
        spread_kernel,
        grid=(GROUPS + 1,),
        in_specs=[
            pl.BlockSpec((T, GROUP_X), lambda j: (0, jnp.minimum(j, GROUPS - 1))),
            pl.BlockSpec((T, GROUP_X), lambda j: (0, 0)),
            pl.BlockSpec((TAPS - 1, GROUP_X), lambda j: (0, j)),
            pl.BlockSpec((TAPS, GROUP_X), lambda j: (0, j)),
        ],
        out_specs=pl.BlockSpec((T, GROUP_X), lambda j: (0, j)),
        out_shape=jax.ShapeDtypeStruct((T, WIDTH_X + 2 * GROUPS * STATE), BF16),
        scratch_shapes=[pltpu.VMEM((T + 8, GROUP_X), F32)],
        compiler_params=params(),
        name="spread",
    )(px, pbc, halo, weight)


CTX = ("chip", "core")
ALL = ("dp", "chip", "core")


def all_to_all(value, axis):
    return lax.all_to_all(value, axis, 0, 0, tiled=True)


def local(conv_input, conv_weight, step_raw, decay_log, skip_gain, cotangent):
    chips = lax.axis_size("chip")
    devices = 2 * chips
    tokens = conv_input[0]
    raw = step_raw[0]
    cot = cotangent[0]
    core = lax.axis_index("core").astype(jnp.int32).reshape(1)
    swap = [(0, 1), (1, 0)]
    halo = lax.ppermute(tokens[T - TAPS + 1 :], CTX, [(i, i + 1) for i in range(devices - 1)])
    dt, seg, cols, rise, keep, tot, skip, decay = run_rates(raw, jnp.stack([decay_log, skip_gain], axis=1))
    tot_other = lax.ppermute(tot, "core", swap)
    x, b, c, own, out = run_enter(core, tokens, halo, conv_weight, cot, rise, keep)
    got = lax.ppermute(out, "core", swap)
    packed = run_pack(core, own, got, tot, tot_other)
    chained = run_chain(chips, all_to_all(packed, "chip"))
    y, gb, gc = run_inner(core, x, b, c, cot, seg, dt, cols)
    back = all_to_all(chained, "chip")
    late_b, late_c, _ = lax.optimization_barrier((b, c, chained))
    gx, sx, sb, sc = run_slopes(core, late_b, late_c, cot, seg, dt, cols, tokens, halo, conv_weight)
    mine, send = run_unpack(core, back, own, got, tot, tot_other)
    theirs = lax.ppermute(send, "core", swap)
    out_tokens, px, pbc, grad_step, sums = run_leave(
        core, x, b, c, cot, y, gx, gb, gc, sx, sb, sc, tokens, halo, mine, theirs, rise, keep, tot, skip, dt, raw, decay
    )
    first = jnp.concatenate([px[: TAPS - 1], pbc[: TAPS - 1]], axis=1).astype(BF16)
    after = lax.ppermute(first, CTX, [(i + 1, i) for i in range(devices - 1)])
    count = lax.axis_size("dp") * devices
    shares = all_to_all(sums, ALL).reshape(count, SUM_ROWS // count, LANES)
    share = jnp.sum(shares, axis=0)
    total = all_to_all(jnp.broadcast_to(share[None], shares.shape).reshape(SUM_ROWS, LANES), ALL)
    grad_tokens = run_spread(px, pbc, after, conv_weight)
    conv_x = total[:128].reshape(PAIRS, TAPS, LANES)
    conv_bc = total[128:160].reshape(GROUPS, 2, TAPS, LANES)
    grad_conv = jnp.concatenate([conv_x, conv_bc[:, 0], conv_bc[:, 1]], axis=0)
    grad_conv = jnp.swapaxes(grad_conv, 0, 1).reshape(TAPS, WIDTH_X + 2 * GROUPS * STATE)
    grad_skip = jnp.sum(total[160:192].reshape(HEADS, HEAD_DIM), axis=1)
    grad_decay = jnp.sum(total[192:256], axis=1)
    return (
        out_tokens[None],
        grad_tokens[None],
        grad_step[None],
        grad_conv,
        grad_decay,
        grad_skip,
    )


def solution(mesh):
    dp, ctx = mesh.devices.shape
    fine = Mesh(mesh.devices.reshape(dp, ctx // 2, 2), ALL)
    seq = P("dp", CTX, None)
    rate = P("dp", None, CTX)
    in_specs = (seq, P(), rate, P(), P(), seq)
    out_specs = (seq, seq, rate, P(), P(), P())
    return jax.shard_map(local, mesh=fine, in_specs=in_specs, out_specs=out_specs, check_vma=False)
```

time: 1100 us -> 146 us (0.13); the launches traced: 1090 us -> 143 us
  waiting for transfers between devices: 471 us -> 17.8 us
  other arithmetic: 280 us -> 3.34 us
  local copies, waits for them, and re-layouts: 108 us -> 12.3 us
  blocking collectives: 135 us -> 42.1 us
  matrix products: 68.3 us -> 0 us
  Pallas kernels: 0 us -> 40.2 us
  starting transfers between devices: 5.23 us -> 26.7 us
  between operations: 17.2 us -> 0.89 us
    all_gather x2 -> x0, waiting for transfers between devices: 328 us -> none  [prefix(): pieces = jax.tree.map(lambda part: lax.all_gather(part, axis), value)]
    select_n x62 -> x0, other arithmetic: 186 us -> none  [step(): jnp.where(position < mine, new, old)]
    psum x1 -> x0, waiting for transfers between devices: 144 us -> none  [local(): lax.psum((conv_terms, grad_decay * decay_rate, grad_skip), ('dp', 'ctx'))]
    psum x1 -> x0, blocking collectives: 75.3 us -> none  [local(): lax.psum((conv_terms, grad_decay * decay_rate, grad_skip), ('dp', 'ctx'))]
    dot_general x55 -> x0, matrix products: 68.3 us -> none  [the longest x12 21.7 us: advance(): jnp.einsum('hts,shp->thp', kernel * scores[None], x_part, precision=split...]
    unnamed x1 -> x0, blocking collectives: 59.5 us -> none
    rev x2 -> x0, local copies, waits for them, and re-layouts: 44.2 us -> none  [prefix(): pieces = jax.tree.map(lambda part: part[::-1], pieces)]
    all_to_all x0 -> x2, blocking collectives: none -> 42.1 us  [all_to_all(): return lax.all_to_all(value, axis, 0, 0, tiled=True)]
  transfers between devices with their start and end apart: 5 -> 7, of which waited for: 3 -> 5; matrix products, arithmetic and copies ran while one was open for 5% -> 2% of each run, Pallas kernels for 0% -> 11%
where the time goes in v1:
time: 146 us; the launch traced here: 143 us
  blocking collectives  42.1 us (29%)
  Pallas kernels  40.2 us (28%)
  starting transfers between devices  26.7 us (18%)
  waiting for transfers between devices  17.8 us (12%)
  local copies, waits for them, and re-layouts  12.3 us (8%)
  other arithmetic  3.34 us (2%)
    all_to_all x2, blocking collectives, all_to_all(): return lax.all_to_all(value, axis, 0, 0, tiled=True)  42.1 us
    all_to_all x2, starting transfers between devices, all_to_all(): return lax.all_to_all(value, axis, 0, 0, tiled=True)  19.5 us
    pallas_call x1, Pallas kernels, run_leave(): pl.pallas_call(leave_kernel, grid_spec=pltpu.PrefetchScalarGridSpec(num_s...  12.9 us
    all_to_all x2, waiting for transfers between devices, all_to_all(): return lax.all_to_all(value, axis, 0, 0, tiled=True)  11.9 us
    pallas_call x1, Pallas kernels, run_enter(): pl.pallas_call(enter_kernel, grid_spec=pltpu.PrefetchScalarGridSpec(num_s...  9.39 us
    unnamed x42, local copies, waits for them, and re-layouts  8.95 us
    pallas_call x1, Pallas kernels, run_slopes(): pl.pallas_call(slopes_kernel, grid_spec=pltpu.PrefetchScalarGridSpec(num_...  7.09 us
    ppermute x1, starting transfers between devices, local(): after = lax.ppermute(first, CTX, [(i + 1, i) for i in range(devices - 1)])  4.52 us
  transfers between devices with their start and end apart: 7, of which 5 were waited for; matrix products, arithmetic and copies ran while one was open for 2% of the time, Pallas kernels for 11%

profile of v1, /device:TPU:2, one launch (start us, length us, event | category | flops | bytes accessed | tf_op | source)
XLA Modules:
  0.0 143.3 jit_solution(13115612425565647102)
XLA Ops:
  0.6 0.9 slice_bitcast_fusion
  1.5 1.9 %collective-permute-start = (bf16[3,5120]{1,0:T(4,128)(2,1)S(1)}, bf16[3,5120]{1,0:T(4,128)(2,1)S(1)}, u32[]{:S(2)}, u32[]{:S(2)}) collective-permute-start(bf16[3,5120]{1,0:T(4,128)(2,1)S(1)} %slice_bitcast_fusion), channel_id=1, source_target_pairs={{0,1},{1,2},{2,3},{3,4},{4,5},{5,6},{6,7},{7,8},{8,9},{9,10},{10,1... | collective-permute-start | bytes 92168 | tf_op jit(solution)/shard_map/ppermute | solution.py:619
  3.5 0.7 pad_maximum_fusion.1
  4.2 0.7 copy.18.head_ref
  4.9 2.0 %rates.1 = (f32[64,128]{1,0:T(8,128)}, f32[64,128]{1,0:T(8,128)}, f32[128,128]{1,0:T(8,128)}, bf16[128,128]{1,0:T(8,128)(2,1)}, bf16[128,128]{1,0:T(8,128)(2,1)}...) custom-call(f32[64,128]{1,0:T(8,128)} %bitcast.42, f32[64,2]{1,0:T(8,128)} %copy.18.head_ref), custom_call_target="tpu_custom_call" | custom-call | tf_op jit(solution)/shard_map/rates/pallas_call | solution.py:97
  6.9 2.1 %collective-permute-done.hx_ref.hb_ref.hc_ref = bf16[3,5120]{1,0:T(4,128)(2,1)S(1)} collective-permute-done((bf16[3,5120]{1,0:T(4,128)(2,1)S(1)}, bf16[3,5120]{1,0:T(4,128)(2,1)S(1)}, u32[]{:S(2)}, u32[]{:S(2)}) %collective-permute-start) | collective-permute-done | bytes 30752 | tf_op jit(solution)/shard_map/ppermute | solution.py:619
  9.0 1.3 copy-done
  10.3 1.2 copy-done.2
  11.5 0.9 copy-done.4
  12.4 0.8 copy-done.12
  13.2 0.8 copy-done.14
  13.9 9.4 %enter.1 = (bf16[128,4096]{1,0:T(8,128)(2,1)S(1)}, bf16[128,512]{1,0:T(8,128)(2,1)S(1)}, bf16[128,512]{1,0:T(8,128)(2,1)S(1)}, bf16[2,16,128,128]{3,2,1,0:T(8,128)(2,1)S(1)}, bf16[2,16,128,128]{3,2,1,0:T(8,128)(2,1)S(1)}) custom-call(s32[1]{0:T(128)} %bitcast.core_ref, bf16[128,5120]{1,0:T(8,128)(2,1)S(1)} %bitcast.32, bf16[128,5120]{1,0:T(8,128)(2,1)S(1)} %bitcast.33, ...), custom_call_target="tpu_custom_call" | custom-call | tf_op jit(solution)/shard_map/enter/pallas_call | solution.py:180
  23.3 0.1 collective-permute-start.1
  23.4 0.5 collective-permute-start.2
  23.9 2.2 %collective-permute-done.2.other_ref = f32[32,128]{1,0:T(8,128)S(1)} collective-permute-done((f32[32,128]{1,0:T(8,128)S(1)}, f32[32,128]{1,0:T(8,128)S(1)}, u32[]{:S(2)}, u32[]{:S(2)}) %collective-permute-start.2) | collective-permute-done | bytes 16416 | tf_op jit(solution)/shard_map/ppermute | solution.py:621
  26.1 0.0 collective-permute-done.1.got_ref
  26.1 0.7 pack.1
  26.8 23.1 %all_to_all.25.in_ref = bf16[16,272,128]{2,1,0:T(8,128)(2,1)S(1)} all-to-all(bf16[16,272,128]{2,1,0:T(8,128)(2,1)S(1)} %pack.1), channel_id=1, replica_groups=mesh['dp'=8,'chip'=16,'core'=2] {'chip'}, dimensions={0} | all-to-all | bytes 2228224 | tf_op jit(solution)/shard_map/all_to_all | solution.py:608
  50.0 0.3 chain.1
  50.3 18.9 %all_to_all.26.back_ref = bf16[16,256,128]{2,1,0:T(8,128)(2,1)S(1)} all-to-all(bf16[16,256,128]{2,1,0:T(8,128)(2,1)S(1)} %chain.1), channel_id=1, replica_groups=mesh['dp'=8,'chip'=16,'core'=2] {'chip'}, dimensions={0} | all-to-all | bytes 2097152 | tf_op jit(solution)/shard_map/all_to_all | solution.py:608
  69.2 1.0 unpack.1
  70.3 0.0 copy-start.1
  70.3 0.0 copy-start.5
  70.3 0.1 collective-permute-start.3
  70.4 0.0 copy-done.3
  70.4 0.0 copy-done.9
  70.4 3.3 %inner.1 = (f32[128,4096]{1,0:T(8,128)S(1)}, f32[128,512]{1,0:T(8,128)S(1)}, f32[128,512]{1,0:T(8,128)S(1)}) custom-call(s32[1]{0:T(128)} %bitcast.core_ref, bf16[128,4096]{1,0:T(8,128)(2,1)S(1)} %get-tuple-element.37.x_ref, bf16[128,512]{1,0:T(8,128)(2,1)S(1)} %get-tuple-element.47.b_ref, bf16[128,512]{1,0:T(8,128)(2,1)S(1)} %get-tuple-element.48.c_ref, ...), custom_call_target="tpu_custom_call" | custom-call | tf_op jit(solution)/shard_map/inner/pallas_call | solution.py:364
  73.8 0.0 copy-start.17
  73.8 7.1 %slopes.1 = (f32[128,4096]{1,0:T(8,128)S(1)}, f32[128,4096]{1,0:T(8,128)}, f32[128,512]{1,0:T(8,128)S(1)}, f32[128,512]{1,0:T(8,128)S(1)}) custom-call(s32[1]{0:T(128)} %bitcast.core_ref, bf16[128,512]{1,0:T(8,128)(2,1)S(1)} %get-tuple-element.47.b_ref, bf16[128,512]{1,0:T(8,128)(2,1)S(1)} %get-tuple-element.48.c_ref, bf16[128,4096]{1,0:T(8,128)(2,1)S(1)} %bitcast.40, ...), custom_call_target="tpu_custom_call" | custom-call | tf_op jit(solution)/shard_map/slopes/pallas_call | solution.py:414
  80.9 1.3 copy-done.8
  82.3 0.0 collective-permute-done.3.got_ref
  82.3 1.0 copy-done.20
  83.3 12.9 %leave.1 = (bf16[128,4096]{1,0:T(8,128)(2,1)}, f32[128,4096]{1,0:T(8,128)}, f32[128,1024]{1,0:T(8,128)S(1)}, f32[64,128]{1,0:T(8,128)}, f32[256,128]{1,0:T(8,128)}) custom-call(s32[1]{0:T(128)} %bitcast.core_ref, bf16[128,4096]{1,0:T(8,128)(2,1)S(1)} %get-tuple-element.37.x_ref, bf16[128,512]{1,0:T(8,128)(2,1)S(1)} %get-tuple-element.47.b_ref, ...), custom_call_target="tpu_custom_call" | custom-call | tf_op jit(solution)/shard_map/leave/pallas_call | solution.py:525
  96.1 13.1 %all-to-all-start.2 = ((f32[256,1,128]{2,1,0:T(1,128)}), f32[256,1,128]{2,1,0:T(1,128)S(1)}, u32[]{:S(2)}, u32[]{:S(2)}) async-start(f32[256,1,128]{2,1,0:T(1,128)} %bitcast.11), calls=%async_computation.2 | async-start | bytes 262144 | tf_op jit(solution)/shard_map/all_to_all | solution.py:608
  109.2 0.9 slice.61
  110.1 11.1 %all-to-all-done.2 = f32[256,1,128]{2,1,0:T(1,128)S(1)} async-done(((f32[256,1,128]{2,1,0:T(1,128)}), f32[256,1,128]{2,1,0:T(1,128)S(1)}, u32[]{:S(2)}, u32[]{:S(2)}) %all-to-all-start.2) | async-done | bytes 131104 | tf_op jit(solution)/shard_map/all_to_all | solution.py:608
  121.2 0.3 reduce_sum.27
  121.5 0.7 reshape.52
  122.2 6.5 %all-to-all-start.3 = ((f32[256,1,128]{2,1,0:T(1,128)}), f32[256,1,128]{2,1,0:T(1,128)S(1)}, u32[]{:S(2)}, u32[]{:S(2)}) async-start(f32[256,1,128]{2,1,0:T(1,128)} %reshape.52), calls=%async_computation.3 | async-start | bytes 262144 | tf_op jit(solution)/shard_map/all_to_all | solution.py:608
  128.7 4.5 %collective-permute-start.4 = (bf16[3,5120]{1,0:T(4,128)(2,1)S(1)}, bf16[3,5120]{1,0:T(4,128)(2,1)S(1)}, u32[]{:S(2)}, u32[]{:S(2)}) collective-permute-start(bf16[3,5120]{1,0:T(4,128)(2,1)S(1)} %pad_maximum_fusion), channel_id=1, source_target_pairs={{1,0},{2,1},{3,2},{4,3},{5,4},{6,5},{7,6},{8,7},{9,8},{10,9},{11,1... | collective-permute-start | bytes 92168 | tf_op jit(solution)/shard_map/ppermute | solution.py:636
  133.2 1.7 %collective-permute-done.4.halo_ref = bf16[3,5120]{1,0:T(4,128)(2,1)S(1)} collective-permute-done((bf16[3,5120]{1,0:T(4,128)(2,1)S(1)}, bf16[3,5120]{1,0:T(4,128)(2,1)S(1)}, u32[]{:S(2)}, u32[]{:S(2)}) %collective-permute-start.4) | collective-permute-done | bytes 30752 | tf_op jit(solution)/shard_map/ppermute | solution.py:636
  134.9 1.6 %copy-done.6 = f32[128,4096]{1,0:T(8,128)S(1)} copy-done((f32[128,4096]{1,0:T(8,128)S(1)}, f32[128,4096]{1,0:T(8,128)}, u32[]{:S(2)}) %copy-start.6) | copy-done | bytes 2097176
  136.5 3.5 %spread.1 = bf16[128,5120]{1,0:T(8,128)(2,1)} custom-call(f32[128,4096]{1,0:T(8,128)S(1)} %copy-done.6, f32[128,1024]{1,0:T(8,128)S(1)} %get-tuple-element.61.pbc_ref, bf16[3,5120]{1,0:T(4,128)(2,1)S(1)} %collective-permute-done.4.halo_ref, f32[4,5120]{1,0:T(4,128)S(1)} %copy-done.5), custom_call_target="tpu_custom_call" | custom-call | tf_op jit(solution)/shard_map/spread/pallas_call | solution.py:586
  140.0 0.8 all-to-all-done.3
  140.9 0.1 reshape.56
  141.0 0.6 reduce_sum.29
  141.6 0.7 maximum_bitcast_fusion
  142.3 1.1 slice_reduce_fusion
  (35 shorter events, 0.1 us)
Async XLA Ops:
  1.5 7.4 %collective-permute-start = (bf16[3,5120]{1,0:T(4,128)(2,1)S(1)}, bf16[3,5120]{1,0:T(4,128)(2,1)S(1)}, u32[]{:S(2)}, u32[]{:S(2)}) collective-permute-start(bf16[3,5120]{1,0:T(4,128)(2,1)S(1)} %slice_bitcast_fusion), channel_id=1, source_target_pairs={{0,1},{1,2},{2,3},{3,4},{4,5},{5,6},{6,7},{7,8},{8,9},{9,10},{10,1... | collective-permute-start | bytes 92168 | tf_op jit(solution)/shard_map/ppermute | solution.py:619
  9.0 1.3 copy-start
  10.3 1.2 copy-start.2
  11.5 0.9 copy-start.4
  12.4 0.8 copy-start.12
  13.2 0.8 copy-start.14
  13.9 9.5 %copy-start.11 = (f32[32,128]{1,0:T(8,128)S(1)}, f32[32,128]{1,0:T(8,128)}, u32[]{:S(2)}) copy-start(f32[32,128]{1,0:T(8,128)} %get-tuple-element.46.tot_ref) | copy-start | bytes 49156
  23.3 2.8 %collective-permute-start.1 = (bf16[2,16,128,128]{3,2,1,0:T(8,128)(2,1)S(1)}, bf16[2,16,128,128]{3,2,1,0:T(8,128)(2,1)S(1)}, u32[]{:S(2)}, u32[]{:S(2)}) collective-permute-start(bf16[2,16,128,128]{3,2,1,0:T(8,128)(2,1)S(1)} %get-tuple-element.45), channel_id=1, source_target_pairs={{0,1},{1,0},{2,3},{3,2},{4,5},{5,4},{6,7},{7,6},{8,9},{9,8},{10,11... | collective-permute-start | bytes 3145736 | tf_op jit(solution)/shard_map/ppermute | solution.py:623
  23.4 2.7 %collective-permute-start.2 = (f32[32,128]{1,0:T(8,128)S(1)}, f32[32,128]{1,0:T(8,128)S(1)}, u32[]{:S(2)}, u32[]{:S(2)}) collective-permute-start(f32[32,128]{1,0:T(8,128)S(1)} %copy-done.11), channel_id=1, source_target_pairs={{0,1},{1,0},{2,3},{3,2},{4,5},{5,4},{6,7},{7,6},{8,9},{9,8},{10,11... | collective-permute-start | bytes 49160 | tf_op jit(solution)/shard_map/ppermute | solution.py:621
  69.2 1.2 copy-start.3
  69.2 1.2 copy-start.9
  69.2 1.2 copy-start.10
  69.2 1.2 copy-start.16
  70.3 3.5 %copy-start.1 = (bf16[1,128,5120]{2,1,0:T(8,128)(2,1)S(1)}, bf16[1,128,5120]{2,1,0:T(8,128)(2,1)}, u32[]{:S(2)}) copy-start(bf16[1,128,5120]{2,1,0:T(8,128)(2,1)} %param.6) | copy-start | bytes 3932164
  70.3 3.5 %copy-start.5 = (f32[4,5120]{1,0:T(4,128)S(1)}, f32[4,5120]{1,0:T(4,128)}, u32[]{:S(2)}) copy-start(f32[4,5120]{1,0:T(4,128)} %weight_ref.1) | copy-start | bytes 245764
  70.3 12.0 %collective-permute-start.3 = (bf16[2,16,128,128]{3,2,1,0:T(8,128)(2,1)S(1)}, bf16[2,16,128,128]{3,2,1,0:T(8,128)(2,1)S(1)}, u32[]{:S(2)}, u32[]{:S(2)}) collective-permute-start(bf16[2,16,128,128]{3,2,1,0:T(8,128)(2,1)S(1)} %get-tuple-element.56), channel_id=1, source_target_pairs={{0,1},{1,0},{2,3},{3,2},{4,5},{5,4},{6,7},{7,6},{8,9},{9,8},{10,11... | collective-permute-start | bytes 3145736 | tf_op jit(solution)/shard_map/ppermute | solution.py:631
  73.8 7.2 %copy-start.7 = (f32[128,4096]{1,0:T(8,128)}, f32[128,4096]{1,0:T(8,128)S(1)}, u32[]{:S(2)}) copy-start(f32[128,4096]{1,0:T(8,128)S(1)} %get-tuple-element.43.y_ref) | copy-start | bytes 6291460
  73.8 9.5 %copy-start.13 = (bf16[128,128]{1,0:T(8,128)(2,1)S(1)}, bf16[128,128]{1,0:T(8,128)(2,1)}, u32[]{:S(2)}) copy-start(bf16[128,128]{1,0:T(8,128)(2,1)} %get-tuple-element.35.rise_ref) | copy-start | bytes 98308
  73.8 9.5 %copy-start.15 = (bf16[128,128]{1,0:T(8,128)(2,1)S(1)}, bf16[128,128]{1,0:T(8,128)(2,1)}, u32[]{:S(2)}) copy-start(bf16[128,128]{1,0:T(8,128)(2,1)} %get-tuple-element.36.keep_ref) | copy-start | bytes 98308
  73.8 9.5 %copy-start.17 = (f32[1,64,128]{2,1,0:T(8,128)S(1)}, f32[1,64,128]{2,1,0:T(8,128)}, u32[]{:S(2)}) copy-start(f32[1,64,128]{2,1,0:T(8,128)} %param.8) | copy-start | bytes 98308
  73.8 9.4 %copy-start.18 = (f32[64,128]{1,0:T(8,128)S(1)}, f32[64,128]{1,0:T(8,128)}, u32[]{:S(2)}) copy-start(f32[64,128]{1,0:T(8,128)} %get-tuple-element.58.decay_ref) | copy-start | bytes 98308
  73.8 9.4 %copy-start.19 = (f32[32,128]{1,0:T(8,128)S(1)}, f32[32,128]{1,0:T(8,128)}, u32[]{:S(2)}) copy-start(f32[32,128]{1,0:T(8,128)} %get-tuple-element.57.skip_ref) | copy-start | bytes 49156
  80.9 1.3 copy-start.8
  82.3 1.0 copy-start.20
  96.1 25.1 %all-to-all-start.2 = ((f32[256,1,128]{2,1,0:T(1,128)}), f32[256,1,128]{2,1,0:T(1,128)S(1)}, u32[]{:S(2)}, u32[]{:S(2)}) async-start(f32[256,1,128]{2,1,0:T(1,128)} %bitcast.11), calls=%async_computation.2 | async-start | bytes 262144 | tf_op jit(solution)/shard_map/all_to_all | solution.py:608
  122.2 18.6 %all-to-all-start.3 = ((f32[256,1,128]{2,1,0:T(1,128)}), f32[256,1,128]{2,1,0:T(1,128)S(1)}, u32[]{:S(2)}, u32[]{:S(2)}) async-start(f32[256,1,128]{2,1,0:T(1,128)} %reshape.52), calls=%async_computation.3 | async-start | bytes 262144 | tf_op jit(solution)/shard_map/all_to_all | solution.py:608
  128.7 6.2 %collective-permute-start.4 = (bf16[3,5120]{1,0:T(4,128)(2,1)S(1)}, bf16[3,5120]{1,0:T(4,128)(2,1)S(1)}, u32[]{:S(2)}, u32[]{:S(2)}) collective-permute-start(bf16[3,5120]{1,0:T(4,128)(2,1)S(1)} %pad_maximum_fusion), channel_id=1, source_target_pairs={{1,0},{2,1},{3,2},{4,3},{5,4},{6,5},{7,6},{8,7},{9,8},{10,9},{11,1... | collective-permute-start | bytes 92168 | tf_op jit(solution)/shard_map/ppermute | solution.py:636
  134.9 1.6 %copy-start.6 = (f32[128,4096]{1,0:T(8,128)S(1)}, f32[128,4096]{1,0:T(8,128)}, u32[]{:S(2)}) copy-start(f32[128,4096]{1,0:T(8,128)} %get-tuple-element.60.px_ref) | copy-start | bytes 6291460

commit v2 on v0

v2 whole, which is shorter than its diff:
```python
import functools

import jax
import jax.numpy as jnp
from jax import lax
from jax.experimental import pallas as pl
from jax.experimental.pallas import tpu as pltpu
from jax.sharding import Mesh
from jax.sharding import PartitionSpec as P

HEADS = 64
HEAD_DIM = 64
GROUPS = 4
STATE = 128
TAPS = 4
T = 128
LANES = 128
WIDTH_X = HEADS * HEAD_DIM
WIDTH_B = GROUPS * STATE
CHANNELS = WIDTH_X + 2 * WIDTH_B
GROUP_X = WIDTH_X // GROUPS
PAIRS = HEADS // 2
GROUP_PAIRS = PAIRS // GROUPS
GROUP_HEADS = HEADS // GROUPS
HALF_PAIRS = PAIRS // 2
HALF_GROUPS = GROUPS // 2
F32 = jnp.float32
BF16 = jnp.bfloat16
EXACT = lax.Precision.HIGHEST
NN = (((1,), (0,)), ((), ()))
NT = (((1,), (1,)), ((), ()))
SUM_ROWS = 256
PACK_ROWS = 2 * STATE + 16


def dot(a, b, dims=NN):
    return lax.dot_general(a, b, dims, preferred_element_type=F32)


def exact_dot(a, b, dims=NN):
    return lax.dot_general(a, b, dims, precision=EXACT, preferred_element_type=F32)


def iota(shape, dim):
    return lax.broadcasted_iota(jnp.int32, shape, dim)


def sigmoid(v):
    return 0.5 + 0.5 * jnp.tanh(0.5 * v)


def split_two(v):
    high = v.astype(BF16)
    return high, (v - high.astype(F32)).astype(BF16)


def span(index, size):
    return pl.ds(pl.multiple_of(index * size, size), size)


def call(kernel, name, out_shape, specs, micros, scratch=(), mib=28):
    cost = pl.CostEstimate(
        flops=int(micros * 1e9), transcendentals=0, bytes_accessed=int(micros * 3.6e6)
    )
    places = {
        "s": pl.BlockSpec(memory_space=pltpu.SMEM),
        "v": pl.BlockSpec(memory_space=pltpu.VMEM),
        "h": pl.BlockSpec(memory_space=pltpu.HBM),
    }
    return pl.pallas_call(
        kernel,
        out_shape=[jax.ShapeDtypeStruct(s, d) for s, d in out_shape],
        in_specs=[places[p] for p in specs],
        out_specs=[places["v"]] * len(out_shape),
        scratch_shapes=list(scratch),
        cost_estimate=cost,
        compiler_params=pltpu.CompilerParams(vmem_limit_bytes=mib << 20),
        name=name,
    )


def fill_window(win_ref, tokens, halo):
    width = tokens.shape[1]
    win_ref[5:8, :width] = halo.astype(F32)
    win_ref[8 : 8 + T, :width] = tokens.astype(F32)


def pre_conv(win_ref, weights, lo):
    cols = slice(lo, lo + LANES)
    acc = weights[0:1, cols] * win_ref[5 : 5 + T, cols]
    for k in range(1, TAPS):
        acc = acc + weights[k : k + 1, cols] * win_ref[5 + k : 5 + k + T, cols]
    return acc


BLOCKS = CHANNELS // GROUP_X


def begin_kernel(raw_ref, decay_log_ref, skip_gain_ref, tok_ref, weight_ref,
                 dt_ref, seg_ref, cols_ref, scale_ref, tot_ref, skip_ref, decay_ref,
                 x_ref, bc_ref, head_ref, hold_ref, win_ref, sems):
    copies = [
        pltpu.make_async_copy(
            tok_ref.at[:, pl.ds(i * GROUP_X, GROUP_X)],
            hold_ref.at[:, pl.ds(i * GROUP_X, GROUP_X)],
            sems.at[i],
        )
        for i in range(BLOCKS)
    ]
    for copy in copies:
        copy.start()
    diagonal = iota((HEADS, HEADS), 0) == iota((HEADS, HEADS), 1)

    def column(row):
        return jnp.sum(jnp.where(diagonal, row, 0.0), axis=1, keepdims=True)

    raw = raw_ref[...]
    dt = jnp.log1p(jnp.exp(raw))
    decay = -jnp.exp(column(decay_log_ref[...]))
    upper = (iota((T, T), 0) <= iota((T, T), 1)).astype(F32)
    seg = exact_dot(dt * decay, upper)
    total = seg[:, T - 1 : T]
    dt_ref[...] = dt
    seg_ref[...] = seg
    cols_ref[...] = jnp.transpose(jnp.concatenate([seg, dt], axis=0))
    scale_ref[...] = jnp.transpose(
        jnp.concatenate([jnp.exp(seg), jnp.exp(total - seg) * dt], axis=0)
    )
    first = iota((PAIRS, LANES), 1) < HEAD_DIM
    even = (iota((PAIRS, HEADS), 1) == 2 * iota((PAIRS, HEADS), 0)).astype(F32)
    odd = (iota((PAIRS, HEADS), 1) == 2 * iota((PAIRS, HEADS), 0) + 1).astype(F32)

    def paired(col):
        wide = jnp.broadcast_to(col, (HEADS, LANES))
        return jnp.where(first, exact_dot(even, wide), exact_dot(odd, wide))

    tot_ref[...] = paired(total)
    skip_ref[...] = paired(column(skip_gain_ref[...]))
    decay_ref[...] = jnp.broadcast_to(decay, (HEADS, LANES))
    win_ref[0:8, :] = jnp.zeros((8, GROUP_X), F32)
    for i in range(BLOCKS):
        copies[i].wait()
        cols = slice(i * GROUP_X, (i + 1) * GROUP_X)
        win_ref[8 : 8 + T, :] = hold_ref[:, cols].astype(F32)
        for lo in range(0, GROUP_X, LANES):
            at = i * GROUP_X + lo
            pre = pre_conv(win_ref, weight_ref[:, cols], lo)
            mixed = (pre * sigmoid(pre)).astype(BF16)
            head_ref[:, at : at + LANES] = pre[0:8]
            if at < WIDTH_X:
                x_ref[:, at : at + LANES] = mixed
            else:
                bc_ref[:, at - WIDTH_X : at - WIDTH_X + LANES] = mixed


def run_begin(raw, decay_log, skip_gain, tokens, weight):
    out = [
        ((HEADS, T), F32),
        ((HEADS, T), F32),
        ((T, 2 * HEADS), F32),
        ((T, 2 * HEADS), F32),
        ((PAIRS, LANES), F32),
        ((PAIRS, LANES), F32),
        ((HEADS, LANES), F32),
        ((T, WIDTH_X), BF16),
        ((T, 2 * WIDTH_B), BF16),
        ((8, CHANNELS), F32),
    ]
    scratch = [
        pltpu.VMEM((T, CHANNELS), BF16),
        pltpu.VMEM((8 + T, GROUP_X), F32),
        pltpu.SemaphoreType.DMA((BLOCKS,)),
    ]
    return call(begin_kernel, "begin", out, "vvvhv", 5, scratch)(
        raw, decay_log, skip_gain, tokens, weight
    )


def rolled(ref, group):
    return pltpu.roll(ref[...], (LANES - group * GROUP_HEADS) % LANES, 1)


def widen(cols, base, pair):
    first = iota((T, LANES), 1) < HEAD_DIM
    at = base + 2 * pair
    return jnp.where(first, cols[:, at : at + 1], cols[:, at + 1 : at + 2])


def widen_two(cols, base, pair):
    return jnp.concatenate([widen(cols, base, pair), widen(cols, base, pair + 1)], axis=1)


def enter_kernel(core_ref, x0_ref, bc0_ref, head_ref, halo_ref, weight_ref, g_ref, scale_ref,
                 x_ref, bc_ref, own_ref, out_ref):
    row = iota((8, GROUP_X), 0)
    for i in range(BLOCKS):
        cols = slice(i * GROUP_X, (i + 1) * GROUP_X)
        halo = halo_ref[:, cols].astype(F32)
        weight = weight_ref[:, cols]
        pre = head_ref[:, cols]
        for t in range(TAPS - 1):
            extra = jnp.zeros((1, GROUP_X), F32)
            for k in range(TAPS - 1 - t):
                extra = extra + weight[k : k + 1] * halo[t + k : t + k + 1]
            pre = pre + jnp.where(row == t, extra, 0.0)
        fixed = pre * sigmoid(pre)
        src, dst, at = (x0_ref, x_ref, cols) if i < GROUPS else (bc0_ref, bc_ref, slice(0, GROUP_X))
        rest = src[0:16, at].astype(F32)
        dst[16:T, at] = src[16:T, at]
        dst[0:16, at] = jnp.concatenate([fixed, rest[8:16]], axis=0).astype(BF16)

    def fill(dst_ref, first):
        @pl.loop(0, HALF_GROUPS)
        def _(jj):
            j = first * HALF_GROUPS + jj
            b_flip = jnp.transpose(bc_ref[:, span(j, STATE)].astype(F32)).astype(BF16)
            c_flip = jnp.transpose(bc_ref[:, span(GROUPS + j, STATE)].astype(F32)).astype(BF16)
            cols = rolled(scale_ref, j)
            for q in range(0, GROUP_PAIRS, 2):
                lanes = pl.ds(pl.multiple_of(j * GROUP_X + q * LANES, 2 * LANES), 2 * LANES)
                xw = (x_ref[:, lanes].astype(F32) * widen_two(cols, HEADS, q)).astype(BF16)
                gw = (g_ref[:, lanes].astype(F32) * widen_two(cols, 0, q)).astype(BF16)
                state = dot(b_flip, xw).astype(BF16)
                grad = dot(c_flip, gw).astype(BF16)
                for k in range(2):
                    at = jj * GROUP_PAIRS + q + k
                    dst_ref[0, at] = state[:, k * LANES : (k + 1) * LANES]
                    dst_ref[1, at] = grad[:, k * LANES : (k + 1) * LANES]

    fill(out_ref, 1 - core_ref[0])
    fill(own_ref, core_ref[0])


def run_enter(core, x0, bc0, head, halo, weight, cot, scale):
    out = [
        ((T, WIDTH_X), BF16),
        ((T, 2 * WIDTH_B), BF16),
        ((2, HALF_PAIRS, STATE, LANES), BF16),
        ((2, HALF_PAIRS, STATE, LANES), BF16),
    ]
    return call(enter_kernel, "enter", out, "svvvvvvv", 4)(
        core, x0, bc0, head, halo, weight, cot, scale
    )


def pack_kernel(core_ref, own_ref, got_ref, tot_ref, other_ref, out_ref):
    second = core_ref[0] == 1

    @pl.loop(0, HALF_PAIRS)
    def _(i):
        at = core_ref[0] * HALF_PAIRS + i
        tot = tot_ref[pl.ds(at, 1), :]
        other = other_ref[pl.ds(at, 1), :]
        one = jnp.ones_like(tot)
        by_own = jnp.exp(tot)
        by_other = jnp.exp(other)
        state = (
            jnp.where(second, one, by_other) * own_ref[0, i].astype(F32)
            + jnp.where(second, by_own, one) * got_ref[0, i].astype(F32)
        )
        grad = (
            jnp.where(second, by_other, one) * own_ref[1, i].astype(F32)
            + jnp.where(second, one, by_own) * got_ref[1, i].astype(F32)
        )
        out_ref[i, 0:STATE, :] = state.astype(BF16)
        out_ref[i, STATE : 2 * STATE, :] = grad.astype(BF16)
        both = tot + other
        high = both.astype(BF16).astype(F32)
        mid = (both - high).astype(BF16).astype(F32)
        low = both - high - mid
        row = iota((16, LANES), 0)
        wide = jnp.where(row == 0, high, jnp.where(row == 1, mid, jnp.where(row == 2, low, 0.0)))
        out_ref[i, 2 * STATE : PACK_ROWS, :] = wide.astype(BF16)


def run_pack(core, own, got, tot, other):
    out = [((HALF_PAIRS, PACK_ROWS, LANES), BF16)]
    return call(pack_kernel, "pack", out, "svvvv", 1, mib=16)(core, own, got, tot, other)[0]


def chain_kernel(chips, per, in_ref, out_ref):
    for q in range(per):
        def decay(k):
            rows = in_ref[k * per + q, 2 * STATE : PACK_ROWS, :].astype(F32)
            return jnp.exp(rows[0:1] + rows[1:2] + rows[2:3])

        carry = jnp.zeros((STATE, LANES), F32)
        for k in range(chips):
            out_ref[k * per + q, 0:STATE, :] = carry.astype(BF16)
            if k < chips - 1:
                carry = decay(k) * carry + in_ref[k * per + q, 0:STATE, :].astype(F32)
        carry = jnp.zeros((STATE, LANES), F32)
        for k in reversed(range(chips)):
            out_ref[k * per + q, STATE : 2 * STATE, :] = carry.astype(BF16)
            if k > 0:
                carry = decay(k) * carry + in_ref[k * per + q, STATE : 2 * STATE, :].astype(F32)


def run_chain(chips, packed):
    kernel = functools.partial(chain_kernel, chips, HALF_PAIRS // chips)
    out = [((HALF_PAIRS, 2 * STATE, LANES), BF16)]
    return call(kernel, "chain", out, "v", 0.5, mib=16)(packed)[0]


def unpack_kernel(core_ref, back_ref, own_ref, got_ref, tot_ref, other_ref, mine_ref, send_ref):
    second = core_ref[0] == 1

    @pl.loop(0, HALF_PAIRS)
    def _(i):
        at = core_ref[0] * HALF_PAIRS + i
        tot = tot_ref[pl.ds(at, 1), :]
        other = other_ref[pl.ds(at, 1), :]
        decay_zero = jnp.exp(jnp.where(second, other, tot))
        decay_one = jnp.exp(jnp.where(second, tot, other))
        state_zero = back_ref[i, 0:STATE, :].astype(F32)
        grad_one = back_ref[i, STATE : 2 * STATE, :].astype(F32)
        left = jnp.where(second, got_ref[0, i].astype(F32), own_ref[0, i].astype(F32))
        right = jnp.where(second, own_ref[1, i].astype(F32), got_ref[1, i].astype(F32))
        state_one = decay_zero * state_zero + left
        grad_zero = decay_one * grad_one + right
        mine_ref[0, i] = jnp.where(second, state_one, state_zero).astype(BF16)
        mine_ref[1, i] = jnp.where(second, grad_one, grad_zero).astype(BF16)
        send_ref[0, i] = jnp.where(second, state_zero, state_one).astype(BF16)
        send_ref[1, i] = jnp.where(second, grad_zero, grad_one).astype(BF16)


def run_unpack(core, back, own, got, tot, other):
    out = [((2, HALF_PAIRS, STATE, LANES), BF16)] * 2
    return call(unpack_kernel, "unpack", out, "svvvvv", 1, mib=16)(core, back, own, got, tot, other)


def by_lane_half(v):
    first = iota(v.shape, 1) < HEAD_DIM
    wide = v.astype(F32)
    return jnp.concatenate(
        [jnp.where(first, wide, 0.0).astype(BF16), jnp.where(first, 0.0, wide).astype(BF16)], axis=0
    )


def inner_kernel(x_ref, bc_ref, g_ref, seg_ref, dt_ref, cols_ref, y_ref, gbc_ref):
    lower = iota((T, T), 0) >= iota((T, T), 1)

    @pl.loop(0, GROUPS)
    def _(j):
        b = bc_ref[:, span(j, STATE)]
        c = bc_ref[:, span(GROUPS + j, STATE)]
        seg = seg_ref[span(j, GROUP_HEADS), :]
        dt = dt_ref[span(j, GROUP_HEADS), :]
        scores = dot(c, b, NT)
        cols = rolled(cols_ref, j)
        total = jnp.zeros((T, T), F32)
        for i in range(GROUP_PAIRS):
            lanes = pl.ds(pl.multiple_of(j * GROUP_X + i * LANES, LANES), LANES)
            x = x_ref[:, lanes]
            inner = dot(by_lane_half(g_ref[:, lanes]), x, NT)
            weights = []
            for k in range(2):
                h = 2 * i + k
                spread = cols[:, h : h + 1] - seg[h : h + 1, :]
                kernel = jnp.exp(jnp.where(lower, spread, -1e30)) * dt[h : h + 1, :]
                total = total + kernel * inner[k * T : (k + 1) * T]
                weights.append((kernel * scores).astype(BF16))
            y_ref[:, lanes] = dot(jnp.concatenate(weights, axis=1), by_lane_half(x))
        gbc_ref[:, span(GROUPS + j, STATE)] = dot(total.astype(BF16), b)
        gbc_ref[:, span(j, STATE)] = dot(jnp.transpose(total).astype(BF16), c)


def run_inner(x, bc, cot, seg, dt, cols):
    out = [((T, WIDTH_X), F32), ((T, 2 * WIDTH_B), F32)]
    return call(inner_kernel, "inner", out, "vvvvvv", 3)(x, bc, cot, seg, dt, cols)


def slopes_kernel(bc_ref, g_ref, seg_ref, cols_ref, tok_ref, halo_ref, weight_ref,
                  gx_ref, slope_ref, win_ref):
    upper = iota((T, T), 0) <= iota((T, T), 1)

    @pl.loop(0, GROUPS)
    def _(j):
        b = bc_ref[:, span(j, STATE)]
        c = bc_ref[:, span(GROUPS + j, STATE)]
        seg = seg_ref[span(j, GROUP_HEADS), :]
        scores = jnp.transpose(dot(c, b, NT))
        cols = rolled(cols_ref, j)
        for i in range(GROUP_PAIRS):
            lanes = pl.ds(pl.multiple_of(j * GROUP_X + i * LANES, LANES), LANES)
            weights = []
            for k in range(2):
                h = 2 * i + k
                spread = seg[h : h + 1, :] - cols[:, h : h + 1]
                kernel = jnp.exp(jnp.where(upper, spread, -1e30)) * cols[:, HEADS + h : HEADS + h + 1]
                weights.append((kernel * scores).astype(BF16))
            gx_ref[:, lanes] = dot(jnp.concatenate(weights, axis=1), by_lane_half(g_ref[:, lanes]))

    @pl.loop(0, BLOCKS)
    def _(i):
        cols = span(i, GROUP_X)
        fill_window(win_ref, tok_ref[:, cols], halo_ref[:, cols])
        weights = weight_ref[:, cols]
        for lo in range(0, GROUP_X, LANES):
            pre = pre_conv(win_ref, weights, lo)
            s = sigmoid(pre)
            at = pl.ds(pl.multiple_of(i * GROUP_X + lo, LANES), LANES)
            slope_ref[:, at] = s * (1.0 + pre * (1.0 - s))


def run_slopes(bc, cot, seg, cols, tokens, halo, weight):
    out = [((T, WIDTH_X), F32), ((T, CHANNELS), F32)]
    scratch = [pltpu.VMEM((8 + T, GROUP_X), F32)]
    return call(slopes_kernel, "slopes", out, "vvvvvvv", 5, scratch)(
        bc, cot, seg, cols, tokens, halo, weight
    )


def leave_kernel(core_ref, x_ref, bc_ref, g_ref, y_ref, gx_ref, gbc_ref, slope_ref, tok_ref, halo_ref,
                 mine_ref, got_ref, scale_ref, tot_ref, skip_ref, dt_ref, raw_ref, decay_ref,
                 out_ref, pre_ref, first_ref, step_ref, sum_ref, win_ref):
    last = iota((T, 2 * LANES), 0) == T - 1
    lower = (iota((T, T), 0) >= iota((T, T), 1)).astype(F32)

    def tap_sums(grad_pre, lo):
        width = grad_pre.shape[1]
        return [
            jnp.sum(grad_pre * win_ref[5 + k : 5 + k + T, lo : lo + width], axis=0, keepdims=True)
            for k in range(TAPS)
        ]

    def by_rows(sums):
        return [s[:, lo : lo + LANES] for lo in range(0, sums[0].shape[1], LANES) for s in sums]

    def group(j, jj, state_ref):
        b = bc_ref[:, span(j, STATE)]
        c = bc_ref[:, span(GROUPS + j, STATE)]
        grad_b = gbc_ref[:, span(j, STATE)]
        grad_c = gbc_ref[:, span(GROUPS + j, STATE)]
        cols = rolled(scale_ref, j)
        skip_rows = skip_ref[span(j, GROUP_PAIRS), :]
        tot_rows = tot_ref[span(j, GROUP_PAIRS), :]
        seg_grad = jnp.zeros((GROUP_HEADS, T), F32)
        dt_grad = jnp.zeros((GROUP_HEADS, T), F32)
        skips = []
        terms = []
        wide = span(j, GROUP_X)
        fill_window(win_ref, tok_ref[:, wide], halo_ref[:, wide])
        for q in range(0, GROUP_PAIRS, 2):
            lanes = pl.ds(pl.multiple_of(j * GROUP_X + q * LANES, 2 * LANES), 2 * LANES)
            rise = widen_two(cols, 0, q)
            keep = widen_two(cols, HEADS, q)
            at = jj * GROUP_PAIRS + q
            state = jnp.concatenate([state_ref[0, at], state_ref[0, at + 1]], axis=1)
            exits = jnp.concatenate([state_ref[1, at], state_ref[1, at + 1]], axis=1)
            skip = jnp.concatenate([skip_rows[q : q + 1], skip_rows[q + 1 : q + 2]], axis=1)
            tot = jnp.concatenate([tot_rows[q : q + 1], tot_rows[q + 1 : q + 2]], axis=1)
            x = x_ref[:, lanes].astype(F32)
            g = g_ref[:, lanes].astype(F32)
            y = y_ref[:, lanes] + rise * dot(c, state)
            through = keep * dot(b, exits)
            gx = gx_ref[:, lanes] + through
            grad_c = grad_c + dot((g * rise).astype(BF16), state, NT)
            grad_b = grad_b + dot((x * keep).astype(BF16), exits, NT)
            out_ref[:, lanes] = (y + skip * x).astype(BF16)
            grad_pre = (gx + skip * g) * slope_ref[:, lanes]
            pre_ref[:, lanes] = grad_pre
            first_ref[:, lanes] = grad_pre[0 : TAPS - 1].astype(BF16)
            terms += by_rows(tap_sums(grad_pre, q * LANES))
            skips += by_rows([jnp.sum(g * x, axis=0, keepdims=True)])
            x_gx = x * gx
            end = jnp.sum(x * through, axis=0, keepdims=True) + jnp.exp(tot) * jnp.sum(
                exits.astype(F32) * state.astype(F32), axis=0, keepdims=True
            )
            moved = g * y - x_gx + jnp.where(last, end, 0.0)
            pick = (
                iota((GROUP_HEADS, 2 * LANES), 0)
                == 2 * q + iota((GROUP_HEADS, 2 * LANES), 1) // HEAD_DIM
            ).astype(F32).astype(BF16)
            for part in split_two(moved):
                seg_grad = seg_grad + dot(pick, part, NT)
            for part in split_two(x_gx):
                dt_grad = dt_grad + dot(pick, part, NT)
        sum_ref[span(j, 32), :] = jnp.concatenate(terms, axis=0)
        terms = []
        for grad, base in ((grad_b, 0), (grad_c, GROUPS)):
            at = span(WIDTH_X // STATE + base + j, STATE)
            fill_window(win_ref, tok_ref[:, at], halo_ref[:, at])
            grad_pre = grad * slope_ref[:, at]
            pre_ref[:, at] = grad_pre
            first_ref[:, at] = grad_pre[0 : TAPS - 1].astype(BF16)
            terms += tap_sums(grad_pre, 0)
        sum_ref[pl.ds(pl.multiple_of(128 + j * 8, 8), 8), :] = jnp.concatenate(terms, axis=0)
        sum_ref[pl.ds(pl.multiple_of(160 + j * 8, 8), 8), :] = jnp.concatenate(skips, axis=0)
        heads = span(j, GROUP_HEADS)
        behind = exact_dot(seg_grad, lower)
        dt = dt_ref[heads, :]
        decay = decay_ref[heads, :]
        step_ref[heads, :] = (dt_grad / dt + decay * behind) * sigmoid(raw_ref[heads, :])
        sum_ref[pl.ds(pl.multiple_of(192 + j * 16, 16), 16), :] = dt * behind * decay

    for state_ref, half in ((mine_ref, core_ref[0]), (got_ref, 1 - core_ref[0])):
        @pl.loop(0, HALF_GROUPS)
        def _(jj):
            group(half * HALF_GROUPS + jj, jj, state_ref)


def run_leave(*args):
    out = [
        ((T, WIDTH_X), BF16),
        ((T, CHANNELS), F32),
        ((TAPS - 1, CHANNELS), BF16),
        ((HEADS, T), F32),
        ((SUM_ROWS, LANES), F32),
    ]
    scratch = [pltpu.VMEM((8 + T, GROUP_X), F32)]
    return call(leave_kernel, "leave", out, "s" + "v" * 17, 8, scratch)(*args)


def spread_kernel(pre_ref, halo_ref, weight_ref, out_ref, win_ref):
    @pl.loop(0, BLOCKS)
    def _(i):
        cols = span(i, GROUP_X)
        win_ref[0:T, :] = pre_ref[:, cols]
        win_ref[T : T + TAPS - 1, :] = halo_ref[:, cols].astype(F32)
        weights = weight_ref[:, cols]
        for lo in range(0, GROUP_X, LANES):
            at = slice(lo, lo + LANES)
            acc = weights[0:1, at] * win_ref[3 : 3 + T, at]
            for k in range(1, TAPS):
                acc = acc + weights[k : k + 1, at] * win_ref[3 - k : 3 - k + T, at]
            out_ref[:, pl.ds(pl.multiple_of(i * GROUP_X + lo, LANES), LANES)] = acc.astype(BF16)


def run_spread(pre, halo, weight):
    out = [((T, CHANNELS), BF16)]
    scratch = [pltpu.VMEM((T + 8, GROUP_X), F32)]
    return call(spread_kernel, "spread", out, "vvv", 3, scratch, mib=16)(pre, halo, weight)[0]


def finish_kernel(sum_ref, conv_ref, decay_ref, skip_ref):
    for i in range(CHANNELS // LANES):
        if i < PAIRS:
            row = TAPS * i
        else:
            group = (i - PAIRS) % GROUPS
            row = 128 + 8 * group + TAPS * ((i - PAIRS) // GROUPS)
        conv_ref[:, i * LANES : (i + 1) * LANES] = sum_ref[row : row + TAPS, :]
    ones = jnp.ones((8, LANES), F32)
    decay_ref[...] = exact_dot(ones, sum_ref[192:256, :], NT)[0:1]
    first = iota((8, LANES), 1) < HEAD_DIM
    skips = sum_ref[160:192, :]
    even = exact_dot(jnp.where(first, 1.0, 0.0), skips, NT)
    odd = exact_dot(jnp.where(first, 0.0, 1.0), skips, NT)
    at_even = (iota((PAIRS, HEADS), 1) == 2 * iota((PAIRS, HEADS), 0)).astype(F32)
    at_odd = (iota((PAIRS, HEADS), 1) == 2 * iota((PAIRS, HEADS), 0) + 1).astype(F32)
    skip_ref[...] = (exact_dot(even, at_even) + exact_dot(odd, at_odd))[0:1]


def run_finish(sums):
    out = [((TAPS, CHANNELS), F32), ((1, HEADS), F32), ((1, HEADS), F32)]
    return call(finish_kernel, "finish", out, "v", 0.5, mib=16)(sums)


CTX = ("chip", "core")
ALL = ("dp", "chip", "core")


def all_to_all(value, axis):
    return lax.all_to_all(value, axis, 0, 0, tiled=True)


def tie(*values):
    return lax.optimization_barrier(values)


def sum_everywhere(sums, chips):
    share = SUM_ROWS // chips
    parts = all_to_all(sums, "chip").reshape(chips, share, LANES)
    total = jnp.sum(parts, axis=0)
    total = total + lax.ppermute(total, "core", [(0, 1), (1, 0)])
    count = lax.axis_size("dp")
    flip = 1
    while flip < count:
        mask = flip if 2 * flip < count else count - 1
        total = total + lax.ppermute(total, "dp", [(i, i ^ mask) for i in range(count)])
        flip *= 2
    return all_to_all(jnp.broadcast_to(total[None], (chips, share, LANES)).reshape(SUM_ROWS, LANES), "chip")


def local(conv_input, conv_weight, step_raw, decay_log, skip_gain, cotangent):
    chips = lax.axis_size("chip")
    devices = 2 * chips
    tokens = conv_input[0]
    raw = step_raw[0]
    cot = cotangent[0]
    core = lax.axis_index("core").astype(jnp.int32).reshape(1)
    swap = [(0, 1), (1, 0)]
    halo = lax.ppermute(tokens[T - TAPS + 1 :], CTX, [(i, i + 1) for i in range(devices - 1)])
    dt, seg, cols, scale, tot, skip, decay, x0, bc0, head = run_begin(
        raw, decay_log.reshape(1, HEADS), skip_gain.reshape(1, HEADS), tokens, conv_weight
    )
    other = lax.ppermute(tot, "core", swap)
    x, bc, own, out = run_enter(core, x0, bc0, head, halo, conv_weight, cot, scale)
    got = lax.ppermute(out, "core", swap)
    packed = run_pack(core, own, got, tot, other)
    heard = all_to_all(packed, "chip")
    y, gbc = run_inner(x, bc, cot, seg, dt, cols)
    heard, y, gbc = tie(heard, y, gbc)
    chained = run_chain(chips, heard)
    late, chained = tie(bc, chained)
    back = all_to_all(chained, "chip")
    gx, slope = run_slopes(late, cot, seg, cols, tokens, halo, conv_weight)
    back, gx, slope = tie(back, gx, slope)
    mine, send = run_unpack(core, back, own, got, tot, other)
    theirs = lax.ppermute(send, "core", swap)
    out_tokens, pre, first, grad_step, sums = run_leave(
        core, x, bc, cot, y, gx, gbc, slope, tokens, halo, mine, theirs, scale, tot, skip, dt, raw, decay
    )
    after = lax.ppermute(first, CTX, [(i + 1, i) for i in range(devices - 1)])
    grad_tokens = run_spread(pre, after, conv_weight)
    grad_conv, grad_decay, grad_skip = run_finish(sum_everywhere(sums, chips))
    return (
        out_tokens[None],
        grad_tokens[None],
        grad_step[None],
        grad_conv,
        grad_decay.reshape(HEADS),
        grad_skip.reshape(HEADS),
    )


def solution(mesh):
    dp, ctx = mesh.devices.shape
    fine = Mesh(mesh.devices.reshape(dp, ctx // 2, 2), ALL)
    seq = P("dp", CTX, None)
    rate = P("dp", None, CTX)
    in_specs = (seq, P(), rate, P(), P(), seq)
    out_specs = (seq, seq, rate, P(), P(), P())
    return jax.shard_map(local, mesh=fine, in_specs=in_specs, out_specs=out_specs, check_vma=False)
```

time: 1100 us -> 144 us (0.13); the launches traced: 1090 us -> 142 us
  waiting for transfers between devices: 471 us -> 24.6 us
  other arithmetic: 280 us -> 0.03 us
  blocking collectives: 135 us -> 11.6 us
  local copies, waits for them, and re-layouts: 108 us -> 35.5 us
  matrix products: 68.3 us -> 0 us
  Pallas kernels: 0 us -> 32.4 us
  starting transfers between devices: 5.23 us -> 36.5 us
  between operations: 17.2 us -> 0.9 us
    all_gather x2 -> x0, waiting for transfers between devices: 328 us -> none  [prefix(): pieces = jax.tree.map(lambda part: lax.all_gather(part, axis), value)]
    select_n x62 -> x0, other arithmetic: 186 us -> none  [step(): jnp.where(position < mine, new, old)]
    psum x1 -> x0, waiting for transfers between devices: 144 us -> none  [local(): lax.psum((conv_terms, grad_decay * decay_rate, grad_skip), ('dp', 'ctx'))]
    psum x1 -> x0, blocking collectives: 75.3 us -> none  [local(): lax.psum((conv_terms, grad_decay * decay_rate, grad_skip), ('dp', 'ctx'))]
    dot_general x55 -> x0, matrix products: 68.3 us -> none  [the longest x12 21.7 us: advance(): jnp.einsum('hts,shp->thp', kernel * scores[None], x_part, precision=split...]
    unnamed x1 -> x0, blocking collectives: 59.5 us -> none
    rev x2 -> x0, local copies, waits for them, and re-layouts: 44.2 us -> none  [prefix(): pieces = jax.tree.map(lambda part: part[::-1], pieces)]
    pallas_call x0 -> x10, Pallas kernels: none -> 32.4 us  [the longest x1 8.12 us: run_leave(): return call(leave_kernel, 'leave', out, 's' + 'v' * 17, 8, scratch)(*args)]
  transfers between devices with their start and end apart: 5 -> 12, of which waited for: 3 -> 8; matrix products, arithmetic and copies ran while one was open for 5% -> 0% of each run, Pallas kernels for 0% -> 11%
where the time goes in v2:
time: 144 us; the launch traced here: 142 us
  starting transfers between devices  36.5 us (25%)
  local copies, waits for them, and re-layouts  35.5 us (25%)
  Pallas kernels  32.4 us (22%)
  waiting for transfers between devices  24.6 us (17%)
  blocking collectives  11.6 us (8%)
    unnamed x94, local copies, waits for them, and re-layouts  34 us
    all_to_all x3, starting transfers between devices, all_to_all(): return lax.all_to_all(value, axis, 0, 0, tiled=True)  17.5 us
    all_to_all x3, waiting for transfers between devices, all_to_all(): return lax.all_to_all(value, axis, 0, 0, tiled=True)  14.7 us
    all_to_all x1, blocking collectives, all_to_all(): return lax.all_to_all(value, axis, 0, 0, tiled=True)  11.6 us
    ppermute x3, starting transfers between devices, sum_everywhere(): lax.ppermute(total, 'dp', [(i, i ^ mask) for i in range(count)])  10.8 us
    pallas_call x1, Pallas kernels, run_leave(): return call(leave_kernel, 'leave', out, 's' + 'v' * 17, 8, scratch)(*args)  8.12 us
    pallas_call x1, Pallas kernels, run_slopes(): call(slopes_kernel, 'slopes', out, 'vvvvvvv', 5, scratch)  6.15 us
    ppermute x3, waiting for transfers between devices, sum_everywhere(): lax.ppermute(total, 'dp', [(i, i ^ mask) for i in range(count)])  4.99 us
  transfers between devices with their start and end apart: 12, of which 8 were waited for; matrix products, arithmetic and copies ran while one was open for 0% of the time, Pallas kernels for 11%

profile of v2, /device:TPU:2, one launch (start us, length us, event | category | flops | bytes accessed | tf_op | source)
XLA Modules:
  0.0 141.6 jit_solution(16163155909608851055)
XLA Ops:
  0.6 0.9 slice_bitcast_fusion
  1.5 1.9 %collective-permute-start = (bf16[3,5120]{1,0:T(4,128)(2,1)S(1)}, bf16[3,5120]{1,0:T(4,128)(2,1)S(1)}, u32[]{:S(2)}, u32[]{:S(2)}) collective-permute-start(bf16[3,5120]{1,0:T(4,128)(2,1)S(1)} %slice_bitcast_fusion), channel_id=1, source_target_pairs={{0,1},{1,2},{2,3},{3,4},{4,5},{5,6},{6,7},{7,8},{8,9},{9,10},{10,1... | collective-permute-start | bytes 92168 | tf_op jit(solution)/shard_map/ppermute | solution.py:594
  3.5 1.3 copy-done
  4.8 0.9 copy-done.5
  7.8 3.3 %begin.1 = (f32[64,128]{1,0:T(8,128)S(1)}, f32[64,128]{1,0:T(8,128)S(1)}, f32[128,128]{1,0:T(8,128)S(1)}, f32[128,128]{1,0:T(8,128)S(1)}, f32[32,128]{1,0:T(8,12...) custom-call(f32[64,128]{1,0:T(8,128)S(1)} %bitcast.24, ...), custom_call_target="tpu_custom_call" | custom-call | flops 5000000000 | bytes 18000000 | tf_op jit(solution)/shard_map/begin/pallas_call | solution.py:174
  14.3 1.0 copy-done.32
  15.3 4.1 %enter.1 = (bf16[128,4096]{1,0:T(8,128)(2,1)S(1)}, bf16[128,1024]{1,0:T(8,128)(2,1)S(1)}, bf16[2,16,128,128]{3,2,1,0:T(8,128)(2,1)S(1)}, bf16[2,16,128,128]{3,2,1,0:T(8,128)(2,1)S(1)}) custom-call(s32[1]{0:T(128)} %bitcast.core_ref, bf16[128,4096]{1,0:T(8,128)(2,1)S(1)} %get-tuple-element.42.x0_ref, bf16[128,1024]{1,0:T(8,128)(2,1)S(1)} %copy-done.32, ...), custom_call_target="tpu_custom_call" | custom-call | flops 4000000000 | bytes 14400000 | tf_op jit(solution)/shard_map/enter/pallas_call | solution.py:241
  20.1 1.7 %collective-permute-start.1 = (bf16[2,16,128,128]{3,2,1,0:T(8,128)(2,1)S(1)}, bf16[2,16,128,128]{3,2,1,0:T(8,128)(2,1)S(1)}, u32[]{:S(2)}, u32[]{:S(2)}) collective-permute-start(bf16[2,16,128,128]{3,2,1,0:T(8,128)(2,1)S(1)} %get-tuple-element.49), channel_id=1, source_target_pairs={{0,1},{1,0},{2,3},{3,2},{4,5},{5,4},{6,7},{7,6},{8,9},{9,8},{10,11... | collective-permute-start | bytes 3145736 | tf_op jit(solution)/shard_map/ppermute | solution.py:600
  21.8 2.3 %collective-permute-done.2.other_ref = f32[32,128]{1,0:T(8,128)S(1)} collective-permute-done((f32[32,128]{1,0:T(8,128)S(1)}, f32[32,128]{1,0:T(8,128)S(1)}, u32[]{:S(2)}, u32[]{:S(2)}) %collective-permute-start.2) | collective-permute-done | bytes 16416 | tf_op jit(solution)/shard_map/ppermute | solution.py:598
  24.1 1.6 %pack.1 = bf16[16,272,128]{2,1,0:T(8,128)(2,1)} custom-call(s32[1]{0:T(128)} %bitcast.core_ref, bf16[2,16,128,128]{3,2,1,0:T(8,128)(2,1)S(1)} %get-tuple-element.48.own_ref, bf16[2,16,128,128]{3,2,1,0:T(8,128)(2,1)S(1)} %collective-permute-done.1.got_ref, f32[32,128]{1,0:T(8,128)S(1)} %get-tuple-element.50.tot_ref, ...), custom_call_target="tpu_custom_call" | custom-call | flops 1000000000 | bytes 3600000 | tf_op jit(solution)/shard_map/pack/pallas_call | solution.py:278
  25.7 1.0 copy-done.3
  27.4 1.1 copy-done.13
  28.4 7.3 %all-to-all-start = ((bf16[16,272,128]{2,1,0:T(8,128)(2,1)}), bf16[16,272,128]{2,1,0:T(8,128)(2,1)S(1)}, u32[]{:S(2)}, u32[]{:S(2)}) async-start(bf16[16,272,128]{2,1,0:T(8,128)(2,1)} %pack.1), calls=%async_computation | async-start | bytes 2228224 | tf_op jit(solution)/shard_map/all_to_all | solution.py:565
  35.8 0.9 copy-done.28
  36.8 3.0 %inner.1 = (f32[128,4096]{1,0:T(8,128)S(1)}, f32[128,1024]{1,0:T(8,128)S(1)}) custom-call(bf16[128,4096]{1,0:T(8,128)(2,1)S(1)} %get-tuple-element.46.x_ref, bf16[128,1024]{1,0:T(8,128)(2,1)S(1)} %copy-done.28, bf16[128,4096]{1,0:T(8,128)(2,1)S(1)} %bitcast.21, f32[64,128]{1,0:T(8,128)S(1)} %copy-done.41, f32[64,128]{1,0:T(8,128)S(1)} %get-tuple-element.52.dt_ref, ...), custom_call_target="tpu_custom_call" | custom-call | flops 3000000000 | bytes 10800000 | tf_op jit(solution)/shard_map/inner/pallas_call | solution.py:370
  39.7 1.4 copy-done.17
  41.1 0.8 copy-done.25
  41.9 10.4 %all-to-all-done.in_ref = bf16[16,272,128]{2,1,0:T(8,128)(2,1)S(1)} async-done(((bf16[16,272,128]{2,1,0:T(8,128)(2,1)}), bf16[16,272,128]{2,1,0:T(8,128)(2,1)S(1)}, u32[]{:S(2)}, u32[]{:S(2)}) %all-to-all-start) | async-done | bytes 1114144 | tf_op jit(solution)/shard_map/all_to_all | solution.py:565
  52.3 1.3 chain.1
  53.5 6.3 %all-to-all-start.1 = ((bf16[16,256,128]{2,1,0:T(8,128)(2,1)}), bf16[16,256,128]{2,1,0:T(8,128)(2,1)S(1)}, u32[]{:S(2)}, u32[]{:S(2)}) async-start(bf16[16,256,128]{2,1,0:T(8,128)(2,1)} %chain.1), calls=%async_computation.1 | async-start | bytes 2097152 | tf_op jit(solution)/shard_map/all_to_all | solution.py:565
  59.9 0.9 copy-done.29
  60.8 0.8 copy-done.35
  62.4 6.2 %slopes.1 = (f32[128,4096]{1,0:T(8,128)S(1)}, f32[128,5120]{1,0:T(8,128)S(1)}) custom-call(bf16[128,1024]{1,0:T(8,128)(2,1)S(1)} %copy-done.29, bf16[128,4096]{1,0:T(8,128)(2,1)S(1)} %bitcast.22, f32[64,128]{1,0:T(8,128)S(1)} %copy-done.42, f32[128,128]{1,0:T(8,128)S(1)} %copy-done.35, bf16[128,5120]{1,0:T(8,128)(2,1)S(1)} %bitcast.18, ...), custom_call_target="tpu_custom_call" | custom-call | flops 5000000000 | bytes 18000000 | tf_op jit(solution)/shard_map/slopes/pallas_call | solution.py:409
  68.6 1.5 %copy-done.21 = f32[128,5120]{1,0:T(8,128)} copy-done((f32[128,5120]{1,0:T(8,128)}, f32[128,5120]{1,0:T(8,128)S(1)}, u32[]{:S(2)}) %copy-start.21) | copy-done | bytes 2621464
  70.0 1.3 copy-done.23
  71.4 2.8 %all-to-all-done.1.back_ref = bf16[16,256,128]{2,1,0:T(8,128)(2,1)S(1)} async-done(((bf16[16,256,128]{2,1,0:T(8,128)(2,1)}), bf16[16,256,128]{2,1,0:T(8,128)(2,1)S(1)}, u32[]{:S(2)}, u32[]{:S(2)}) %all-to-all-start.1) | async-done | bytes 1048608 | tf_op jit(solution)/shard_map/all_to_all | solution.py:565
  74.2 1.2 copy-done.4
  76.1 1.2 copy-done.14
  78.4 2.6 %collective-permute-done.3.got_ref = bf16[2,16,128,128]{3,2,1,0:T(8,128)(2,1)S(1)} collective-permute-done((bf16[2,16,128,128]{3,2,1,0:T(8,128)(2,1)S(1)}, bf16[2,16,128,128]{3,2,1,0:T(8,128)(2,1)S(1)}, u32[]{:S(2)}, u32[]{:S(2)}) %collective-permute-start.3) | collective-permute-done | bytes 1048608 | tf_op jit(solution)/shard_map/ppermute | solution.py:611
  81.0 1.7 %copy-done.22 = f32[128,5120]{1,0:T(8,128)S(1)} copy-done((f32[128,5120]{1,0:T(8,128)S(1)}, f32[128,5120]{1,0:T(8,128)}, u32[]{:S(2)}) %copy-start.22) | copy-done | bytes 2621464
  82.8 1.6 %copy-done.24 = f32[128,4096]{1,0:T(8,128)S(1)} copy-done((f32[128,4096]{1,0:T(8,128)S(1)}, f32[128,4096]{1,0:T(8,128)}, u32[]{:S(2)}) %copy-start.24) | copy-done | bytes 2097176
  84.4 0.9 copy-done.30
  85.3 0.8 copy-done.37
  88.4 8.1 %leave.1 = (bf16[128,4096]{1,0:T(8,128)(2,1)}, f32[128,5120]{1,0:T(8,128)S(1)}, bf16[3,5120]{1,0:T(4,128)(2,1)S(1)}, f32[64,128]{1,0:T(8,128)}, f32[256,128]{1,0:T(8,128)S(1)}) custom-call(s32[1]{0:T(128)} %bitcast.core_ref, bf16[128,4096]{1,0:T(8,128)(2,1)S(1)} %copy-done.20, bf16[128,1024]{1,0:T(8,128)(2,1)S(1)} %copy-done.30, ...), custom_call_target="tpu_custom_call" | custom-call | flops 8000000000 | bytes 28800000 | tf_op jit(solution)/shard_map/leave/pallas_call | solution.py:512
  96.5 1.5 %copy-done.15 = f32[128,5120]{1,0:T(8,128)} copy-done((f32[128,5120]{1,0:T(8,128)}, f32[128,5120]{1,0:T(8,128)S(1)}, u32[]{:S(2)}) %copy-start.15) | copy-done | bytes 2621464
  98.0 11.6 %all_to_all.27 = f32[16,16,128]{2,1,0:T(8,128)S(1)} all-to-all(f32[16,16,128]{2,1,0:T(8,128)S(1)} %bitcast.15), channel_id=1, replica_groups=mesh['dp'=8,'chip'=16,'core'=2] {'chip'}, dimensions={0} | all-to-all | bytes 262144 | tf_op jit(solution)/shard_map/all_to_all | solution.py:565
  109.7 4.2 %collective-permute-start.4 = (bf16[3,5120]{1,0:T(4,128)(2,1)S(1)}, bf16[3,5120]{1,0:T(4,128)(2,1)S(1)}, u32[]{:S(2)}, u32[]{:S(2)}) collective-permute-start(bf16[3,5120]{1,0:T(4,128)(2,1)S(1)} %get-tuple-element.72), channel_id=1, source_target_pairs={{1,0},{2,1},{3,2},{4,3},{5,4},{6,5},{7,6},{8,7},{9,8},{10,9},{11,1... | collective-permute-start | bytes 92168 | tf_op jit(solution)/shard_map/ppermute | solution.py:615
  114.0 2.0 %collective-permute-start.6 = (f32[16,128]{1,0:T(8,128)S(1)}, f32[16,128]{1,0:T(8,128)S(1)}, u32[]{:S(2)}, u32[]{:S(2)}) collective-permute-start(f32[16,128]{1,0:T(8,128)S(1)} %add.12), channel_id=1, source_target_pairs={{0,32},{32,0},{64,96},{96,64},{128,160},{160,128},{192,224},{224,1... | collective-permute-start | bytes 24584 | tf_op jit(solution)/shard_map/ppermute | solution.py:581
  116.0 1.7 %collective-permute-done.6 = f32[16,128]{1,0:T(8,128)S(1)} collective-permute-done((f32[16,128]{1,0:T(8,128)S(1)}, f32[16,128]{1,0:T(8,128)S(1)}, u32[]{:S(2)}, u32[]{:S(2)}) %collective-permute-start.6) | collective-permute-done | bytes 8224 | tf_op jit(solution)/shard_map/ppermute | solution.py:581
  117.7 3.3 %collective-permute-start.7 = (f32[16,128]{1,0:T(8,128)S(1)}, f32[16,128]{1,0:T(8,128)S(1)}, u32[]{:S(2)}, u32[]{:S(2)}) collective-permute-start(f32[16,128]{1,0:T(8,128)S(1)} %add.13), channel_id=1, source_target_pairs={{0,64},{32,96},{64,0},{96,32},{128,192},{160,224},{192,128},{224,1... | collective-permute-start | bytes 24584 | tf_op jit(solution)/shard_map/ppermute | solution.py:581
  121.0 1.6 %collective-permute-done.7 = f32[16,128]{1,0:T(8,128)S(1)} collective-permute-done((f32[16,128]{1,0:T(8,128)S(1)}, f32[16,128]{1,0:T(8,128)S(1)}, u32[]{:S(2)}, u32[]{:S(2)}) %collective-permute-start.7) | collective-permute-done | bytes 8224 | tf_op jit(solution)/shard_map/ppermute | solution.py:581
  122.6 5.5 %collective-permute-start.8 = (f32[16,128]{1,0:T(8,128)S(1)}, f32[16,128]{1,0:T(8,128)S(1)}, u32[]{:S(2)}, u32[]{:S(2)}) collective-permute-start(f32[16,128]{1,0:T(8,128)S(1)} %add.14), channel_id=1, source_target_pairs={{0,224},{32,192},{64,160},{96,128},{128,96},{160,64},{192,32},{224... | collective-permute-start | bytes 24584 | tf_op jit(solution)/shard_map/ppermute | solution.py:581
  128.1 1.6 %collective-permute-done.8 = f32[16,128]{1,0:T(8,128)S(1)} collective-permute-done((f32[16,128]{1,0:T(8,128)S(1)}, f32[16,128]{1,0:T(8,128)S(1)}, u32[]{:S(2)}, u32[]{:S(2)}) %collective-permute-start.8) | collective-permute-done | bytes 8224 | tf_op jit(solution)/shard_map/ppermute | solution.py:581
  130.4 3.8 %all-to-all-start.3 = ((f32[16,16,128]{2,1,0:T(8,128)}), f32[16,16,128]{2,1,0:T(8,128)S(1)}, u32[]{:S(2)}, u32[]{:S(2)}) async-start(f32[16,16,128]{2,1,0:T(8,128)} %broadcast_in_dim.18), calls=%async_computation.3 | async-start | bytes 262144 | tf_op jit(solution)/shard_map/all_to_all | solution.py:565
  134.3 1.7 %copy-done.16 = f32[128,5120]{1,0:T(8,128)S(1)} copy-done((f32[128,5120]{1,0:T(8,128)S(1)}, f32[128,5120]{1,0:T(8,128)}, u32[]{:S(2)}) %copy-start.16) | copy-done | bytes 2621464
  136.0 3.2 %spread.1 = bf16[128,5120]{1,0:T(8,128)(2,1)} custom-call(f32[128,5120]{1,0:T(8,128)S(1)} %copy-done.16, bf16[3,5120]{1,0:T(4,128)(2,1)S(1)} %collective-permute-done.4.halo_ref, f32[4,5120]{1,0:T(4,128)S(1)} %copy-done.6), custom_call_target="tpu_custom_call" | custom-call | flops 3000000000 | bytes 10800000 | tf_op jit(solution)/shard_map/spread/pallas_call | solution.py:533
  139.2 1.5 %all-to-all-done.3 = f32[16,16,128]{2,1,0:T(8,128)S(1)} async-done(((f32[16,16,128]{2,1,0:T(8,128)}), f32[16,16,128]{2,1,0:T(8,128)S(1)}, u32[]{:S(2)}, u32[]{:S(2)}) %all-to-all-start.3) | async-done | bytes 131104 | tf_op jit(solution)/shard_map/all_to_all | solution.py:565
  140.7 0.9 finish.1
  (88 shorter events, 12.1 us)
Async XLA Ops:
  1.5 12.7 %collective-permute-start = (bf16[3,5120]{1,0:T(4,128)(2,1)S(1)}, bf16[3,5120]{1,0:T(4,128)(2,1)S(1)}, u32[]{:S(2)}, u32[]{:S(2)}) collective-permute-start(bf16[3,5120]{1,0:T(4,128)(2,1)S(1)} %slice_bitcast_fusion), channel_id=1, source_target_pairs={{0,1},{1,2},{2,3},{3,4},{4,5},{5,6},{6,7},{7,8},{8,9},{9,10},{10,1... | collective-permute-start | bytes 92168 | tf_op jit(solution)/shard_map/ppermute | solution.py:594
  3.5 1.3 copy-start
  4.8 0.9 copy-start.5
  5.7 0.8 copy-start.7
  7.8 6.5 %copy-start.2 = (bf16[1,128,4096]{2,1,0:T(8,128)(2,1)S(1)}, bf16[1,128,4096]{2,1,0:T(8,128)(2,1)}, u32[]{:S(2)}) copy-start(bf16[1,128,4096]{2,1,0:T(8,128)(2,1)} %param.11) | copy-start | bytes 3145732
  7.8 6.5 %copy-start.6 = (f32[4,5120]{1,0:T(4,128)S(1)}, f32[4,5120]{1,0:T(4,128)}, u32[]{:S(2)}) copy-start(f32[4,5120]{1,0:T(4,128)} %weight_ref.7) | copy-start | bytes 245764
  14.3 5.1 %copy-start.36 = (f32[128,128]{1,0:T(8,128)}, f32[128,128]{1,0:T(8,128)S(1)}, u32[]{:S(2)}) copy-start(f32[128,128]{1,0:T(8,128)S(1)} %get-tuple-element.45.scale_ref) | copy-start | bytes 196612
  14.3 21.5 %copy-start.38 = (f32[64,128]{1,0:T(8,128)}, f32[64,128]{1,0:T(8,128)S(1)}, u32[]{:S(2)}) copy-start(f32[64,128]{1,0:T(8,128)S(1)} %get-tuple-element.52.dt_ref) | copy-start | bytes 98308
  14.3 1.0 copy-start.32
  20.1 15.7 %copy-start.19 = (bf16[128,4096]{1,0:T(8,128)(2,1)}, bf16[128,4096]{1,0:T(8,128)(2,1)S(1)}, u32[]{:S(2)}) copy-start(bf16[128,4096]{1,0:T(8,128)(2,1)S(1)} %get-tuple-element.46.x_ref) | copy-start | bytes 3145732
  20.1 4.0 %collective-permute-start.1 = (bf16[2,16,128,128]{3,2,1,0:T(8,128)(2,1)S(1)}, bf16[2,16,128,128]{3,2,1,0:T(8,128)(2,1)S(1)}, u32[]{:S(2)}, u32[]{:S(2)}) collective-permute-start(bf16[2,16,128,128]{3,2,1,0:T(8,128)(2,1)S(1)} %get-tuple-element.49), channel_id=1, source_target_pairs={{0,1},{1,0},{2,3},{3,2},{4,5},{5,4},{6,7},{7,6},{8,9},{9,8},{10,11... | collective-permute-start | bytes 3145736 | tf_op jit(solution)/shard_map/ppermute | solution.py:600
  21.8 2.3 %collective-permute-start.2 = (f32[32,128]{1,0:T(8,128)S(1)}, f32[32,128]{1,0:T(8,128)S(1)}, u32[]{:S(2)}, u32[]{:S(2)}) collective-permute-start(f32[32,128]{1,0:T(8,128)S(1)} %get-tuple-element.50.tot_ref), channel_id=1, source_target_pairs={{0,1},{1,0},{2,3},{3,2},{4,5},{5,4},{6,7},{7,6},{8,9},{9,8},{10,11... | collective-permute-start | bytes 49160 | tf_op jit(solution)/shard_map/ppermute | solution.py:598
  25.7 1.0 copy-start.3
  27.3 1.1 copy-start.13
  28.4 7.4 %copy-start.34 = (f32[128,128]{1,0:T(8,128)S(1)}, f32[128,128]{1,0:T(8,128)}, u32[]{:S(2)}) copy-start(f32[128,128]{1,0:T(8,128)} %copy-done.33) | copy-start | bytes 196612
  28.4 7.4 %copy-start.41 = (f32[64,128]{1,0:T(8,128)S(1)}, f32[64,128]{1,0:T(8,128)}, u32[]{:S(2)}) copy-start(f32[64,128]{1,0:T(8,128)} %copy-done.40) | copy-start | bytes 98308
  28.4 23.8 %all-to-all-start = ((bf16[16,272,128]{2,1,0:T(8,128)(2,1)}), bf16[16,272,128]{2,1,0:T(8,128)(2,1)S(1)}, u32[]{:S(2)}, u32[]{:S(2)}) async-start(bf16[16,272,128]{2,1,0:T(8,128)(2,1)} %pack.1), calls=%async_computation | async-start | bytes 2228224 | tf_op jit(solution)/shard_map/all_to_all | solution.py:565
  35.8 1.0 copy-start.28
  39.7 1.4 copy-start.17
  41.1 0.8 copy-start.25
  53.5 6.3 %copy-start.1 = (bf16[1,128,5120]{2,1,0:T(8,128)(2,1)S(1)}, bf16[1,128,5120]{2,1,0:T(8,128)(2,1)}, u32[]{:S(2)}) copy-start(bf16[1,128,5120]{2,1,0:T(8,128)(2,1)} %param.6) | copy-start | bytes 3932164
  53.5 20.6 %all-to-all-start.1 = ((bf16[16,256,128]{2,1,0:T(8,128)(2,1)}), bf16[16,256,128]{2,1,0:T(8,128)(2,1)S(1)}, u32[]{:S(2)}, u32[]{:S(2)}) async-start(bf16[16,256,128]{2,1,0:T(8,128)(2,1)} %chain.1), calls=%async_computation.1 | async-start | bytes 2097152 | tf_op jit(solution)/shard_map/all_to_all | solution.py:565
  59.9 1.0 copy-start.29
  60.8 0.8 copy-start.35
  61.6 0.8 copy-start.42
  68.6 1.5 %copy-start.21 = (f32[128,5120]{1,0:T(8,128)}, f32[128,5120]{1,0:T(8,128)S(1)}, u32[]{:S(2)}) copy-start(f32[128,5120]{1,0:T(8,128)S(1)} %get-tuple-element.64.slope_ref) | copy-start | bytes 7864324
  70.0 1.3 copy-start.23
  74.2 1.2 copy-start.4
  76.1 1.2 copy-start.14
  77.3 3.7 %copy-start.8 = (f32[1,64,128]{2,1,0:T(8,128)S(1)}, f32[1,64,128]{2,1,0:T(8,128)}, u32[]{:S(2)}) copy-start(f32[1,64,128]{2,1,0:T(8,128)} %param.8) | copy-start | bytes 98308
  77.3 3.7 %copy-start.18 = (f32[128,4096]{1,0:T(8,128)S(1)}, f32[128,4096]{1,0:T(8,128)}, u32[]{:S(2)}) copy-start(f32[128,4096]{1,0:T(8,128)} %copy-done.17) | copy-start | bytes 6291460
  77.3 3.7 %copy-start.20 = (bf16[128,4096]{1,0:T(8,128)(2,1)S(1)}, bf16[128,4096]{1,0:T(8,128)(2,1)}, u32[]{:S(2)}) copy-start(bf16[128,4096]{1,0:T(8,128)(2,1)} %copy-done.19) | copy-start | bytes 3145732
  77.3 3.7 %copy-start.26 = (f32[128,1024]{1,0:T(8,128)S(1)}, f32[128,1024]{1,0:T(8,128)}, u32[]{:S(2)}) copy-start(f32[128,1024]{1,0:T(8,128)} %copy-done.25) | copy-start | bytes 1572868
  78.1 2.9 %collective-permute-start.3 = (bf16[2,16,128,128]{3,2,1,0:T(8,128)(2,1)S(1)}, bf16[2,16,128,128]{3,2,1,0:T(8,128)(2,1)S(1)}, u32[]{:S(2)}, u32[]{:S(2)}) collective-permute-start(bf16[2,16,128,128]{3,2,1,0:T(8,128)(2,1)S(1)} %get-tuple-element.67), channel_id=1, source_target_pairs={{0,1},{1,0},{2,3},{3,2},{4,5},{5,4},{6,7},{7,6},{8,9},{9,8},{10,11... | collective-permute-start | bytes 3145736 | tf_op jit(solution)/shard_map/ppermute | solution.py:611
  81.0 1.7 %copy-start.22 = (f32[128,5120]{1,0:T(8,128)S(1)}, f32[128,5120]{1,0:T(8,128)}, u32[]{:S(2)}) copy-start(f32[128,5120]{1,0:T(8,128)} %copy-done.21) | copy-start | bytes 7864324
  82.8 1.6 %copy-start.24 = (f32[128,4096]{1,0:T(8,128)S(1)}, f32[128,4096]{1,0:T(8,128)}, u32[]{:S(2)}) copy-start(f32[128,4096]{1,0:T(8,128)} %copy-done.23) | copy-start | bytes 6291460
  84.4 0.9 copy-start.30
  85.3 0.8 copy-start.37
  86.1 0.8 copy-start.39
  86.9 0.8 copy-start.44
  96.5 1.5 %copy-start.15 = (f32[128,5120]{1,0:T(8,128)}, f32[128,5120]{1,0:T(8,128)S(1)}, u32[]{:S(2)}) copy-start(f32[128,5120]{1,0:T(8,128)S(1)} %get-tuple-element.71.pre_ref) | copy-start | bytes 7864324
  109.6 4.3 %collective-permute-start.5 = (f32[16,128]{1,0:T(8,128)S(1)}, f32[16,128]{1,0:T(8,128)S(1)}, u32[]{:S(2)}, u32[]{:S(2)}) collective-permute-start(f32[16,128]{1,0:T(8,128)S(1)} %reduce_sum.9), channel_id=1, source_target_pairs={{0,1},{1,0},{2,3},{3,2},{4,5},{5,4},{6,7},{7,6},{8,9},{9,8},{10,11... | collective-permute-start | bytes 24584 | tf_op jit(solution)/shard_map/ppermute | solution.py:576
  109.7 24.6 %collective-permute-start.4 = (bf16[3,5120]{1,0:T(4,128)(2,1)S(1)}, bf16[3,5120]{1,0:T(4,128)(2,1)S(1)}, u32[]{:S(2)}, u32[]{:S(2)}) collective-permute-start(bf16[3,5120]{1,0:T(4,128)(2,1)S(1)} %get-tuple-element.72), channel_id=1, source_target_pairs={{1,0},{2,1},{3,2},{4,3},{5,4},{6,5},{7,6},{8,7},{9,8},{10,9},{11,1... | collective-permute-start | bytes 92168 | tf_op jit(solution)/shard_map/ppermute | solution.py:615
  114.0 3.7 %collective-permute-start.6 = (f32[16,128]{1,0:T(8,128)S(1)}, f32[16,128]{1,0:T(8,128)S(1)}, u32[]{:S(2)}, u32[]{:S(2)}) collective-permute-start(f32[16,128]{1,0:T(8,128)S(1)} %add.12), channel_id=1, source_target_pairs={{0,32},{32,0},{64,96},{96,64},{128,160},{160,128},{192,224},{224,1... | collective-permute-start | bytes 24584 | tf_op jit(solution)/shard_map/ppermute | solution.py:581
  117.7 4.9 %collective-permute-start.7 = (f32[16,128]{1,0:T(8,128)S(1)}, f32[16,128]{1,0:T(8,128)S(1)}, u32[]{:S(2)}, u32[]{:S(2)}) collective-permute-start(f32[16,128]{1,0:T(8,128)S(1)} %add.13), channel_id=1, source_target_pairs={{0,64},{32,96},{64,0},{96,32},{128,192},{160,224},{192,128},{224,1... | collective-permute-start | bytes 24584 | tf_op jit(solution)/shard_map/ppermute | solution.py:581
  122.6 7.1 %collective-permute-start.8 = (f32[16,128]{1,0:T(8,128)S(1)}, f32[16,128]{1,0:T(8,128)S(1)}, u32[]{:S(2)}, u32[]{:S(2)}) collective-permute-start(f32[16,128]{1,0:T(8,128)S(1)} %add.14), channel_id=1, source_target_pairs={{0,224},{32,192},{64,160},{96,128},{128,96},{160,64},{192,32},{224... | collective-permute-start | bytes 24584 | tf_op jit(solution)/shard_map/ppermute | solution.py:581
  130.4 10.2 %all-to-all-start.3 = ((f32[16,16,128]{2,1,0:T(8,128)}), f32[16,16,128]{2,1,0:T(8,128)S(1)}, u32[]{:S(2)}, u32[]{:S(2)}) async-start(f32[16,16,128]{2,1,0:T(8,128)} %broadcast_in_dim.18), calls=%async_computation.3 | async-start | bytes 262144 | tf_op jit(solution)/shard_map/all_to_all | solution.py:565
  134.3 1.7 %copy-start.16 = (f32[128,5120]{1,0:T(8,128)S(1)}, f32[128,5120]{1,0:T(8,128)}, u32[]{:S(2)}) copy-start(f32[128,5120]{1,0:T(8,128)} %copy-done.15) | copy-start | bytes 7864324
  (11 other events, 7.2 us)

commit v3 on v2

v3 whole, which is shorter than its diff:
```python
import functools

import jax
import jax.numpy as jnp
from jax import lax
from jax.experimental import pallas as pl
from jax.experimental.pallas import tpu as pltpu
from jax.sharding import Mesh
from jax.sharding import PartitionSpec as P

HEADS = 64
HEAD_DIM = 64
GROUPS = 4
STATE = 128
TAPS = 4
T = 128
LANES = 128
WIDTH_X = HEADS * HEAD_DIM
WIDTH_B = GROUPS * STATE
CHANNELS = WIDTH_X + 2 * WIDTH_B
GROUP_X = WIDTH_X // GROUPS
PAIRS = HEADS // 2
GROUP_PAIRS = PAIRS // GROUPS
GROUP_HEADS = HEADS // GROUPS
HALF_PAIRS = PAIRS // 2
HALF_GROUPS = GROUPS // 2
F32 = jnp.float32
BF16 = jnp.bfloat16
EXACT = lax.Precision.HIGHEST
NN = (((1,), (0,)), ((), ()))
NT = (((1,), (1,)), ((), ()))
SUM_ROWS = 256
SUM_GROUP = SUM_ROWS // GROUPS
PACK_ROWS = 2 * STATE + 16


def dot(a, b, dims=NN):
    return lax.dot_general(a, b, dims, preferred_element_type=F32)


def exact_dot(a, b, dims=NN):
    return lax.dot_general(a, b, dims, precision=EXACT, preferred_element_type=F32)


def iota(shape, dim):
    return lax.broadcasted_iota(jnp.int32, shape, dim)


def sigmoid(v):
    return 0.5 + 0.5 * jnp.tanh(0.5 * v)


def split_two(v):
    high = v.astype(BF16)
    return high, (v - high.astype(F32)).astype(BF16)


def span(index, size):
    return pl.ds(pl.multiple_of(index * size, size), size)


def pin(value, space):
    return pltpu.with_memory_space_constraint(value, space)


def placed(space, shape, dtype):
    return space(shape, dtype)


def call(kernel, name, outs, specs, micros, scratch=(), mib=28, aliases=None):
    cost = pl.CostEstimate(
        flops=int(micros * 1e9), transcendentals=0, bytes_accessed=int(micros * 3.6e6)
    )
    blocks = {
        "s": pl.BlockSpec(memory_space=pltpu.SMEM),
        "v": pl.BlockSpec(memory_space=pltpu.VMEM),
        "V": pl.BlockSpec(memory_space=pltpu.VMEM),
        "h": pl.BlockSpec(memory_space=pltpu.HBM),
    }
    spaces = {"V": pltpu.VMEM, "h": pltpu.HBM}
    shapes = [
        placed(spaces[p], shape, dtype) if p in spaces else jax.ShapeDtypeStruct(shape, dtype)
        for p, shape, dtype in outs
    ]
    run = pl.pallas_call(
        kernel,
        out_shape=shapes,
        in_specs=[blocks[p] for p in specs],
        out_specs=[blocks[p] for p, _, _ in outs],
        scratch_shapes=list(scratch),
        input_output_aliases=aliases or {},
        cost_estimate=cost,
        compiler_params=pltpu.CompilerParams(vmem_limit_bytes=mib << 20),
        name=name,
    )

    def go(*args):
        return run(*[pin(a, spaces[p]) if p in spaces else a for a, p in zip(args, specs, strict=True)])

    return go


def start_all(pairs, sems):
    copies = [pltpu.make_async_copy(a, b, sems.at[i]) for i, (a, b) in enumerate(pairs)]
    for copy in copies:
        copy.start()
    return copies


def wait_all(copies):
    for copy in copies:
        copy.wait()


def DMA(*shape):
    return pltpu.SemaphoreType.DMA(shape)


def fill_window(win_ref, before, tokens):
    width = tokens.shape[1]
    win_ref[0:8, :width] = before
    win_ref[8 : 8 + T, :width] = tokens.astype(F32)


def pre_conv(win_ref, weights, lo):
    cols = slice(lo, lo + LANES)
    acc = weights[0:1, cols] * win_ref[5 : 5 + T, cols]
    for k in range(1, TAPS):
        acc = acc + weights[k : k + 1, cols] * win_ref[5 + k : 5 + k + T, cols]
    return acc


BLOCKS = CHANNELS // GROUP_X


ROW_DT, ROW_SEG, ROW_COLS, ROW_SCALE, ROW_TOT, ROW_SKIP, ROW_DECAY, SMALL_ROWS = (
    0, 64, 128, 256, 384, 416, 448, 512
)


def begin_kernel(raw_h, decay_log_h, skip_gain_h, tok_h, weight_h,
                 small_h, small_ref, tot_ref, x_ref, bc_ref, head_ref,
                 raw_ref, decay_log_ref, skip_gain_ref, weight_ref, hold_ref, win_ref, sems):
    first = start_all(
        [(raw_h, raw_ref), (decay_log_h, decay_log_ref), (skip_gain_h, skip_gain_ref), (weight_h, weight_ref)],
        sems.at[0],
    )
    blocks = [pl.ds(i * GROUP_X, GROUP_X) for i in range(BLOCKS)]
    copies = start_all([(tok_h.at[:, at], hold_ref.at[:, at]) for at in blocks], sems.at[1])
    diagonal = iota((HEADS, HEADS), 0) == iota((HEADS, HEADS), 1)

    def column(row):
        return jnp.sum(jnp.where(diagonal, row, 0.0), axis=1, keepdims=True)

    wait_all(first)
    raw = raw_ref[...]
    dt = jnp.log1p(jnp.exp(raw))
    decay = -jnp.exp(column(decay_log_ref[...]))
    upper = (iota((T, T), 0) <= iota((T, T), 1)).astype(F32)
    seg = exact_dot(dt * decay, upper)
    total = seg[:, T - 1 : T]
    small_ref[ROW_DT : ROW_DT + HEADS] = dt
    small_ref[ROW_SEG : ROW_SEG + HEADS] = seg
    small_ref[ROW_COLS : ROW_COLS + T] = jnp.transpose(jnp.concatenate([seg, dt], axis=0))
    small_ref[ROW_SCALE : ROW_SCALE + T] = jnp.transpose(
        jnp.concatenate([jnp.exp(seg), jnp.exp(total - seg) * dt], axis=0)
    )
    left = iota((PAIRS, LANES), 1) < HEAD_DIM
    even = (iota((PAIRS, HEADS), 1) == 2 * iota((PAIRS, HEADS), 0)).astype(F32)
    odd = (iota((PAIRS, HEADS), 1) == 2 * iota((PAIRS, HEADS), 0) + 1).astype(F32)

    def paired(col):
        wide = jnp.broadcast_to(col, (HEADS, LANES))
        return jnp.where(left, exact_dot(even, wide), exact_dot(odd, wide))

    tot = paired(total)
    tot_ref[...] = tot
    small_ref[ROW_TOT : ROW_TOT + PAIRS] = tot
    small_ref[ROW_SKIP : ROW_SKIP + PAIRS] = paired(column(skip_gain_ref[...]))
    small_ref[ROW_DECAY : ROW_DECAY + HEADS] = jnp.broadcast_to(decay, (HEADS, LANES))
    save = start_all([(small_ref, small_h)], sems.at[0])
    win_ref[0:8, :] = jnp.zeros((8, GROUP_X), F32)
    for i in range(BLOCKS):
        copies[i].wait()
        cols = slice(i * GROUP_X, (i + 1) * GROUP_X)
        win_ref[8 : 8 + T, :] = hold_ref[:, cols].astype(F32)
        for lo in range(0, GROUP_X, LANES):
            at = i * GROUP_X + lo
            pre = pre_conv(win_ref, weight_ref[:, cols], lo)
            mixed = (pre * sigmoid(pre)).astype(BF16)
            head_ref[:, at : at + LANES] = pre[0:8]
            if at < WIDTH_X:
                x_ref[:, at : at + LANES] = mixed
            else:
                bc_ref[:, at - WIDTH_X : at - WIDTH_X + LANES] = mixed
    wait_all(save)


def run_begin(raw, decay_log, skip_gain, tokens, weight):
    out = [
        ("h", (SMALL_ROWS, LANES), F32),
        ("V", (SMALL_ROWS, LANES), F32),
        ("V", (PAIRS, LANES), F32),
        ("V", (T, WIDTH_X), BF16),
        ("V", (T, 2 * WIDTH_B), BF16),
        ("V", (8, CHANNELS), F32),
    ]
    scratch = [
        pltpu.VMEM((HEADS, T), F32),
        pltpu.VMEM((1, HEADS), F32),
        pltpu.VMEM((1, HEADS), F32),
        pltpu.VMEM((TAPS, CHANNELS), F32),
        pltpu.VMEM((T, CHANNELS), BF16),
        pltpu.VMEM((8 + T, GROUP_X), F32),
        DMA(2, BLOCKS),
    ]
    return call(begin_kernel, "begin", out, "hhhhh", 4, scratch, mib=16)(
        raw, decay_log, skip_gain, tokens, weight
    )


def rolled(cols, group):
    return pltpu.roll(cols, (LANES - group * GROUP_HEADS) % LANES, 1)


def widen(cols, base, pair):
    first = iota((T, LANES), 1) < HEAD_DIM
    at = base + 2 * pair
    return jnp.where(first, cols[:, at : at + 1], cols[:, at + 1 : at + 2])


def widen_two(cols, base, pair):
    return jnp.concatenate([widen(cols, base, pair), widen(cols, base, pair + 1)], axis=1)


def fill_half(half, x_ref, bc_ref, g_ref, copies, scale, dst_ref):
    for jj in range(HALF_GROUPS):
        j = half * HALF_GROUPS + jj
        copies[jj].wait()
        b_flip = jnp.transpose(bc_ref[:, span(j, STATE)].astype(F32)).astype(BF16)
        c_flip = jnp.transpose(bc_ref[:, span(GROUPS + j, STATE)].astype(F32)).astype(BF16)
        cols = rolled(scale, j)
        for q in range(0, GROUP_PAIRS, 2):
            lanes = pl.ds(pl.multiple_of(j * GROUP_X + q * LANES, 2 * LANES), 2 * LANES)
            near = slice(jj * GROUP_X + q * LANES, jj * GROUP_X + (q + 2) * LANES)
            xw = (x_ref[:, lanes].astype(F32) * widen_two(cols, HEADS, q)).astype(BF16)
            gw = (g_ref[:, near].astype(F32) * widen_two(cols, 0, q)).astype(BF16)
            state = dot(b_flip, xw).astype(BF16)
            grad = dot(c_flip, gw).astype(BF16)
            for k in range(2):
                at = jj * GROUP_PAIRS + q + k
                dst_ref[0, at] = state[:, k * LANES : (k + 1) * LANES]
                dst_ref[1, at] = grad[:, k * LANES : (k + 1) * LANES]


def load_half(half, g_h, g_ref, sems):
    return start_all(
        [
            (g_h.at[:, span(half * HALF_GROUPS + jj, GROUP_X)], g_ref.at[:, pl.ds(jj * GROUP_X, GROUP_X)])
            for jj in range(HALF_GROUPS)
        ],
        sems,
    )


def enter_kernel(core_ref, x0_ref, bc0_ref, head_ref, halo_ref, weight_h, g_h, small_ref,
                 x_h, bc_h, before_h, x_ref, bc_ref, out_ref, g_ref, weight_ref, before_ref, sems):
    half = 1 - core_ref[0]
    weight_copy = start_all([(weight_h, weight_ref)], sems.at[0])
    copies = load_half(half, g_h, g_ref, sems.at[1])
    row = iota((8, GROUP_X), 0)
    wait_all(weight_copy)
    for i in range(BLOCKS):
        cols = slice(i * GROUP_X, (i + 1) * GROUP_X)
        halo = halo_ref[:, cols].astype(F32)
        weight = weight_ref[:, cols]
        pre = head_ref[:, cols]
        before = jnp.zeros((8, GROUP_X), F32)
        for t in range(TAPS - 1):
            extra = jnp.zeros((1, GROUP_X), F32)
            for k in range(TAPS - 1 - t):
                extra = extra + weight[k : k + 1] * halo[t + k : t + k + 1]
            pre = pre + jnp.where(row == t, extra, 0.0)
            before = before + jnp.where(row == t + 5, halo[t : t + 1], 0.0)
        before_ref[:, cols] = before
        fixed = pre * sigmoid(pre)
        src, dst, at = (x0_ref, x_ref, cols) if i < GROUPS else (bc0_ref, bc_ref, slice(0, GROUP_X))
        rest = src[0:16, at].astype(F32)
        dst[16:T, at] = src[16:T, at]
        dst[0:16, at] = jnp.concatenate([fixed, rest[8:16]], axis=0).astype(BF16)
    saves = start_all([(x_ref, x_h), (bc_ref, bc_h), (before_ref, before_h)], sems.at[0])
    fill_half(half, x_ref, bc_ref, g_ref, copies, small_ref[ROW_SCALE : ROW_SCALE + T], out_ref)
    wait_all(saves)


def run_enter(core, x0, bc0, head, halo, weight, cot, small):
    out = [
        ("h", (T, WIDTH_X), BF16),
        ("h", (T, 2 * WIDTH_B), BF16),
        ("h", (8, CHANNELS), F32),
        ("V", (T, WIDTH_X), BF16),
        ("V", (T, 2 * WIDTH_B), BF16),
        ("V", (2, HALF_PAIRS, STATE, LANES), BF16),
    ]
    scratch = [
        pltpu.VMEM((T, HALF_GROUPS * GROUP_X), BF16),
        pltpu.VMEM((TAPS, CHANNELS), F32),
        pltpu.VMEM((8, CHANNELS), F32),
        DMA(2, 3),
    ]
    return call(enter_kernel, "enter", out, "sVVVvhhV", 3, scratch, mib=16)(
        core, x0, bc0, head, halo, weight, cot, small
    )


def own_kernel(core_ref, x_ref, bc_ref, g_h, small_ref, own_ref, g_ref, sems):
    copies = load_half(core_ref[0], g_h, g_ref, sems)
    fill_half(core_ref[0], x_ref, bc_ref, g_ref, copies, small_ref[ROW_SCALE : ROW_SCALE + T], own_ref)


def run_own(core, x, bc, cot, small):
    out = [("V", (2, HALF_PAIRS, STATE, LANES), BF16)]
    scratch = [pltpu.VMEM((T, HALF_GROUPS * GROUP_X), BF16), DMA(HALF_GROUPS)]
    return call(own_kernel, "own", out, "sVVhV", 3, scratch, mib=16)(core, x, bc, cot, small)[0]


STEP_PAIRS = 4
STEPS = HALF_PAIRS // STEP_PAIRS


def pack_kernel(core_ref, own_ref, got_ref, tot_ref, other_ref,
                out_h, own_h, got_h, tots_h, out_ref, sems):
    saves = start_all(
        [
            (own_ref, own_h),
            (got_ref, got_h),
            (tot_ref, tots_h.at[pl.ds(0, PAIRS)]),
            (other_ref, tots_h.at[pl.ds(PAIRS, PAIRS)]),
        ],
        sems.at[0],
    )
    second = core_ref[0] == 1
    outs = []
    for i in range(HALF_PAIRS):
        at = core_ref[0] * HALF_PAIRS + i
        tot = tot_ref[pl.ds(at, 1), :]
        other = other_ref[pl.ds(at, 1), :]
        one = jnp.ones_like(tot)
        by_own = jnp.exp(tot)
        by_other = jnp.exp(other)
        state = (
            jnp.where(second, one, by_other) * own_ref[0, i].astype(F32)
            + jnp.where(second, by_own, one) * got_ref[0, i].astype(F32)
        )
        grad = (
            jnp.where(second, by_other, one) * own_ref[1, i].astype(F32)
            + jnp.where(second, one, by_own) * got_ref[1, i].astype(F32)
        )
        out_ref[i, 0:STATE, :] = state.astype(BF16)
        out_ref[i, STATE : 2 * STATE, :] = grad.astype(BF16)
        both = tot + other
        high = both.astype(BF16).astype(F32)
        mid = (both - high).astype(BF16).astype(F32)
        low = both - high - mid
        row = iota((16, LANES), 0)
        wide = jnp.where(row == 0, high, jnp.where(row == 1, mid, jnp.where(row == 2, low, 0.0)))
        out_ref[i, 2 * STATE : PACK_ROWS, :] = wide.astype(BF16)
        if i % STEP_PAIRS == STEP_PAIRS - 1:
            done = pl.ds(i + 1 - STEP_PAIRS, STEP_PAIRS)
            copy = pltpu.make_async_copy(out_ref.at[done], out_h.at[done], sems.at[1, i // STEP_PAIRS])
            copy.start()
            outs.append(copy)
    wait_all(outs + saves)


def run_pack(core, own, got, tot, other):
    half = (2, HALF_PAIRS, STATE, LANES)
    packed = (HALF_PAIRS, PACK_ROWS, LANES)
    out = [("h", packed, BF16), ("h", half, BF16), ("h", half, BF16), ("h", (2 * PAIRS, LANES), F32)]
    scratch = [pltpu.VMEM(packed, BF16), DMA(2, STEPS)]
    return call(pack_kernel, "pack", out, "sVvVv", 2, scratch, mib=16)(core, own, got, tot, other)


def chain_kernel(chips, per, in_ref, out_ref):
    for q in range(per):
        def decay(k):
            rows = in_ref[k * per + q, 2 * STATE : PACK_ROWS, :].astype(F32)
            return jnp.exp(rows[0:1] + rows[1:2] + rows[2:3])

        carry = jnp.zeros((STATE, LANES), F32)
        for k in range(chips):
            out_ref[k * per + q, 0:STATE, :] = carry.astype(BF16)
            if k < chips - 1:
                carry = decay(k) * carry + in_ref[k * per + q, 0:STATE, :].astype(F32)
        carry = jnp.zeros((STATE, LANES), F32)
        for k in reversed(range(chips)):
            out_ref[k * per + q, STATE : 2 * STATE, :] = carry.astype(BF16)
            if k > 0:
                carry = decay(k) * carry + in_ref[k * per + q, STATE : 2 * STATE, :].astype(F32)


def run_chain(chips, packed):
    kernel = functools.partial(chain_kernel, chips, HALF_PAIRS // chips)
    out = [("v", (HALF_PAIRS, 2 * STATE, LANES), BF16)]
    return call(kernel, "chain", out, "v", 1, mib=16)(packed)[0]


def unpack_kernel(core_ref, back_h, own_h, got_h, tots_h, mine_ref, send_ref,
                  back_ref, own_ref, got_ref, tots_ref, sems):
    first = start_all([(tots_h, tots_ref)], sems.at[STEPS])
    steps = []
    for step in range(STEPS):
        at = pl.ds(step * STEP_PAIRS, STEP_PAIRS)
        steps.append(
            start_all(
                [
                    (back_h.at[at], back_ref.at[at]),
                    (own_h.at[:, at], own_ref.at[:, at]),
                    (got_h.at[:, at], got_ref.at[:, at]),
                ],
                sems.at[step],
            )
        )
    wait_all(first)
    second = core_ref[0] == 1
    for i in range(HALF_PAIRS):
        if i % STEP_PAIRS == 0:
            wait_all(steps[i // STEP_PAIRS])
        at = core_ref[0] * HALF_PAIRS + i
        tot = tots_ref[pl.ds(at, 1), :]
        other = tots_ref[pl.ds(PAIRS + at, 1), :]
        decay_zero = jnp.exp(jnp.where(second, other, tot))
        decay_one = jnp.exp(jnp.where(second, tot, other))
        state_zero = back_ref[i, 0:STATE, :].astype(F32)
        grad_one = back_ref[i, STATE : 2 * STATE, :].astype(F32)
        left = jnp.where(second, got_ref[0, i].astype(F32), own_ref[0, i].astype(F32))
        right = jnp.where(second, own_ref[1, i].astype(F32), got_ref[1, i].astype(F32))
        state_one = decay_zero * state_zero + left
        grad_zero = decay_one * grad_one + right
        mine_ref[0, i] = jnp.where(second, state_one, state_zero).astype(BF16)
        mine_ref[1, i] = jnp.where(second, grad_one, grad_zero).astype(BF16)
        send_ref[0, i] = jnp.where(second, state_zero, state_one).astype(BF16)
        send_ref[1, i] = jnp.where(second, grad_zero, grad_one).astype(BF16)


def run_unpack(core, back, own, got, tots):
    half = (2, HALF_PAIRS, STATE, LANES)
    out = [("V", half, BF16)] * 2
    scratch = [
        pltpu.VMEM((HALF_PAIRS, 2 * STATE, LANES), BF16),
        pltpu.VMEM(half, BF16),
        pltpu.VMEM(half, BF16),
        pltpu.VMEM((2 * PAIRS, LANES), F32),
        DMA(STEPS + 1, 3),
    ]
    return call(unpack_kernel, "unpack", out, "shhhh", 2, scratch, mib=16)(core, back, own, got, tots)


def by_lane_half(v):
    first = iota(v.shape, 1) < HEAD_DIM
    wide = v.astype(F32)
    return jnp.concatenate(
        [jnp.where(first, wide, 0.0).astype(BF16), jnp.where(first, 0.0, wide).astype(BF16)], axis=0
    )


def inner_kernel(x_h, bc_h, g_h, small_h, y_h, gbc_h, x_ref, bc_ref, g_ref, small_ref, y_ref, gbc_ref, sems):
    first = start_all([(bc_h, bc_ref), (small_h, small_ref)], sems.at[0])

    def loads(j):
        at = span(j, GROUP_X)
        return [
            pltpu.make_async_copy(x_h.at[:, at], x_ref.at[:, at], sems.at[1, j]),
            pltpu.make_async_copy(g_h.at[:, at], g_ref.at[:, at], sems.at[2, j]),
        ]

    def store(j):
        at = span(j, GROUP_X)
        return pltpu.make_async_copy(y_ref.at[:, at], y_h.at[:, at], sems.at[3, j])

    for j in range(GROUPS):
        for copy in loads(j):
            copy.start()
    wait_all(first)
    lower = iota((T, T), 0) >= iota((T, T), 1)

    @pl.loop(0, GROUPS)
    def _(j):
        wait_all(loads(j))
        b = bc_ref[:, span(j, STATE)]
        c = bc_ref[:, span(GROUPS + j, STATE)]
        seg = small_ref[pl.ds(pl.multiple_of(ROW_SEG + j * GROUP_HEADS, GROUP_HEADS), GROUP_HEADS), :]
        dt = small_ref[pl.ds(pl.multiple_of(ROW_DT + j * GROUP_HEADS, GROUP_HEADS), GROUP_HEADS), :]
        scores = dot(c, b, NT)
        cols = rolled(small_ref[ROW_COLS : ROW_COLS + T], j)
        total = jnp.zeros((T, T), F32)
        for i in range(GROUP_PAIRS):
            lanes = pl.ds(pl.multiple_of(j * GROUP_X + i * LANES, LANES), LANES)
            x = x_ref[:, lanes]
            inner = dot(by_lane_half(g_ref[:, lanes]), x, NT)
            weights = []
            for k in range(2):
                h = 2 * i + k
                spread = cols[:, h : h + 1] - seg[h : h + 1, :]
                kernel = jnp.exp(jnp.where(lower, spread, -1e30)) * dt[h : h + 1, :]
                total = total + kernel * inner[k * T : (k + 1) * T]
                weights.append((kernel * scores).astype(BF16))
            y_ref[:, lanes] = dot(jnp.concatenate(weights, axis=1), by_lane_half(x))
        gbc_ref[:, span(GROUPS + j, STATE)] = dot(total.astype(BF16), b)
        gbc_ref[:, span(j, STATE)] = dot(jnp.transpose(total).astype(BF16), c)
        store(j).start()

    last = start_all([(gbc_ref, gbc_h)], sems.at[0])
    for j in range(GROUPS):
        store(j).wait()
    wait_all(last)


def run_inner(x, bc, cot, small):
    out = [("h", (T, WIDTH_X), F32), ("h", (T, 2 * WIDTH_B), F32)]
    scratch = [
        pltpu.VMEM((T, WIDTH_X), BF16),
        pltpu.VMEM((T, 2 * WIDTH_B), BF16),
        pltpu.VMEM((T, WIDTH_X), BF16),
        pltpu.VMEM((SMALL_ROWS, LANES), F32),
        pltpu.VMEM((T, WIDTH_X), F32),
        pltpu.VMEM((T, 2 * WIDTH_B), F32),
        DMA(4, GROUPS),
    ]
    return call(inner_kernel, "inner", out, "hhhh", 4, scratch, mib=24)(x, bc, cot, small)


def slopes_kernel(bc_h, g_h, small_h, tok_h, before_h, weight_h, gx_h, slope_h,
                  bc_ref, g_ref, small_ref, tok_ref, before_ref, weight_ref, gx_ref, slope_ref, win_ref, sems):
    first = start_all(
        [(bc_h, bc_ref), (small_h, small_ref), (before_h, before_ref), (weight_h, weight_ref), (tok_h, tok_ref)],
        sems.at[0],
    )

    def load(j):
        at = span(j, GROUP_X)
        return pltpu.make_async_copy(g_h.at[:, at], g_ref.at[:, at], sems.at[1, j])

    def store(j):
        at = span(j, GROUP_X)
        return pltpu.make_async_copy(gx_ref.at[:, at], gx_h.at[:, at], sems.at[2, j])

    def store_slope(i):
        at = span(i, GROUP_X)
        return pltpu.make_async_copy(slope_ref.at[:, at], slope_h.at[:, at], sems.at[3, i])

    for j in range(GROUPS):
        load(j).start()
    wait_all(first)
    upper = iota((T, T), 0) <= iota((T, T), 1)

    @pl.loop(0, GROUPS)
    def _(j):
        load(j).wait()
        b = bc_ref[:, span(j, STATE)]
        c = bc_ref[:, span(GROUPS + j, STATE)]
        seg = small_ref[pl.ds(pl.multiple_of(ROW_SEG + j * GROUP_HEADS, GROUP_HEADS), GROUP_HEADS), :]
        scores = jnp.transpose(dot(c, b, NT))
        cols = rolled(small_ref[ROW_COLS : ROW_COLS + T], j)
        for i in range(GROUP_PAIRS):
            lanes = pl.ds(pl.multiple_of(j * GROUP_X + i * LANES, LANES), LANES)
            weights = []
            for k in range(2):
                h = 2 * i + k
                spread = seg[h : h + 1, :] - cols[:, h : h + 1]
                kernel = jnp.exp(jnp.where(upper, spread, -1e30)) * cols[:, HEADS + h : HEADS + h + 1]
                weights.append((kernel * scores).astype(BF16))
            gx_ref[:, lanes] = dot(jnp.concatenate(weights, axis=1), by_lane_half(g_ref[:, lanes]))
        store(j).start()

    @pl.loop(0, BLOCKS)
    def _(i):
        cols = span(i, GROUP_X)
        fill_window(win_ref, before_ref[:, cols], tok_ref[:, cols])
        weights = weight_ref[:, cols]
        for lo in range(0, GROUP_X, LANES):
            pre = pre_conv(win_ref, weights, lo)
            s = sigmoid(pre)
            at = pl.ds(pl.multiple_of(i * GROUP_X + lo, LANES), LANES)
            slope_ref[:, at] = s * (1.0 + pre * (1.0 - s))
        store_slope(i).start()

    for j in range(GROUPS):
        store(j).wait()
    for i in range(BLOCKS):
        store_slope(i).wait()


def run_slopes(bc, cot, small, tokens, before, weight):
    out = [("h", (T, WIDTH_X), F32), ("h", (T, CHANNELS), F32)]
    scratch = [
        pltpu.VMEM((T, 2 * WIDTH_B), BF16),
        pltpu.VMEM((T, WIDTH_X), BF16),
        pltpu.VMEM((SMALL_ROWS, LANES), F32),
        pltpu.VMEM((T, CHANNELS), BF16),
        pltpu.VMEM((8, CHANNELS), F32),
        pltpu.VMEM((TAPS, CHANNELS), F32),
        pltpu.VMEM((T, WIDTH_X), F32),
        pltpu.VMEM((T, CHANNELS), F32),
        pltpu.VMEM((8 + T, GROUP_X), F32),
        DMA(4, BLOCKS),
    ]
    return call(slopes_kernel, "slopes", out, "hhhhhh", 6, scratch, mib=24)(
        bc, cot, small, tokens, before, weight
    )


def leave_kernel(theirs, core_ref, x_h, bc_h, g_h, y_h, gx_h, gbc_h, slope_h, tok_h, before_h, state_ref,
                 small_h, raw_h, *rest):
    (out_h, pre_h, step_h, sum_h, x_ref, bc_ref, g_ref, y_ref, gx_ref, gbc_ref, slope_ref, tok_ref,
     before_ref, small_ref, raw_ref, out_ref, pre_ref, step_ref, sum_ref, win_ref, sems) = rest[-21:]
    half = 1 - core_ref[0] if theirs else core_ref[0]

    def loads(jj):
        j = half * HALF_GROUPS + jj
        far, near = span(j, GROUP_X), span(jj, GROUP_X)
        pairs = [(h.at[:, far], v.at[:, near]) for h, v in (
            (x_h, x_ref), (g_h, g_ref), (y_h, y_ref), (gx_h, gx_ref), (slope_h, slope_ref), (tok_h, tok_ref)
        )]
        return [pltpu.make_async_copy(a, b, sems.at[1 + jj, i]) for i, (a, b) in enumerate(pairs)]

    def thin(jj):
        pairs = []
        for base in range(2):
            far = span(base * GROUPS + half * HALF_GROUPS + jj, STATE)
            wide = span(WIDTH_X // STATE + base * GROUPS + half * HALF_GROUPS + jj, STATE)
            near = span(base * HALF_GROUPS + jj, STATE)
            at = pl.ds(HALF_GROUPS * GROUP_X + (base * HALF_GROUPS + jj) * STATE, STATE)
            pairs += [
                (bc_h.at[:, far], bc_ref.at[:, near]),
                (gbc_h.at[:, far], gbc_ref.at[:, near]),
                (slope_h.at[:, wide], slope_ref.at[:, at]),
                (tok_h.at[:, wide], tok_ref.at[:, at]),
            ]
        return [pltpu.make_async_copy(a, b, sems.at[3 + jj, i]) for i, (a, b) in enumerate(pairs)]

    first = start_all([(small_h, small_ref), (before_h, before_ref), (raw_h, raw_ref)], sems.at[0])
    for jj in range(HALF_GROUPS):
        for copy in loads(jj) + thin(jj):
            copy.start()
    wait_all(first)
    last = iota((T, 2 * LANES), 0) == T - 1
    lower = (iota((T, T), 0) >= iota((T, T), 1)).astype(F32)

    def tap_sums(grad_pre, lo):
        width = grad_pre.shape[1]
        return [
            jnp.sum(grad_pre * win_ref[5 + k : 5 + k + T, lo : lo + width], axis=0, keepdims=True)
            for k in range(TAPS)
        ]

    def by_rows(sums):
        return [s[:, lo : lo + LANES] for lo in range(0, sums[0].shape[1], LANES) for s in sums]

    saves = []

    def save(src, dst):
        copy = pltpu.make_async_copy(src, dst, sems.at[5 + len(saves) // 8, len(saves) % 8])
        copy.start()
        saves.append(copy)

    for jj in range(HALF_GROUPS):
        j = half * HALF_GROUPS + jj
        wait_all(loads(jj) + thin(jj))
        near_b = slice(jj * STATE, (jj + 1) * STATE)
        near_c = slice((HALF_GROUPS + jj) * STATE, (HALF_GROUPS + jj + 1) * STATE)
        b = bc_ref[:, near_b]
        c = bc_ref[:, near_c]
        grad_b = gbc_ref[:, near_b]
        grad_c = gbc_ref[:, near_c]
        cols = rolled(small_ref[ROW_SCALE : ROW_SCALE + T], j)
        skip_rows = small_ref[pl.ds(pl.multiple_of(ROW_SKIP + j * GROUP_PAIRS, GROUP_PAIRS), GROUP_PAIRS), :]
        tot_rows = small_ref[pl.ds(pl.multiple_of(ROW_TOT + j * GROUP_PAIRS, GROUP_PAIRS), GROUP_PAIRS), :]
        seg_grad = jnp.zeros((GROUP_HEADS, T), F32)
        dt_grad = jnp.zeros((GROUP_HEADS, T), F32)
        skips = []
        terms = []
        near = slice(jj * GROUP_X, (jj + 1) * GROUP_X)
        fill_window(win_ref, before_ref[:, span(j, GROUP_X)], tok_ref[:, near])
        for q in range(0, GROUP_PAIRS, 2):
            lanes = slice(jj * GROUP_X + q * LANES, jj * GROUP_X + (q + 2) * LANES)
            rise = widen_two(cols, 0, q)
            keep = widen_two(cols, HEADS, q)
            at = jj * GROUP_PAIRS + q
            state = jnp.concatenate([state_ref[0, at], state_ref[0, at + 1]], axis=1)
            exits = jnp.concatenate([state_ref[1, at], state_ref[1, at + 1]], axis=1)
            skip = jnp.concatenate([skip_rows[q : q + 1], skip_rows[q + 1 : q + 2]], axis=1)
            tot = jnp.concatenate([tot_rows[q : q + 1], tot_rows[q + 1 : q + 2]], axis=1)
            x = x_ref[:, lanes].astype(F32)
            g = g_ref[:, lanes].astype(F32)
            y = y_ref[:, lanes] + rise * dot(c, state)
            through = keep * dot(b, exits)
            gx = gx_ref[:, lanes] + through
            grad_c = grad_c + dot((g * rise).astype(BF16), state, NT)
            grad_b = grad_b + dot((x * keep).astype(BF16), exits, NT)
            out_ref[:, lanes] = (y + skip * x).astype(BF16)
            grad_pre = (gx + skip * g) * slope_ref[:, lanes]
            pre_ref[:, lanes] = grad_pre
            terms += by_rows(tap_sums(grad_pre, q * LANES))
            skips += by_rows([jnp.sum(g * x, axis=0, keepdims=True)])
            x_gx = x * gx
            end = jnp.sum(x * through, axis=0, keepdims=True) + jnp.exp(tot) * jnp.sum(
                exits.astype(F32) * state.astype(F32), axis=0, keepdims=True
            )
            moved = g * y - x_gx + jnp.where(last, end, 0.0)
            pick = (
                iota((GROUP_HEADS, 2 * LANES), 0)
                == 2 * q + iota((GROUP_HEADS, 2 * LANES), 1) // HEAD_DIM
            ).astype(F32).astype(BF16)
            for part in split_two(moved):
                seg_grad = seg_grad + dot(pick, part, NT)
            for part in split_two(x_gx):
                dt_grad = dt_grad + dot(pick, part, NT)
        save(out_ref.at[:, pl.ds(jj * GROUP_X, GROUP_X)], out_h.at[:, span(j, GROUP_X)])
        save(pre_ref.at[:, pl.ds(jj * GROUP_X, GROUP_X)], pre_h.at[:, span(j, GROUP_X)])
        for grad, base in ((grad_b, 0), (grad_c, 1)):
            at = HALF_GROUPS * GROUP_X + (base * HALF_GROUPS + jj) * STATE
            far = span(WIDTH_X // STATE + base * GROUPS + j, STATE)
            fill_window(win_ref, before_ref[:, far], tok_ref[:, at : at + STATE])
            grad_pre = grad * slope_ref[:, at : at + STATE]
            pre_ref[:, at : at + STATE] = grad_pre
            terms += tap_sums(grad_pre, 0)
            save(pre_ref.at[:, pl.ds(at, STATE)], pre_h.at[:, far])
        heads = span(j, GROUP_HEADS)
        behind = exact_dot(seg_grad, lower)
        dt = small_ref[pl.ds(pl.multiple_of(ROW_DT + j * GROUP_HEADS, GROUP_HEADS), GROUP_HEADS), :]
        decay = small_ref[pl.ds(pl.multiple_of(ROW_DECAY + j * GROUP_HEADS, GROUP_HEADS), GROUP_HEADS), :]
        near = pl.ds(jj * GROUP_HEADS, GROUP_HEADS)
        step_ref[near, :] = (dt_grad / dt + decay * behind) * sigmoid(raw_ref[heads, :])
        save(step_ref.at[near], step_h.at[heads])
        rows = jj * SUM_GROUP
        sum_ref[rows : rows + SUM_GROUP, :] = jnp.concatenate(terms + skips + [dt * behind * decay], axis=0)
        save(sum_ref.at[pl.ds(rows, SUM_GROUP)], sum_h.at[span(j, SUM_GROUP)])
    wait_all(saves)


def run_leave(core, inputs, state, small, raw, before_out):
    out = [
        ("h", (T, WIDTH_X), BF16),
        ("h", (T, CHANNELS), F32),
        ("h", (HEADS, T), F32),
        ("h", (SUM_ROWS, LANES), F32),
    ]
    half_x = HALF_GROUPS * GROUP_X
    half_b = 2 * HALF_GROUPS * STATE
    scratch = [
        pltpu.VMEM((T, half_x), BF16),
        pltpu.VMEM((T, half_b), BF16),
        pltpu.VMEM((T, half_x), BF16),
        pltpu.VMEM((T, half_x), F32),
        pltpu.VMEM((T, half_x), F32),
        pltpu.VMEM((T, half_b), F32),
        pltpu.VMEM((T, half_x + half_b), F32),
        pltpu.VMEM((T, half_x + half_b), BF16),
        pltpu.VMEM((8, CHANNELS), F32),
        pltpu.VMEM((SMALL_ROWS, LANES), F32),
        pltpu.VMEM((HEADS, T), F32),
        pltpu.VMEM((T, half_x), BF16),
        pltpu.VMEM((T, half_x + half_b), F32),
        pltpu.VMEM((HALF_GROUPS * GROUP_HEADS, T), F32),
        pltpu.VMEM((HALF_GROUPS * SUM_GROUP, LANES), F32),
        pltpu.VMEM((8 + T, GROUP_X), F32),
        DMA(7, 8),
    ]
    args = [core, *inputs, state, small, raw]
    specs = "s" + "h" * 9 + ("V" if before_out is None else "v") + "hh"
    aliases = {}
    if before_out is not None:
        aliases = {len(args) + i: i for i in range(len(out))}
        args += before_out
        specs += "h" * len(out)
    kernel = functools.partial(leave_kernel, before_out is not None)
    return call(kernel, "leave", out, specs, 5, scratch, mib=24, aliases=aliases)(*args)


def spread_kernel(pre_h, halo_ref, weight_h, out_h, pre_ref, weight_ref, out_ref, win_ref, sems):
    first = start_all([(weight_h, weight_ref)], sems.at[0])

    def load(i):
        at = span(i, GROUP_X)
        return pltpu.make_async_copy(pre_h.at[:, at], pre_ref.at[:, at], sems.at[1, i])

    def store(i):
        at = span(i, GROUP_X)
        return pltpu.make_async_copy(out_ref.at[:, at], out_h.at[:, at], sems.at[2, i])

    for i in range(BLOCKS):
        load(i).start()
    wait_all(first)

    @pl.loop(0, BLOCKS)
    def _(i):
        load(i).wait()
        cols = span(i, GROUP_X)
        win_ref[0:T, :] = pre_ref[:, cols]
        win_ref[T : T + TAPS - 1, :] = halo_ref[:, cols].astype(F32)
        weights = weight_ref[:, cols]
        for lo in range(0, GROUP_X, LANES):
            at = slice(lo, lo + LANES)
            acc = weights[0:1, at] * win_ref[3 : 3 + T, at]
            for k in range(1, TAPS):
                acc = acc + weights[k : k + 1, at] * win_ref[3 - k : 3 - k + T, at]
            out_ref[:, pl.ds(pl.multiple_of(i * GROUP_X + lo, LANES), LANES)] = acc.astype(BF16)
        store(i).start()

    for i in range(BLOCKS):
        store(i).wait()


def run_spread(pre, halo, weight):
    out = [("h", (T, CHANNELS), BF16)]
    scratch = [
        pltpu.VMEM((T, CHANNELS), F32),
        pltpu.VMEM((TAPS, CHANNELS), F32),
        pltpu.VMEM((T, CHANNELS), BF16),
        pltpu.VMEM((T + 8, GROUP_X), F32),
        DMA(3, BLOCKS),
    ]
    return call(spread_kernel, "spread", out, "hvh", 4, scratch, mib=16)(pre, halo, weight)[0]


def finish_kernel(sum_ref, conv_ref, decay_ref, skip_ref):
    for i in range(CHANNELS // LANES):
        if i < PAIRS:
            row = SUM_GROUP * (i // GROUP_PAIRS) + TAPS * (i % GROUP_PAIRS)
        else:
            kind, group = divmod(i - PAIRS, GROUPS)
            row = SUM_GROUP * group + TAPS * (GROUP_PAIRS + kind)
        conv_ref[:, i * LANES : (i + 1) * LANES] = sum_ref[row : row + TAPS, :]
    skip_at, decay_at = TAPS * (GROUP_PAIRS + 2), SUM_GROUP - GROUP_HEADS
    skips = jnp.concatenate(
        [sum_ref[SUM_GROUP * j + skip_at : SUM_GROUP * j + decay_at, :] for j in range(GROUPS)], axis=0
    )
    decays = jnp.concatenate(
        [sum_ref[SUM_GROUP * j + decay_at : SUM_GROUP * (j + 1), :] for j in range(GROUPS)], axis=0
    )
    ones = jnp.ones((8, LANES), F32)
    decay_ref[...] = exact_dot(ones, decays, NT)[0:1]
    left = iota((8, LANES), 1) < HEAD_DIM
    even = exact_dot(jnp.where(left, 1.0, 0.0), skips, NT)
    odd = exact_dot(jnp.where(left, 0.0, 1.0), skips, NT)
    at_even = (iota((PAIRS, HEADS), 1) == 2 * iota((PAIRS, HEADS), 0)).astype(F32)
    at_odd = (iota((PAIRS, HEADS), 1) == 2 * iota((PAIRS, HEADS), 0) + 1).astype(F32)
    skip_ref[...] = (exact_dot(even, at_even) + exact_dot(odd, at_odd))[0:1]


def run_finish(sums):
    out = [("v", (TAPS, CHANNELS), F32), ("v", (1, HEADS), F32), ("v", (1, HEADS), F32)]
    return call(finish_kernel, "finish", out, "v", 1, mib=16)(sums)


CTX = ("chip", "core")
ALL = ("dp", "chip", "core")


def all_to_all(value, axis):
    return lax.all_to_all(value, axis, 0, 0, tiled=True)


def tie(*values):
    return lax.optimization_barrier(values)


def sum_everywhere(parts, chips):
    share = SUM_ROWS // chips
    total = jnp.sum(parts.reshape(chips, share, LANES), axis=0)
    total = total + lax.ppermute(total, "core", [(0, 1), (1, 0)])
    count = lax.axis_size("dp")
    flip = 1
    while flip < count:
        mask = flip if 2 * flip < count else count - 1
        total = total + lax.ppermute(total, "dp", [(i, i ^ mask) for i in range(count)])
        flip *= 2
    return all_to_all(jnp.broadcast_to(total[None], (chips, share, LANES)).reshape(SUM_ROWS, LANES), "chip")


def local(conv_input, conv_weight, step_raw, decay_log, skip_gain, cotangent):
    chips = lax.axis_size("chip")
    devices = 2 * chips
    tokens = conv_input[0]
    raw = step_raw[0]
    cot = cotangent[0]
    core = lax.axis_index("core").astype(jnp.int32).reshape(1)
    swap = [(0, 1), (1, 0)]
    halo = lax.ppermute(tokens[T - TAPS + 1 :], CTX, [(i, i + 1) for i in range(devices - 1)])
    small, small_near, tot, x0, bc0, head = run_begin(
        raw, decay_log.reshape(1, HEADS), skip_gain.reshape(1, HEADS), tokens, conv_weight
    )
    other = lax.ppermute(tot, "core", swap)
    x, bc, before, x_near, bc_near, out = run_enter(
        core, x0, bc0, head, halo, conv_weight, cot, small_near
    )
    got_near = lax.ppermute(out, "core", swap)
    own_near = run_own(core, x_near, bc_near, cot, small_near)
    packed, own, got, tots = run_pack(core, own_near, got_near, tot, other)
    heard = all_to_all(packed, "chip")
    y, gbc = run_inner(x, bc, cot, small)
    heard, y, gbc = tie(heard, y, gbc)
    chained = run_chain(chips, heard)
    late, chained = tie(bc, chained)
    back = all_to_all(chained, "chip")
    gx, slope = run_slopes(late, cot, small, tokens, before, conv_weight)
    back, gx, slope = tie(back, gx, slope)
    mine, send = run_unpack(core, back, own, got, tots)
    theirs = lax.ppermute(send, "core", swap)
    inputs = (x, bc, cot, y, gx, gbc, slope, tokens, before)
    half = run_leave(core, inputs, mine, small, raw, None)
    out_tokens, pre, grad_step, sums = run_leave(core, inputs, theirs, small, raw, half)
    parts = all_to_all(sums, "chip")
    first = pre[: TAPS - 1].astype(BF16)
    after = lax.ppermute(first, CTX, [(i + 1, i) for i in range(devices - 1)])
    parts, after = tie(parts, after)
    grad_conv, grad_decay, grad_skip = run_finish(sum_everywhere(parts, chips))
    grad_tokens = run_spread(pre, after, conv_weight)
    return (
        out_tokens[None],
        grad_tokens[None],
        grad_step[None],
        grad_conv,
        grad_decay.reshape(HEADS),
        grad_skip.reshape(HEADS),
    )


def solution(mesh):
    dp, ctx = mesh.devices.shape
    fine = Mesh(mesh.devices.reshape(dp, ctx // 2, 2), ALL)
    seq = P("dp", CTX, None)
    rate = P("dp", None, CTX)
    in_specs = (seq, P(), rate, P(), P(), seq)
    out_specs = (seq, seq, rate, P(), P(), P())
    return jax.shard_map(local, mesh=fine, in_specs=in_specs, out_specs=out_specs, check_vma=False)
```

time: 144 us -> 127 us (0.88)
  local copies, waits for them, and re-layouts: 35.5 us -> 3.46 us
  Pallas kernels: 32.4 us -> 47.5 us
  blocking collectives: 11.6 us -> 0 us
  starting transfers between devices: 36.5 us -> 45 us
  waiting for transfers between devices: 24.6 us -> 28.3 us
    unnamed x94 -> x2, local copies, waits for them, and re-layouts: 34 us -> 0.97 us
    pallas_call x10 -> x12, Pallas kernels: 32.4 us -> 47.5 us  [go(): run(*[pin(a, spaces[p]) if p in spaces else a for a, p in zip(args, specs...]
    all_to_all x1 -> x0, blocking collectives: 11.6 us -> none  [all_to_all(): return lax.all_to_all(value, axis, 0, 0, tiled=True)]
    all_to_all x3 -> x4, starting transfers between devices: 17.5 us -> 27.1 us  [all_to_all(): return lax.all_to_all(value, axis, 0, 0, tiled=True)]
    all_to_all x3 -> x4, waiting for transfers between devices: 14.7 us -> 19.2 us  [all_to_all(): return lax.all_to_all(value, axis, 0, 0, tiled=True)]
    ppermute x1, waiting for transfers between devices: 2.65 us -> 0.01 us  [local(): theirs = lax.ppermute(send, 'core', swap)]
    ppermute x1, waiting for transfers between devices: 2.31 us -> 0.01 us  [local(): other = lax.ppermute(tot, 'core', swap)]
    ppermute x1, waiting for transfers between devices: 0.01 us -> 1.65 us  [local(): after = lax.ppermute(first, CTX, [(i + 1, i) for i in range(devices - 1)])]
  transfers between devices with their start and end apart: 12 -> 13, of which waited for: 8 -> 9; matrix products, arithmetic and copies ran while one was open for 0% -> 1% of each run, Pallas kernels for 11% -> 25%
where the time goes in v3:
time: 127 us; the launch traced here: 125 us
  Pallas kernels  47.5 us (37%)
  starting transfers between devices  45 us (35%)
  waiting for transfers between devices  28.3 us (22%)
  local copies, waits for them, and re-layouts  3.46 us (3%)
    pallas_call x12, Pallas kernels, go(): run(*[pin(a, spaces[p]) if p in spaces else a for a, p in zip(args, specs...  47.5 us
    all_to_all x4, starting transfers between devices, all_to_all(): return lax.all_to_all(value, axis, 0, 0, tiled=True)  27.1 us
    all_to_all x4, waiting for transfers between devices, all_to_all(): return lax.all_to_all(value, axis, 0, 0, tiled=True)  19.2 us
    ppermute x3, starting transfers between devices, sum_everywhere(): lax.ppermute(total, 'dp', [(i, i ^ mask) for i in range(count)])  10.7 us
    ppermute x3, waiting for transfers between devices, sum_everywhere(): lax.ppermute(total, 'dp', [(i, i ^ mask) for i in range(count)])  4.99 us
    ppermute x1, starting transfers between devices, local(): after = lax.ppermute(first, CTX, [(i + 1, i) for i in range(devices - 1)])  4.33 us
  transfers between devices with their start and end apart: 13, of which 9 were waited for; matrix products, arithmetic and copies ran while one was open for 1% of the time, Pallas kernels for 25%

profile of v3, /device:TPU:2, one launch (start us, length us, event | category | flops | bytes accessed | tf_op | source)
XLA Modules:
  0.0 125.1 jit_solution(10192254472096423191)
XLA Ops:
  0.6 0.9 slice_bitcast_fusion
  1.5 1.9 %collective-permute-start = (bf16[3,5120]{1,0:T(4,128)(2,1)S(1)}, bf16[3,5120]{1,0:T(4,128)(2,1)S(1)}, u32[]{:S(2)}, u32[]{:S(2)}) collective-permute-start(bf16[3,5120]{1,0:T(4,128)(2,1)S(1)} %slice_bitcast_fusion), channel_id=1, source_target_pairs={{0,1},{1,2},{2,3},{3,4},{4,5},{5,6},{6,7},{7,8},{8,9},{9,10},{10,1... | collective-permute-start | bytes 92168 | tf_op jit(solution)/shard_map/ppermute | solution.py:890
  3.5 4.2 %begin.1 = (f32[512,128]{1,0:T(8,128)}, f32[512,128]{1,0:T(8,128)S(1)}, f32[32,128]{1,0:T(8,128)S(1)}, bf16[128,4096]{1,0:T(8,128)(2,1)S(1)}, bf16[128,1024]{1,0:T(8,128)(2,1)S(1)}, /*index=5*/f32[8,5120]{1,0:T(8,128)S(1)}) custom-call(f32[64,128]{1,0:T(8,128)} %bitcast.29, f32[1,64]{1,0:T(1,128)} %bitcast.32, f32[1,64]{1,0:T(1,128)} %bitcast.33, ...), custom_call_target="tpu_custom_call" | custom-call | flops 4000000000 | bytes 14400000 | tf_op jit(solution)/shard_map/begin/pallas_call | solution.py:98
  7.7 1.3 %collective-permute-done.halo_ref = bf16[3,5120]{1,0:T(4,128)(2,1)S(1)} collective-permute-done((bf16[3,5120]{1,0:T(4,128)(2,1)S(1)}, bf16[3,5120]{1,0:T(4,128)(2,1)S(1)}, u32[]{:S(2)}, u32[]{:S(2)}) %collective-permute-start) | collective-permute-done | bytes 30752 | tf_op jit(solution)/shard_map/ppermute | solution.py:890
  9.0 3.1 %enter.1 = (bf16[128,4096]{1,0:T(8,128)(2,1)}, bf16[128,1024]{1,0:T(8,128)(2,1)}, f32[8,5120]{1,0:T(8,128)}, bf16[128,4096]{1,0:T(8,128)(2,1)S(1)}, bf16[128,102...) custom-call(s32[1]{0:T(128)} %bitcast.core_ref, bf16[128,4096]{1,0:T(8,128)(2,1)S(1)} %get-tuple-element.49.x0_ref, ...), custom_call_target="tpu_custom_call" | custom-call | flops 3000000000 | bytes 10800000 | tf_op jit(solution)/shard_map/enter/pallas_call | solution.py:98
  12.1 0.5 collective-permute-start.1
  12.6 0.1 collective-permute-start.2
  12.7 2.9 %own.1.own_ref = bf16[2,16,128,128]{3,2,1,0:T(8,128)(2,1)S(1)} custom-call(s32[1]{0:T(128)} %bitcast.core_ref, bf16[128,4096]{1,0:T(8,128)(2,1)S(1)} %get-tuple-element.55.x_ref, bf16[128,1024]{1,0:T(8,128)(2,1)S(1)} %get-tuple-element.56.bc_ref, bf16[128,4096]{1,0:T(8,128)(2,1)} %bitcast.24, f32[512,128]{1,0:T(8,128)S(1)} %get-tuple-element.52.small_ref), custom_call_target="tpu_custom_call" | custom-call | flops 3000000000 | bytes 10800000 | tf_op jit(solution)/shard_map/own/pallas_call | solution.py:98
  15.7 0.0 collective-permute-done.2.other_ref
  15.7 0.0 collective-permute-done.1.got_ref
  15.7 1.8 %pack.1 = (bf16[16,272,128]{2,1,0:T(8,128)(2,1)}, bf16[2,16,128,128]{3,2,1,0:T(8,128)(2,1)}, bf16[2,16,128,128]{3,2,1,0:T(8,128)(2,1)}, f32[64,128]{1,0:T(8,128)}) custom-call(s32[1]{0:T(128)} %bitcast.core_ref, bf16[2,16,128,128]{3,2,1,0:T(8,128)(2,1)S(1)} %own.1.own_ref, bf16[2,16,128,128]{3,2,1,0:T(8,128)(2,1)S(1)} %collective-permute-done.1.got_ref, ...), custom_call_target="tpu_custom_call" | custom-call | flops 2000000000 | bytes 7200000 | tf_op jit(solution)/shard_map/pack/pallas_call | solution.py:98
  17.4 7.2 %all-to-all-start = ((bf16[16,272,128]{2,1,0:T(8,128)(2,1)}), bf16[16,272,128]{2,1,0:T(8,128)(2,1)S(1)}, u32[]{:S(2)}, u32[]{:S(2)}) async-start(bf16[16,272,128]{2,1,0:T(8,128)(2,1)} %get-tuple-element.59), calls=%async_computation | async-start | bytes 2228224 | tf_op jit(solution)/shard_map/all_to_all | solution.py:862
  24.6 5.3 %inner.1 = (f32[128,4096]{1,0:T(8,128)}, f32[128,1024]{1,0:T(8,128)}) custom-call(bf16[128,4096]{1,0:T(8,128)(2,1)} %get-tuple-element.53.x_h, bf16[128,1024]{1,0:T(8,128)(2,1)} %get-tuple-element.66.bc_h, bf16[128,4096]{1,0:T(8,128)(2,1)} %bitcast.25, f32[512,128]{1,0:T(8,128)} %get-tuple-element.60.small_h), custom_call_target="tpu_custom_call" | custom-call | flops 4000000000 | bytes 14400000 | tf_op jit(solution)/shard_map/inner/pallas_call | solution.py:98
  29.9 11.3 %all-to-all-done.in_ref = bf16[16,272,128]{2,1,0:T(8,128)(2,1)S(1)} async-done(((bf16[16,272,128]{2,1,0:T(8,128)(2,1)}), bf16[16,272,128]{2,1,0:T(8,128)(2,1)S(1)}, u32[]{:S(2)}, u32[]{:S(2)}) %all-to-all-start) | async-done | bytes 1114144 | tf_op jit(solution)/shard_map/all_to_all | solution.py:862
  41.2 1.3 %chain.1 = bf16[16,256,128]{2,1,0:T(8,128)(2,1)} custom-call(bf16[16,272,128]{2,1,0:T(8,128)(2,1)S(1)} %all-to-all-done.in_ref), custom_call_target="tpu_custom_call" | custom-call | flops 1000000000 | bytes 3600000 | tf_op jit(solution)/shard_map/chain/pallas_call | solution.py:98
  42.5 6.2 %all-to-all-start.1 = ((bf16[16,256,128]{2,1,0:T(8,128)(2,1)}), bf16[16,256,128]{2,1,0:T(8,128)(2,1)S(1)}, u32[]{:S(2)}, u32[]{:S(2)}) async-start(bf16[16,256,128]{2,1,0:T(8,128)(2,1)} %chain.1), calls=%async_computation.1 | async-start | bytes 2097152 | tf_op jit(solution)/shard_map/all_to_all | solution.py:862
  48.6 8.7 %slopes.1 = (f32[128,4096]{1,0:T(8,128)}, f32[128,5120]{1,0:T(8,128)}) custom-call(bf16[128,1024]{1,0:T(8,128)(2,1)} %get-tuple-element.66.bc_h, bf16[128,4096]{1,0:T(8,128)(2,1)} %bitcast.26, f32[512,128]{1,0:T(8,128)} %get-tuple-element.60.small_h, bf16[128,5120]{1,0:T(8,128)(2,1)} %bitcast.20, f32[8,5120]{1,0:T(8,128)} %get-tuple-element.67.before_h, ...), custom_call_target="tpu_custom_call" | custom-call | flops 6000000000 | bytes 21600000 | tf_op jit(solution)/shard_map/slopes/pallas_call | solution.py:98
  57.4 5.6 %all-to-all-done.1.back_h = bf16[16,256,128]{2,1,0:T(8,128)(2,1)S(1)} async-done(((bf16[16,256,128]{2,1,0:T(8,128)(2,1)}), bf16[16,256,128]{2,1,0:T(8,128)(2,1)S(1)}, u32[]{:S(2)}, u32[]{:S(2)}) %all-to-all-start.1) | async-done | bytes 1048608 | tf_op jit(solution)/shard_map/all_to_all | solution.py:862
  63.0 0.0 copy-start
  63.0 1.0 copy-done
  64.0 2.1 %unpack.1 = (bf16[2,16,128,128]{3,2,1,0:T(8,128)(2,1)S(1)}, bf16[2,16,128,128]{3,2,1,0:T(8,128)(2,1)S(1)}) custom-call(s32[1]{0:T(128)} %bitcast.core_ref, bf16[16,256,128]{2,1,0:T(8,128)(2,1)} %copy-done, bf16[2,16,128,128]{3,2,1,0:T(8,128)(2,1)} %get-tuple-element.74.own_h, bf16[2,16,128,128]{3,2,1,0:T(8,128)(2,1)} %get-tuple-element.75.got_h, ...), custom_call_target="tpu_custom_call" | custom-call | flops 2000000000 | bytes 7200000 | tf_op jit(solution)/shard_map/unpack/pallas_call | solution.py:98
  66.1 0.3 collective-permute-start.3
  66.4 6.5 %leave.2 = (bf16[128,4096]{1,0:T(8,128)(2,1)}, f32[128,5120]{1,0:T(8,128)}, f32[64,128]{1,0:T(8,128)}, f32[256,128]{1,0:T(8,128)}) custom-call(s32[1]{0:T(128)} %bitcast.core_ref, bf16[128,4096]{1,0:T(8,128)(2,1)} %get-tuple-element.53.x_h, bf16[128,1024]{1,0:T(8,128)(2,1)} %get-tuple-element.66.bc_h, bf16[128,4096]{1,0:T(8,128)(2,1)} %bitcast.27, ...), custom_call_target="tpu_custom_call" | custom-call | flops 5000000000 | bytes 18000000 | tf_op jit(solution)/shard_map/leave/pallas_call | solution.py:98
  72.9 0.0 collective-permute-done.3.state_ref
  73.0 6.5 %leave.3 = (bf16[128,4096]{1,0:T(8,128)(2,1)}, f32[128,5120]{1,0:T(8,128)}, f32[64,128]{1,0:T(8,128)}, f32[256,128]{1,0:T(8,128)}) custom-call(s32[1]{0:T(128)} %bitcast.core_ref, bf16[128,4096]{1,0:T(8,128)(2,1)} %get-tuple-element.53.x_h, ...), custom_call_target="tpu_custom_call", output_to_operand_aliasing={{0}: (13, {}), {1}: (14, {}), {2}: (15, {}), {3}: (16, {})} | custom-call | flops 5000000000 | bytes 18000000 | tf_op jit(solution)/shard_map/leave/pallas_call | solution.py:98
  79.5 5.4 %all-to-all-start.2 = ((f32[16,16,128]{2,1,0:T(8,128)}), f32[16,16,128]{2,1,0:T(8,128)S(1)}, u32[]{:S(2)}, u32[]{:S(2)}) async-start(f32[16,16,128]{2,1,0:T(8,128)} %bitcast.18), calls=%async_computation.2 | async-start | bytes 262144 | tf_op jit(solution)/shard_map/all_to_all | solution.py:862
  84.9 0.9 slice.16
  85.8 4.3 %collective-permute-start.4 = (bf16[3,5120]{1,0:T(4,128)(2,1)S(1)}, bf16[3,5120]{1,0:T(4,128)(2,1)S(1)}, u32[]{:S(2)}, u32[]{:S(2)}) collective-permute-start(bf16[3,5120]{1,0:T(4,128)(2,1)S(1)} %slice.16), channel_id=1, source_target_pairs={{1,0},{2,1},{3,2},{4,3},{5,4},{6,5},{7,6},{8,7},{9,8},{10,9},{11,1... | collective-permute-start | bytes 92168 | tf_op jit(solution)/shard_map/ppermute | solution.py:916
  90.2 1.7 %collective-permute-done.4.halo_ref = bf16[3,5120]{1,0:T(4,128)(2,1)S(1)} collective-permute-done((bf16[3,5120]{1,0:T(4,128)(2,1)S(1)}, bf16[3,5120]{1,0:T(4,128)(2,1)S(1)}, u32[]{:S(2)}, u32[]{:S(2)}) %collective-permute-start.4) | collective-permute-done | bytes 30752 | tf_op jit(solution)/shard_map/ppermute | solution.py:916
  91.8 0.0 all-to-all-done.2
  91.9 0.1 collective-permute-start.5
  92.0 1.2 collective-permute-done.5
  93.1 1.9 %collective-permute-start.6 = (f32[16,128]{1,0:T(8,128)S(1)}, f32[16,128]{1,0:T(8,128)S(1)}, u32[]{:S(2)}, u32[]{:S(2)}) collective-permute-start(f32[16,128]{1,0:T(8,128)S(1)} %add.12), channel_id=1, source_target_pairs={{0,32},{32,0},{64,96},{96,64},{128,160},{160,128},{192,224},{224,1... | collective-permute-start | bytes 24584 | tf_op jit(solution)/shard_map/ppermute | solution.py:877
  95.0 1.7 %collective-permute-done.6 = f32[16,128]{1,0:T(8,128)S(1)} collective-permute-done((f32[16,128]{1,0:T(8,128)S(1)}, f32[16,128]{1,0:T(8,128)S(1)}, u32[]{:S(2)}, u32[]{:S(2)}) %collective-permute-start.6) | collective-permute-done | bytes 8224 | tf_op jit(solution)/shard_map/ppermute | solution.py:877
  96.8 3.3 %collective-permute-start.7 = (f32[16,128]{1,0:T(8,128)S(1)}, f32[16,128]{1,0:T(8,128)S(1)}, u32[]{:S(2)}, u32[]{:S(2)}) collective-permute-start(f32[16,128]{1,0:T(8,128)S(1)} %add.13), channel_id=1, source_target_pairs={{0,64},{32,96},{64,0},{96,32},{128,192},{160,224},{192,128},{224,1... | collective-permute-start | bytes 24584 | tf_op jit(solution)/shard_map/ppermute | solution.py:877
  100.1 1.6 %collective-permute-done.7 = f32[16,128]{1,0:T(8,128)S(1)} collective-permute-done((f32[16,128]{1,0:T(8,128)S(1)}, f32[16,128]{1,0:T(8,128)S(1)}, u32[]{:S(2)}, u32[]{:S(2)}) %collective-permute-start.7) | collective-permute-done | bytes 8224 | tf_op jit(solution)/shard_map/ppermute | solution.py:877
  101.7 5.5 %collective-permute-start.8 = (f32[16,128]{1,0:T(8,128)S(1)}, f32[16,128]{1,0:T(8,128)S(1)}, u32[]{:S(2)}, u32[]{:S(2)}) collective-permute-start(f32[16,128]{1,0:T(8,128)S(1)} %add.14), channel_id=1, source_target_pairs={{0,224},{32,192},{64,160},{96,128},{128,96},{160,64},{192,32},{224... | collective-permute-start | bytes 24584 | tf_op jit(solution)/shard_map/ppermute | solution.py:877
  107.2 1.6 %collective-permute-done.8 = f32[16,128]{1,0:T(8,128)S(1)} collective-permute-done((f32[16,128]{1,0:T(8,128)S(1)}, f32[16,128]{1,0:T(8,128)S(1)}, u32[]{:S(2)}, u32[]{:S(2)}) %collective-permute-start.8) | collective-permute-done | bytes 8224 | tf_op jit(solution)/shard_map/ppermute | solution.py:877
  108.8 0.7 broadcast_in_dim.18
  109.5 8.3 %all-to-all-start.3 = ((f32[16,16,128]{2,1,0:T(8,128)}), f32[16,16,128]{2,1,0:T(8,128)S(1)}, u32[]{:S(2)}, u32[]{:S(2)}) async-start(f32[16,16,128]{2,1,0:T(8,128)} %broadcast_in_dim.18), calls=%async_computation.3 | async-start | bytes 262144 | tf_op jit(solution)/shard_map/all_to_all | solution.py:862
  117.8 4.0 %spread.1 = bf16[128,5120]{1,0:T(8,128)(2,1)} custom-call(f32[128,5120]{1,0:T(8,128)} %get-tuple-element.84.pre_h, bf16[3,5120]{1,0:T(4,128)(2,1)S(1)} %collective-permute-done.4.halo_ref, f32[4,5120]{1,0:T(4,128)} %weight_h.7), custom_call_target="tpu_custom_call" | custom-call | flops 4000000000 | bytes 14400000 | tf_op jit(solution)/shard_map/spread/pallas_call | solution.py:98
  121.8 2.3 %all-to-all-done.3 = f32[16,16,128]{2,1,0:T(8,128)S(1)} async-done(((f32[16,16,128]{2,1,0:T(8,128)}), f32[16,16,128]{2,1,0:T(8,128)S(1)}, u32[]{:S(2)}, u32[]{:S(2)}) %all-to-all-start.3) | async-done | bytes 131104 | tf_op jit(solution)/shard_map/all_to_all | solution.py:862
  124.2 0.9 finish.1
  (5 shorter events, 0.0 us)
Async XLA Ops:
  1.5 7.4 %collective-permute-start = (bf16[3,5120]{1,0:T(4,128)(2,1)S(1)}, bf16[3,5120]{1,0:T(4,128)(2,1)S(1)}, u32[]{:S(2)}, u32[]{:S(2)}) collective-permute-start(bf16[3,5120]{1,0:T(4,128)(2,1)S(1)} %slice_bitcast_fusion), channel_id=1, source_target_pairs={{0,1},{1,2},{2,3},{3,4},{4,5},{5,6},{6,7},{7,8},{8,9},{9,10},{10,1... | collective-permute-start | bytes 92168 | tf_op jit(solution)/shard_map/ppermute | solution.py:890
  12.1 3.6 %collective-permute-start.1 = (bf16[2,16,128,128]{3,2,1,0:T(8,128)(2,1)S(1)}, bf16[2,16,128,128]{3,2,1,0:T(8,128)(2,1)S(1)}, u32[]{:S(2)}, u32[]{:S(2)}) collective-permute-start(bf16[2,16,128,128]{3,2,1,0:T(8,128)(2,1)S(1)} %get-tuple-element.57), channel_id=1, source_target_pairs={{0,1},{1,0},{2,3},{3,2},{4,5},{5,4},{6,7},{7,6},{8,9},{9,8},{10,11... | collective-permute-start | bytes 3145736 | tf_op jit(solution)/shard_map/ppermute | solution.py:898
  12.6 3.0 %collective-permute-start.2 = (f32[32,128]{1,0:T(8,128)S(1)}, f32[32,128]{1,0:T(8,128)S(1)}, u32[]{:S(2)}, u32[]{:S(2)}) collective-permute-start(f32[32,128]{1,0:T(8,128)S(1)} %get-tuple-element.58.tot_ref), channel_id=1, source_target_pairs={{0,1},{1,0},{2,3},{3,2},{4,5},{5,4},{6,7},{7,6},{8,9},{9,8},{10,11... | collective-permute-start | bytes 49160 | tf_op jit(solution)/shard_map/ppermute | solution.py:894
  17.4 23.8 %all-to-all-start = ((bf16[16,272,128]{2,1,0:T(8,128)(2,1)}), bf16[16,272,128]{2,1,0:T(8,128)(2,1)S(1)}, u32[]{:S(2)}, u32[]{:S(2)}) async-start(bf16[16,272,128]{2,1,0:T(8,128)(2,1)} %get-tuple-element.59), calls=%async_computation | async-start | bytes 2228224 | tf_op jit(solution)/shard_map/all_to_all | solution.py:862
  42.5 20.6 %all-to-all-start.1 = ((bf16[16,256,128]{2,1,0:T(8,128)(2,1)}), bf16[16,256,128]{2,1,0:T(8,128)(2,1)S(1)}, u32[]{:S(2)}, u32[]{:S(2)}) async-start(bf16[16,256,128]{2,1,0:T(8,128)(2,1)} %chain.1), calls=%async_computation.1 | async-start | bytes 2097152 | tf_op jit(solution)/shard_map/all_to_all | solution.py:862
  63.0 1.0 copy-start
  66.1 6.8 %collective-permute-start.3 = (bf16[2,16,128,128]{3,2,1,0:T(8,128)(2,1)S(1)}, bf16[2,16,128,128]{3,2,1,0:T(8,128)(2,1)S(1)}, u32[]{:S(2)}, u32[]{:S(2)}) collective-permute-start(bf16[2,16,128,128]{3,2,1,0:T(8,128)(2,1)S(1)} %get-tuple-element.77), channel_id=1, source_target_pairs={{0,1},{1,0},{2,3},{3,2},{4,5},{5,4},{6,7},{7,6},{8,9},{9,8},{10,11... | collective-permute-start | bytes 3145736 | tf_op jit(solution)/shard_map/ppermute | solution.py:910
  79.5 12.3 %all-to-all-start.2 = ((f32[16,16,128]{2,1,0:T(8,128)}), f32[16,16,128]{2,1,0:T(8,128)S(1)}, u32[]{:S(2)}, u32[]{:S(2)}) async-start(f32[16,16,128]{2,1,0:T(8,128)} %bitcast.18), calls=%async_computation.2 | async-start | bytes 262144 | tf_op jit(solution)/shard_map/all_to_all | solution.py:862
  85.8 6.0 %collective-permute-start.4 = (bf16[3,5120]{1,0:T(4,128)(2,1)S(1)}, bf16[3,5120]{1,0:T(4,128)(2,1)S(1)}, u32[]{:S(2)}, u32[]{:S(2)}) collective-permute-start(bf16[3,5120]{1,0:T(4,128)(2,1)S(1)} %slice.16), channel_id=1, source_target_pairs={{1,0},{2,1},{3,2},{4,3},{5,4},{6,5},{7,6},{8,7},{9,8},{10,9},{11,1... | collective-permute-start | bytes 92168 | tf_op jit(solution)/shard_map/ppermute | solution.py:916
  91.9 1.3 %collective-permute-start.5 = (f32[16,128]{1,0:T(8,128)S(1)}, f32[16,128]{1,0:T(8,128)S(1)}, u32[]{:S(2)}, u32[]{:S(2)}) collective-permute-start(f32[16,128]{1,0:T(8,128)S(1)} %reduce_sum.9), channel_id=1, source_target_pairs={{0,1},{1,0},{2,3},{3,2},{4,5},{5,4},{6,7},{7,6},{8,9},{9,8},{10,11... | collective-permute-start | bytes 24584 | tf_op jit(solution)/shard_map/ppermute | solution.py:872
  93.1 3.7 %collective-permute-start.6 = (f32[16,128]{1,0:T(8,128)S(1)}, f32[16,128]{1,0:T(8,128)S(1)}, u32[]{:S(2)}, u32[]{:S(2)}) collective-permute-start(f32[16,128]{1,0:T(8,128)S(1)} %add.12), channel_id=1, source_target_pairs={{0,32},{32,0},{64,96},{96,64},{128,160},{160,128},{192,224},{224,1... | collective-permute-start | bytes 24584 | tf_op jit(solution)/shard_map/ppermute | solution.py:877
  96.8 4.9 %collective-permute-start.7 = (f32[16,128]{1,0:T(8,128)S(1)}, f32[16,128]{1,0:T(8,128)S(1)}, u32[]{:S(2)}, u32[]{:S(2)}) collective-permute-start(f32[16,128]{1,0:T(8,128)S(1)} %add.13), channel_id=1, source_target_pairs={{0,64},{32,96},{64,0},{96,32},{128,192},{160,224},{192,128},{224,1... | collective-permute-start | bytes 24584 | tf_op jit(solution)/shard_map/ppermute | solution.py:877
  101.7 7.1 %collective-permute-start.8 = (f32[16,128]{1,0:T(8,128)S(1)}, f32[16,128]{1,0:T(8,128)S(1)}, u32[]{:S(2)}, u32[]{:S(2)}) collective-permute-start(f32[16,128]{1,0:T(8,128)S(1)} %add.14), channel_id=1, source_target_pairs={{0,224},{32,192},{64,160},{96,128},{128,96},{160,64},{192,32},{224... | collective-permute-start | bytes 24584 | tf_op jit(solution)/shard_map/ppermute | solution.py:877
  109.5 14.7 %all-to-all-start.3 = ((f32[16,16,128]{2,1,0:T(8,128)}), f32[16,16,128]{2,1,0:T(8,128)S(1)}, u32[]{:S(2)}, u32[]{:S(2)}) async-start(f32[16,16,128]{2,1,0:T(8,128)} %broadcast_in_dim.18), calls=%async_computation.3 | async-start | bytes 262144 | tf_op jit(solution)/shard_map/all_to_all | solution.py:862

commit v4 on v3

--- a/solution.py
+++ b/solution.py
@@ -138,15 +138,16 @@
 )
 
 
-def begin_kernel(raw_h, decay_log_h, skip_gain_h, tok_h, weight_h,
-                 small_h, small_ref, tot_ref, x_ref, bc_ref, head_ref,
-                 raw_ref, decay_log_ref, skip_gain_ref, weight_ref, hold_ref, win_ref, sems):
+def begin_kernel(raw_h, decay_log_h, skip_gain_h, tok_h, weight_h, g_h,
+                 small_h, small_ref, tot_ref, x_ref, bc_ref, head_ref, weight_ref, g_ref,
+                 raw_ref, decay_log_ref, skip_gain_ref, hold_ref, win_ref, sems):
     first = start_all(
         [(raw_h, raw_ref), (decay_log_h, decay_log_ref), (skip_gain_h, skip_gain_ref), (weight_h, weight_ref)],
         sems.at[0],
     )
     blocks = [pl.ds(i * GROUP_X, GROUP_X) for i in range(BLOCKS)]
     copies = start_all([(tok_h.at[:, at], hold_ref.at[:, at]) for at in blocks], sems.at[1])
+    later = start_all([(g_h, g_ref)], sems.at[2])
     diagonal = iota((HEADS, HEADS), 0) == iota((HEADS, HEADS), 1)
 
     def column(row):
@@ -193,10 +194,10 @@
                 x_ref[:, at : at + LANES] = mixed
             else:
                 bc_ref[:, at - WIDTH_X : at - WIDTH_X + LANES] = mixed
-    wait_all(save)
-
-
-def run_begin(raw, decay_log, skip_gain, tokens, weight):
+    wait_all(save + later)
+
+
+def run_begin(raw, decay_log, skip_gain, tokens, weight, cot):
     out = [
         ("h", (SMALL_ROWS, LANES), F32),
         ("V", (SMALL_ROWS, LANES), F32),
@@ -204,18 +205,19 @@
         ("V", (T, WIDTH_X), BF16),
         ("V", (T, 2 * WIDTH_B), BF16),
         ("V", (8, CHANNELS), F32),
+        ("V", (TAPS, CHANNELS), F32),
+        ("V", (T, WIDTH_X), BF16),
     ]
     scratch = [
         pltpu.VMEM((HEADS, T), F32),
         pltpu.VMEM((1, HEADS), F32),
         pltpu.VMEM((1, HEADS), F32),
-        pltpu.VMEM((TAPS, CHANNELS), F32),
         pltpu.VMEM((T, CHANNELS), BF16),
         pltpu.VMEM((8 + T, GROUP_X), F32),
-        DMA(2, BLOCKS),
-    ]
-    return call(begin_kernel, "begin", out, "hhhhh", 4, scratch, mib=16)(
-        raw, decay_log, skip_gain, tokens, weight
+        DMA(3, BLOCKS),
+    ]
+    return call(begin_kernel, "begin", out, "hhhhhh", 4, scratch, mib=16)(
+        raw, decay_log, skip_gain, tokens, weight, cot
     )
 
 
@@ -233,18 +235,16 @@
     return jnp.concatenate([widen(cols, base, pair), widen(cols, base, pair + 1)], axis=1)
 
 
-def fill_half(half, x_ref, bc_ref, g_ref, copies, scale, dst_ref):
+def fill_half(half, x_ref, bc_ref, g_ref, scale, dst_ref):
     for jj in range(HALF_GROUPS):
         j = half * HALF_GROUPS + jj
-        copies[jj].wait()
         b_flip = jnp.transpose(bc_ref[:, span(j, STATE)].astype(F32)).astype(BF16)
         c_flip = jnp.transpose(bc_ref[:, span(GROUPS + j, STATE)].astype(F32)).astype(BF16)
         cols = rolled(scale, j)
         for q in range(0, GROUP_PAIRS, 2):
             lanes = pl.ds(pl.multiple_of(j * GROUP_X + q * LANES, 2 * LANES), 2 * LANES)
-            near = slice(jj * GROUP_X + q * LANES, jj * GROUP_X + (q + 2) * LANES)
             xw = (x_ref[:, lanes].astype(F32) * widen_two(cols, HEADS, q)).astype(BF16)
-            gw = (g_ref[:, near].astype(F32) * widen_two(cols, 0, q)).astype(BF16)
+            gw = (g_ref[:, lanes].astype(F32) * widen_two(cols, 0, q)).astype(BF16)
             state = dot(b_flip, xw).astype(BF16)
             grad = dot(c_flip, gw).astype(BF16)
             for k in range(2):
@@ -253,23 +253,10 @@
                 dst_ref[1, at] = grad[:, k * LANES : (k + 1) * LANES]
 
 
-def load_half(half, g_h, g_ref, sems):
-    return start_all(
-        [
-            (g_h.at[:, span(half * HALF_GROUPS + jj, GROUP_X)], g_ref.at[:, pl.ds(jj * GROUP_X, GROUP_X)])
-            for jj in range(HALF_GROUPS)
-        ],
-        sems,
-    )
-
-
-def enter_kernel(core_ref, x0_ref, bc0_ref, head_ref, halo_ref, weight_h, g_h, small_ref,
-                 x_h, bc_h, before_h, x_ref, bc_ref, out_ref, g_ref, weight_ref, before_ref, sems):
+def enter_kernel(core_ref, x0_ref, bc0_ref, head_ref, halo_ref, weight_ref, g_ref, small_ref,
+                 x_h, bc_h, before_h, x_ref, bc_ref, out_ref, before_ref, sems):
     half = 1 - core_ref[0]
-    weight_copy = start_all([(weight_h, weight_ref)], sems.at[0])
-    copies = load_half(half, g_h, g_ref, sems.at[1])
     row = iota((8, GROUP_X), 0)
-    wait_all(weight_copy)
     for i in range(BLOCKS):
         cols = slice(i * GROUP_X, (i + 1) * GROUP_X)
         halo = halo_ref[:, cols].astype(F32)
@@ -288,8 +275,8 @@
         rest = src[0:16, at].astype(F32)
         dst[16:T, at] = src[16:T, at]
         dst[0:16, at] = jnp.concatenate([fixed, rest[8:16]], axis=0).astype(BF16)
-    saves = start_all([(x_ref, x_h), (bc_ref, bc_h), (before_ref, before_h)], sems.at[0])
-    fill_half(half, x_ref, bc_ref, g_ref, copies, small_ref[ROW_SCALE : ROW_SCALE + T], out_ref)
+    saves = start_all([(x_ref, x_h), (bc_ref, bc_h), (before_ref, before_h)], sems)
+    fill_half(half, x_ref, bc_ref, g_ref, small_ref[ROW_SCALE : ROW_SCALE + T], out_ref)
     wait_all(saves)
 
 
@@ -302,26 +289,19 @@
         ("V", (T, 2 * WIDTH_B), BF16),
         ("V", (2, HALF_PAIRS, STATE, LANES), BF16),
     ]
-    scratch = [
-        pltpu.VMEM((T, HALF_GROUPS * GROUP_X), BF16),
-        pltpu.VMEM((TAPS, CHANNELS), F32),
-        pltpu.VMEM((8, CHANNELS), F32),
-        DMA(2, 3),
-    ]
-    return call(enter_kernel, "enter", out, "sVVVvhhV", 3, scratch, mib=16)(
+    scratch = [pltpu.VMEM((8, CHANNELS), F32), DMA(3)]
+    return call(enter_kernel, "enter", out, "sVVVvVVV", 3, scratch, mib=16)(
         core, x0, bc0, head, halo, weight, cot, small
     )
 
 
-def own_kernel(core_ref, x_ref, bc_ref, g_h, small_ref, own_ref, g_ref, sems):
-    copies = load_half(core_ref[0], g_h, g_ref, sems)
-    fill_half(core_ref[0], x_ref, bc_ref, g_ref, copies, small_ref[ROW_SCALE : ROW_SCALE + T], own_ref)
+def own_kernel(core_ref, x_ref, bc_ref, g_ref, small_ref, own_ref):
+    fill_half(core_ref[0], x_ref, bc_ref, g_ref, small_ref[ROW_SCALE : ROW_SCALE + T], own_ref)
 
 
 def run_own(core, x, bc, cot, small):
     out = [("V", (2, HALF_PAIRS, STATE, LANES), BF16)]
-    scratch = [pltpu.VMEM((T, HALF_GROUPS * GROUP_X), BF16), DMA(HALF_GROUPS)]
-    return call(own_kernel, "own", out, "sVVhV", 3, scratch, mib=16)(core, x, bc, cot, small)[0]
+    return call(own_kernel, "own", out, "sVVVV", 3, mib=16)(core, x, bc, cot, small)[0]
 
 
 STEP_PAIRS = 4
@@ -405,22 +385,65 @@
     return call(kernel, "chain", out, "v", 1, mib=16)(packed)[0]
 
 
-def unpack_kernel(core_ref, back_h, own_h, got_h, tots_h, mine_ref, send_ref,
-                  back_ref, own_ref, got_ref, tots_ref, sems):
+HALF_X = HALF_GROUPS * GROUP_X
+HALF_B = 2 * HALF_GROUPS * STATE
+
+NEAR = [
+    ("V", (T, HALF_X), BF16),
+    ("V", (T, HALF_X), BF16),
+    ("V", (T, HALF_X), F32),
+    ("V", (T, HALF_X), F32),
+    ("V", (T, HALF_X + HALF_B), F32),
+    ("V", (T, HALF_X + HALF_B), BF16),
+    ("V", (T, HALF_B), BF16),
+    ("V", (T, HALF_B), F32),
+]
+COMMON = [
+    ("V", (8, CHANNELS), F32),
+    ("V", (SMALL_ROWS, LANES), F32),
+    ("V", (HEADS, T), F32),
+    ("V", (PAIRS, LANES), F32),
+]
+FETCHES = 6 + 8
+
+
+def fetch_half(half, far, near, sems):
+    x_h, g_h, y_h, gx_h, slope_h, tok_h, bc_h, gbc_h = far
+    x_v, g_v, y_v, gx_v, slope_v, tok_v, bc_v, gbc_v = near
+    wide = pl.ds(0, HALF_X)
+    pairs = [
+        (a.at[:, span(half, HALF_X)], b.at[:, wide])
+        for a, b in ((x_h, x_v), (g_h, g_v), (y_h, y_v), (gx_h, gx_v), (slope_h, slope_v), (tok_h, tok_v))
+    ]
+    size = HALF_GROUPS * STATE
+    for base in range(2):
+        at = span(base * 2 + half, size)
+        off = span(WIDTH_X // size + base * 2 + half, size)
+        pairs += [
+            (bc_h.at[:, at], bc_v.at[:, pl.ds(base * size, size)]),
+            (gbc_h.at[:, at], gbc_v.at[:, pl.ds(base * size, size)]),
+            (slope_h.at[:, off], slope_v.at[:, pl.ds(HALF_X + base * size, size)]),
+            (tok_h.at[:, off], tok_v.at[:, pl.ds(HALF_X + base * size, size)]),
+        ]
+    return start_all(pairs, sems)
+
+
+def unpack_kernel(core_ref, back_ref, own_h, got_h, tots_h, *rest):
+    far, rest = rest[: len(NEAR)], rest[len(NEAR) :]
+    common_far, rest = rest[: len(COMMON)], rest[len(COMMON) :]
+    mine_ref, send_ref, *rest = rest
+    near, rest = rest[: len(NEAR)], rest[len(NEAR) :]
+    common, rest = rest[: len(COMMON)], rest[len(COMMON) :]
+    own_ref, got_ref, tots_ref, sems, fetch_sems = rest
     first = start_all([(tots_h, tots_ref)], sems.at[STEPS])
     steps = []
     for step in range(STEPS):
         at = pl.ds(step * STEP_PAIRS, STEP_PAIRS)
         steps.append(
-            start_all(
-                [
-                    (back_h.at[at], back_ref.at[at]),
-                    (own_h.at[:, at], own_ref.at[:, at]),
-                    (got_h.at[:, at], got_ref.at[:, at]),
-                ],
-                sems.at[step],
-            )
+            start_all([(own_h.at[:, at], own_ref.at[:, at]), (got_h.at[:, at], got_ref.at[:, at])], sems.at[step])
         )
+    fetches = start_all(list(zip(common_far, common)), fetch_sems.at[1])
+    fetches += fetch_half(core_ref[0], far, near, fetch_sems.at[0])
     wait_all(first)
     second = core_ref[0] == 1
     for i in range(HALF_PAIRS):
@@ -441,19 +464,24 @@
         mine_ref[1, i] = jnp.where(second, grad_one, grad_zero).astype(BF16)
         send_ref[0, i] = jnp.where(second, state_zero, state_one).astype(BF16)
         send_ref[1, i] = jnp.where(second, grad_zero, grad_one).astype(BF16)
-
-
-def run_unpack(core, back, own, got, tots):
+    wait_all(fetches)
+
+
+def run_unpack(core, back, own, got, tots, far, common):
     half = (2, HALF_PAIRS, STATE, LANES)
-    out = [("V", half, BF16)] * 2
+    out = [("V", half, BF16)] * 2 + NEAR + COMMON
     scratch = [
-        pltpu.VMEM((HALF_PAIRS, 2 * STATE, LANES), BF16),
         pltpu.VMEM(half, BF16),
         pltpu.VMEM(half, BF16),
         pltpu.VMEM((2 * PAIRS, LANES), F32),
-        DMA(STEPS + 1, 3),
-    ]
-    return call(unpack_kernel, "unpack", out, "shhhh", 2, scratch, mib=16)(core, back, own, got, tots)
+        DMA(STEPS + 1, 2),
+        DMA(2, FETCHES),
+    ]
+    specs = "svhhh" + "h" * (len(NEAR) + len(COMMON))
+    outs = call(unpack_kernel, "unpack", out, specs, 3, scratch, mib=16)(
+        core, back, own, got, tots, *far, *common
+    )
+    return outs[0], outs[1], outs[2 : 2 + len(NEAR)], outs[2 + len(NEAR) :]
 
 
 def by_lane_half(v):
@@ -464,7 +492,8 @@
     )
 
 
-def inner_kernel(x_h, bc_h, g_h, small_h, y_h, gbc_h, x_ref, bc_ref, g_ref, small_ref, y_ref, gbc_ref, sems):
+def inner_kernel(x_h, bc_h, g_h, small_h, y_h, gbc_h, skips_h,
+                 x_ref, bc_ref, g_ref, small_ref, y_ref, gbc_ref, skips_ref, sems):
     first = start_all([(bc_h, bc_ref), (small_h, small_ref)], sems.at[0])
 
     def loads(j):
@@ -494,10 +523,13 @@
         scores = dot(c, b, NT)
         cols = rolled(small_ref[ROW_COLS : ROW_COLS + T], j)
         total = jnp.zeros((T, T), F32)
+        skips = []
         for i in range(GROUP_PAIRS):
             lanes = pl.ds(pl.multiple_of(j * GROUP_X + i * LANES, LANES), LANES)
             x = x_ref[:, lanes]
-            inner = dot(by_lane_half(g_ref[:, lanes]), x, NT)
+            g = g_ref[:, lanes]
+            skips.append(jnp.sum(g.astype(F32) * x.astype(F32), axis=0, keepdims=True))
+            inner = dot(by_lane_half(g), x, NT)
             weights = []
             for k in range(2):
                 h = 2 * i + k
@@ -506,18 +538,19 @@
                 total = total + kernel * inner[k * T : (k + 1) * T]
                 weights.append((kernel * scores).astype(BF16))
             y_ref[:, lanes] = dot(jnp.concatenate(weights, axis=1), by_lane_half(x))
+        skips_ref[span(j, GROUP_PAIRS), :] = jnp.concatenate(skips, axis=0)
         gbc_ref[:, span(GROUPS + j, STATE)] = dot(total.astype(BF16), b)
         gbc_ref[:, span(j, STATE)] = dot(jnp.transpose(total).astype(BF16), c)
         store(j).start()
 
-    last = start_all([(gbc_ref, gbc_h)], sems.at[0])
+    last = start_all([(gbc_ref, gbc_h), (skips_ref, skips_h)], sems.at[0])
     for j in range(GROUPS):
         store(j).wait()
     wait_all(last)
 
 
 def run_inner(x, bc, cot, small):
-    out = [("h", (T, WIDTH_X), F32), ("h", (T, 2 * WIDTH_B), F32)]
+    out = [("h", (T, WIDTH_X), F32), ("h", (T, 2 * WIDTH_B), F32), ("h", (PAIRS, LANES), F32)]
     scratch = [
         pltpu.VMEM((T, WIDTH_X), BF16),
         pltpu.VMEM((T, 2 * WIDTH_B), BF16),
@@ -525,6 +558,7 @@
         pltpu.VMEM((SMALL_ROWS, LANES), F32),
         pltpu.VMEM((T, WIDTH_X), F32),
         pltpu.VMEM((T, 2 * WIDTH_B), F32),
+        pltpu.VMEM((PAIRS, LANES), F32),
         DMA(4, GROUPS),
     ]
     return call(inner_kernel, "inner", out, "hhhh", 4, scratch, mib=24)(x, bc, cot, small)
@@ -610,41 +644,18 @@
     )
 
 
-def leave_kernel(theirs, core_ref, x_h, bc_h, g_h, y_h, gx_h, gbc_h, slope_h, tok_h, before_h, state_ref,
-                 small_h, raw_h, *rest):
-    (out_h, pre_h, step_h, sum_h, x_ref, bc_ref, g_ref, y_ref, gx_ref, gbc_ref, slope_ref, tok_ref,
-     before_ref, small_ref, raw_ref, out_ref, pre_ref, step_ref, sum_ref, win_ref, sems) = rest[-21:]
+def leave_kernel(theirs, core_ref, state_ref, *rest):
+    near, rest = rest[: len(NEAR)], rest[len(NEAR) :]
+    x_ref, g_ref, y_ref, gx_ref, slope_ref, tok_ref, bc_ref, gbc_ref = near
+    (before_ref, small_ref, raw_ref, skips_ref), rest = rest[: len(COMMON)], rest[len(COMMON) :]
+    far, rest = rest[: len(NEAR)], rest[len(NEAR) :]
+    out_ref, pre_ref, step_ref, sum_ref, win_ref, sems = rest[-6:]
+    if theirs:
+        far, rest = (), far[4:] + rest
+    out_h, pre_h, step_h, sum_h = rest[:4]
     half = 1 - core_ref[0] if theirs else core_ref[0]
-
-    def loads(jj):
-        j = half * HALF_GROUPS + jj
-        far, near = span(j, GROUP_X), span(jj, GROUP_X)
-        pairs = [(h.at[:, far], v.at[:, near]) for h, v in (
-            (x_h, x_ref), (g_h, g_ref), (y_h, y_ref), (gx_h, gx_ref), (slope_h, slope_ref), (tok_h, tok_ref)
-        )]
-        return [pltpu.make_async_copy(a, b, sems.at[1 + jj, i]) for i, (a, b) in enumerate(pairs)]
-
-    def thin(jj):
-        pairs = []
-        for base in range(2):
-            far = span(base * GROUPS + half * HALF_GROUPS + jj, STATE)
-            wide = span(WIDTH_X // STATE + base * GROUPS + half * HALF_GROUPS + jj, STATE)
-            near = span(base * HALF_GROUPS + jj, STATE)
-            at = pl.ds(HALF_GROUPS * GROUP_X + (base * HALF_GROUPS + jj) * STATE, STATE)
-            pairs += [
-                (bc_h.at[:, far], bc_ref.at[:, near]),
-                (gbc_h.at[:, far], gbc_ref.at[:, near]),
-                (slope_h.at[:, wide], slope_ref.at[:, at]),
-                (tok_h.at[:, wide], tok_ref.at[:, at]),
-            ]
-        return [pltpu.make_async_copy(a, b, sems.at[3 + jj, i]) for i, (a, b) in enumerate(pairs)]
-
-    first = start_all([(small_h, small_ref), (before_h, before_ref), (raw_h, raw_ref)], sems.at[0])
-    for jj in range(HALF_GROUPS):
-        for copy in loads(jj) + thin(jj):
-            copy.start()
-    wait_all(first)
-    last = iota((T, 2 * LANES), 0) == T - 1
+    fetches = [] if theirs else fetch_half(1 - core_ref[0], far, rest[4 : 4 + len(NEAR)], sems.at[2])
+    last = iota((8, 2 * LANES), 0) == 7
     lower = (iota((T, T), 0) >= iota((T, T), 1)).astype(F32)
 
     def tap_sums(grad_pre, lo):
@@ -660,13 +671,12 @@
     saves = []
 
     def save(src, dst):
-        copy = pltpu.make_async_copy(src, dst, sems.at[5 + len(saves) // 8, len(saves) % 8])
+        copy = pltpu.make_async_copy(src, dst, sems.at[len(saves) // 8, len(saves) % 8])
         copy.start()
         saves.append(copy)
 
     for jj in range(HALF_GROUPS):
         j = half * HALF_GROUPS + jj
-        wait_all(loads(jj) + thin(jj))
         near_b = slice(jj * STATE, (jj + 1) * STATE)
         near_c = slice((HALF_GROUPS + jj) * STATE, (HALF_GROUPS + jj + 1) * STATE)
         b = bc_ref[:, near_b]
@@ -678,7 +688,7 @@
         tot_rows = small_ref[pl.ds(pl.multiple_of(ROW_TOT + j * GROUP_PAIRS, GROUP_PAIRS), GROUP_PAIRS), :]
         seg_grad = jnp.zeros((GROUP_HEADS, T), F32)
         dt_grad = jnp.zeros((GROUP_HEADS, T), F32)
-        skips = []
+        skips = [skips_ref[span(j, GROUP_PAIRS), :]]
         terms = []
         near = slice(jj * GROUP_X, (jj + 1) * GROUP_X)
         fill_window(win_ref, before_ref[:, span(j, GROUP_X)], tok_ref[:, near])
@@ -702,12 +712,12 @@
             grad_pre = (gx + skip * g) * slope_ref[:, lanes]
             pre_ref[:, lanes] = grad_pre
             terms += by_rows(tap_sums(grad_pre, q * LANES))
-            skips += by_rows([jnp.sum(g * x, axis=0, keepdims=True)])
             x_gx = x * gx
             end = jnp.sum(x * through, axis=0, keepdims=True) + jnp.exp(tot) * jnp.sum(
                 exits.astype(F32) * state.astype(F32), axis=0, keepdims=True
             )
-            moved = g * y - x_gx + jnp.where(last, end, 0.0)
+            moved = g * y - x_gx
+            moved = jnp.concatenate([moved[: T - 8], moved[T - 8 :] + jnp.where(last, end, 0.0)], axis=0)
             pick = (
                 iota((GROUP_HEADS, 2 * LANES), 0)
                 == 2 * q + iota((GROUP_HEADS, 2 * LANES), 1) // HEAD_DIM
@@ -719,7 +729,7 @@
         save(out_ref.at[:, pl.ds(jj * GROUP_X, GROUP_X)], out_h.at[:, span(j, GROUP_X)])
         save(pre_ref.at[:, pl.ds(jj * GROUP_X, GROUP_X)], pre_h.at[:, span(j, GROUP_X)])
         for grad, base in ((grad_b, 0), (grad_c, 1)):
-            at = HALF_GROUPS * GROUP_X + (base * HALF_GROUPS + jj) * STATE
+            at = HALF_X + (base * HALF_GROUPS + jj) * STATE
             far = span(WIDTH_X // STATE + base * GROUPS + j, STATE)
             fill_window(win_ref, before_ref[:, far], tok_ref[:, at : at + STATE])
             grad_pre = grad * slope_ref[:, at : at + STATE]
@@ -736,46 +746,35 @@
         rows = jj * SUM_GROUP
         sum_ref[rows : rows + SUM_GROUP, :] = jnp.concatenate(terms + skips + [dt * behind * decay], axis=0)
         save(sum_ref.at[pl.ds(rows, SUM_GROUP)], sum_h.at[span(j, SUM_GROUP)])
-    wait_all(saves)
-
-
-def run_leave(core, inputs, state, small, raw, before_out):
+    wait_all(saves + fetches)
+
+
+def run_leave(core, state, near, common, far, before_out):
+    theirs = before_out is not None
     out = [
         ("h", (T, WIDTH_X), BF16),
         ("h", (T, CHANNELS), F32),
         ("h", (HEADS, T), F32),
         ("h", (SUM_ROWS, LANES), F32),
     ]
-    half_x = HALF_GROUPS * GROUP_X
-    half_b = 2 * HALF_GROUPS * STATE
     scratch = [
-        pltpu.VMEM((T, half_x), BF16),
-        pltpu.VMEM((T, half_b), BF16),
-        pltpu.VMEM((T, half_x), BF16),
-        pltpu.VMEM((T, half_x), F32),
-        pltpu.VMEM((T, half_x), F32),
-        pltpu.VMEM((T, half_b), F32),
-        pltpu.VMEM((T, half_x + half_b), F32),
-        pltpu.VMEM((T, half_x + half_b), BF16),
-        pltpu.VMEM((8, CHANNELS), F32),
-        pltpu.VMEM((SMALL_ROWS, LANES), F32),
-        pltpu.VMEM((HEADS, T), F32),
-        pltpu.VMEM((T, half_x), BF16),
-        pltpu.VMEM((T, half_x + half_b), F32),
+        pltpu.VMEM((T, HALF_X), BF16),
+        pltpu.VMEM((T, HALF_X + HALF_B), F32),
         pltpu.VMEM((HALF_GROUPS * GROUP_HEADS, T), F32),
         pltpu.VMEM((HALF_GROUPS * SUM_GROUP, LANES), F32),
         pltpu.VMEM((8 + T, GROUP_X), F32),
-        DMA(7, 8),
-    ]
-    args = [core, *inputs, state, small, raw]
-    specs = "s" + "h" * 9 + ("V" if before_out is None else "v") + "hh"
+        DMA(3, FETCHES),
+    ]
+    args = [core, state, *near, *common, *far]
+    specs = "s" + ("v" if theirs else "V") + "V" * (len(NEAR) + len(COMMON)) + "h" * len(far)
     aliases = {}
-    if before_out is not None:
+    if theirs:
         aliases = {len(args) + i: i for i in range(len(out))}
         args += before_out
         specs += "h" * len(out)
-    kernel = functools.partial(leave_kernel, before_out is not None)
-    return call(kernel, "leave", out, specs, 5, scratch, mib=24, aliases=aliases)(*args)
+    kernel = functools.partial(leave_kernel, theirs)
+    outs = call(kernel, "leave", out + ([] if theirs else NEAR), specs, 5, scratch, mib=16, aliases=aliases)(*args)
+    return outs[:4], outs[4:]
 
 
 def spread_kernel(pre_h, halo_ref, weight_h, out_h, pre_ref, weight_ref, out_ref, win_ref, sems):
@@ -866,57 +865,61 @@
     return lax.optimization_barrier(values)
 
 
-def sum_everywhere(parts, chips):
-    share = SUM_ROWS // chips
-    total = jnp.sum(parts.reshape(chips, share, LANES), axis=0)
-    total = total + lax.ppermute(total, "core", [(0, 1), (1, 0)])
-    count = lax.axis_size("dp")
-    flip = 1
-    while flip < count:
-        mask = flip if 2 * flip < count else count - 1
-        total = total + lax.ppermute(total, "dp", [(i, i ^ mask) for i in range(count)])
-        flip *= 2
-    return all_to_all(jnp.broadcast_to(total[None], (chips, share, LANES)).reshape(SUM_ROWS, LANES), "chip")
+def fold_kernel(parts, copies, in_ref, out_ref):
+    share = in_ref.shape[0] // parts
+    total = in_ref[0:share, :]
+    for i in range(1, parts):
+        total = total + in_ref[i * share : (i + 1) * share, :]
+    for i in range(copies):
+        out_ref[i * share : (i + 1) * share, :] = total
+
+
+def run_fold(value, parts, copies):
+    out = [("v", (value.shape[0] // parts * copies, LANES), F32)]
+    return call(functools.partial(fold_kernel, parts, copies), "fold", out, "v", 1, mib=16)(value)[0]
 
 
 def local(conv_input, conv_weight, step_raw, decay_log, skip_gain, cotangent):
     chips = lax.axis_size("chip")
     devices = 2 * chips
+    across = 2 * lax.axis_size("dp")
     tokens = conv_input[0]
     raw = step_raw[0]
     cot = cotangent[0]
     core = lax.axis_index("core").astype(jnp.int32).reshape(1)
     swap = [(0, 1), (1, 0)]
     halo = lax.ppermute(tokens[T - TAPS + 1 :], CTX, [(i, i + 1) for i in range(devices - 1)])
-    small, small_near, tot, x0, bc0, head = run_begin(
-        raw, decay_log.reshape(1, HEADS), skip_gain.reshape(1, HEADS), tokens, conv_weight
+    small, small_near, tot, x0, bc0, head, weight_near, cot_near = run_begin(
+        raw, decay_log.reshape(1, HEADS), skip_gain.reshape(1, HEADS), tokens, conv_weight, cot
     )
     other = lax.ppermute(tot, "core", swap)
     x, bc, before, x_near, bc_near, out = run_enter(
-        core, x0, bc0, head, halo, conv_weight, cot, small_near
+        core, x0, bc0, head, halo, weight_near, cot_near, small_near
     )
     got_near = lax.ppermute(out, "core", swap)
-    own_near = run_own(core, x_near, bc_near, cot, small_near)
+    own_near = run_own(core, x_near, bc_near, cot_near, small_near)
     packed, own, got, tots = run_pack(core, own_near, got_near, tot, other)
     heard = all_to_all(packed, "chip")
-    y, gbc = run_inner(x, bc, cot, small)
-    heard, y, gbc = tie(heard, y, gbc)
+    y, gbc, skips = run_inner(x, bc, cot, small)
+    heard, y, gbc, skips = tie(heard, y, gbc, skips)
     chained = run_chain(chips, heard)
     late, chained = tie(bc, chained)
     back = all_to_all(chained, "chip")
     gx, slope = run_slopes(late, cot, small, tokens, before, conv_weight)
     back, gx, slope = tie(back, gx, slope)
-    mine, send = run_unpack(core, back, own, got, tots)
+    far = (x, cot, y, gx, slope, tokens, bc, gbc)
+    mine, send, near, common = run_unpack(core, back, own, got, tots, far, (before, small, raw, skips))
     theirs = lax.ppermute(send, "core", swap)
-    inputs = (x, bc, cot, y, gx, gbc, slope, tokens, before)
-    half = run_leave(core, inputs, mine, small, raw, None)
-    out_tokens, pre, grad_step, sums = run_leave(core, inputs, theirs, small, raw, half)
+    half, near = run_leave(core, mine, near, common, far, None)
+    (out_tokens, pre, grad_step, sums), _ = run_leave(core, theirs, near, common, (), half)
     parts = all_to_all(sums, "chip")
     first = pre[: TAPS - 1].astype(BF16)
     after = lax.ppermute(first, CTX, [(i + 1, i) for i in range(devices - 1)])
+    parts = all_to_all(run_fold(parts, chips, across), ("dp", "core"))
     parts, after = tie(parts, after)
-    grad_conv, grad_decay, grad_skip = run_finish(sum_everywhere(parts, chips))
+    sums = all_to_all(run_fold(parts, across, chips), "chip")
     grad_tokens = run_spread(pre, after, conv_weight)
+    grad_conv, grad_decay, grad_skip = run_finish(sums)
     return (
         out_tokens[None],
         grad_tokens[None],

time: 127 us -> 120 us (0.945)
  the two profiles are of different devices: /device:TPU:2 before, /device:TPU:1 now
where the time goes in v4:
time: 120 us
  Pallas kernels  44.7 us (37%)
  starting transfers between devices  34.7 us (29%)
  waiting for transfers between devices  27.5 us (23%)
  blocking collectives  10.2 us (8%)
  local copies, waits for them, and re-layouts  1.84 us (2%)
    pallas_call x14, Pallas kernels, go(): run(*[pin(a, spaces[p]) if p in spaces else a for a, p in zip(args, specs...  44.7 us
    all_to_all x4, starting transfers between devices, all_to_all(): return lax.all_to_all(value, axis, 0, 0, tiled=True)  24.1 us
    all_to_all x4, waiting for transfers between devices, all_to_all(): return lax.all_to_all(value, axis, 0, 0, tiled=True)  23.4 us
    all_to_all x1, blocking collectives, all_to_all(): return lax.all_to_all(value, axis, 0, 0, tiled=True)  10.2 us
    ppermute x1, starting transfers between devices, local(): lax.ppermute(tokens[T - TAPS + 1:], CTX, [(i, i + 1) for i in range(devic...  4.59 us
    ppermute x1, waiting for transfers between devices, local(): after = lax.ppermute(first, CTX, [(i + 1, i) for i in range(devices - 1)])  3.6 us
    ppermute x1, starting transfers between devices, local(): theirs = lax.ppermute(send, 'core', swap)  3.4 us
  transfers between devices with their start and end apart: 9, of which 6 were waited for; matrix products, arithmetic and copies ran while one was open for 1% of the time, Pallas kernels for 24%

profile of v4, /device:TPU:1, one launch (start us, length us, event | category | flops | bytes accessed | tf_op | source)
XLA Modules:
  0.0 119.7 jit_solution(12423116784639928412)
XLA Ops:
  0.6 0.9 slice_bitcast_fusion
  1.5 4.6 %collective-permute-start = (bf16[3,5120]{1,0:T(4,128)(2,1)S(1)}, bf16[3,5120]{1,0:T(4,128)(2,1)S(1)}, u32[]{:S(2)}, u32[]{:S(2)}) collective-permute-start(bf16[3,5120]{1,0:T(4,128)(2,1)S(1)} %slice_bitcast_fusion), channel_id=1, source_target_pairs={{0,1},{1,2},{2,3},{3,4},{4,5},{5,6},{6,7},{7,8},{8,9},{9,10},{10,1... | collective-permute-start | bytes 92168 | tf_op jit(solution)/shard_map/ppermute | solution.py:891
  6.2 4.3 %begin.1 = (f32[512,128]{1,0:T(8,128)}, f32[512,128]{1,0:T(8,128)S(1)}, f32[32,128]{1,0:T(8,128)S(1)}, bf16[128,4096]{1,0:T(8,128)(2,1)S(1)}, bf16[128,1024]{1,0...) custom-call(f32[64,128]{1,0:T(8,128)} %bitcast.32, ...), custom_call_target="tpu_custom_call" | custom-call | flops 4000000000 | bytes 14400000 | tf_op jit(solution)/shard_map/begin/pallas_call | solution.py:98
  10.5 0.0 collective-permute-done.halo_ref
  10.5 2.4 %enter.1 = (bf16[128,4096]{1,0:T(8,128)(2,1)}, bf16[128,1024]{1,0:T(8,128)(2,1)}, f32[8,5120]{1,0:T(8,128)}, bf16[128,4096]{1,0:T(8,128)(2,1)S(1)}, bf16[128,102...) custom-call(s32[1]{0:T(128)} %bitcast.core_ref, bf16[128,4096]{1,0:T(8,128)(2,1)S(1)} %get-tuple-element.73.x0_ref, ...), custom_call_target="tpu_custom_call" | custom-call | flops 3000000000 | bytes 10800000 | tf_op jit(solution)/shard_map/enter/pallas_call | solution.py:98
  12.9 0.1 collective-permute-start.1
  13.0 0.5 collective-permute-start.2
  13.5 1.6 %own.1.own_ref = bf16[2,16,128,128]{3,2,1,0:T(8,128)(2,1)S(1)} custom-call(s32[1]{0:T(128)} %bitcast.core_ref, bf16[128,4096]{1,0:T(8,128)(2,1)S(1)} %get-tuple-element.80.x_ref, bf16[128,1024]{1,0:T(8,128)(2,1)S(1)} %get-tuple-element.81.bc_ref, bf16[128,4096]{1,0:T(8,128)(2,1)S(1)} %get-tuple-element.77.g_ref, f32[512,128]{1,0:T(8,128)S(1)} %get-tuple-element.78.small_ref), custom_call_target="tpu_custom_call" | custom-call | flops 3000000000 | bytes 10800000 | tf_op jit(solution)/shard_map/own/pallas_call | solution.py:98
  15.1 0.5 collective-permute-done.2.other_ref
  15.6 0.0 collective-permute-done.1.got_ref
  15.6 1.8 %pack.1 = (bf16[16,272,128]{2,1,0:T(8,128)(2,1)}, bf16[2,16,128,128]{3,2,1,0:T(8,128)(2,1)}, bf16[2,16,128,128]{3,2,1,0:T(8,128)(2,1)}, f32[64,128]{1,0:T(8,128)}) custom-call(s32[1]{0:T(128)} %bitcast.core_ref, bf16[2,16,128,128]{3,2,1,0:T(8,128)(2,1)S(1)} %own.1.own_ref, bf16[2,16,128,128]{3,2,1,0:T(8,128)(2,1)S(1)} %collective-permute-done.1.got_ref, ...), custom_call_target="tpu_custom_call" | custom-call | flops 2000000000 | bytes 7200000 | tf_op jit(solution)/shard_map/pack/pallas_call | solution.py:98
  17.4 6.5 %all-to-all-start = ((bf16[16,272,128]{2,1,0:T(8,128)(2,1)}), bf16[16,272,128]{2,1,0:T(8,128)(2,1)S(1)}, u32[]{:S(2)}, u32[]{:S(2)}) async-start(bf16[16,272,128]{2,1,0:T(8,128)(2,1)} %get-tuple-element.84), calls=%async_computation | async-start | bytes 2228224 | tf_op jit(solution)/shard_map/all_to_all | solution.py:861
  23.9 5.6 %inner.1 = (f32[128,4096]{1,0:T(8,128)}, f32[128,1024]{1,0:T(8,128)}, f32[32,128]{1,0:T(8,128)}) custom-call(bf16[128,4096]{1,0:T(8,128)(2,1)} %get-tuple-element.85.x_h.rest_0_.rest_12_, bf16[128,1024]{1,0:T(8,128)(2,1)} %get-tuple-element.92.bc_h.rest_6_.rest_18_, bf16[128,4096]{1,0:T(8,128)(2,1)} %bitcast.27, f32[512,128]{1,0:T(8,128)} %get-tuple-element.86.small_h.rest_9_), custom_call_target="tpu_custom_call" | custom-call | flops 4000000000 | bytes 14400000 | tf_op jit(solution)/shard_map/inner/pallas_call | solution.py:98
  29.5 11.4 %all-to-all-done.in_ref = bf16[16,272,128]{2,1,0:T(8,128)(2,1)S(1)} async-done(((bf16[16,272,128]{2,1,0:T(8,128)(2,1)}), bf16[16,272,128]{2,1,0:T(8,128)(2,1)S(1)}, u32[]{:S(2)}, u32[]{:S(2)}) %all-to-all-start) | async-done | bytes 1114144 | tf_op jit(solution)/shard_map/all_to_all | solution.py:861
  40.9 1.3 %chain.1 = bf16[16,256,128]{2,1,0:T(8,128)(2,1)} custom-call(bf16[16,272,128]{2,1,0:T(8,128)(2,1)S(1)} %all-to-all-done.in_ref), custom_call_target="tpu_custom_call" | custom-call | flops 1000000000 | bytes 3600000 | tf_op jit(solution)/shard_map/chain/pallas_call | solution.py:98
  42.1 4.2 %all-to-all-start.1 = ((bf16[16,256,128]{2,1,0:T(8,128)(2,1)}), bf16[16,256,128]{2,1,0:T(8,128)(2,1)S(1)}, u32[]{:S(2)}, u32[]{:S(2)}) async-start(bf16[16,256,128]{2,1,0:T(8,128)(2,1)} %chain.1), calls=%async_computation.1 | async-start | bytes 2097152 | tf_op jit(solution)/shard_map/all_to_all | solution.py:861
  46.4 8.7 %slopes.1 = (f32[128,4096]{1,0:T(8,128)}, f32[128,5120]{1,0:T(8,128)}) custom-call(bf16[128,1024]{1,0:T(8,128)(2,1)} %get-tuple-element.92.bc_h.rest_6_.rest_18_, bf16[128,4096]{1,0:T(8,128)(2,1)} %bitcast.28, f32[512,128]{1,0:T(8,128)} %get-tuple-element.86.small_h.rest_9_, bf16[128,5120]{1,0:T(8,128)(2,1)} %bitcast.23, ...), custom_call_target="tpu_custom_call" | custom-call | flops 6000000000 | bytes 21600000 | tf_op jit(solution)/shard_map/slopes/pallas_call | solution.py:98
  55.0 6.2 %all-to-all-done.1.back_ref = bf16[16,256,128]{2,1,0:T(8,128)(2,1)S(1)} async-done(((bf16[16,256,128]{2,1,0:T(8,128)(2,1)}), bf16[16,256,128]{2,1,0:T(8,128)(2,1)S(1)}, u32[]{:S(2)}, u32[]{:S(2)}) %all-to-all-start.1) | async-done | bytes 1048608 | tf_op jit(solution)/shard_map/all_to_all | solution.py:861
  61.3 3.8 %unpack.1 = (bf16[2,16,128,128]{3,2,1,0:T(8,128)(2,1)S(1)}, bf16[2,16,128,128]{3,2,1,0:T(8,128)(2,1)S(1)}, bf16[128,2048]{1,0:T(8,128)(2,1)S(1)}, bf16[128,2048]...) custom-call(s32[1]{0:T(128)} %bitcast.core_ref, ...), custom_call_target="tpu_custom_call" | custom-call | flops 3000000000 | bytes 10800000 | tf_op jit(solution)/shard_map/unpack/pallas_call | solution.py:98
  65.1 3.4 %collective-permute-start.3 = (bf16[2,16,128,128]{3,2,1,0:T(8,128)(2,1)S(1)}, bf16[2,16,128,128]{3,2,1,0:T(8,128)(2,1)S(1)}, u32[]{:S(2)}, u32[]{:S(2)}) collective-permute-start(bf16[2,16,128,128]{3,2,1,0:T(8,128)(2,1)S(1)} %get-tuple-element.105), channel_id=1, source_target_pairs={{0,1},{1,0},{2,3},{3,2},{4,5},{5,4},{6,7},{7,6},{8,9},{9,8},{10,11... | collective-permute-start | bytes 3145736 | tf_op jit(solution)/shard_map/ppermute | solution.py:912
  68.5 4.8 %leave.2 = (bf16[128,4096]{1,0:T(8,128)(2,1)}, f32[128,5120]{1,0:T(8,128)}, f32[64,128]{1,0:T(8,128)}, f32[256,128]{1,0:T(8,128)}, bf16[128,2048]{1,0:T(8,128)(2...) custom-call(s32[1]{0:T(128)} %bitcast.core_ref, ...), custom_call_target="tpu_custom_call" | custom-call | flops 5000000000 | bytes 18000000 | tf_op jit(solution)/shard_map/leave/pallas_call | solution.py:98
  73.4 0.0 collective-permute-done.3.state_ref
  73.4 4.1 %leave.3 = (bf16[128,4096]{1,0:T(8,128)(2,1)}, f32[128,5120]{1,0:T(8,128)}, f32[64,128]{1,0:T(8,128)}, f32[256,128]{1,0:T(8,128)}) custom-call(s32[1]{0:T(128)} %bitcast.core_ref, bf16[2,16,128,128]{3,2,1,0:T(8,128)(2,1)S(1)} %collective-permute-done.3.state_ref, ...), custom_call_target="tpu_custom_call", output_to_operand_aliasing={{0}: (14, {}), {1}: (15, {}), {2}: (16, {}), {3}: (17, {})} | custom-call | flops 5000000000 | bytes 18000000 | tf_op jit(solution)/shard_map/leave/pallas_call | solution.py:98
  77.5 10.2 %all_to_all.44 = f32[16,16,128]{2,1,0:T(8,128)S(1)} all-to-all(f32[16,16,128]{2,1,0:T(8,128)} %bitcast.31), channel_id=1, replica_groups=mesh['dp'=8,'chip'=16,'core'=2] {'chip'}, dimensions={0} | all-to-all | bytes 262144 | tf_op jit(solution)/shard_map/all_to_all | solution.py:861
  87.7 0.7 fold.2
  88.4 9.9 %all-to-all-start.3 = ((f32[16,16,128]{2,1,0:T(8,128)}), f32[16,16,128]{2,1,0:T(8,128)S(1)}, u32[]{:S(2)}, u32[]{:S(2)}) async-start(f32[16,16,128]{2,1,0:T(8,128)} %bitcast.10), calls=%async_computation.3 | async-start | bytes 262144 | tf_op jit(solution)/shard_map/all_to_all | solution.py:861
  98.3 0.9 slice.16
  99.2 2.0 %collective-permute-start.4 = (bf16[3,5120]{1,0:T(4,128)(2,1)S(1)}, bf16[3,5120]{1,0:T(4,128)(2,1)S(1)}, u32[]{:S(2)}, u32[]{:S(2)}) collective-permute-start(bf16[3,5120]{1,0:T(4,128)(2,1)S(1)} %slice.16), channel_id=1, source_target_pairs={{1,0},{2,1},{3,2},{4,3},{5,4},{6,5},{7,6},{8,7},{9,8},{10,9},{11,1... | collective-permute-start | bytes 92168 | tf_op jit(solution)/shard_map/ppermute | solution.py:917
  101.2 3.6 %collective-permute-done.4.halo_ref = bf16[3,5120]{1,0:T(4,128)(2,1)S(1)} collective-permute-done((bf16[3,5120]{1,0:T(4,128)(2,1)S(1)}, bf16[3,5120]{1,0:T(4,128)(2,1)S(1)}, u32[]{:S(2)}, u32[]{:S(2)}) %collective-permute-start.4) | collective-permute-done | bytes 30752 | tf_op jit(solution)/shard_map/ppermute | solution.py:917
  104.8 2.6 %all-to-all-done.3 = f32[16,16,128]{2,1,0:T(8,128)S(1)} async-done(((f32[16,16,128]{2,1,0:T(8,128)}), f32[16,16,128]{2,1,0:T(8,128)S(1)}, u32[]{:S(2)}, u32[]{:S(2)}) %all-to-all-start.3) | async-done | bytes 131104 | tf_op jit(solution)/shard_map/all_to_all | solution.py:861
  107.4 0.7 fold.3
  108.1 3.5 %all-to-all-start.4 = ((f32[16,16,128]{2,1,0:T(8,128)}), f32[16,16,128]{2,1,0:T(8,128)S(1)}, u32[]{:S(2)}, u32[]{:S(2)}) async-start(f32[16,16,128]{2,1,0:T(8,128)} %bitcast.14), calls=%async_computation.4 | async-start | bytes 262144 | tf_op jit(solution)/shard_map/all_to_all | solution.py:861
  111.6 4.0 %spread.1 = bf16[128,5120]{1,0:T(8,128)(2,1)} custom-call(f32[128,5120]{1,0:T(8,128)} %get-tuple-element.132.pre_h, bf16[3,5120]{1,0:T(4,128)(2,1)S(1)} %collective-permute-done.4.halo_ref, f32[4,5120]{1,0:T(4,128)} %weight_h.5), custom_call_target="tpu_custom_call" | custom-call | flops 4000000000 | bytes 14400000 | tf_op jit(solution)/shard_map/spread/pallas_call | solution.py:98
  115.7 3.2 %all-to-all-done.4 = f32[16,16,128]{2,1,0:T(8,128)S(1)} async-done(((f32[16,16,128]{2,1,0:T(8,128)}), f32[16,16,128]{2,1,0:T(8,128)S(1)}, u32[]{:S(2)}, u32[]{:S(2)}) %all-to-all-start.4) | async-done | bytes 131104 | tf_op jit(solution)/shard_map/all_to_all | solution.py:861
  118.8 0.9 finish.1
Async XLA Ops:
  1.5 8.9 %collective-permute-start = (bf16[3,5120]{1,0:T(4,128)(2,1)S(1)}, bf16[3,5120]{1,0:T(4,128)(2,1)S(1)}, u32[]{:S(2)}, u32[]{:S(2)}) collective-permute-start(bf16[3,5120]{1,0:T(4,128)(2,1)S(1)} %slice_bitcast_fusion), channel_id=1, source_target_pairs={{0,1},{1,2},{2,3},{3,4},{4,5},{5,6},{6,7},{7,8},{8,9},{9,10},{10,1... | collective-permute-start | bytes 92168 | tf_op jit(solution)/shard_map/ppermute | solution.py:891
  12.9 2.8 %collective-permute-start.1 = (bf16[2,16,128,128]{3,2,1,0:T(8,128)(2,1)S(1)}, bf16[2,16,128,128]{3,2,1,0:T(8,128)(2,1)S(1)}, u32[]{:S(2)}, u32[]{:S(2)}) collective-permute-start(bf16[2,16,128,128]{3,2,1,0:T(8,128)(2,1)S(1)} %get-tuple-element.82), channel_id=1, source_target_pairs={{0,1},{1,0},{2,3},{3,2},{4,5},{5,4},{6,7},{7,6},{8,9},{9,8},{10,11... | collective-permute-start | bytes 3145736 | tf_op jit(solution)/shard_map/ppermute | solution.py:899
  13.0 2.7 %collective-permute-start.2 = (f32[32,128]{1,0:T(8,128)S(1)}, f32[32,128]{1,0:T(8,128)S(1)}, u32[]{:S(2)}, u32[]{:S(2)}) collective-permute-start(f32[32,128]{1,0:T(8,128)S(1)} %get-tuple-element.83.tot_ref), channel_id=1, source_target_pairs={{0,1},{1,0},{2,3},{3,2},{4,5},{5,4},{6,7},{7,6},{8,9},{9,8},{10,11... | collective-permute-start | bytes 49160 | tf_op jit(solution)/shard_map/ppermute | solution.py:895
  17.4 23.5 %all-to-all-start = ((bf16[16,272,128]{2,1,0:T(8,128)(2,1)}), bf16[16,272,128]{2,1,0:T(8,128)(2,1)S(1)}, u32[]{:S(2)}, u32[]{:S(2)}) async-start(bf16[16,272,128]{2,1,0:T(8,128)(2,1)} %get-tuple-element.84), calls=%async_computation | async-start | bytes 2228224 | tf_op jit(solution)/shard_map/all_to_all | solution.py:861
  42.1 19.2 %all-to-all-start.1 = ((bf16[16,256,128]{2,1,0:T(8,128)(2,1)}), bf16[16,256,128]{2,1,0:T(8,128)(2,1)S(1)}, u32[]{:S(2)}, u32[]{:S(2)}) async-start(bf16[16,256,128]{2,1,0:T(8,128)(2,1)} %chain.1), calls=%async_computation.1 | async-start | bytes 2097152 | tf_op jit(solution)/shard_map/all_to_all | solution.py:861
  65.1 8.2 %collective-permute-start.3 = (bf16[2,16,128,128]{3,2,1,0:T(8,128)(2,1)S(1)}, bf16[2,16,128,128]{3,2,1,0:T(8,128)(2,1)S(1)}, u32[]{:S(2)}, u32[]{:S(2)}) collective-permute-start(bf16[2,16,128,128]{3,2,1,0:T(8,128)(2,1)S(1)} %get-tuple-element.105), channel_id=1, source_target_pairs={{0,1},{1,0},{2,3},{3,2},{4,5},{5,4},{6,7},{7,6},{8,9},{9,8},{10,11... | collective-permute-start | bytes 3145736 | tf_op jit(solution)/shard_map/ppermute | solution.py:912
  88.4 19.0 %all-to-all-start.3 = ((f32[16,16,128]{2,1,0:T(8,128)}), f32[16,16,128]{2,1,0:T(8,128)S(1)}, u32[]{:S(2)}, u32[]{:S(2)}) async-start(f32[16,16,128]{2,1,0:T(8,128)} %bitcast.10), calls=%async_computation.3 | async-start | bytes 262144 | tf_op jit(solution)/shard_map/all_to_all | solution.py:861
  99.2 5.6 %collective-permute-start.4 = (bf16[3,5120]{1,0:T(4,128)(2,1)S(1)}, bf16[3,5120]{1,0:T(4,128)(2,1)S(1)}, u32[]{:S(2)}, u32[]{:S(2)}) collective-permute-start(bf16[3,5120]{1,0:T(4,128)(2,1)S(1)} %slice.16), channel_id=1, source_target_pairs={{1,0},{2,1},{3,2},{4,3},{5,4},{6,5},{7,6},{8,7},{9,8},{10,9},{11,1... | collective-permute-start | bytes 92168 | tf_op jit(solution)/shard_map/ppermute | solution.py:917
  108.1 10.7 %all-to-all-start.4 = ((f32[16,16,128]{2,1,0:T(8,128)}), f32[16,16,128]{2,1,0:T(8,128)S(1)}, u32[]{:S(2)}, u32[]{:S(2)}) async-start(f32[16,16,128]{2,1,0:T(8,128)} %bitcast.14), calls=%async_computation.4 | async-start | bytes 262144 | tf_op jit(solution)/shard_map/all_to_all | solution.py:861

commit v5 on v4

--- a/solution.py
+++ b/solution.py
@@ -148,6 +148,8 @@
     blocks = [pl.ds(i * GROUP_X, GROUP_X) for i in range(BLOCKS)]
     copies = start_all([(tok_h.at[:, at], hold_ref.at[:, at]) for at in blocks], sems.at[1])
     later = start_all([(g_h, g_ref)], sems.at[2])
+    win_ref[0:8, :] = jnp.zeros((8, GROUP_X), F32)
+    copies[0].wait()
     diagonal = iota((HEADS, HEADS), 0) == iota((HEADS, HEADS), 1)
 
     def column(row):
@@ -180,9 +182,9 @@
     small_ref[ROW_SKIP : ROW_SKIP + PAIRS] = paired(column(skip_gain_ref[...]))
     small_ref[ROW_DECAY : ROW_DECAY + HEADS] = jnp.broadcast_to(decay, (HEADS, LANES))
     save = start_all([(small_ref, small_h)], sems.at[0])
-    win_ref[0:8, :] = jnp.zeros((8, GROUP_X), F32)
     for i in range(BLOCKS):
-        copies[i].wait()
+        if i:
+            copies[i].wait()
         cols = slice(i * GROUP_X, (i + 1) * GROUP_X)
         win_ref[8 : 8 + T, :] = hold_ref[:, cols].astype(F32)
         for lo in range(0, GROUP_X, LANES):
@@ -389,14 +391,14 @@
 HALF_B = 2 * HALF_GROUPS * STATE
 
 NEAR = [
-    ("V", (T, HALF_X), BF16),
-    ("V", (T, HALF_X), BF16),
-    ("V", (T, HALF_X), F32),
-    ("V", (T, HALF_X), F32),
-    ("V", (T, HALF_X + HALF_B), F32),
-    ("V", (T, HALF_X + HALF_B), BF16),
-    ("V", (T, HALF_B), BF16),
-    ("V", (T, HALF_B), F32),
+    ("V", (T, GROUP_X), BF16),
+    ("V", (T, GROUP_X), BF16),
+    ("V", (T, GROUP_X), F32),
+    ("V", (T, GROUP_X), F32),
+    ("V", (T, GROUP_X + 2 * STATE), F32),
+    ("V", (T, GROUP_X + 2 * STATE), BF16),
+    ("V", (T, 2 * STATE), BF16),
+    ("V", (T, 2 * STATE), F32),
 ]
 COMMON = [
     ("V", (8, CHANNELS), F32),
@@ -407,23 +409,24 @@
 FETCHES = 6 + 8
 
 
-def fetch_half(half, far, near, sems):
+def fetch_group(j, far, near, sems):
     x_h, g_h, y_h, gx_h, slope_h, tok_h, bc_h, gbc_h = far
     x_v, g_v, y_v, gx_v, slope_v, tok_v, bc_v, gbc_v = near
-    wide = pl.ds(0, HALF_X)
+    wide = pl.ds(0, GROUP_X)
     pairs = [
-        (a.at[:, span(half, HALF_X)], b.at[:, wide])
+        (a.at[:, span(j, GROUP_X)], b.at[:, wide])
         for a, b in ((x_h, x_v), (g_h, g_v), (y_h, y_v), (gx_h, gx_v), (slope_h, slope_v), (tok_h, tok_v))
     ]
-    size = HALF_GROUPS * STATE
     for base in range(2):
-        at = span(base * 2 + half, size)
-        off = span(WIDTH_X // size + base * 2 + half, size)
+        at = span(base * GROUPS + j, STATE)
+        off = span(WIDTH_X // STATE + base * GROUPS + j, STATE)
+        thin = pl.ds(base * STATE, STATE)
+        tail = pl.ds(GROUP_X + base * STATE, STATE)
         pairs += [
-            (bc_h.at[:, at], bc_v.at[:, pl.ds(base * size, size)]),
-            (gbc_h.at[:, at], gbc_v.at[:, pl.ds(base * size, size)]),
-            (slope_h.at[:, off], slope_v.at[:, pl.ds(HALF_X + base * size, size)]),
-            (tok_h.at[:, off], tok_v.at[:, pl.ds(HALF_X + base * size, size)]),
+            (bc_h.at[:, at], bc_v.at[:, thin]),
+            (gbc_h.at[:, at], gbc_v.at[:, thin]),
+            (slope_h.at[:, off], slope_v.at[:, tail]),
+            (tok_h.at[:, off], tok_v.at[:, tail]),
         ]
     return start_all(pairs, sems)
 
@@ -443,7 +446,7 @@
             start_all([(own_h.at[:, at], own_ref.at[:, at]), (got_h.at[:, at], got_ref.at[:, at])], sems.at[step])
         )
     fetches = start_all(list(zip(common_far, common)), fetch_sems.at[1])
-    fetches += fetch_half(core_ref[0], far, near, fetch_sems.at[0])
+    fetches += fetch_group(core_ref[0] * HALF_GROUPS, far, near, fetch_sems.at[0])
     wait_all(first)
     second = core_ref[0] == 1
     for i in range(HALF_PAIRS):
@@ -645,16 +648,38 @@
 
 
 def leave_kernel(theirs, core_ref, state_ref, *rest):
-    near, rest = rest[: len(NEAR)], rest[len(NEAR) :]
-    x_ref, g_ref, y_ref, gx_ref, slope_ref, tok_ref, bc_ref, gbc_ref = near
-    (before_ref, small_ref, raw_ref, skips_ref), rest = rest[: len(COMMON)], rest[len(COMMON) :]
-    far, rest = rest[: len(NEAR)], rest[len(NEAR) :]
-    out_ref, pre_ref, step_ref, sum_ref, win_ref, sems = rest[-6:]
+    rest = list(rest)
+
+    def take(count):
+        taken = rest[:count]
+        del rest[:count]
+        return taken
+
+    sets = [take(len(NEAR))]
     if theirs:
-        far, rest = (), far[4:] + rest
-    out_h, pre_h, step_h, sum_h = rest[:4]
+        sets.append(take(len(NEAR)))
+    before_ref, small_ref, raw_ref, skips_ref = take(len(COMMON))
+    far = take(4 if theirs else len(NEAR))
+    out_h, pre_h, step_h, sum_h = take(4)
     half = 1 - core_ref[0] if theirs else core_ref[0]
-    fetches = [] if theirs else fetch_half(1 - core_ref[0], far, rest[4 : 4 + len(NEAR)], sems.at[2])
+    arrivals, fetches = [], []
+    if theirs:
+        first_ref, = take(1)
+        head_ref, = take(1)
+    else:
+        after = [take(len(NEAR)) for _ in range(HALF_GROUPS)]
+        sets.append(take(len(NEAR)))
+    out_ref, pre_ref, step_ref, sum_ref, win_ref, sems = rest
+    if theirs:
+        own = core_ref[0]
+        pieces = [span(own, HALF_X)] + [
+            span(WIDTH_X // (HALF_GROUPS * STATE) + 2 * base + own, HALF_GROUPS * STATE) for base in range(2)
+        ]
+        fetches = start_all([(pre_h.at[pl.ds(0, 8), at], head_ref.at[:, at]) for at in pieces], sems.at[2])
+    else:
+        arrivals = fetch_group(half * HALF_GROUPS + 1, far, sets[1], sems.at[2])
+        for jj in range(HALF_GROUPS):
+            fetches += fetch_group((1 - half) * HALF_GROUPS + jj, far, after[jj], sems.at[3 + jj])
     last = iota((8, 2 * LANES), 0) == 7
     lower = (iota((T, T), 0) >= iota((T, T), 1)).astype(F32)
 
@@ -677,12 +702,13 @@
 
     for jj in range(HALF_GROUPS):
         j = half * HALF_GROUPS + jj
-        near_b = slice(jj * STATE, (jj + 1) * STATE)
-        near_c = slice((HALF_GROUPS + jj) * STATE, (HALF_GROUPS + jj + 1) * STATE)
-        b = bc_ref[:, near_b]
-        c = bc_ref[:, near_c]
-        grad_b = gbc_ref[:, near_b]
-        grad_c = gbc_ref[:, near_c]
+        x_ref, g_ref, y_ref, gx_ref, slope_ref, tok_ref, bc_ref, gbc_ref = sets[jj]
+        if jj:
+            wait_all(arrivals)
+        b = bc_ref[:, 0:STATE]
+        c = bc_ref[:, STATE:]
+        grad_b = gbc_ref[:, 0:STATE]
+        grad_c = gbc_ref[:, STATE:]
         cols = rolled(small_ref[ROW_SCALE : ROW_SCALE + T], j)
         skip_rows = small_ref[pl.ds(pl.multiple_of(ROW_SKIP + j * GROUP_PAIRS, GROUP_PAIRS), GROUP_PAIRS), :]
         tot_rows = small_ref[pl.ds(pl.multiple_of(ROW_TOT + j * GROUP_PAIRS, GROUP_PAIRS), GROUP_PAIRS), :]
@@ -690,10 +716,10 @@
         dt_grad = jnp.zeros((GROUP_HEADS, T), F32)
         skips = [skips_ref[span(j, GROUP_PAIRS), :]]
         terms = []
-        near = slice(jj * GROUP_X, (jj + 1) * GROUP_X)
-        fill_window(win_ref, before_ref[:, span(j, GROUP_X)], tok_ref[:, near])
+        fill_window(win_ref, before_ref[:, span(j, GROUP_X)], tok_ref[:, 0:GROUP_X])
         for q in range(0, GROUP_PAIRS, 2):
-            lanes = slice(jj * GROUP_X + q * LANES, jj * GROUP_X + (q + 2) * LANES)
+            lanes = slice(q * LANES, (q + 2) * LANES)
+            wide = slice(jj * GROUP_X + q * LANES, jj * GROUP_X + (q + 2) * LANES)
             rise = widen_two(cols, 0, q)
             keep = widen_two(cols, HEADS, q)
             at = jj * GROUP_PAIRS + q
@@ -708,9 +734,12 @@
             gx = gx_ref[:, lanes] + through
             grad_c = grad_c + dot((g * rise).astype(BF16), state, NT)
             grad_b = grad_b + dot((x * keep).astype(BF16), exits, NT)
-            out_ref[:, lanes] = (y + skip * x).astype(BF16)
+            out_ref[:, wide] = (y + skip * x).astype(BF16)
             grad_pre = (gx + skip * g) * slope_ref[:, lanes]
-            pre_ref[:, lanes] = grad_pre
+            pre_ref[:, wide] = grad_pre
+            if theirs:
+                at = pl.ds(pl.multiple_of(j * GROUP_X + q * LANES, 2 * LANES), 2 * LANES)
+                head_ref[:, at] = grad_pre[0:8]
             terms += by_rows(tap_sums(grad_pre, q * LANES))
             x_gx = x * gx
             end = jnp.sum(x * through, axis=0, keepdims=True) + jnp.exp(tot) * jnp.sum(
@@ -726,16 +755,23 @@
                 seg_grad = seg_grad + dot(pick, part, NT)
             for part in split_two(x_gx):
                 dt_grad = dt_grad + dot(pick, part, NT)
-        save(out_ref.at[:, pl.ds(jj * GROUP_X, GROUP_X)], out_h.at[:, span(j, GROUP_X)])
-        save(pre_ref.at[:, pl.ds(jj * GROUP_X, GROUP_X)], pre_h.at[:, span(j, GROUP_X)])
+            if q % 4 == 2:
+                size = GROUP_X // 2
+                near_at = pl.ds(jj * GROUP_X + (q // 4) * size, size)
+                far_at = span(2 * j + q // 4, size)
+                save(out_ref.at[:, near_at], out_h.at[:, far_at])
+                save(pre_ref.at[:, near_at], pre_h.at[:, far_at])
         for grad, base in ((grad_b, 0), (grad_c, 1)):
             at = HALF_X + (base * HALF_GROUPS + jj) * STATE
-            far = span(WIDTH_X // STATE + base * GROUPS + j, STATE)
-            fill_window(win_ref, before_ref[:, far], tok_ref[:, at : at + STATE])
-            grad_pre = grad * slope_ref[:, at : at + STATE]
+            tail = slice(GROUP_X + base * STATE, GROUP_X + (base + 1) * STATE)
+            far_at = span(WIDTH_X // STATE + base * GROUPS + j, STATE)
+            fill_window(win_ref, before_ref[:, far_at], tok_ref[:, tail])
+            grad_pre = grad * slope_ref[:, tail]
             pre_ref[:, at : at + STATE] = grad_pre
+            if theirs:
+                head_ref[:, far_at] = grad_pre[0:8]
             terms += tap_sums(grad_pre, 0)
-            save(pre_ref.at[:, pl.ds(at, STATE)], pre_h.at[:, far])
+            save(pre_ref.at[:, pl.ds(at, STATE)], pre_h.at[:, far_at])
         heads = span(j, GROUP_HEADS)
         behind = exact_dot(seg_grad, lower)
         dt = small_ref[pl.ds(pl.multiple_of(ROW_DT + j * GROUP_HEADS, GROUP_HEADS), GROUP_HEADS), :]
@@ -746,7 +782,10 @@
         rows = jj * SUM_GROUP
         sum_ref[rows : rows + SUM_GROUP, :] = jnp.concatenate(terms + skips + [dt * behind * decay], axis=0)
         save(sum_ref.at[pl.ds(rows, SUM_GROUP)], sum_h.at[span(j, SUM_GROUP)])
-    wait_all(saves + fetches)
+    wait_all(fetches)
+    if theirs:
+        first_ref[...] = head_ref[0 : TAPS - 1, :].astype(BF16)
+    wait_all(saves)
 
 
 def run_leave(core, state, near, common, far, before_out):
@@ -763,17 +802,22 @@
         pltpu.VMEM((HALF_GROUPS * GROUP_HEADS, T), F32),
         pltpu.VMEM((HALF_GROUPS * SUM_GROUP, LANES), F32),
         pltpu.VMEM((8 + T, GROUP_X), F32),
-        DMA(3, FETCHES),
+        DMA(3 + HALF_GROUPS, FETCHES + 2),
     ]
     args = [core, state, *near, *common, *far]
-    specs = "s" + ("v" if theirs else "V") + "V" * (len(NEAR) + len(COMMON)) + "h" * len(far)
+    specs = "s" + ("v" if theirs else "V") + "V" * (len(near) + len(COMMON)) + "h" * len(far)
     aliases = {}
     if theirs:
         aliases = {len(args) + i: i for i in range(len(out))}
         args += before_out
         specs += "h" * len(out)
+        more = [("V", (TAPS - 1, CHANNELS), BF16)]
+        scratch = [pltpu.VMEM((8, CHANNELS), F32)] + scratch
+    else:
+        more = NEAR * HALF_GROUPS
+        scratch = [pltpu.VMEM(shape, dtype) for _, shape, dtype in NEAR] + scratch
     kernel = functools.partial(leave_kernel, theirs)
-    outs = call(kernel, "leave", out + ([] if theirs else NEAR), specs, 5, scratch, mib=16, aliases=aliases)(*args)
+    outs = call(kernel, "leave", out + more, specs, 5, scratch, mib=16, aliases=aliases)(*args)
     return outs[:4], outs[4:]
 
 
@@ -911,14 +955,14 @@
     mine, send, near, common = run_unpack(core, back, own, got, tots, far, (before, small, raw, skips))
     theirs = lax.ppermute(send, "core", swap)
     half, near = run_leave(core, mine, near, common, far, None)
-    (out_tokens, pre, grad_step, sums), _ = run_leave(core, theirs, near, common, (), half)
+    (out_tokens, pre, grad_step, sums), (first,) = run_leave(core, theirs, near, common, (), half)
     parts = all_to_all(sums, "chip")
-    first = pre[: TAPS - 1].astype(BF16)
     after = lax.ppermute(first, CTX, [(i + 1, i) for i in range(devices - 1)])
+    parts, after = tie(parts, after)
     parts = all_to_all(run_fold(parts, chips, across), ("dp", "core"))
-    parts, after = tie(parts, after)
+    grad_tokens = run_spread(pre, after, conv_weight)
+    parts, grad_tokens = tie(parts, grad_tokens)
     sums = all_to_all(run_fold(parts, across, chips), "chip")
-    grad_tokens = run_spread(pre, after, conv_weight)
     grad_conv, grad_decay, grad_skip = run_finish(sums)
     return (
         out_tokens[None],

time: 120 us -> 122 us (1.017)
  the two profiles are of different devices: /device:TPU:1 before, /device:TPU:2 now
where the time goes in v5:
time: 122 us; the launch traced here: 120 us
  Pallas kernels  44.8 us (37%)
  starting transfers between devices  34.7 us (28%)
  waiting for transfers between devices  25.1 us (21%)
  blocking collectives  14 us (11%)
    pallas_call x14, Pallas kernels, go(): run(*[pin(a, spaces[p]) if p in spaces else a for a, p in zip(args, specs...  44.8 us
    all_to_all x4, starting transfers between devices, all_to_all(): return lax.all_to_all(value, axis, 0, 0, tiled=True)  27.4 us
    all_to_all x4, waiting for transfers between devices, all_to_all(): return lax.all_to_all(value, axis, 0, 0, tiled=True)  21.8 us
    all_to_all x1, blocking collectives, all_to_all(): return lax.all_to_all(value, axis, 0, 0, tiled=True)  14 us
    ppermute x1, starting transfers between devices, local(): after = lax.ppermute(first, CTX, [(i + 1, i) for i in range(devices - 1)])  4.18 us
  transfers between devices with their start and end apart: 9, of which 7 were waited for; matrix products, arithmetic and copies ran while one was open for 0% of the time, Pallas kernels for 25%

profile of v5, /device:TPU:2, one launch (start us, length us, event | category | flops | bytes accessed | tf_op | source)
XLA Modules:
  0.0 120.2 jit_solution(8286510149963935292)
XLA Ops:
  0.6 0.9 slice_bitcast_fusion
  1.5 1.9 %collective-permute-start = (bf16[3,5120]{1,0:T(4,128)(2,1)S(1)}, bf16[3,5120]{1,0:T(4,128)(2,1)S(1)}, u32[]{:S(2)}, u32[]{:S(2)}) collective-permute-start(bf16[3,5120]{1,0:T(4,128)(2,1)S(1)} %slice_bitcast_fusion), channel_id=1, source_target_pairs={{0,1},{1,2},{2,3},{3,4},{4,5},{5,6},{6,7},{7,8},{8,9},{9,10},{10,1... | collective-permute-start | bytes 92168 | tf_op jit(solution)/shard_map/ppermute | solution.py:935
  3.5 4.5 %begin.1 = (f32[512,128]{1,0:T(8,128)}, f32[512,128]{1,0:T(8,128)S(1)}, f32[32,128]{1,0:T(8,128)S(1)}, bf16[128,4096]{1,0:T(8,128)(2,1)S(1)}, bf16[128,1024]{1,0...) custom-call(f32[64,128]{1,0:T(8,128)} %bitcast.33, ...), custom_call_target="tpu_custom_call" | custom-call | flops 4000000000 | bytes 14400000 | tf_op jit(solution)/shard_map/begin/pallas_call | solution.py:98
  7.9 1.0 collective-permute-done.halo_ref
  9.0 2.4 %enter.1 = (bf16[128,4096]{1,0:T(8,128)(2,1)}, bf16[128,1024]{1,0:T(8,128)(2,1)}, f32[8,5120]{1,0:T(8,128)}, bf16[128,4096]{1,0:T(8,128)(2,1)S(1)}, bf16[128,102...) custom-call(s32[1]{0:T(128)} %bitcast.core_ref, bf16[128,4096]{1,0:T(8,128)(2,1)S(1)} %get-tuple-element.84.x0_ref, ...), custom_call_target="tpu_custom_call" | custom-call | flops 3000000000 | bytes 10800000 | tf_op jit(solution)/shard_map/enter/pallas_call | solution.py:98
  11.4 0.7 collective-permute-start.1
  12.1 0.1 collective-permute-start.2
  12.2 1.6 %own.1.own_ref = bf16[2,16,128,128]{3,2,1,0:T(8,128)(2,1)S(1)} custom-call(s32[1]{0:T(128)} %bitcast.core_ref, bf16[128,4096]{1,0:T(8,128)(2,1)S(1)} %get-tuple-element.91.x_ref, bf16[128,1024]{1,0:T(8,128)(2,1)S(1)} %get-tuple-element.92.bc_ref, bf16[128,4096]{1,0:T(8,128)(2,1)S(1)} %get-tuple-element.88.g_ref, f32[512,128]{1,0:T(8,128)S(1)} %get-tuple-element.89.small_ref), custom_call_target="tpu_custom_call" | custom-call | flops 3000000000 | bytes 10800000 | tf_op jit(solution)/shard_map/own/pallas_call | solution.py:98
  13.9 0.6 collective-permute-done.2.other_ref
  14.4 0.0 collective-permute-done.1.got_ref
  14.4 1.8 %pack.1 = (bf16[16,272,128]{2,1,0:T(8,128)(2,1)}, bf16[2,16,128,128]{3,2,1,0:T(8,128)(2,1)}, bf16[2,16,128,128]{3,2,1,0:T(8,128)(2,1)}, f32[64,128]{1,0:T(8,128)}) custom-call(s32[1]{0:T(128)} %bitcast.core_ref, bf16[2,16,128,128]{3,2,1,0:T(8,128)(2,1)S(1)} %own.1.own_ref, bf16[2,16,128,128]{3,2,1,0:T(8,128)(2,1)S(1)} %collective-permute-done.1.got_ref, ...), custom_call_target="tpu_custom_call" | custom-call | flops 2000000000 | bytes 7200000 | tf_op jit(solution)/shard_map/pack/pallas_call | solution.py:98
  16.2 7.2 %all-to-all-start = ((bf16[16,272,128]{2,1,0:T(8,128)(2,1)}), bf16[16,272,128]{2,1,0:T(8,128)(2,1)S(1)}, u32[]{:S(2)}, u32[]{:S(2)}) async-start(bf16[16,272,128]{2,1,0:T(8,128)(2,1)} %get-tuple-element.95), calls=%async_computation | async-start | bytes 2228224 | tf_op jit(solution)/shard_map/all_to_all | solution.py:905
  23.4 5.6 %inner.1 = (f32[128,4096]{1,0:T(8,128)}, f32[128,1024]{1,0:T(8,128)}, f32[32,128]{1,0:T(8,128)}) custom-call(bf16[128,4096]{1,0:T(8,128)(2,1)} %get-tuple-element.96.x_h.rest_0_.rest_12_, bf16[128,1024]{1,0:T(8,128)(2,1)} %get-tuple-element.103.bc_h.rest_6_.rest_18_, bf16[128,4096]{1,0:T(8,128)(2,1)} %bitcast.28, f32[512,128]{1,0:T(8,128)} %get-tuple-element.97.small_h.rest_9_), custom_call_target="tpu_custom_call" | custom-call | flops 4000000000 | bytes 14400000 | tf_op jit(solution)/shard_map/inner/pallas_call | solution.py:98
  29.0 10.9 %all-to-all-done.in_ref = bf16[16,272,128]{2,1,0:T(8,128)(2,1)S(1)} async-done(((bf16[16,272,128]{2,1,0:T(8,128)(2,1)}), bf16[16,272,128]{2,1,0:T(8,128)(2,1)S(1)}, u32[]{:S(2)}, u32[]{:S(2)}) %all-to-all-start) | async-done | bytes 1114144 | tf_op jit(solution)/shard_map/all_to_all | solution.py:905
  39.9 1.3 %chain.1 = bf16[16,256,128]{2,1,0:T(8,128)(2,1)} custom-call(bf16[16,272,128]{2,1,0:T(8,128)(2,1)S(1)} %all-to-all-done.in_ref), custom_call_target="tpu_custom_call" | custom-call | flops 1000000000 | bytes 3600000 | tf_op jit(solution)/shard_map/chain/pallas_call | solution.py:98
  41.2 6.2 %all-to-all-start.1 = ((bf16[16,256,128]{2,1,0:T(8,128)(2,1)}), bf16[16,256,128]{2,1,0:T(8,128)(2,1)S(1)}, u32[]{:S(2)}, u32[]{:S(2)}) async-start(bf16[16,256,128]{2,1,0:T(8,128)(2,1)} %chain.1), calls=%async_computation.1 | async-start | bytes 2097152 | tf_op jit(solution)/shard_map/all_to_all | solution.py:905
  47.4 8.7 %slopes.1 = (f32[128,4096]{1,0:T(8,128)}, f32[128,5120]{1,0:T(8,128)}) custom-call(bf16[128,1024]{1,0:T(8,128)(2,1)} %get-tuple-element.103.bc_h.rest_6_.rest_18_, bf16[128,4096]{1,0:T(8,128)(2,1)} %bitcast.29, f32[512,128]{1,0:T(8,128)} %get-tuple-element.97.small_h.rest_9_, bf16[128,5120]{1,0:T(8,128)(2,1)} %bitcast.24, ...), custom_call_target="tpu_custom_call" | custom-call | flops 6000000000 | bytes 21600000 | tf_op jit(solution)/shard_map/slopes/pallas_call | solution.py:98
  56.0 5.6 %all-to-all-done.1.back_ref = bf16[16,256,128]{2,1,0:T(8,128)(2,1)S(1)} async-done(((bf16[16,256,128]{2,1,0:T(8,128)(2,1)}), bf16[16,256,128]{2,1,0:T(8,128)(2,1)S(1)}, u32[]{:S(2)}, u32[]{:S(2)}) %all-to-all-start.1) | async-done | bytes 1048608 | tf_op jit(solution)/shard_map/all_to_all | solution.py:905
  61.7 3.1 %unpack.1 = (bf16[2,16,128,128]{3,2,1,0:T(8,128)(2,1)S(1)}, bf16[2,16,128,128]{3,2,1,0:T(8,128)(2,1)S(1)}, bf16[128,1024]{1,0:T(8,128)(2,1)S(1)}, bf16[128,1024]...) custom-call(s32[1]{0:T(128)} %bitcast.core_ref, ...), custom_call_target="tpu_custom_call" | custom-call | flops 3000000000 | bytes 10800000 | tf_op jit(solution)/shard_map/unpack/pallas_call | solution.py:98
  64.7 0.3 collective-permute-start.3
  65.0 5.9 %leave.2 = (bf16[128,4096]{1,0:T(8,128)(2,1)}, f32[128,5120]{1,0:T(8,128)}, f32[64,128]{1,0:T(8,128)}, f32[256,128]{1,0:T(8,128)}, bf16[128,1024]{1,0:T(8,128)(2...) custom-call(s32[1]{0:T(128)} %bitcast.core_ref, ...), custom_call_target="tpu_custom_call" | custom-call | flops 5000000000 | bytes 18000000 | tf_op jit(solution)/shard_map/leave/pallas_call | solution.py:98
  70.9 0.0 collective-permute-done.3.state_ref
  70.9 4.4 %leave.3 = (bf16[128,4096]{1,0:T(8,128)(2,1)}, f32[128,5120]{1,0:T(8,128)}, f32[64,128]{1,0:T(8,128)}, f32[256,128]{1,0:T(8,128)}, bf16[3,5120]{1,0:T(4,128)(2,1)S(1)}) custom-call(s32[1]{0:T(128)} %bitcast.core_ref, ...), custom_call_target="tpu_custom_call", output_to_operand_aliasing={{0}: (22, {}), {1}: (23, {}), {2}: (24, {}), {3}: (25, {})} | custom-call | flops 5000000000 | bytes 18000000 | tf_op jit(solution)/shard_map/leave/pallas_call | solution.py:98
  75.4 5.5 %all-to-all-start.2 = ((f32[16,16,128]{2,1,0:T(8,128)}), f32[16,16,128]{2,1,0:T(8,128)S(1)}, u32[]{:S(2)}, u32[]{:S(2)}) async-start(f32[16,16,128]{2,1,0:T(8,128)} %bitcast.32), calls=%async_computation.2 | async-start | bytes 262144 | tf_op jit(solution)/shard_map/all_to_all | solution.py:905
  80.8 4.2 %collective-permute-start.4 = (bf16[3,5120]{1,0:T(4,128)(2,1)S(1)}, bf16[3,5120]{1,0:T(4,128)(2,1)S(1)}, u32[]{:S(2)}, u32[]{:S(2)}) collective-permute-start(bf16[3,5120]{1,0:T(4,128)(2,1)S(1)} %get-tuple-element.152), channel_id=1, source_target_pairs={{1,0},{2,1},{3,2},{4,3},{5,4},{6,5},{7,6},{8,7},{9,8},{10,9},{11,1... | collective-permute-start | bytes 92168 | tf_op jit(solution)/shard_map/ppermute | solution.py:960
  85.0 1.7 %collective-permute-done.4.halo_ref = bf16[3,5120]{1,0:T(4,128)(2,1)S(1)} collective-permute-done((bf16[3,5120]{1,0:T(4,128)(2,1)S(1)}, bf16[3,5120]{1,0:T(4,128)(2,1)S(1)}, u32[]{:S(2)}, u32[]{:S(2)}) %collective-permute-start.4) | collective-permute-done | bytes 30752 | tf_op jit(solution)/shard_map/ppermute | solution.py:960
  86.7 0.6 all-to-all-done.2
  87.3 0.7 fold.2
  88.0 8.6 %all-to-all-start.3 = ((f32[16,16,128]{2,1,0:T(8,128)}), f32[16,16,128]{2,1,0:T(8,128)S(1)}, u32[]{:S(2)}, u32[]{:S(2)}) async-start(f32[16,16,128]{2,1,0:T(8,128)} %bitcast.10), calls=%async_computation.3 | async-start | bytes 262144 | tf_op jit(solution)/shard_map/all_to_all | solution.py:905
  96.5 4.0 %spread.1 = bf16[128,5120]{1,0:T(8,128)(2,1)} custom-call(f32[128,5120]{1,0:T(8,128)} %get-tuple-element.154.pre_h, bf16[3,5120]{1,0:T(4,128)(2,1)S(1)} %collective-permute-done.4.halo_ref, f32[4,5120]{1,0:T(4,128)} %weight_h.5), custom_call_target="tpu_custom_call" | custom-call | flops 4000000000 | bytes 14400000 | tf_op jit(solution)/shard_map/spread/pallas_call | solution.py:98
  100.6 4.7 %all-to-all-done.3 = f32[16,16,128]{2,1,0:T(8,128)S(1)} async-done(((f32[16,16,128]{2,1,0:T(8,128)}), f32[16,16,128]{2,1,0:T(8,128)S(1)}, u32[]{:S(2)}, u32[]{:S(2)}) %all-to-all-start.3) | async-done | bytes 131104 | tf_op jit(solution)/shard_map/all_to_all | solution.py:905
  105.3 14.0 %all_to_all.45 = f32[16,16,128]{2,1,0:T(8,128)S(1)} all-to-all(f32[16,16,128]{2,1,0:T(8,128)S(1)} %bitcast.22), channel_id=1, replica_groups=mesh['dp'=8,'chip'=16,'core'=2] {'chip'}, dimensions={0} | all-to-all | bytes 262144 | tf_op jit(solution)/shard_map/all_to_all | solution.py:905
  119.3 0.9 finish.1
  (1 shorter events, 0.0 us)
Async XLA Ops:
  1.5 7.4 %collective-permute-start = (bf16[3,5120]{1,0:T(4,128)(2,1)S(1)}, bf16[3,5120]{1,0:T(4,128)(2,1)S(1)}, u32[]{:S(2)}, u32[]{:S(2)}) collective-permute-start(bf16[3,5120]{1,0:T(4,128)(2,1)S(1)} %slice_bitcast_fusion), channel_id=1, source_target_pairs={{0,1},{1,2},{2,3},{3,4},{4,5},{5,6},{6,7},{7,8},{8,9},{9,10},{10,1... | collective-permute-start | bytes 92168 | tf_op jit(solution)/shard_map/ppermute | solution.py:935
  11.4 3.1 %collective-permute-start.1 = (bf16[2,16,128,128]{3,2,1,0:T(8,128)(2,1)S(1)}, bf16[2,16,128,128]{3,2,1,0:T(8,128)(2,1)S(1)}, u32[]{:S(2)}, u32[]{:S(2)}) collective-permute-start(bf16[2,16,128,128]{3,2,1,0:T(8,128)(2,1)S(1)} %get-tuple-element.93), channel_id=1, source_target_pairs={{0,1},{1,0},{2,3},{3,2},{4,5},{5,4},{6,7},{7,6},{8,9},{9,8},{10,11... | collective-permute-start | bytes 3145736 | tf_op jit(solution)/shard_map/ppermute | solution.py:943
  12.1 2.3 %collective-permute-start.2 = (f32[32,128]{1,0:T(8,128)S(1)}, f32[32,128]{1,0:T(8,128)S(1)}, u32[]{:S(2)}, u32[]{:S(2)}) collective-permute-start(f32[32,128]{1,0:T(8,128)S(1)} %get-tuple-element.94.tot_ref), channel_id=1, source_target_pairs={{0,1},{1,0},{2,3},{3,2},{4,5},{5,4},{6,7},{7,6},{8,9},{9,8},{10,11... | collective-permute-start | bytes 49160 | tf_op jit(solution)/shard_map/ppermute | solution.py:939
  16.2 23.7 %all-to-all-start = ((bf16[16,272,128]{2,1,0:T(8,128)(2,1)}), bf16[16,272,128]{2,1,0:T(8,128)(2,1)S(1)}, u32[]{:S(2)}, u32[]{:S(2)}) async-start(bf16[16,272,128]{2,1,0:T(8,128)(2,1)} %get-tuple-element.95), calls=%async_computation | async-start | bytes 2228224 | tf_op jit(solution)/shard_map/all_to_all | solution.py:905
  41.2 20.5 %all-to-all-start.1 = ((bf16[16,256,128]{2,1,0:T(8,128)(2,1)}), bf16[16,256,128]{2,1,0:T(8,128)(2,1)S(1)}, u32[]{:S(2)}, u32[]{:S(2)}) async-start(bf16[16,256,128]{2,1,0:T(8,128)(2,1)} %chain.1), calls=%async_computation.1 | async-start | bytes 2097152 | tf_op jit(solution)/shard_map/all_to_all | solution.py:905
  64.7 6.2 %collective-permute-start.3 = (bf16[2,16,128,128]{3,2,1,0:T(8,128)(2,1)S(1)}, bf16[2,16,128,128]{3,2,1,0:T(8,128)(2,1)S(1)}, u32[]{:S(2)}, u32[]{:S(2)}) collective-permute-start(bf16[2,16,128,128]{3,2,1,0:T(8,128)(2,1)S(1)} %get-tuple-element.116), channel_id=1, source_target_pairs={{0,1},{1,0},{2,3},{3,2},{4,5},{5,4},{6,7},{7,6},{8,9},{9,8},{10,11... | collective-permute-start | bytes 3145736 | tf_op jit(solution)/shard_map/ppermute | solution.py:956
  75.4 11.9 %all-to-all-start.2 = ((f32[16,16,128]{2,1,0:T(8,128)}), f32[16,16,128]{2,1,0:T(8,128)S(1)}, u32[]{:S(2)}, u32[]{:S(2)}) async-start(f32[16,16,128]{2,1,0:T(8,128)} %bitcast.32), calls=%async_computation.2 | async-start | bytes 262144 | tf_op jit(solution)/shard_map/all_to_all | solution.py:905
  80.8 5.8 %collective-permute-start.4 = (bf16[3,5120]{1,0:T(4,128)(2,1)S(1)}, bf16[3,5120]{1,0:T(4,128)(2,1)S(1)}, u32[]{:S(2)}, u32[]{:S(2)}) collective-permute-start(bf16[3,5120]{1,0:T(4,128)(2,1)S(1)} %get-tuple-element.152), channel_id=1, source_target_pairs={{1,0},{2,1},{3,2},{4,3},{5,4},{6,5},{7,6},{8,7},{9,8},{10,9},{11,1... | collective-permute-start | bytes 92168 | tf_op jit(solution)/shard_map/ppermute | solution.py:960
  88.0 17.3 %all-to-all-start.3 = ((f32[16,16,128]{2,1,0:T(8,128)}), f32[16,16,128]{2,1,0:T(8,128)S(1)}, u32[]{:S(2)}, u32[]{:S(2)}) async-start(f32[16,16,128]{2,1,0:T(8,128)} %bitcast.10), calls=%async_computation.3 | async-start | bytes 262144 | tf_op jit(solution)/shard_map/all_to_all | solution.py:905

commit v6 on v5

--- a/solution.py
+++ b/solution.py
@@ -29,8 +29,7 @@
 EXACT = lax.Precision.HIGHEST
 NN = (((1,), (0,)), ((), ()))
 NT = (((1,), (1,)), ((), ()))
-SUM_ROWS = 256
-SUM_GROUP = SUM_ROWS // GROUPS
+SUM_GROUP = 64
 PACK_ROWS = 2 * STATE + 16
 
 
@@ -405,6 +404,7 @@
     ("V", (SMALL_ROWS, LANES), F32),
     ("V", (HEADS, T), F32),
     ("V", (PAIRS, LANES), F32),
+    ("V", (TAPS, CHANNELS), F32),
 ]
 FETCHES = 6 + 8
 
@@ -435,7 +435,8 @@
     far, rest = rest[: len(NEAR)], rest[len(NEAR) :]
     common_far, rest = rest[: len(COMMON)], rest[len(COMMON) :]
     mine_ref, send_ref, *rest = rest
-    near, rest = rest[: len(NEAR)], rest[len(NEAR) :]
+    near = [rest[i * len(NEAR) : (i + 1) * len(NEAR)] for i in range(HALF_GROUPS)]
+    rest = rest[HALF_GROUPS * len(NEAR) :]
     common, rest = rest[: len(COMMON)], rest[len(COMMON) :]
     own_ref, got_ref, tots_ref, sems, fetch_sems = rest
     first = start_all([(tots_h, tots_ref)], sems.at[STEPS])
@@ -445,8 +446,9 @@
         steps.append(
             start_all([(own_h.at[:, at], own_ref.at[:, at]), (got_h.at[:, at], got_ref.at[:, at])], sems.at[step])
         )
-    fetches = start_all(list(zip(common_far, common)), fetch_sems.at[1])
-    fetches += fetch_group(core_ref[0] * HALF_GROUPS, far, near, fetch_sems.at[0])
+    fetches = start_all(list(zip(common_far, common)), fetch_sems.at[HALF_GROUPS])
+    for jj in range(HALF_GROUPS):
+        fetches += fetch_group(core_ref[0] * HALF_GROUPS + jj, far, near[jj], fetch_sems.at[jj])
     wait_all(first)
     second = core_ref[0] == 1
     for i in range(HALF_PAIRS):
@@ -472,19 +474,20 @@
 
 def run_unpack(core, back, own, got, tots, far, common):
     half = (2, HALF_PAIRS, STATE, LANES)
-    out = [("V", half, BF16)] * 2 + NEAR + COMMON
+    out = [("V", half, BF16)] * 2 + NEAR * HALF_GROUPS + COMMON
     scratch = [
         pltpu.VMEM(half, BF16),
         pltpu.VMEM(half, BF16),
         pltpu.VMEM((2 * PAIRS, LANES), F32),
         DMA(STEPS + 1, 2),
-        DMA(2, FETCHES),
+        DMA(HALF_GROUPS + 1, FETCHES),
     ]
     specs = "svhhh" + "h" * (len(NEAR) + len(COMMON))
     outs = call(unpack_kernel, "unpack", out, specs, 3, scratch, mib=16)(
         core, back, own, got, tots, *far, *common
     )
-    return outs[0], outs[1], outs[2 : 2 + len(NEAR)], outs[2 + len(NEAR) :]
+    at = 2 + HALF_GROUPS * len(NEAR)
+    return outs[0], outs[1], outs[2:at], outs[at:]
 
 
 def by_lane_half(v):
@@ -655,31 +658,27 @@
         del rest[:count]
         return taken
 
-    sets = [take(len(NEAR))]
+    sets = [take(len(NEAR)) for _ in range(HALF_GROUPS)]
+    before_ref, small_ref, raw_ref, skips_ref, _ = take(len(COMMON))
+    half = 1 - core_ref[0] if theirs else core_ref[0]
+    fetches = []
     if theirs:
-        sets.append(take(len(NEAR)))
-    before_ref, small_ref, raw_ref, skips_ref = take(len(COMMON))
-    far = take(4 if theirs else len(NEAR))
-    out_h, pre_h, step_h, sum_h = take(4)
-    half = 1 - core_ref[0] if theirs else core_ref[0]
-    arrivals, fetches = [], []
-    if theirs:
-        first_ref, = take(1)
-        head_ref, = take(1)
+        pre_own_ref, _, _ = take(3)
+        out_h, step_h, pre_ref, sum_ref, first_ref = take(5)
+        head_ref, out_ref, step_ref, win_ref, sems = rest
+        own = core_ref[0]
+        head_ref[:, span(own, HALF_X)] = pre_own_ref[0:8, 0:HALF_X]
+        size = HALF_GROUPS * STATE
+        for base in range(2):
+            at = HALF_X + base * size
+            head_ref[:, span(WIDTH_X // size + 2 * base + own, size)] = pre_own_ref[0:8, at : at + size]
     else:
+        far = take(len(NEAR))
+        out_h, step_h, pre_ref, sum_ref = take(4)
         after = [take(len(NEAR)) for _ in range(HALF_GROUPS)]
-        sets.append(take(len(NEAR)))
-    out_ref, pre_ref, step_ref, sum_ref, win_ref, sems = rest
-    if theirs:
-        own = core_ref[0]
-        pieces = [span(own, HALF_X)] + [
-            span(WIDTH_X // (HALF_GROUPS * STATE) + 2 * base + own, HALF_GROUPS * STATE) for base in range(2)
-        ]
-        fetches = start_all([(pre_h.at[pl.ds(0, 8), at], head_ref.at[:, at]) for at in pieces], sems.at[2])
-    else:
-        arrivals = fetch_group(half * HALF_GROUPS + 1, far, sets[1], sems.at[2])
+        out_ref, step_ref, win_ref, sems = rest
         for jj in range(HALF_GROUPS):
-            fetches += fetch_group((1 - half) * HALF_GROUPS + jj, far, after[jj], sems.at[3 + jj])
+            fetches += fetch_group((1 - half) * HALF_GROUPS + jj, far, after[jj], sems.at[2 + jj])
     last = iota((8, 2 * LANES), 0) == 7
     lower = (iota((T, T), 0) >= iota((T, T), 1)).astype(F32)
 
@@ -703,8 +702,6 @@
     for jj in range(HALF_GROUPS):
         j = half * HALF_GROUPS + jj
         x_ref, g_ref, y_ref, gx_ref, slope_ref, tok_ref, bc_ref, gbc_ref = sets[jj]
-        if jj:
-            wait_all(arrivals)
         b = bc_ref[:, 0:STATE]
         c = bc_ref[:, STATE:]
         grad_b = gbc_ref[:, 0:STATE]
@@ -760,7 +757,6 @@
                 near_at = pl.ds(jj * GROUP_X + (q // 4) * size, size)
                 far_at = span(2 * j + q // 4, size)
                 save(out_ref.at[:, near_at], out_h.at[:, far_at])
-                save(pre_ref.at[:, near_at], pre_h.at[:, far_at])
         for grad, base in ((grad_b, 0), (grad_c, 1)):
             at = HALF_X + (base * HALF_GROUPS + jj) * STATE
             tail = slice(GROUP_X + base * STATE, GROUP_X + (base + 1) * STATE)
@@ -771,7 +767,6 @@
             if theirs:
                 head_ref[:, far_at] = grad_pre[0:8]
             terms += tap_sums(grad_pre, 0)
-            save(pre_ref.at[:, pl.ds(at, STATE)], pre_h.at[:, far_at])
         heads = span(j, GROUP_HEADS)
         behind = exact_dot(seg_grad, lower)
         dt = small_ref[pl.ds(pl.multiple_of(ROW_DT + j * GROUP_HEADS, GROUP_HEADS), GROUP_HEADS), :]
@@ -781,7 +776,6 @@
         save(step_ref.at[near], step_h.at[heads])
         rows = jj * SUM_GROUP
         sum_ref[rows : rows + SUM_GROUP, :] = jnp.concatenate(terms + skips + [dt * behind * decay], axis=0)
-        save(sum_ref.at[pl.ds(rows, SUM_GROUP)], sum_h.at[span(j, SUM_GROUP)])
     wait_all(fetches)
     if theirs:
         first_ref[...] = head_ref[0 : TAPS - 1, :].astype(BF16)
@@ -792,109 +786,159 @@
     theirs = before_out is not None
     out = [
         ("h", (T, WIDTH_X), BF16),
-        ("h", (T, CHANNELS), F32),
         ("h", (HEADS, T), F32),
-        ("h", (SUM_ROWS, LANES), F32),
+        ("V", (T, HALF_X + HALF_B), F32),
+        ("V", (HALF_GROUPS * SUM_GROUP, LANES), F32),
     ]
     scratch = [
         pltpu.VMEM((T, HALF_X), BF16),
-        pltpu.VMEM((T, HALF_X + HALF_B), F32),
         pltpu.VMEM((HALF_GROUPS * GROUP_HEADS, T), F32),
-        pltpu.VMEM((HALF_GROUPS * SUM_GROUP, LANES), F32),
         pltpu.VMEM((8 + T, GROUP_X), F32),
-        DMA(3 + HALF_GROUPS, FETCHES + 2),
+        DMA(2 + HALF_GROUPS, FETCHES),
     ]
     args = [core, state, *near, *common, *far]
     specs = "s" + ("v" if theirs else "V") + "V" * (len(near) + len(COMMON)) + "h" * len(far)
     aliases = {}
     if theirs:
-        aliases = {len(args) + i: i for i in range(len(out))}
-        args += before_out
-        specs += "h" * len(out)
-        more = [("V", (TAPS - 1, CHANNELS), BF16)]
+        done, pre_own = before_out
+        args += [pre_own]
+        aliases = {len(args) + i: i for i in range(2)}
+        args += done
+        specs += "Vhh"
+        out += [("V", (TAPS - 1, CHANNELS), BF16)]
         scratch = [pltpu.VMEM((8, CHANNELS), F32)] + scratch
     else:
-        more = NEAR * HALF_GROUPS
-        scratch = [pltpu.VMEM(shape, dtype) for _, shape, dtype in NEAR] + scratch
+        out += NEAR * HALF_GROUPS
     kernel = functools.partial(leave_kernel, theirs)
-    outs = call(kernel, "leave", out + more, specs, 5, scratch, mib=16, aliases=aliases)(*args)
-    return outs[:4], outs[4:]
-
-
-def spread_kernel(pre_h, halo_ref, weight_h, out_h, pre_ref, weight_ref, out_ref, win_ref, sems):
-    first = start_all([(weight_h, weight_ref)], sems.at[0])
-
-    def load(i):
-        at = span(i, GROUP_X)
-        return pltpu.make_async_copy(pre_h.at[:, at], pre_ref.at[:, at], sems.at[1, i])
-
-    def store(i):
-        at = span(i, GROUP_X)
-        return pltpu.make_async_copy(out_ref.at[:, at], out_h.at[:, at], sems.at[2, i])
-
-    for i in range(BLOCKS):
-        load(i).start()
-    wait_all(first)
-
-    @pl.loop(0, BLOCKS)
-    def _(i):
-        load(i).wait()
-        cols = span(i, GROUP_X)
-        win_ref[0:T, :] = pre_ref[:, cols]
-        win_ref[T : T + TAPS - 1, :] = halo_ref[:, cols].astype(F32)
-        weights = weight_ref[:, cols]
-        for lo in range(0, GROUP_X, LANES):
-            at = slice(lo, lo + LANES)
-            acc = weights[0:1, at] * win_ref[3 : 3 + T, at]
-            for k in range(1, TAPS):
-                acc = acc + weights[k : k + 1, at] * win_ref[3 - k : 3 - k + T, at]
-            out_ref[:, pl.ds(pl.multiple_of(i * GROUP_X + lo, LANES), LANES)] = acc.astype(BF16)
-        store(i).start()
-
-    for i in range(BLOCKS):
-        store(i).wait()
-
-
-def run_spread(pre, halo, weight):
+    outs = call(kernel, "leave", out, specs, 5, scratch, mib=16, aliases=aliases)(*args)
+    return outs[:2], outs[2], outs[3], outs[4:]
+
+
+def spread_kernel(core_ref, own_ref, theirs_ref, halo_ref, weight_ref, out_h, out_ref, win_ref, sems):
+    saves = []
+    size = HALF_GROUPS * STATE
+    for side, pre_ref in enumerate((own_ref, theirs_ref)):
+        half = 1 - core_ref[0] if side else core_ref[0]
+        blocks = [(jj * GROUP_X, span(half * HALF_GROUPS + jj, GROUP_X), GROUP_X) for jj in range(HALF_GROUPS)]
+        blocks += [
+            (HALF_X + base * size, span(WIDTH_X // size + 2 * base + half, size), size) for base in range(2)
+        ]
+        for near, far, width in blocks:
+            win_ref[0:T, 0:width] = pre_ref[:, near : near + width]
+            win_ref[T : T + TAPS - 1, 0:width] = halo_ref[:, far].astype(F32)
+            weights = weight_ref[:, far]
+            base = side * (HALF_X + HALF_B) + near
+            for lo in range(0, width, LANES):
+                at = slice(lo, lo + LANES)
+                acc = weights[0:1, at] * win_ref[3 : 3 + T, at]
+                for k in range(1, TAPS):
+                    acc = acc + weights[k : k + 1, at] * win_ref[3 - k : 3 - k + T, at]
+                out_ref[:, base + lo : base + lo + LANES] = acc.astype(BF16)
+            copy = pltpu.make_async_copy(out_ref.at[:, pl.ds(base, width)], out_h.at[:, far], sems.at[len(saves)])
+            copy.start()
+            saves.append(copy)
+    wait_all(saves)
+
+
+def run_spread(core, own, theirs, halo, weight):
     out = [("h", (T, CHANNELS), BF16)]
-    scratch = [
-        pltpu.VMEM((T, CHANNELS), F32),
-        pltpu.VMEM((TAPS, CHANNELS), F32),
-        pltpu.VMEM((T, CHANNELS), BF16),
-        pltpu.VMEM((T + 8, GROUP_X), F32),
-        DMA(3, BLOCKS),
-    ]
-    return call(spread_kernel, "spread", out, "hvh", 4, scratch, mib=16)(pre, halo, weight)[0]
-
-
-def finish_kernel(sum_ref, conv_ref, decay_ref, skip_ref):
+    scratch = [pltpu.VMEM((T, CHANNELS), BF16), pltpu.VMEM((T + 8, GROUP_X), F32), DMA(8)]
+    return call(spread_kernel, "spread", out, "sVVvV", 3, scratch, mib=16)(core, own, theirs, halo, weight)[0]
+
+
+CONV_ROWS = TAPS * (CHANNELS // LANES)
+CONV_GROUP = CONV_ROWS // GROUPS
+SEND_ROWS = CONV_ROWS + 16
+
+
+def write_send(out_ref, conv, thin):
+    high = thin.astype(BF16).astype(F32)
+    low = thin - high
+    row = iota((16, LANES), 0)
+    out_ref[0:CONV_ROWS, :] = conv.astype(BF16)
+    out_ref[CONV_ROWS:SEND_ROWS, :] = jnp.where(row == 0, high, jnp.where(row == 1, low, 0.0)).astype(BF16)
+
+
+def read_send(value):
+    wide = value.astype(F32)
+    return wide[0:CONV_ROWS], wide[CONV_ROWS : CONV_ROWS + 1] + wide[CONV_ROWS + 1 : CONV_ROWS + 2]
+
+
+def merge_kernel(core_ref, own_ref, own_got_ref, theirs_ref, theirs_got_ref, out_ref):
+    thin = jnp.zeros((8, LANES), F32)
+    left = iota((8, LANES), 1) < HEAD_DIM
+    count = HEADS // 2
+    parts = []
+    for side, (mine, other) in enumerate(((own_ref, theirs_got_ref), (theirs_ref, own_got_ref))):
+        half = 1 - core_ref[0] if side else core_ref[0]
+        total = mine[...] + other[...]
+        rows, skips, decays = [], [], []
+        for jj in range(HALF_GROUPS):
+            at = jj * SUM_GROUP
+            rows.append(total[at : at + CONV_GROUP])
+            skips.append(total[at + CONV_GROUP : at + SUM_GROUP - GROUP_HEADS])
+            decays.append(total[at + SUM_GROUP - GROUP_HEADS : at + SUM_GROUP])
+        skips = jnp.concatenate(skips, axis=0)
+        even = exact_dot(jnp.where(left, 1.0, 0.0), skips, NT)
+        odd = exact_dot(jnp.where(left, 0.0, 1.0), skips, NT)
+        decay = exact_dot(jnp.ones((8, LANES), F32), jnp.concatenate(decays, axis=0), NT)
+        for part, step, shift in ((even, 2, 0), (odd, 2, 1), (decay, 1, HEADS)):
+            size = part.shape[1]
+            spot = (iota((size, LANES), 1) == step * iota((size, LANES), 0) + shift + half * count).astype(F32)
+            thin = thin + exact_dot(part, spot)
+        parts.append(jnp.concatenate(rows, axis=0))
+    first = core_ref[0] == 0
+    conv = jnp.concatenate(
+        [jnp.where(first, parts[0], parts[1]), jnp.where(first, parts[1], parts[0])], axis=0
+    )
+    write_send(out_ref, conv, thin[0:1])
+
+
+def run_merge(core, own, own_got, theirs, theirs_got):
+    out = [("v", (SEND_ROWS, LANES), BF16)]
+    return call(merge_kernel, "merge", out, "svvvv", 1, mib=16)(core, own, own_got, theirs, theirs_got)[0]
+
+
+def ring_sum(me_ref, refs, hold_ref):
+    count = len(refs)
+    for d in range(count):
+        hold_ref[d] = refs[d][...]
+    conv, thin = read_send(hold_ref[lax.rem(me_ref[0], count)])
+    for k in range(1, count):
+        more, little = read_send(hold_ref[lax.rem(me_ref[0] + count - k, count)])
+        conv, thin = conv + more, thin + little
+    return conv, thin
+
+
+def fold_kernel(me_ref, *rest):
+    *refs, out_ref, hold_ref = rest
+    write_send(out_ref, *ring_sum(me_ref, refs, hold_ref))
+
+
+def run_fold(me, values):
+    out = [("v", (SEND_ROWS, LANES), BF16)]
+    scratch = [pltpu.VMEM((len(values), SEND_ROWS, LANES), BF16)]
+    return call(fold_kernel, "fold", out, "s" + "v" * len(values), 1, scratch, mib=16)(me, *values)[0]
+
+
+def finish_kernel(me_ref, *rest):
+    *refs, conv_ref, decay_ref, skip_ref, hold_ref = rest
+    conv, thin = ring_sum(me_ref, refs, hold_ref)
     for i in range(CHANNELS // LANES):
         if i < PAIRS:
-            row = SUM_GROUP * (i // GROUP_PAIRS) + TAPS * (i % GROUP_PAIRS)
+            row = CONV_GROUP * (i // GROUP_PAIRS) + TAPS * (i % GROUP_PAIRS)
         else:
             kind, group = divmod(i - PAIRS, GROUPS)
-            row = SUM_GROUP * group + TAPS * (GROUP_PAIRS + kind)
-        conv_ref[:, i * LANES : (i + 1) * LANES] = sum_ref[row : row + TAPS, :]
-    skip_at, decay_at = TAPS * (GROUP_PAIRS + 2), SUM_GROUP - GROUP_HEADS
-    skips = jnp.concatenate(
-        [sum_ref[SUM_GROUP * j + skip_at : SUM_GROUP * j + decay_at, :] for j in range(GROUPS)], axis=0
-    )
-    decays = jnp.concatenate(
-        [sum_ref[SUM_GROUP * j + decay_at : SUM_GROUP * (j + 1), :] for j in range(GROUPS)], axis=0
-    )
-    ones = jnp.ones((8, LANES), F32)
-    decay_ref[...] = exact_dot(ones, decays, NT)[0:1]
-    left = iota((8, LANES), 1) < HEAD_DIM
-    even = exact_dot(jnp.where(left, 1.0, 0.0), skips, NT)
-    odd = exact_dot(jnp.where(left, 0.0, 1.0), skips, NT)
-    at_even = (iota((PAIRS, HEADS), 1) == 2 * iota((PAIRS, HEADS), 0)).astype(F32)
-    at_odd = (iota((PAIRS, HEADS), 1) == 2 * iota((PAIRS, HEADS), 0) + 1).astype(F32)
-    skip_ref[...] = (exact_dot(even, at_even) + exact_dot(odd, at_odd))[0:1]
-
-
-def run_finish(sums):
+            row = CONV_GROUP * group + TAPS * (GROUP_PAIRS + kind)
+        conv_ref[:, i * LANES : (i + 1) * LANES] = conv[row : row + TAPS]
+    skip_ref[...] = thin[:, 0:HEADS]
+    decay_ref[...] = thin[:, HEADS:]
+
+
+def run_finish(me, values):
     out = [("v", (TAPS, CHANNELS), F32), ("v", (1, HEADS), F32), ("v", (1, HEADS), F32)]
-    return call(finish_kernel, "finish", out, "v", 1, mib=16)(sums)
+    scratch = [pltpu.VMEM((len(values), SEND_ROWS, LANES), BF16)]
+    return call(finish_kernel, "finish", out, "s" + "v" * len(values), 1, scratch, mib=16)(me, *values)
 
 
 CTX = ("chip", "core")
@@ -909,24 +953,23 @@
     return lax.optimization_barrier(values)
 
 
-def fold_kernel(parts, copies, in_ref, out_ref):
-    share = in_ref.shape[0] // parts
-    total = in_ref[0:share, :]
-    for i in range(1, parts):
-        total = total + in_ref[i * share : (i + 1) * share, :]
-    for i in range(copies):
-        out_ref[i * share : (i + 1) * share, :] = total
-
-
-def run_fold(value, parts, copies):
-    out = [("v", (value.shape[0] // parts * copies, LANES), F32)]
-    return call(functools.partial(fold_kernel, parts, copies), "fold", out, "v", 1, mib=16)(value)[0]
+SIDE = 4
+
+
+def around(value, axis, count, ring, move):
+    return [value] + [
+        lax.ppermute(value, axis, [(i, move(i, d)) for i in range(count)]) for d in range(1, ring)
+    ]
+
+
+def scalar(value):
+    return value.astype(jnp.int32).reshape(1)
 
 
 def local(conv_input, conv_weight, step_raw, decay_log, skip_gain, cotangent):
     chips = lax.axis_size("chip")
     devices = 2 * chips
-    across = 2 * lax.axis_size("dp")
+    sequences = lax.axis_size("dp")
     tokens = conv_input[0]
     raw = step_raw[0]
     cot = cotangent[0]
@@ -952,18 +995,27 @@
     gx, slope = run_slopes(late, cot, small, tokens, before, conv_weight)
     back, gx, slope = tie(back, gx, slope)
     far = (x, cot, y, gx, slope, tokens, bc, gbc)
-    mine, send, near, common = run_unpack(core, back, own, got, tots, far, (before, small, raw, skips))
+    mine, send, near, common = run_unpack(
+        core, back, own, got, tots, far, (before, small, raw, skips, conv_weight)
+    )
     theirs = lax.ppermute(send, "core", swap)
-    half, near = run_leave(core, mine, near, common, far, None)
-    (out_tokens, pre, grad_step, sums), (first,) = run_leave(core, theirs, near, common, (), half)
-    parts = all_to_all(sums, "chip")
+    half, pre_own, sum_own, near = run_leave(core, mine, near, common, far, None)
+    sum_own_got = lax.ppermute(sum_own, "core", swap)
+    (out_tokens, grad_step), pre_theirs, sum_theirs, (first,) = run_leave(
+        core, theirs, near, common, (), (half, pre_own)
+    )
+    sum_theirs_got = lax.ppermute(sum_theirs, "core", swap)
     after = lax.ppermute(first, CTX, [(i + 1, i) for i in range(devices - 1)])
-    parts, after = tie(parts, after)
-    parts = all_to_all(run_fold(parts, chips, across), ("dp", "core"))
-    grad_tokens = run_spread(pre, after, conv_weight)
-    parts, grad_tokens = tie(parts, grad_tokens)
-    sums = all_to_all(run_fold(parts, across, chips), "chip")
-    grad_conv, grad_decay, grad_skip = run_finish(sums)
+    sums = run_merge(core, sum_own, sum_own_got, sum_theirs, sum_theirs_got)
+    chip = lax.axis_index("chip")
+    values = around(sums, "chip", chips, SIDE, lambda i, d: i // SIDE * SIDE + (i % SIDE + d) % SIDE)
+    grad_tokens = run_spread(core, pre_own, pre_theirs, after, common[4])
+    values, grad_tokens = tie(values, grad_tokens)
+    sums = run_fold(scalar(lax.rem(chip, SIDE)), values)
+    values = around(sums, "chip", chips, chips // SIDE, lambda i, d: (i + d * SIDE) % chips)
+    sums = run_fold(scalar(lax.div(chip, SIDE)), values)
+    values = around(sums, "dp", sequences, sequences, lambda i, d: (i + d) % sequences)
+    grad_conv, grad_decay, grad_skip = run_finish(scalar(lax.axis_index("dp")), values)
     return (
         out_tokens[None],
         grad_tokens[None],

time: 122 us -> 118 us (0.967); the launches traced: 120 us -> 118 us
  blocking collectives: 14 us -> 0 us
  starting transfers between devices: 34.7 us -> 47.2 us
  Pallas kernels: 44.8 us -> 42.3 us
    ppermute x0 -> x15, starting transfers between devices: none -> 26.6 us  [the longest x13 26 us: around(): lax.ppermute(value, axis, [(i, move(i, d)) for i in range(count)])]
    all_to_all x4 -> x2, starting transfers between devices: 27.4 us -> 13.4 us  [all_to_all(): return lax.all_to_all(value, axis, 0, 0, tiled=True)]
    all_to_all x1 -> x0, blocking collectives: 14 us -> none  [all_to_all(): return lax.all_to_all(value, axis, 0, 0, tiled=True)]
    ppermute x0 -> x15, waiting for transfers between devices: none -> 7.06 us  [the longest x13 7.06 us: around(): lax.ppermute(value, axis, [(i, move(i, d)) for i in range(count)])]
    all_to_all x4 -> x2, waiting for transfers between devices: 21.8 us -> 16.5 us  [all_to_all(): return lax.all_to_all(value, axis, 0, 0, tiled=True)]
    pallas_call x14 -> x15, Pallas kernels: 44.8 us -> 42.3 us  [go(): run(*[pin(a, spaces[p]) if p in spaces else a for a, p in zip(args, specs...]
    ppermute x1, waiting for transfers between devices: 1.65 us -> 0.01 us  [local(): after = lax.ppermute(first, CTX, [(i + 1, i) for i in range(devices - 1)])]
  transfers between devices with their start and end apart: 9 -> 22, of which waited for: 7 -> 10; matrix products, arithmetic and copies ran while one was open for 0% -> 0% of each run, Pallas kernels for 25% -> 27%
where the time goes in v6:
time: 118 us
  starting transfers between devices  47.2 us (40%)
  Pallas kernels  42.3 us (36%)
  waiting for transfers between devices  25.2 us (21%)
  local copies, waits for them, and re-layouts  1.97 us (2%)
    pallas_call x15, Pallas kernels, go(): run(*[pin(a, spaces[p]) if p in spaces else a for a, p in zip(args, specs...  42.3 us
    ppermute x13, starting transfers between devices, around(): lax.ppermute(value, axis, [(i, move(i, d)) for i in range(count)])  26 us
    all_to_all x2, waiting for transfers between devices, all_to_all(): return lax.all_to_all(value, axis, 0, 0, tiled=True)  16.5 us
    all_to_all x2, starting transfers between devices, all_to_all(): return lax.all_to_all(value, axis, 0, 0, tiled=True)  13.4 us
    ppermute x13, waiting for transfers between devices, around(): lax.ppermute(value, axis, [(i, move(i, d)) for i in range(count)])  7.06 us
    ppermute x1, starting transfers between devices, local(): after = lax.ppermute(first, CTX, [(i + 1, i) for i in range(devices - 1)])  4.21 us
  transfers between devices with their start and end apart: 22, of which 10 were waited for; matrix products, arithmetic and copies ran while one was open for 0% of the time, Pallas kernels for 27%

profile of v6, /device:TPU:2, one launch (start us, length us, event | category | flops | bytes accessed | tf_op | source)
XLA Modules:
  0.0 117.5 jit_solution(15132058960945916439)
XLA Ops:
  0.6 0.9 slice_bitcast_fusion
  1.5 1.9 %collective-permute-start = (bf16[3,5120]{1,0:T(4,128)(2,1)S(1)}, bf16[3,5120]{1,0:T(4,128)(2,1)S(1)}, u32[]{:S(2)}, u32[]{:S(2)}) collective-permute-start(bf16[3,5120]{1,0:T(4,128)(2,1)S(1)} %slice_bitcast_fusion), channel_id=1, source_target_pairs={{0,1},{1,2},{2,3},{3,4},{4,5},{5,6},{6,7},{7,8},{8,9},{9,10},{10,1... | collective-permute-start | bytes 92168 | tf_op jit(solution)/shard_map/ppermute | solution.py:978
  3.5 4.5 %begin.1 = (f32[512,128]{1,0:T(8,128)}, f32[512,128]{1,0:T(8,128)S(1)}, f32[32,128]{1,0:T(8,128)S(1)}, bf16[128,4096]{1,0:T(8,128)(2,1)S(1)}, bf16[128,1024]{1,0...) custom-call(f32[64,128]{1,0:T(8,128)} %bitcast.25, ...), custom_call_target="tpu_custom_call" | custom-call | flops 4000000000 | bytes 14400000 | tf_op jit(solution)/shard_map/begin/pallas_call | solution.py:97
  7.9 1.0 collective-permute-done.halo_ref
  9.0 2.4 %enter.1 = (bf16[128,4096]{1,0:T(8,128)(2,1)}, bf16[128,1024]{1,0:T(8,128)(2,1)}, f32[8,5120]{1,0:T(8,128)}, bf16[128,4096]{1,0:T(8,128)(2,1)S(1)}, bf16[128,102...) custom-call(s32[1]{0:T(128)} %bitcast.core_ref, bf16[128,4096]{1,0:T(8,128)(2,1)S(1)} %get-tuple-element.94.x0_ref, ...), custom_call_target="tpu_custom_call" | custom-call | flops 3000000000 | bytes 10800000 | tf_op jit(solution)/shard_map/enter/pallas_call | solution.py:97
  11.4 0.7 collective-permute-start.1
  12.1 0.1 collective-permute-start.2
  12.2 1.6 %own.1.own_ref = bf16[2,16,128,128]{3,2,1,0:T(8,128)(2,1)S(1)} custom-call(s32[1]{0:T(128)} %bitcast.core_ref, bf16[128,4096]{1,0:T(8,128)(2,1)S(1)} %get-tuple-element.101.x_ref, bf16[128,1024]{1,0:T(8,128)(2,1)S(1)} %get-tuple-element.102.bc_ref, bf16[128,4096]{1,0:T(8,128)(2,1)S(1)} %get-tuple-element.98.g_ref, f32[512,128]{1,0:T(8,128)S(1)} %get-tuple-element.99.small_ref), custom_call_target="tpu_custom_call" | custom-call | flops 3000000000 | bytes 10800000 | tf_op jit(solution)/shard_map/own/pallas_call | solution.py:97
  13.9 0.6 collective-permute-done.2.other_ref
  14.4 1.8 %pack.1 = (bf16[16,272,128]{2,1,0:T(8,128)(2,1)}, bf16[2,16,128,128]{3,2,1,0:T(8,128)(2,1)}, bf16[2,16,128,128]{3,2,1,0:T(8,128)(2,1)}, f32[64,128]{1,0:T(8,128)}) custom-call(s32[1]{0:T(128)} %bitcast.core_ref, bf16[2,16,128,128]{3,2,1,0:T(8,128)(2,1)S(1)} %own.1.own_ref, bf16[2,16,128,128]{3,2,1,0:T(8,128)(2,1)S(1)} %collective-permute-done.1.got_ref, ...), custom_call_target="tpu_custom_call" | custom-call | flops 2000000000 | bytes 7200000 | tf_op jit(solution)/shard_map/pack/pallas_call | solution.py:97
  16.2 7.2 %all-to-all-start = ((bf16[16,272,128]{2,1,0:T(8,128)(2,1)}), bf16[16,272,128]{2,1,0:T(8,128)(2,1)S(1)}, u32[]{:S(2)}, u32[]{:S(2)}) async-start(bf16[16,272,128]{2,1,0:T(8,128)(2,1)} %get-tuple-element.105), calls=%async_computation | async-start | bytes 2228224 | tf_op jit(solution)/shard_map/all_to_all | solution.py:949
  23.4 5.6 %inner.1 = (f32[128,4096]{1,0:T(8,128)}, f32[128,1024]{1,0:T(8,128)}, f32[32,128]{1,0:T(8,128)}) custom-call(bf16[128,4096]{1,0:T(8,128)(2,1)} %get-tuple-element.106.x_h.rest_0_.rest_21_, bf16[128,1024]{1,0:T(8,128)(2,1)} %get-tuple-element.113.bc_h.rest_6_.rest_27_, bf16[128,4096]{1,0:T(8,128)(2,1)} %bitcast.21, f32[512,128]{1,0:T(8,128)} %get-tuple-element.107.small_h.rest_9_), custom_call_target="tpu_custom_call" | custom-call | flops 4000000000 | bytes 14400000 | tf_op jit(solution)/shard_map/inner/pallas_call | solution.py:97
  29.0 10.9 %all-to-all-done.in_ref = bf16[16,272,128]{2,1,0:T(8,128)(2,1)S(1)} async-done(((bf16[16,272,128]{2,1,0:T(8,128)(2,1)}), bf16[16,272,128]{2,1,0:T(8,128)(2,1)S(1)}, u32[]{:S(2)}, u32[]{:S(2)}) %all-to-all-start) | async-done | bytes 1114144 | tf_op jit(solution)/shard_map/all_to_all | solution.py:949
  39.9 1.3 %chain.1 = bf16[16,256,128]{2,1,0:T(8,128)(2,1)} custom-call(bf16[16,272,128]{2,1,0:T(8,128)(2,1)S(1)} %all-to-all-done.in_ref), custom_call_target="tpu_custom_call" | custom-call | flops 1000000000 | bytes 3600000 | tf_op jit(solution)/shard_map/chain/pallas_call | solution.py:97
  41.2 6.2 %all-to-all-start.1 = ((bf16[16,256,128]{2,1,0:T(8,128)(2,1)}), bf16[16,256,128]{2,1,0:T(8,128)(2,1)S(1)}, u32[]{:S(2)}, u32[]{:S(2)}) async-start(bf16[16,256,128]{2,1,0:T(8,128)(2,1)} %chain.1), calls=%async_computation.1 | async-start | bytes 2097152 | tf_op jit(solution)/shard_map/all_to_all | solution.py:949
  47.3 8.7 %slopes.1 = (f32[128,4096]{1,0:T(8,128)}, f32[128,5120]{1,0:T(8,128)}) custom-call(bf16[128,1024]{1,0:T(8,128)(2,1)} %get-tuple-element.113.bc_h.rest_6_.rest_27_, bf16[128,4096]{1,0:T(8,128)(2,1)} %bitcast.22, f32[512,128]{1,0:T(8,128)} %get-tuple-element.107.small_h.rest_9_, bf16[128,5120]{1,0:T(8,128)(2,1)} %bitcast.17, ...), custom_call_target="tpu_custom_call" | custom-call | flops 6000000000 | bytes 21600000 | tf_op jit(solution)/shard_map/slopes/pallas_call | solution.py:97
  56.1 5.6 %all-to-all-done.1.back_ref = bf16[16,256,128]{2,1,0:T(8,128)(2,1)S(1)} async-done(((bf16[16,256,128]{2,1,0:T(8,128)(2,1)}), bf16[16,256,128]{2,1,0:T(8,128)(2,1)S(1)}, u32[]{:S(2)}, u32[]{:S(2)}) %all-to-all-start.1) | async-done | bytes 1048608 | tf_op jit(solution)/shard_map/all_to_all | solution.py:949
  61.7 4.1 %unpack.1 = (bf16[2,16,128,128]{3,2,1,0:T(8,128)(2,1)S(1)}, bf16[2,16,128,128]{3,2,1,0:T(8,128)(2,1)S(1)}, bf16[128,1024]{1,0:T(8,128)(2,1)S(1)}, bf16[128,1024]...) custom-call(s32[1]{0:T(128)} %bitcast.core_ref, ...), custom_call_target="tpu_custom_call" | custom-call | flops 3000000000 | bytes 10800000 | tf_op jit(solution)/shard_map/unpack/pallas_call | solution.py:97
  65.7 0.3 collective-permute-start.3
  66.0 4.2 %leave.2 = (bf16[128,4096]{1,0:T(8,128)(2,1)}, f32[64,128]{1,0:T(8,128)}, f32[128,2560]{1,0:T(8,128)S(1)}, f32[128,128]{1,0:T(8,128)S(1)}, bf16[128,1024]{1,0:T(...) custom-call(s32[1]{0:T(128)} %bitcast.core_ref, ...), custom_call_target="tpu_custom_call" | custom-call | flops 5000000000 | bytes 18000000 | tf_op jit(solution)/shard_map/leave/pallas_call | solution.py:97
  70.2 0.6 collective-permute-start.4
  70.8 0.0 collective-permute-done.3.state_ref
  70.8 4.2 %leave.3 = (bf16[128,4096]{1,0:T(8,128)(2,1)}, f32[64,128]{1,0:T(8,128)}, f32[128,2560]{1,0:T(8,128)S(1)}, f32[128,128]{1,0:T(8,128)S(1)}, bf16[3,5120]{1,0:T(4,128)(2,1)S(1)}) custom-call(s32[1]{0:T(128)} %bitcast.core_ref, bf16[2,16,128,128]{3,2,1,0:T(8,128)(2,1)S(1)} %collective-permute-done.3.state_ref, ...), custom_call_target="tpu_custom_call", output_to_operand_aliasing={{0}: (24, {}), {1}: (25, {})} | custom-call | flops 5000000000 | bytes 18000000 | tf_op jit(solution)/shard_map/leave/pallas_call | solution.py:97
  75.0 0.0 copy-start
  75.0 1.0 copy-done
  76.1 0.0 collective-permute-start.5
  76.1 4.2 %collective-permute-start.9 = (bf16[3,5120]{1,0:T(4,128)(2,1)S(1)}, bf16[3,5120]{1,0:T(4,128)(2,1)S(1)}, u32[]{:S(2)}, u32[]{:S(2)}) collective-permute-start(bf16[3,5120]{1,0:T(4,128)(2,1)S(1)} %get-tuple-element.172), channel_id=1, source_target_pairs={{1,0},{2,1},{3,2},{4,3},{5,4},{6,5},{7,6},{8,7},{9,8},{10,9},{11,1... | collective-permute-start | bytes 92168 | tf_op jit(solution)/shard_map/ppermute | solution.py:1008
  80.4 0.6 merge.1.rest_0_
  80.9 1.8 %collective-permute-start.7 = (bf16[176,128]{1,0:T(8,128)(2,1)S(1)}, bf16[176,128]{1,0:T(8,128)(2,1)S(1)}, u32[]{:S(2)}, u32[]{:S(2)}) collective-permute-start(bf16[176,128]{1,0:T(8,128)(2,1)S(1)} %merge.1.rest_0_), channel_id=1, source_target_pairs={{0,4},{2,6},{4,0},{6,2},{8,12},{10,14},{12,8},{14,10},{16,20},{18,... | collective-permute-start | bytes 135176 | tf_op jit(solution)/shard_map/ppermute | solution.py:961
  82.7 1.4 %collective-permute-start.8 = (bf16[176,128]{1,0:T(8,128)(2,1)S(1)}, bf16[176,128]{1,0:T(8,128)(2,1)S(1)}, u32[]{:S(2)}, u32[]{:S(2)}) collective-permute-start(bf16[176,128]{1,0:T(8,128)(2,1)S(1)} %merge.1.rest_0_), channel_id=1, source_target_pairs={{0,6},{2,0},{4,2},{6,4},{8,14},{10,8},{12,10},{14,12},{16,22},{18,... | collective-permute-start | bytes 135176 | tf_op jit(solution)/shard_map/ppermute | solution.py:961
  84.2 2.7 %spread.1 = bf16[128,5120]{1,0:T(8,128)(2,1)} custom-call(s32[1]{0:T(128)} %bitcast.core_ref, f32[128,2560]{1,0:T(8,128)S(1)} %get-tuple-element.165.rest_21_.own_ref, f32[128,2560]{1,0:T(8,128)S(1)} %copy-done.1, bf16[3,5120]{1,0:T(4,128)(2,1)S(1)} %collective-permute-done.9.halo_ref, f32[4,5120]{1,0:T(4,128)S(1)} %get-tuple-element.148.rest_20_.weight_ref), custom_call_target="tpu_custom_call" | custom-call | flops 3000000000 | bytes 10800000 | tf_op jit(solution)/shard_map/spread/pallas_call | solution.py:97
  86.9 0.6 collective-permute-done.8.rest_3_
  87.6 0.9 collective-permute-start.10
  88.5 2.7 %collective-permute-start.11 = (bf16[176,128]{1,0:T(8,128)(2,1)S(1)}, bf16[176,128]{1,0:T(8,128)(2,1)S(1)}, u32[]{:S(2)}, u32[]{:S(2)}) collective-permute-start(bf16[176,128]{1,0:T(8,128)(2,1)S(1)} %fold.2.rest_0_), channel_id=1, source_target_pairs={{0,16},{2,18},{4,20},{6,22},{8,24},{10,26},{12,28},{14,30},{16,0},... | collective-permute-start | bytes 135176 | tf_op jit(solution)/shard_map/ppermute | solution.py:961
  91.2 0.7 collective-permute-start.12
  91.8 0.1 collective-permute-done.10.rest_1_
  91.9 2.1 %collective-permute-done.11.rest_2_ = bf16[176,128]{1,0:T(8,128)(2,1)S(1)} collective-permute-done((bf16[176,128]{1,0:T(8,128)(2,1)S(1)}, bf16[176,128]{1,0:T(8,128)(2,1)S(1)}, u32[]{:S(2)}, u32[]{:S(2)}) %collective-permute-start.11) | collective-permute-done | bytes 45088 | tf_op jit(solution)/shard_map/ppermute | solution.py:961
  94.1 1.2 %collective-permute-done.12.rest_3_ = bf16[176,128]{1,0:T(8,128)(2,1)S(1)} collective-permute-done((bf16[176,128]{1,0:T(8,128)(2,1)S(1)}, bf16[176,128]{1,0:T(8,128)(2,1)S(1)}, u32[]{:S(2)}, u32[]{:S(2)}) %collective-permute-start.12) | collective-permute-done | bytes 45088 | tf_op jit(solution)/shard_map/ppermute | solution.py:961
  95.3 2.0 %collective-permute-start.13 = (bf16[176,128]{1,0:T(8,128)(2,1)S(1)}, bf16[176,128]{1,0:T(8,128)(2,1)S(1)}, u32[]{:S(2)}, u32[]{:S(2)}) collective-permute-start(bf16[176,128]{1,0:T(8,128)(2,1)S(1)} %fold.3.rest_0_), channel_id=1, source_target_pairs={{0,32},{32,64},{64,96},{96,128},{128,160},{160,192},{192,224},{224... | collective-permute-start | bytes 135176 | tf_op jit(solution)/shard_map/ppermute | solution.py:961
  97.3 3.3 %collective-permute-start.14 = (bf16[176,128]{1,0:T(8,128)(2,1)S(1)}, bf16[176,128]{1,0:T(8,128)(2,1)S(1)}, u32[]{:S(2)}, u32[]{:S(2)}) collective-permute-start(bf16[176,128]{1,0:T(8,128)(2,1)S(1)} %fold.3.rest_0_), channel_id=1, source_target_pairs={{0,64},{32,96},{64,128},{96,160},{128,192},{160,224},{192,0},{224,... | collective-permute-start | bytes 135176 | tf_op jit(solution)/shard_map/ppermute | solution.py:961
  100.5 4.0 %collective-permute-start.15 = (bf16[176,128]{1,0:T(8,128)(2,1)S(1)}, bf16[176,128]{1,0:T(8,128)(2,1)S(1)}, u32[]{:S(2)}, u32[]{:S(2)}) collective-permute-start(bf16[176,128]{1,0:T(8,128)(2,1)S(1)} %fold.3.rest_0_), channel_id=1, source_target_pairs={{0,96},{32,128},{64,160},{96,192},{128,224},{160,0},{192,32},{224,... | collective-permute-start | bytes 135176 | tf_op jit(solution)/shard_map/ppermute | solution.py:961
  104.6 0.5 collective-permute-start.16
  105.1 4.9 %collective-permute-start.17 = (bf16[176,128]{1,0:T(8,128)(2,1)S(1)}, bf16[176,128]{1,0:T(8,128)(2,1)S(1)}, u32[]{:S(2)}, u32[]{:S(2)}) collective-permute-start(bf16[176,128]{1,0:T(8,128)(2,1)S(1)} %fold.3.rest_0_), channel_id=1, source_target_pairs={{0,160},{32,192},{64,224},{96,0},{128,32},{160,64},{192,96},{224,1... | collective-permute-start | bytes 135176 | tf_op jit(solution)/shard_map/ppermute | solution.py:961
  110.1 2.7 %collective-permute-start.18 = (bf16[176,128]{1,0:T(8,128)(2,1)S(1)}, bf16[176,128]{1,0:T(8,128)(2,1)S(1)}, u32[]{:S(2)}, u32[]{:S(2)}) collective-permute-start(bf16[176,128]{1,0:T(8,128)(2,1)S(1)} %fold.3.rest_0_), channel_id=1, source_target_pairs={{0,192},{32,224},{64,0},{96,32},{128,64},{160,96},{192,128},{224,1... | collective-permute-start | bytes 135176 | tf_op jit(solution)/shard_map/ppermute | solution.py:961
  112.7 1.0 collective-permute-start.19
  113.8 1.4 %collective-permute-done.18.rest_6_ = bf16[176,128]{1,0:T(8,128)(2,1)S(1)} collective-permute-done((bf16[176,128]{1,0:T(8,128)(2,1)S(1)}, bf16[176,128]{1,0:T(8,128)(2,1)S(1)}, u32[]{:S(2)}, u32[]{:S(2)}) %collective-permute-start.18) | collective-permute-done | bytes 45088 | tf_op jit(solution)/shard_map/ppermute | solution.py:961
  115.1 1.7 %collective-permute-done.19.rest_7_ = bf16[176,128]{1,0:T(8,128)(2,1)S(1)} collective-permute-done((bf16[176,128]{1,0:T(8,128)(2,1)S(1)}, bf16[176,128]{1,0:T(8,128)(2,1)S(1)}, u32[]{:S(2)}, u32[]{:S(2)}) %collective-permute-start.19) | collective-permute-done | bytes 45088 | tf_op jit(solution)/shard_map/ppermute | solution.py:961
  116.8 0.7 finish.1
  (16 shorter events, 0.1 us)
Async XLA Ops:
  1.5 7.4 %collective-permute-start = (bf16[3,5120]{1,0:T(4,128)(2,1)S(1)}, bf16[3,5120]{1,0:T(4,128)(2,1)S(1)}, u32[]{:S(2)}, u32[]{:S(2)}) collective-permute-start(bf16[3,5120]{1,0:T(4,128)(2,1)S(1)} %slice_bitcast_fusion), channel_id=1, source_target_pairs={{0,1},{1,2},{2,3},{3,4},{4,5},{5,6},{6,7},{7,8},{8,9},{9,10},{10,1... | collective-permute-start | bytes 92168 | tf_op jit(solution)/shard_map/ppermute | solution.py:978
  11.4 3.1 %collective-permute-start.1 = (bf16[2,16,128,128]{3,2,1,0:T(8,128)(2,1)S(1)}, bf16[2,16,128,128]{3,2,1,0:T(8,128)(2,1)S(1)}, u32[]{:S(2)}, u32[]{:S(2)}) collective-permute-start(bf16[2,16,128,128]{3,2,1,0:T(8,128)(2,1)S(1)} %get-tuple-element.103), channel_id=1, source_target_pairs={{0,1},{1,0},{2,3},{3,2},{4,5},{5,4},{6,7},{7,6},{8,9},{9,8},{10,11... | collective-permute-start | bytes 3145736 | tf_op jit(solution)/shard_map/ppermute | solution.py:986
  12.1 2.3 %collective-permute-start.2 = (f32[32,128]{1,0:T(8,128)S(1)}, f32[32,128]{1,0:T(8,128)S(1)}, u32[]{:S(2)}, u32[]{:S(2)}) collective-permute-start(f32[32,128]{1,0:T(8,128)S(1)} %get-tuple-element.104.tot_ref), channel_id=1, source_target_pairs={{0,1},{1,0},{2,3},{3,2},{4,5},{5,4},{6,7},{7,6},{8,9},{9,8},{10,11... | collective-permute-start | bytes 49160 | tf_op jit(solution)/shard_map/ppermute | solution.py:982
  16.2 23.7 %all-to-all-start = ((bf16[16,272,128]{2,1,0:T(8,128)(2,1)}), bf16[16,272,128]{2,1,0:T(8,128)(2,1)S(1)}, u32[]{:S(2)}, u32[]{:S(2)}) async-start(bf16[16,272,128]{2,1,0:T(8,128)(2,1)} %get-tuple-element.105), calls=%async_computation | async-start | bytes 2228224 | tf_op jit(solution)/shard_map/all_to_all | solution.py:949
  41.2 20.5 %all-to-all-start.1 = ((bf16[16,256,128]{2,1,0:T(8,128)(2,1)}), bf16[16,256,128]{2,1,0:T(8,128)(2,1)S(1)}, u32[]{:S(2)}, u32[]{:S(2)}) async-start(bf16[16,256,128]{2,1,0:T(8,128)(2,1)} %chain.1), calls=%async_computation.1 | async-start | bytes 2097152 | tf_op jit(solution)/shard_map/all_to_all | solution.py:949
  65.7 5.1 %collective-permute-start.3 = (bf16[2,16,128,128]{3,2,1,0:T(8,128)(2,1)S(1)}, bf16[2,16,128,128]{3,2,1,0:T(8,128)(2,1)S(1)}, u32[]{:S(2)}, u32[]{:S(2)}) collective-permute-start(bf16[2,16,128,128]{3,2,1,0:T(8,128)(2,1)S(1)} %get-tuple-element.126), channel_id=1, source_target_pairs={{0,1},{1,0},{2,3},{3,2},{4,5},{5,4},{6,7},{7,6},{8,9},{9,8},{10,11... | collective-permute-start | bytes 3145736 | tf_op jit(solution)/shard_map/ppermute | solution.py:1001
  70.2 10.1 %collective-permute-start.4 = (f32[128,128]{1,0:T(8,128)S(1)}, f32[128,128]{1,0:T(8,128)S(1)}, u32[]{:S(2)}, u32[]{:S(2)}) collective-permute-start(f32[128,128]{1,0:T(8,128)S(1)} %get-tuple-element.169.own_ref), channel_id=1, source_target_pairs={{0,1},{1,0},{2,3},{3,2},{4,5},{5,4},{6,7},{7,6},{8,9},{9,8},{10,11... | collective-permute-start | bytes 196616 | tf_op jit(solution)/shard_map/ppermute | solution.py:1003
  75.0 1.1 copy-start
  76.1 4.3 %collective-permute-start.5 = (f32[128,128]{1,0:T(8,128)S(1)}, f32[128,128]{1,0:T(8,128)S(1)}, u32[]{:S(2)}, u32[]{:S(2)}) collective-permute-start(f32[128,128]{1,0:T(8,128)S(1)} %get-tuple-element.170.theirs_ref), channel_id=1, source_target_pairs={{0,1},{1,0},{2,3},{3,2},{4,5},{5,4},{6,7},{7,6},{8,9},{9,8},{10,11... | collective-permute-start | bytes 196616 | tf_op jit(solution)/shard_map/ppermute | solution.py:1007
  76.1 8.1 %copy-start.1 = (f32[128,2560]{1,0:T(8,128)S(1)}, f32[128,2560]{1,0:T(8,128)}, u32[]{:S(2)}) copy-start(f32[128,2560]{1,0:T(8,128)} %copy-done) | copy-start | bytes 3932164
  76.1 8.0 %collective-permute-start.9 = (bf16[3,5120]{1,0:T(4,128)(2,1)S(1)}, bf16[3,5120]{1,0:T(4,128)(2,1)S(1)}, u32[]{:S(2)}, u32[]{:S(2)}) collective-permute-start(bf16[3,5120]{1,0:T(4,128)(2,1)S(1)} %get-tuple-element.172), channel_id=1, source_target_pairs={{1,0},{2,1},{3,2},{4,3},{5,4},{6,5},{7,6},{8,7},{9,8},{10,9},{11,1... | collective-permute-start | bytes 92168 | tf_op jit(solution)/shard_map/ppermute | solution.py:1008
  80.9 6.0 %collective-permute-start.6 = (bf16[176,128]{1,0:T(8,128)(2,1)S(1)}, bf16[176,128]{1,0:T(8,128)(2,1)S(1)}, u32[]{:S(2)}, u32[]{:S(2)}) collective-permute-start(bf16[176,128]{1,0:T(8,128)(2,1)S(1)} %merge.1.rest_0_), channel_id=1, source_target_pairs={{0,2},{2,4},{4,6},{6,0},{8,10},{10,12},{12,14},{14,8},{16,18},{18,... | collective-permute-start | bytes 135176 | tf_op jit(solution)/shard_map/ppermute | solution.py:961
  80.9 6.0 %collective-permute-start.7 = (bf16[176,128]{1,0:T(8,128)(2,1)S(1)}, bf16[176,128]{1,0:T(8,128)(2,1)S(1)}, u32[]{:S(2)}, u32[]{:S(2)}) collective-permute-start(bf16[176,128]{1,0:T(8,128)(2,1)S(1)} %merge.1.rest_0_), channel_id=1, source_target_pairs={{0,4},{2,6},{4,0},{6,2},{8,12},{10,14},{12,8},{14,10},{16,20},{18,... | collective-permute-start | bytes 135176 | tf_op jit(solution)/shard_map/ppermute | solution.py:961
  82.7 4.8 %collective-permute-start.8 = (bf16[176,128]{1,0:T(8,128)(2,1)S(1)}, bf16[176,128]{1,0:T(8,128)(2,1)S(1)}, u32[]{:S(2)}, u32[]{:S(2)}) collective-permute-start(bf16[176,128]{1,0:T(8,128)(2,1)S(1)} %merge.1.rest_0_), channel_id=1, source_target_pairs={{0,6},{2,0},{4,2},{6,4},{8,14},{10,8},{12,10},{14,12},{16,22},{18,... | collective-permute-start | bytes 135176 | tf_op jit(solution)/shard_map/ppermute | solution.py:961
  87.6 4.3 %collective-permute-start.10 = (bf16[176,128]{1,0:T(8,128)(2,1)S(1)}, bf16[176,128]{1,0:T(8,128)(2,1)S(1)}, u32[]{:S(2)}, u32[]{:S(2)}) collective-permute-start(bf16[176,128]{1,0:T(8,128)(2,1)S(1)} %fold.2.rest_0_), channel_id=1, source_target_pairs={{0,8},{2,10},{4,12},{6,14},{8,16},{10,18},{12,20},{14,22},{16,24},... | collective-permute-start | bytes 135176 | tf_op jit(solution)/shard_map/ppermute | solution.py:961
  88.5 5.6 %collective-permute-start.11 = (bf16[176,128]{1,0:T(8,128)(2,1)S(1)}, bf16[176,128]{1,0:T(8,128)(2,1)S(1)}, u32[]{:S(2)}, u32[]{:S(2)}) collective-permute-start(bf16[176,128]{1,0:T(8,128)(2,1)S(1)} %fold.2.rest_0_), channel_id=1, source_target_pairs={{0,16},{2,18},{4,20},{6,22},{8,24},{10,26},{12,28},{14,30},{16,0},... | collective-permute-start | bytes 135176 | tf_op jit(solution)/shard_map/ppermute | solution.py:961
  91.2 4.0 %collective-permute-start.12 = (bf16[176,128]{1,0:T(8,128)(2,1)S(1)}, bf16[176,128]{1,0:T(8,128)(2,1)S(1)}, u32[]{:S(2)}, u32[]{:S(2)}) collective-permute-start(bf16[176,128]{1,0:T(8,128)(2,1)S(1)} %fold.2.rest_0_), channel_id=1, source_target_pairs={{0,24},{2,26},{4,28},{6,30},{8,0},{10,2},{12,4},{14,6},{16,8},{18,... | collective-permute-start | bytes 135176 | tf_op jit(solution)/shard_map/ppermute | solution.py:961
  95.3 14.8 %collective-permute-start.13 = (bf16[176,128]{1,0:T(8,128)(2,1)S(1)}, bf16[176,128]{1,0:T(8,128)(2,1)S(1)}, u32[]{:S(2)}, u32[]{:S(2)}) collective-permute-start(bf16[176,128]{1,0:T(8,128)(2,1)S(1)} %fold.3.rest_0_), channel_id=1, source_target_pairs={{0,32},{32,64},{64,96},{96,128},{128,160},{160,192},{192,224},{224... | collective-permute-start | bytes 135176 | tf_op jit(solution)/shard_map/ppermute | solution.py:961
  97.3 15.5 %collective-permute-start.14 = (bf16[176,128]{1,0:T(8,128)(2,1)S(1)}, bf16[176,128]{1,0:T(8,128)(2,1)S(1)}, u32[]{:S(2)}, u32[]{:S(2)}) collective-permute-start(bf16[176,128]{1,0:T(8,128)(2,1)S(1)} %fold.3.rest_0_), channel_id=1, source_target_pairs={{0,64},{32,96},{64,128},{96,160},{128,192},{160,224},{192,0},{224,... | collective-permute-start | bytes 135176 | tf_op jit(solution)/shard_map/ppermute | solution.py:961
  100.5 13.2 %collective-permute-start.15 = (bf16[176,128]{1,0:T(8,128)(2,1)S(1)}, bf16[176,128]{1,0:T(8,128)(2,1)S(1)}, u32[]{:S(2)}, u32[]{:S(2)}) collective-permute-start(bf16[176,128]{1,0:T(8,128)(2,1)S(1)} %fold.3.rest_0_), channel_id=1, source_target_pairs={{0,96},{32,128},{64,160},{96,192},{128,224},{160,0},{192,32},{224,... | collective-permute-start | bytes 135176 | tf_op jit(solution)/shard_map/ppermute | solution.py:961
  104.6 9.2 %collective-permute-start.16 = (bf16[176,128]{1,0:T(8,128)(2,1)S(1)}, bf16[176,128]{1,0:T(8,128)(2,1)S(1)}, u32[]{:S(2)}, u32[]{:S(2)}) collective-permute-start(bf16[176,128]{1,0:T(8,128)(2,1)S(1)} %fold.3.rest_0_), channel_id=1, source_target_pairs={{0,128},{32,160},{64,192},{96,224},{128,0},{160,32},{192,64},{224,... | collective-permute-start | bytes 135176 | tf_op jit(solution)/shard_map/ppermute | solution.py:961
  105.1 8.6 %collective-permute-start.17 = (bf16[176,128]{1,0:T(8,128)(2,1)S(1)}, bf16[176,128]{1,0:T(8,128)(2,1)S(1)}, u32[]{:S(2)}, u32[]{:S(2)}) collective-permute-start(bf16[176,128]{1,0:T(8,128)(2,1)S(1)} %fold.3.rest_0_), channel_id=1, source_target_pairs={{0,160},{32,192},{64,224},{96,0},{128,32},{160,64},{192,96},{224,1... | collective-permute-start | bytes 135176 | tf_op jit(solution)/shard_map/ppermute | solution.py:961
  110.1 5.0 %collective-permute-start.18 = (bf16[176,128]{1,0:T(8,128)(2,1)S(1)}, bf16[176,128]{1,0:T(8,128)(2,1)S(1)}, u32[]{:S(2)}, u32[]{:S(2)}) collective-permute-start(bf16[176,128]{1,0:T(8,128)(2,1)S(1)} %fold.3.rest_0_), channel_id=1, source_target_pairs={{0,192},{32,224},{64,0},{96,32},{128,64},{160,96},{192,128},{224,1... | collective-permute-start | bytes 135176 | tf_op jit(solution)/shard_map/ppermute | solution.py:961
  112.7 4.0 %collective-permute-start.19 = (bf16[176,128]{1,0:T(8,128)(2,1)S(1)}, bf16[176,128]{1,0:T(8,128)(2,1)S(1)}, u32[]{:S(2)}, u32[]{:S(2)}) collective-permute-start(bf16[176,128]{1,0:T(8,128)(2,1)S(1)} %fold.3.rest_0_), channel_id=1, source_target_pairs={{0,224},{32,0},{64,32},{96,64},{128,96},{160,128},{192,160},{224,1... | collective-permute-start | bytes 135176 | tf_op jit(solution)/shard_map/ppermute | solution.py:961

commit v7 on v6

--- a/solution.py
+++ b/solution.py
@@ -139,7 +139,7 @@
 
 def begin_kernel(raw_h, decay_log_h, skip_gain_h, tok_h, weight_h, g_h,
                  small_h, small_ref, tot_ref, x_ref, bc_ref, head_ref, weight_ref, g_ref,
-                 raw_ref, decay_log_ref, skip_gain_ref, hold_ref, win_ref, sems):
+                 raw_ref, decay_log_ref, skip_gain_ref, wide_ref, hold_ref, win_ref, sems):
     first = start_all(
         [(raw_h, raw_ref), (decay_log_h, decay_log_ref), (skip_gain_h, skip_gain_ref), (weight_h, weight_ref)],
         sems.at[0],
@@ -168,12 +168,10 @@
         jnp.concatenate([jnp.exp(seg), jnp.exp(total - seg) * dt], axis=0)
     )
     left = iota((PAIRS, LANES), 1) < HEAD_DIM
-    even = (iota((PAIRS, HEADS), 1) == 2 * iota((PAIRS, HEADS), 0)).astype(F32)
-    odd = (iota((PAIRS, HEADS), 1) == 2 * iota((PAIRS, HEADS), 0) + 1).astype(F32)
 
     def paired(col):
-        wide = jnp.broadcast_to(col, (HEADS, LANES))
-        return jnp.where(left, exact_dot(even, wide), exact_dot(odd, wide))
+        wide_ref[...] = jnp.broadcast_to(col, (HEADS, LANES))
+        return jnp.where(left, wide_ref[pl.ds(0, PAIRS, 2), :], wide_ref[pl.ds(1, PAIRS, 2), :])
 
     tot = paired(total)
     tot_ref[...] = tot
@@ -213,11 +211,12 @@
         pltpu.VMEM((HEADS, T), F32),
         pltpu.VMEM((1, HEADS), F32),
         pltpu.VMEM((1, HEADS), F32),
+        pltpu.VMEM((HEADS, LANES), F32),
         pltpu.VMEM((T, CHANNELS), BF16),
         pltpu.VMEM((8 + T, GROUP_X), F32),
         DMA(3, BLOCKS),
     ]
-    return call(begin_kernel, "begin", out, "hhhhhh", 4, scratch, mib=16)(
+    return call(begin_kernel, "begin", out, "hhhhhh", 4, scratch, mib=8)(
         raw, decay_log, skip_gain, tokens, weight, cot
     )
 
@@ -291,7 +290,7 @@
         ("V", (2, HALF_PAIRS, STATE, LANES), BF16),
     ]
     scratch = [pltpu.VMEM((8, CHANNELS), F32), DMA(3)]
-    return call(enter_kernel, "enter", out, "sVVVvVVV", 3, scratch, mib=16)(
+    return call(enter_kernel, "enter", out, "sVVVvVVV", 3, scratch, mib=6)(
         core, x0, bc0, head, halo, weight, cot, small
     )
 
@@ -302,7 +301,7 @@
 
 def run_own(core, x, bc, cot, small):
     out = [("V", (2, HALF_PAIRS, STATE, LANES), BF16)]
-    return call(own_kernel, "own", out, "sVVVV", 3, mib=16)(core, x, bc, cot, small)[0]
+    return call(own_kernel, "own", out, "sVVVV", 3, mib=6)(core, x, bc, cot, small)[0]
 
 
 STEP_PAIRS = 4
@@ -310,17 +309,29 @@
 
 
 def pack_kernel(core_ref, own_ref, got_ref, tot_ref, other_ref,
-                out_h, own_h, got_h, tots_h, out_ref, sems):
+                out_h, left_h, right_h, tots_h, out_ref, sems):
     saves = start_all(
-        [
-            (own_ref, own_h),
-            (got_ref, got_h),
-            (tot_ref, tots_h.at[pl.ds(0, PAIRS)]),
-            (other_ref, tots_h.at[pl.ds(PAIRS, PAIRS)]),
-        ],
-        sems.at[0],
+        [(tot_ref, tots_h.at[pl.ds(0, PAIRS)]), (other_ref, tots_h.at[pl.ds(PAIRS, PAIRS)])], sems.at[0]
     )
     second = core_ref[0] == 1
+
+    def keep(first_ref, last_ref):
+        return [
+            pltpu.make_async_copy(first_ref.at[0], left_h, sems.at[0, 2]),
+            pltpu.make_async_copy(last_ref.at[1], right_h, sems.at[0, 3]),
+        ]
+
+    @pl.when(second)
+    def _():
+        for copy in keep(got_ref, own_ref):
+            copy.start()
+
+    @pl.when(jnp.logical_not(second))
+    def _():
+        for copy in keep(own_ref, got_ref):
+            copy.start()
+
+    saves += keep(own_ref, got_ref)
     outs = []
     for i in range(HALF_PAIRS):
         at = core_ref[0] * HALF_PAIRS + i
@@ -355,11 +366,11 @@
 
 
 def run_pack(core, own, got, tot, other):
-    half = (2, HALF_PAIRS, STATE, LANES)
+    half = (HALF_PAIRS, STATE, LANES)
     packed = (HALF_PAIRS, PACK_ROWS, LANES)
     out = [("h", packed, BF16), ("h", half, BF16), ("h", half, BF16), ("h", (2 * PAIRS, LANES), F32)]
     scratch = [pltpu.VMEM(packed, BF16), DMA(2, STEPS)]
-    return call(pack_kernel, "pack", out, "sVvVv", 2, scratch, mib=16)(core, own, got, tot, other)
+    return call(pack_kernel, "pack", out, "sVvVv", 2, scratch, mib=8)(core, own, got, tot, other)
 
 
 def chain_kernel(chips, per, in_ref, out_ref):
@@ -383,7 +394,7 @@
 def run_chain(chips, packed):
     kernel = functools.partial(chain_kernel, chips, HALF_PAIRS // chips)
     out = [("v", (HALF_PAIRS, 2 * STATE, LANES), BF16)]
-    return call(kernel, "chain", out, "v", 1, mib=16)(packed)[0]
+    return call(kernel, "chain", out, "v", 1, mib=8)(packed)[0]
 
 
 HALF_X = HALF_GROUPS * GROUP_X
@@ -431,20 +442,20 @@
     return start_all(pairs, sems)
 
 
-def unpack_kernel(core_ref, back_ref, own_h, got_h, tots_h, *rest):
+def unpack_kernel(core_ref, back_ref, left_h, right_h, tots_h, *rest):
     far, rest = rest[: len(NEAR)], rest[len(NEAR) :]
     common_far, rest = rest[: len(COMMON)], rest[len(COMMON) :]
     mine_ref, send_ref, *rest = rest
     near = [rest[i * len(NEAR) : (i + 1) * len(NEAR)] for i in range(HALF_GROUPS)]
     rest = rest[HALF_GROUPS * len(NEAR) :]
     common, rest = rest[: len(COMMON)], rest[len(COMMON) :]
-    own_ref, got_ref, tots_ref, sems, fetch_sems = rest
+    left_ref, right_ref, tots_ref, sems, fetch_sems = rest
     first = start_all([(tots_h, tots_ref)], sems.at[STEPS])
     steps = []
     for step in range(STEPS):
         at = pl.ds(step * STEP_PAIRS, STEP_PAIRS)
         steps.append(
-            start_all([(own_h.at[:, at], own_ref.at[:, at]), (got_h.at[:, at], got_ref.at[:, at])], sems.at[step])
+            start_all([(left_h.at[at], left_ref.at[at]), (right_h.at[at], right_ref.at[at])], sems.at[step])
         )
     fetches = start_all(list(zip(common_far, common)), fetch_sems.at[HALF_GROUPS])
     for jj in range(HALF_GROUPS):
@@ -461,10 +472,8 @@
         decay_one = jnp.exp(jnp.where(second, tot, other))
         state_zero = back_ref[i, 0:STATE, :].astype(F32)
         grad_one = back_ref[i, STATE : 2 * STATE, :].astype(F32)
-        left = jnp.where(second, got_ref[0, i].astype(F32), own_ref[0, i].astype(F32))
-        right = jnp.where(second, own_ref[1, i].astype(F32), got_ref[1, i].astype(F32))
-        state_one = decay_zero * state_zero + left
-        grad_zero = decay_one * grad_one + right
+        state_one = decay_zero * state_zero + left_ref[i].astype(F32)
+        grad_zero = decay_one * grad_one + right_ref[i].astype(F32)
         mine_ref[0, i] = jnp.where(second, state_one, state_zero).astype(BF16)
         mine_ref[1, i] = jnp.where(second, grad_one, grad_zero).astype(BF16)
         send_ref[0, i] = jnp.where(second, state_zero, state_one).astype(BF16)
@@ -472,19 +481,19 @@
     wait_all(fetches)
 
 
-def run_unpack(core, back, own, got, tots, far, common):
+def run_unpack(core, back, left, right, tots, far, common):
     half = (2, HALF_PAIRS, STATE, LANES)
     out = [("V", half, BF16)] * 2 + NEAR * HALF_GROUPS + COMMON
     scratch = [
-        pltpu.VMEM(half, BF16),
-        pltpu.VMEM(half, BF16),
+        pltpu.VMEM(half[1:], BF16),
+        pltpu.VMEM(half[1:], BF16),
         pltpu.VMEM((2 * PAIRS, LANES), F32),
         DMA(STEPS + 1, 2),
         DMA(HALF_GROUPS + 1, FETCHES),
     ]
     specs = "svhhh" + "h" * (len(NEAR) + len(COMMON))
-    outs = call(unpack_kernel, "unpack", out, specs, 3, scratch, mib=16)(
-        core, back, own, got, tots, *far, *common
+    outs = call(unpack_kernel, "unpack", out, specs, 3, scratch, mib=8)(
+        core, back, left, right, tots, *far, *common
     )
     at = 2 + HALF_GROUPS * len(NEAR)
     return outs[0], outs[1], outs[2:at], outs[at:]
@@ -567,7 +576,7 @@
         pltpu.VMEM((PAIRS, LANES), F32),
         DMA(4, GROUPS),
     ]
-    return call(inner_kernel, "inner", out, "hhhh", 4, scratch, mib=24)(x, bc, cot, small)
+    return call(inner_kernel, "inner", out, "hhhh", 4, scratch, mib=16)(x, bc, cot, small)
 
 
 def slopes_kernel(bc_h, g_h, small_h, tok_h, before_h, weight_h, gx_h, slope_h,
@@ -645,7 +654,7 @@
         pltpu.VMEM((8 + T, GROUP_X), F32),
         DMA(4, BLOCKS),
     ]
-    return call(slopes_kernel, "slopes", out, "hhhhhh", 6, scratch, mib=24)(
+    return call(slopes_kernel, "slopes", out, "hhhhhh", 6, scratch, mib=16)(
         bc, cot, small, tokens, before, weight
     )
 
@@ -810,7 +819,7 @@
     else:
         out += NEAR * HALF_GROUPS
     kernel = functools.partial(leave_kernel, theirs)
-    outs = call(kernel, "leave", out, specs, 5, scratch, mib=16, aliases=aliases)(*args)
+    outs = call(kernel, "leave", out, specs, 5, scratch, mib=8, aliases=aliases)(*args)
     return outs[:2], outs[2], outs[3], outs[4:]
 
 
@@ -843,7 +852,7 @@
 def run_spread(core, own, theirs, halo, weight):
     out = [("h", (T, CHANNELS), BF16)]
     scratch = [pltpu.VMEM((T, CHANNELS), BF16), pltpu.VMEM((T + 8, GROUP_X), F32), DMA(8)]
-    return call(spread_kernel, "spread", out, "sVVvV", 3, scratch, mib=16)(core, own, theirs, halo, weight)[0]
+    return call(spread_kernel, "spread", out, "sVVvV", 3, scratch, mib=6)(core, own, theirs, halo, weight)[0]
 
 
 CONV_ROWS = TAPS * (CHANNELS // LANES)
@@ -896,13 +905,11 @@
 
 def run_merge(core, own, own_got, theirs, theirs_got):
     out = [("v", (SEND_ROWS, LANES), BF16)]
-    return call(merge_kernel, "merge", out, "svvvv", 1, mib=16)(core, own, own_got, theirs, theirs_got)[0]
-
-
-def ring_sum(me_ref, refs, hold_ref):
-    count = len(refs)
-    for d in range(count):
-        hold_ref[d] = refs[d][...]
+    return call(merge_kernel, "merge", out, "svvvv", 1, mib=4)(core, own, own_got, theirs, theirs_got)[0]
+
+
+def ring_sum(me_ref, hold_ref):
+    count = hold_ref.shape[0]
     conv, thin = read_send(hold_ref[lax.rem(me_ref[0], count)])
     for k in range(1, count):
         more, little = read_send(hold_ref[lax.rem(me_ref[0] + count - k, count)])
@@ -912,18 +919,29 @@
 
 def fold_kernel(me_ref, *rest):
     *refs, out_ref, hold_ref = rest
-    write_send(out_ref, *ring_sum(me_ref, refs, hold_ref))
+    for d, ref in enumerate(refs):
+        hold_ref[d] = ref[...]
+    write_send(out_ref, *ring_sum(me_ref, hold_ref))
 
 
 def run_fold(me, values):
     out = [("v", (SEND_ROWS, LANES), BF16)]
     scratch = [pltpu.VMEM((len(values), SEND_ROWS, LANES), BF16)]
-    return call(fold_kernel, "fold", out, "s" + "v" * len(values), 1, scratch, mib=16)(me, *values)[0]
-
-
-def finish_kernel(me_ref, *rest):
+    return call(fold_kernel, "fold", out, "s" + "v" * len(values), 1, scratch, mib=4)(me, *values)[0]
+
+
+def finish_kernel(core_ref, me_ref, *rest):
     *refs, conv_ref, decay_ref, skip_ref, hold_ref = rest
-    conv, thin = ring_sum(me_ref, refs, hold_ref)
+    count = len(refs)
+    sides = (count - 1) // 2
+    hold_ref[0] = refs[0][...]
+    for k in range(1, sides + 1):
+        mine = jnp.where(core_ref[0] == 0, k, count - k)
+        hold_ref[mine] = refs[k][...]
+        hold_ref[count - mine] = refs[sides + k][...]
+    if count % 2 == 0:
+        hold_ref[count // 2] = refs[count - 1][...]
+    conv, thin = ring_sum(me_ref, hold_ref)
     for i in range(CHANNELS // LANES):
         if i < PAIRS:
             row = CONV_GROUP * (i // GROUP_PAIRS) + TAPS * (i % GROUP_PAIRS)
@@ -935,10 +953,10 @@
     decay_ref[...] = thin[:, HEADS:]
 
 
-def run_finish(me, values):
+def run_finish(core, me, values):
     out = [("v", (TAPS, CHANNELS), F32), ("v", (1, HEADS), F32), ("v", (1, HEADS), F32)]
     scratch = [pltpu.VMEM((len(values), SEND_ROWS, LANES), BF16)]
-    return call(finish_kernel, "finish", out, "s" + "v" * len(values), 1, scratch, mib=16)(me, *values)
+    return call(finish_kernel, "finish", out, "ss" + "v" * len(values), 1, scratch, mib=4)(core, me, *values)
 
 
 CTX = ("chip", "core")
@@ -960,6 +978,23 @@
     return [value] + [
         lax.ppermute(value, axis, [(i, move(i, d)) for i in range(count)]) for d in range(1, ring)
     ]
+
+
+def around_by_sides(value, count):
+    def shifts(first, second):
+        return [
+            (2 * i + side, 2 * ((i + move) % count) + side)
+            for i in range(count)
+            for side, move in enumerate((first, second))
+        ]
+
+    def hear(first, second):
+        return lax.ppermute(value, ("dp", "core"), shifts(first, second))
+
+    middle = [hear(count // 2, count // 2)] if count % 2 == 0 else []
+    heard = [hear(k, -k) for k in range((count - 1) // 2, 0, -1)][::-1]
+    swapped = [lax.ppermute(part, "core", [(0, 1), (1, 0)]) for part in heard]
+    return [value] + heard + swapped + middle
 
 
 def scalar(value):
@@ -985,7 +1020,7 @@
     )
     got_near = lax.ppermute(out, "core", swap)
     own_near = run_own(core, x_near, bc_near, cot_near, small_near)
-    packed, own, got, tots = run_pack(core, own_near, got_near, tot, other)
+    packed, left, right, tots = run_pack(core, own_near, got_near, tot, other)
     heard = all_to_all(packed, "chip")
     y, gbc, skips = run_inner(x, bc, cot, small)
     heard, y, gbc, skips = tie(heard, y, gbc, skips)
@@ -996,7 +1031,7 @@
     back, gx, slope = tie(back, gx, slope)
     far = (x, cot, y, gx, slope, tokens, bc, gbc)
     mine, send, near, common = run_unpack(
-        core, back, own, got, tots, far, (before, small, raw, skips, conv_weight)
+        core, back, left, right, tots, far, (before, small, raw, skips, conv_weight)
     )
     theirs = lax.ppermute(send, "core", swap)
     half, pre_own, sum_own, near = run_leave(core, mine, near, common, far, None)
@@ -1005,17 +1040,17 @@
         core, theirs, near, common, (), (half, pre_own)
     )
     sum_theirs_got = lax.ppermute(sum_theirs, "core", swap)
-    after = lax.ppermute(first, CTX, [(i + 1, i) for i in range(devices - 1)])
     sums = run_merge(core, sum_own, sum_own_got, sum_theirs, sum_theirs_got)
     chip = lax.axis_index("chip")
     values = around(sums, "chip", chips, SIDE, lambda i, d: i // SIDE * SIDE + (i % SIDE + d) % SIDE)
+    sums, first = tie(run_fold(scalar(lax.rem(chip, SIDE)), values), first)
+    after = lax.ppermute(first, CTX, [(i + 1, i) for i in range(devices - 1)])
+    values = around(sums, "chip", chips, chips // SIDE, lambda i, d: (i + d * SIDE) % chips)
+    sums, after = tie(run_fold(scalar(lax.div(chip, SIDE)), values), after)
+    values = around_by_sides(sums, sequences)
     grad_tokens = run_spread(core, pre_own, pre_theirs, after, common[4])
     values, grad_tokens = tie(values, grad_tokens)
-    sums = run_fold(scalar(lax.rem(chip, SIDE)), values)
-    values = around(sums, "chip", chips, chips // SIDE, lambda i, d: (i + d * SIDE) % chips)
-    sums = run_fold(scalar(lax.div(chip, SIDE)), values)
-    values = around(sums, "dp", sequences, sequences, lambda i, d: (i + d) % sequences)
-    grad_conv, grad_decay, grad_skip = run_finish(scalar(lax.axis_index("dp")), values)
+    grad_conv, grad_decay, grad_skip = run_finish(core, scalar(lax.axis_index("dp")), values)
     return (
         out_tokens[None],
         grad_tokens[None],

time: 118 us -> 112 us (0.949); the launches traced: 118 us -> 110 us
  starting transfers between devices: 47.2 us -> 41.7 us
  waiting for transfers between devices: 25.2 us -> 23.5 us
    ppermute x13 -> x6, starting transfers between devices: 26 us -> 9.1 us  [around(): lax.ppermute(value, axis, [(i, move(i, d)) for i in range(count)])]
    ppermute x0 -> x7, starting transfers between devices: none -> 12.9 us  [the longest x4 9.68 us: hear(): return lax.ppermute(value, ('dp', 'core'), shifts(first, second))]
    ppermute x13 -> x6, waiting for transfers between devices: 7.06 us -> 2.84 us  [around(): lax.ppermute(value, axis, [(i, move(i, d)) for i in range(count)])]
    ppermute x1, starting transfers between devices: 4.21 us -> 2.8 us  [local(): after = lax.ppermute(first, CTX, [(i + 1, i) for i in range(devices - 1)])]
    ppermute x1, waiting for transfers between devices: 0.01 us -> 1.2 us  [local(): sum_theirs_got = lax.ppermute(sum_theirs, 'core', swap)]
  transfers between devices with their start and end apart: 22 -> 22, of which waited for: 10 -> 11; matrix products, arithmetic and copies ran while one was open for 0% -> 0% of each run, Pallas kernels for 27% -> 29%
where the time goes in v7:
time: 112 us; the launch traced here: 110 us
  starting transfers between devices  41.7 us (37%)
  Pallas kernels  41.6 us (37%)
  waiting for transfers between devices  23.5 us (21%)
  local copies, waits for them, and re-layouts  2.24 us (2%)
    pallas_call x15, Pallas kernels, go(): run(*[pin(a, spaces[p]) if p in spaces else a for a, p in zip(args, specs...  41.6 us
    all_to_all x2, waiting for transfers between devices, all_to_all(): return lax.all_to_all(value, axis, 0, 0, tiled=True)  16.4 us
    all_to_all x2, starting transfers between devices, all_to_all(): return lax.all_to_all(value, axis, 0, 0, tiled=True)  13.4 us
    ppermute x4, starting transfers between devices, hear(): return lax.ppermute(value, ('dp', 'core'), shifts(first, second))  9.68 us
    ppermute x6, starting transfers between devices, around(): lax.ppermute(value, axis, [(i, move(i, d)) for i in range(count)])  9.1 us
    ppermute x3, starting transfers between devices, around_by_sides(): swapped = [lax.ppermute(part, 'core', [(0, 1), (1, 0)]) for part in heard]  3.17 us
    ppermute x6, waiting for transfers between devices, around(): lax.ppermute(value, axis, [(i, move(i, d)) for i in range(count)])  2.84 us
    ppermute x1, starting transfers between devices, local(): after = lax.ppermute(first, CTX, [(i + 1, i) for i in range(devices - 1)])  2.8 us
  transfers between devices with their start and end apart: 22, of which 11 were waited for; matrix products, arithmetic and copies ran while one was open for 0% of the time, Pallas kernels for 29%

profile of v7, /device:TPU:2, one launch (start us, length us, event | category | flops | bytes accessed | tf_op | source)
XLA Modules:
  0.0 109.7 jit_solution(12025924601358281070)
XLA Ops:
  0.6 0.9 slice_bitcast_fusion
  1.5 1.9 %collective-permute-start = (bf16[3,5120]{1,0:T(4,128)(2,1)S(1)}, bf16[3,5120]{1,0:T(4,128)(2,1)S(1)}, u32[]{:S(2)}, u32[]{:S(2)}) collective-permute-start(bf16[3,5120]{1,0:T(4,128)(2,1)S(1)} %slice_bitcast_fusion), channel_id=1, source_target_pairs={{0,1},{1,2},{2,3},{3,4},{4,5},{5,6},{6,7},{7,8},{8,9},{9,10},{10,1... | collective-permute-start | bytes 92168 | tf_op jit(solution)/shard_map/ppermute | solution.py:1013
  3.5 4.2 %begin.1 = (f32[512,128]{1,0:T(8,128)}, f32[512,128]{1,0:T(8,128)S(1)}, f32[32,128]{1,0:T(8,128)S(1)}, bf16[128,4096]{1,0:T(8,128)(2,1)S(1)}, bf16[128,1024]{1,0...) custom-call(f32[64,128]{1,0:T(8,128)} %bitcast.25, ...), custom_call_target="tpu_custom_call" | custom-call | flops 4000000000 | bytes 14400000 | tf_op jit(solution)/shard_map/begin/pallas_call | solution.py:97
  7.7 1.3 %collective-permute-done.halo_ref = bf16[3,5120]{1,0:T(4,128)(2,1)S(1)} collective-permute-done((bf16[3,5120]{1,0:T(4,128)(2,1)S(1)}, bf16[3,5120]{1,0:T(4,128)(2,1)S(1)}, u32[]{:S(2)}, u32[]{:S(2)}) %collective-permute-start) | collective-permute-done | bytes 30752 | tf_op jit(solution)/shard_map/ppermute | solution.py:1013
  9.0 2.4 %enter.1 = (bf16[128,4096]{1,0:T(8,128)(2,1)}, bf16[128,1024]{1,0:T(8,128)(2,1)}, f32[8,5120]{1,0:T(8,128)}, bf16[128,4096]{1,0:T(8,128)(2,1)S(1)}, bf16[128,102...) custom-call(s32[1]{0:T(128)} %bitcast.core_ref, bf16[128,4096]{1,0:T(8,128)(2,1)S(1)} %get-tuple-element.102.x0_ref, ...), custom_call_target="tpu_custom_call" | custom-call | flops 3000000000 | bytes 10800000 | tf_op jit(solution)/shard_map/enter/pallas_call | solution.py:97
  11.4 0.5 collective-permute-start.1
  11.9 0.1 collective-permute-start.2
  12.0 1.6 %own.1.own_ref = bf16[2,16,128,128]{3,2,1,0:T(8,128)(2,1)S(1)} custom-call(s32[1]{0:T(128)} %bitcast.core_ref, bf16[128,4096]{1,0:T(8,128)(2,1)S(1)} %get-tuple-element.109.x_ref, bf16[128,1024]{1,0:T(8,128)(2,1)S(1)} %get-tuple-element.110.bc_ref, bf16[128,4096]{1,0:T(8,128)(2,1)S(1)} %get-tuple-element.106.g_ref, f32[512,128]{1,0:T(8,128)S(1)} %get-tuple-element.107.small_ref), custom_call_target="tpu_custom_call" | custom-call | flops 3000000000 | bytes 10800000 | tf_op jit(solution)/shard_map/own/pallas_call | solution.py:97
  13.6 0.6 collective-permute-done.2.other_ref
  14.2 1.4 %pack.1 = (bf16[16,272,128]{2,1,0:T(8,128)(2,1)}, bf16[16,128,128]{2,1,0:T(8,128)(2,1)}, bf16[16,128,128]{2,1,0:T(8,128)(2,1)}, f32[64,128]{1,0:T(8,128)}) custom-call(s32[1]{0:T(128)} %bitcast.core_ref, bf16[2,16,128,128]{3,2,1,0:T(8,128)(2,1)S(1)} %own.1.own_ref, bf16[2,16,128,128]{3,2,1,0:T(8,128)(2,1)S(1)} %collective-permute-done.1.got_ref, ...), custom_call_target="tpu_custom_call" | custom-call | flops 2000000000 | bytes 7200000 | tf_op jit(solution)/shard_map/pack/pallas_call | solution.py:97
  15.6 7.2 %all-to-all-start = ((bf16[16,272,128]{2,1,0:T(8,128)(2,1)}), bf16[16,272,128]{2,1,0:T(8,128)(2,1)S(1)}, u32[]{:S(2)}, u32[]{:S(2)}) async-start(bf16[16,272,128]{2,1,0:T(8,128)(2,1)} %get-tuple-element.113), calls=%async_computation | async-start | bytes 2228224 | tf_op jit(solution)/shard_map/all_to_all | solution.py:967
  22.8 5.6 %inner.1 = (f32[128,4096]{1,0:T(8,128)}, f32[128,1024]{1,0:T(8,128)}, f32[32,128]{1,0:T(8,128)}) custom-call(bf16[128,4096]{1,0:T(8,128)(2,1)} %get-tuple-element.114.x_h.rest_0_.rest_21_, bf16[128,1024]{1,0:T(8,128)(2,1)} %get-tuple-element.121.bc_h.rest_6_.rest_27_, bf16[128,4096]{1,0:T(8,128)(2,1)} %bitcast.21, f32[512,128]{1,0:T(8,128)} %get-tuple-element.115.small_h.rest_9_), custom_call_target="tpu_custom_call" | custom-call | flops 4000000000 | bytes 14400000 | tf_op jit(solution)/shard_map/inner/pallas_call | solution.py:97
  28.5 10.8 %all-to-all-done.in_ref = bf16[16,272,128]{2,1,0:T(8,128)(2,1)S(1)} async-done(((bf16[16,272,128]{2,1,0:T(8,128)(2,1)}), bf16[16,272,128]{2,1,0:T(8,128)(2,1)S(1)}, u32[]{:S(2)}, u32[]{:S(2)}) %all-to-all-start) | async-done | bytes 1114144 | tf_op jit(solution)/shard_map/all_to_all | solution.py:967
  39.3 1.3 %chain.1 = bf16[16,256,128]{2,1,0:T(8,128)(2,1)} custom-call(bf16[16,272,128]{2,1,0:T(8,128)(2,1)S(1)} %all-to-all-done.in_ref), custom_call_target="tpu_custom_call" | custom-call | flops 1000000000 | bytes 3600000 | tf_op jit(solution)/shard_map/chain/pallas_call | solution.py:97
  40.6 6.2 %all-to-all-start.1 = ((bf16[16,256,128]{2,1,0:T(8,128)(2,1)}), bf16[16,256,128]{2,1,0:T(8,128)(2,1)S(1)}, u32[]{:S(2)}, u32[]{:S(2)}) async-start(bf16[16,256,128]{2,1,0:T(8,128)(2,1)} %chain.1), calls=%async_computation.1 | async-start | bytes 2097152 | tf_op jit(solution)/shard_map/all_to_all | solution.py:967
  46.8 8.7 %slopes.1 = (f32[128,4096]{1,0:T(8,128)}, f32[128,5120]{1,0:T(8,128)}) custom-call(bf16[128,1024]{1,0:T(8,128)(2,1)} %get-tuple-element.121.bc_h.rest_6_.rest_27_, bf16[128,4096]{1,0:T(8,128)(2,1)} %bitcast.22, f32[512,128]{1,0:T(8,128)} %get-tuple-element.115.small_h.rest_9_, bf16[128,5120]{1,0:T(8,128)(2,1)} %bitcast.17, ...), custom_call_target="tpu_custom_call" | custom-call | flops 6000000000 | bytes 21600000 | tf_op jit(solution)/shard_map/slopes/pallas_call | solution.py:97
  55.5 5.6 %all-to-all-done.1.back_ref = bf16[16,256,128]{2,1,0:T(8,128)(2,1)S(1)} async-done(((bf16[16,256,128]{2,1,0:T(8,128)(2,1)}), bf16[16,256,128]{2,1,0:T(8,128)(2,1)S(1)}, u32[]{:S(2)}, u32[]{:S(2)}) %all-to-all-start.1) | async-done | bytes 1048608 | tf_op jit(solution)/shard_map/all_to_all | solution.py:967
  61.1 3.8 %unpack.1 = (bf16[2,16,128,128]{3,2,1,0:T(8,128)(2,1)S(1)}, bf16[2,16,128,128]{3,2,1,0:T(8,128)(2,1)S(1)}, bf16[128,1024]{1,0:T(8,128)(2,1)S(1)}, bf16[128,1024]...) custom-call(s32[1]{0:T(128)} %bitcast.core_ref, ...), custom_call_target="tpu_custom_call" | custom-call | flops 3000000000 | bytes 10800000 | tf_op jit(solution)/shard_map/unpack/pallas_call | solution.py:97
  64.9 0.3 collective-permute-start.3
  65.2 4.2 %leave.2 = (bf16[128,4096]{1,0:T(8,128)(2,1)}, f32[64,128]{1,0:T(8,128)}, f32[128,2560]{1,0:T(8,128)S(1)}, f32[128,128]{1,0:T(8,128)S(1)}, bf16[128,1024]{1,0:T(...) custom-call(s32[1]{0:T(128)} %bitcast.core_ref, ...), custom_call_target="tpu_custom_call" | custom-call | flops 5000000000 | bytes 18000000 | tf_op jit(solution)/shard_map/leave/pallas_call | solution.py:97
  69.4 0.5 collective-permute-start.4
  70.0 4.2 %leave.3 = (bf16[128,4096]{1,0:T(8,128)(2,1)}, f32[64,128]{1,0:T(8,128)}, f32[128,2560]{1,0:T(8,128)S(1)}, f32[128,128]{1,0:T(8,128)S(1)}, bf16[3,5120]{1,0:T(4,128)(2,1)S(1)}) custom-call(s32[1]{0:T(128)} %bitcast.core_ref, bf16[2,16,128,128]{3,2,1,0:T(8,128)(2,1)S(1)} %collective-permute-done.3.state_ref, ...), custom_call_target="tpu_custom_call", output_to_operand_aliasing={{0}: (24, {}), {1}: (25, {})} | custom-call | flops 5000000000 | bytes 18000000 | tf_op jit(solution)/shard_map/leave/pallas_call | solution.py:97
  74.2 0.1 collective-permute-start.5
  74.3 1.2 %collective-permute-done.5.theirs_got_ref = f32[128,128]{1,0:T(8,128)S(1)} collective-permute-done((f32[128,128]{1,0:T(8,128)S(1)}, f32[128,128]{1,0:T(8,128)S(1)}, u32[]{:S(2)}, u32[]{:S(2)}) %collective-permute-start.5) | collective-permute-done | bytes 65568 | tf_op jit(solution)/shard_map/ppermute | solution.py:1042
  75.5 0.6 merge.1.rest_0_
  76.1 0.6 collective-permute-start.6
  76.7 2.2 %collective-permute-start.7 = (bf16[176,128]{1,0:T(8,128)(2,1)S(1)}, bf16[176,128]{1,0:T(8,128)(2,1)S(1)}, u32[]{:S(2)}, u32[]{:S(2)}) collective-permute-start(bf16[176,128]{1,0:T(8,128)(2,1)S(1)} %merge.1.rest_0_), channel_id=1, source_target_pairs={{0,4},{2,6},{4,0},{6,2},{8,12},{10,14},{12,8},{14,10},{16,20},{18,... | collective-permute-start | bytes 135176 | tf_op jit(solution)/shard_map/ppermute | solution.py:979
  78.9 1.8 %collective-permute-start.8 = (bf16[176,128]{1,0:T(8,128)(2,1)S(1)}, bf16[176,128]{1,0:T(8,128)(2,1)S(1)}, u32[]{:S(2)}, u32[]{:S(2)}) collective-permute-start(bf16[176,128]{1,0:T(8,128)(2,1)S(1)} %merge.1.rest_0_), channel_id=1, source_target_pairs={{0,6},{2,0},{4,2},{6,4},{8,14},{10,8},{12,10},{14,12},{16,22},{18,... | collective-permute-start | bytes 135176 | tf_op jit(solution)/shard_map/ppermute | solution.py:979
  80.6 1.1 collective-permute-done.6.rest_1_
  81.7 0.5 collective-permute-done.7.rest_2_
  82.2 0.7 collective-permute-done.8.rest_3_
  83.0 1.3 %collective-permute-start.9 = (bf16[176,128]{1,0:T(8,128)(2,1)S(1)}, bf16[176,128]{1,0:T(8,128)(2,1)S(1)}, u32[]{:S(2)}, u32[]{:S(2)}) collective-permute-start(bf16[176,128]{1,0:T(8,128)(2,1)S(1)} %fold.2.rest_0_), channel_id=1, source_target_pairs={{0,8},{2,10},{4,12},{6,14},{8,16},{10,18},{12,20},{14,22},{16,24},... | collective-permute-start | bytes 135176 | tf_op jit(solution)/shard_map/ppermute | solution.py:979
  84.2 2.6 %collective-permute-start.10 = (bf16[176,128]{1,0:T(8,128)(2,1)S(1)}, bf16[176,128]{1,0:T(8,128)(2,1)S(1)}, u32[]{:S(2)}, u32[]{:S(2)}) collective-permute-start(bf16[176,128]{1,0:T(8,128)(2,1)S(1)} %fold.2.rest_0_), channel_id=1, source_target_pairs={{0,16},{2,18},{4,20},{6,22},{8,24},{10,26},{12,28},{14,30},{16,0},... | collective-permute-start | bytes 135176 | tf_op jit(solution)/shard_map/ppermute | solution.py:979
  86.9 0.7 collective-permute-start.11
  87.5 2.8 %collective-permute-start.12 = (bf16[3,5120]{1,0:T(4,128)(2,1)S(1)}, bf16[3,5120]{1,0:T(4,128)(2,1)S(1)}, u32[]{:S(2)}, u32[]{:S(2)}) collective-permute-start(bf16[3,5120]{1,0:T(4,128)(2,1)S(1)} %get-tuple-element.181), channel_id=1, source_target_pairs={{1,0},{2,1},{3,2},{4,3},{5,4},{6,5},{7,6},{8,7},{9,8},{10,9},{11,1... | collective-permute-start | bytes 92168 | tf_op jit(solution)/shard_map/ppermute | solution.py:1047
  90.4 0.6 collective-permute-done.11.rest_3_
  91.0 1.0 collective-permute-done.12.halo_ref
  92.0 1.9 %collective-permute-start.13 = (bf16[176,128]{1,0:T(8,128)(2,1)S(1)}, bf16[176,128]{1,0:T(8,128)(2,1)S(1)}, u32[]{:S(2)}, u32[]{:S(2)}) collective-permute-start(bf16[176,128]{1,0:T(8,128)(2,1)S(1)} %fold.3.rest_0_), channel_id=1, source_target_pairs={{0,32},{1,225},{32,64},{33,1},{64,96},{65,33},{96,128},{97,65},{12... | collective-permute-start | bytes 135176 | tf_op jit(solution)/shard_map/ppermute | solution.py:992
  93.9 3.3 %collective-permute-start.14 = (bf16[176,128]{1,0:T(8,128)(2,1)S(1)}, bf16[176,128]{1,0:T(8,128)(2,1)S(1)}, u32[]{:S(2)}, u32[]{:S(2)}) collective-permute-start(bf16[176,128]{1,0:T(8,128)(2,1)S(1)} %fold.3.rest_0_), channel_id=1, source_target_pairs={{0,64},{1,193},{32,96},{33,225},{64,128},{65,1},{96,160},{97,33},{... | collective-permute-start | bytes 135176 | tf_op jit(solution)/shard_map/ppermute | solution.py:992
  97.2 3.8 %collective-permute-start.15 = (bf16[176,128]{1,0:T(8,128)(2,1)S(1)}, bf16[176,128]{1,0:T(8,128)(2,1)S(1)}, u32[]{:S(2)}, u32[]{:S(2)}) collective-permute-start(bf16[176,128]{1,0:T(8,128)(2,1)S(1)} %fold.3.rest_0_), channel_id=1, source_target_pairs={{0,96},{1,161},{32,128},{33,193},{64,160},{65,225},{96,192},{97,1}... | collective-permute-start | bytes 135176 | tf_op jit(solution)/shard_map/ppermute | solution.py:992
  100.9 0.7 collective-permute-start.19
  101.7 2.8 %collective-permute-start.16 = (bf16[176,128]{1,0:T(8,128)(2,1)S(1)}, bf16[176,128]{1,0:T(8,128)(2,1)S(1)}, u32[]{:S(2)}, u32[]{:S(2)}) collective-permute-start(bf16[176,128]{1,0:T(8,128)(2,1)S(1)} %collective-permute-done.13.rest_1_), channel_id=1, source_target_pairs={{0,1},{1,0},{2,3},{3,2},{4,5},{5,4},{6,7},{7,6},{8,9},{9,8},{10,11... | collective-permute-start | bytes 135176 | tf_op jit(solution)/shard_map/ppermute | solution.py:996
  104.4 0.1 collective-permute-start.17
  104.5 0.1 collective-permute-done.15.rest_3_
  104.7 0.3 collective-permute-start.18
  105.0 1.3 %copy-done.1 = f32[128,2560]{1,0:T(8,128)S(1)} copy-done((f32[128,2560]{1,0:T(8,128)S(1)}, f32[128,2560]{1,0:T(8,128)}, u32[]{:S(2)}) %copy-start.1) | copy-done | bytes 1310744
  106.3 2.7 %spread.1 = bf16[128,5120]{1,0:T(8,128)(2,1)} custom-call(s32[1]{0:T(128)} %bitcast.core_ref, f32[128,2560]{1,0:T(8,128)S(1)} %get-tuple-element.173.rest_21_.own_ref, f32[128,2560]{1,0:T(8,128)S(1)} %copy-done.1, bf16[3,5120]{1,0:T(4,128)(2,1)S(1)} %collective-permute-done.12.halo_ref, f32[4,5120]{1,0:T(4,128)S(1)} %get-tuple-element.156.rest_20_.weight_ref), custom_call_target="tpu_custom_call" | custom-call | flops 3000000000 | bytes 10800000 | tf_op jit(solution)/shard_map/spread/pallas_call | solution.py:97
  109.0 0.7 finish.1
  (16 shorter events, 0.1 us)
Async XLA Ops:
  1.5 7.4 %collective-permute-start = (bf16[3,5120]{1,0:T(4,128)(2,1)S(1)}, bf16[3,5120]{1,0:T(4,128)(2,1)S(1)}, u32[]{:S(2)}, u32[]{:S(2)}) collective-permute-start(bf16[3,5120]{1,0:T(4,128)(2,1)S(1)} %slice_bitcast_fusion), channel_id=1, source_target_pairs={{0,1},{1,2},{2,3},{3,4},{4,5},{5,6},{6,7},{7,8},{8,9},{9,10},{10,1... | collective-permute-start | bytes 92168 | tf_op jit(solution)/shard_map/ppermute | solution.py:1013
  11.4 2.8 %collective-permute-start.1 = (bf16[2,16,128,128]{3,2,1,0:T(8,128)(2,1)S(1)}, bf16[2,16,128,128]{3,2,1,0:T(8,128)(2,1)S(1)}, u32[]{:S(2)}, u32[]{:S(2)}) collective-permute-start(bf16[2,16,128,128]{3,2,1,0:T(8,128)(2,1)S(1)} %get-tuple-element.111), channel_id=1, source_target_pairs={{0,1},{1,0},{2,3},{3,2},{4,5},{5,4},{6,7},{7,6},{8,9},{9,8},{10,11... | collective-permute-start | bytes 3145736 | tf_op jit(solution)/shard_map/ppermute | solution.py:1021
  11.9 2.3 %collective-permute-start.2 = (f32[32,128]{1,0:T(8,128)S(1)}, f32[32,128]{1,0:T(8,128)S(1)}, u32[]{:S(2)}, u32[]{:S(2)}) collective-permute-start(f32[32,128]{1,0:T(8,128)S(1)} %get-tuple-element.112.tot_ref), channel_id=1, source_target_pairs={{0,1},{1,0},{2,3},{3,2},{4,5},{5,4},{6,7},{7,6},{8,9},{9,8},{10,11... | collective-permute-start | bytes 49160 | tf_op jit(solution)/shard_map/ppermute | solution.py:1017
  15.6 23.7 %all-to-all-start = ((bf16[16,272,128]{2,1,0:T(8,128)(2,1)}), bf16[16,272,128]{2,1,0:T(8,128)(2,1)S(1)}, u32[]{:S(2)}, u32[]{:S(2)}) async-start(bf16[16,272,128]{2,1,0:T(8,128)(2,1)} %get-tuple-element.113), calls=%async_computation | async-start | bytes 2228224 | tf_op jit(solution)/shard_map/all_to_all | solution.py:967
  40.6 20.5 %all-to-all-start.1 = ((bf16[16,256,128]{2,1,0:T(8,128)(2,1)}), bf16[16,256,128]{2,1,0:T(8,128)(2,1)S(1)}, u32[]{:S(2)}, u32[]{:S(2)}) async-start(bf16[16,256,128]{2,1,0:T(8,128)(2,1)} %chain.1), calls=%async_computation.1 | async-start | bytes 2097152 | tf_op jit(solution)/shard_map/all_to_all | solution.py:967
  64.9 5.1 %collective-permute-start.3 = (bf16[2,16,128,128]{3,2,1,0:T(8,128)(2,1)S(1)}, bf16[2,16,128,128]{3,2,1,0:T(8,128)(2,1)S(1)}, u32[]{:S(2)}, u32[]{:S(2)}) collective-permute-start(bf16[2,16,128,128]{3,2,1,0:T(8,128)(2,1)S(1)} %get-tuple-element.134), channel_id=1, source_target_pairs={{0,1},{1,0},{2,3},{3,2},{4,5},{5,4},{6,7},{7,6},{8,9},{9,8},{10,11... | collective-permute-start | bytes 3145736 | tf_op jit(solution)/shard_map/ppermute | solution.py:1036
  69.4 4.9 %collective-permute-start.4 = (f32[128,128]{1,0:T(8,128)S(1)}, f32[128,128]{1,0:T(8,128)S(1)}, u32[]{:S(2)}, u32[]{:S(2)}) collective-permute-start(f32[128,128]{1,0:T(8,128)S(1)} %get-tuple-element.177.own_ref), channel_id=1, source_target_pairs={{0,1},{1,0},{2,3},{3,2},{4,5},{5,4},{6,7},{7,6},{8,9},{9,8},{10,11... | collective-permute-start | bytes 196616 | tf_op jit(solution)/shard_map/ppermute | solution.py:1038
  74.2 1.9 %copy-start = (f32[128,2560]{1,0:T(8,128)}, f32[128,2560]{1,0:T(8,128)S(1)}, u32[]{:S(2)}) copy-start(f32[128,2560]{1,0:T(8,128)S(1)} %get-tuple-element.183.theirs_ref) | copy-start | bytes 3932164
  74.2 1.3 %collective-permute-start.5 = (f32[128,128]{1,0:T(8,128)S(1)}, f32[128,128]{1,0:T(8,128)S(1)}, u32[]{:S(2)}, u32[]{:S(2)}) collective-permute-start(f32[128,128]{1,0:T(8,128)S(1)} %get-tuple-element.178.theirs_ref), channel_id=1, source_target_pairs={{0,1},{1,0},{2,3},{3,2},{4,5},{5,4},{6,7},{7,6},{8,9},{9,8},{10,11... | collective-permute-start | bytes 196616 | tf_op jit(solution)/shard_map/ppermute | solution.py:1042
  76.1 5.6 %collective-permute-start.6 = (bf16[176,128]{1,0:T(8,128)(2,1)S(1)}, bf16[176,128]{1,0:T(8,128)(2,1)S(1)}, u32[]{:S(2)}, u32[]{:S(2)}) collective-permute-start(bf16[176,128]{1,0:T(8,128)(2,1)S(1)} %merge.1.rest_0_), channel_id=1, source_target_pairs={{0,2},{2,4},{4,6},{6,0},{8,10},{10,12},{12,14},{14,8},{16,18},{18,... | collective-permute-start | bytes 135176 | tf_op jit(solution)/shard_map/ppermute | solution.py:979
  76.7 5.6 %collective-permute-start.7 = (bf16[176,128]{1,0:T(8,128)(2,1)S(1)}, bf16[176,128]{1,0:T(8,128)(2,1)S(1)}, u32[]{:S(2)}, u32[]{:S(2)}) collective-permute-start(bf16[176,128]{1,0:T(8,128)(2,1)S(1)} %merge.1.rest_0_), channel_id=1, source_target_pairs={{0,4},{2,6},{4,0},{6,2},{8,12},{10,14},{12,8},{14,10},{16,20},{18,... | collective-permute-start | bytes 135176 | tf_op jit(solution)/shard_map/ppermute | solution.py:979
  78.9 4.0 %collective-permute-start.8 = (bf16[176,128]{1,0:T(8,128)(2,1)S(1)}, bf16[176,128]{1,0:T(8,128)(2,1)S(1)}, u32[]{:S(2)}, u32[]{:S(2)}) collective-permute-start(bf16[176,128]{1,0:T(8,128)(2,1)S(1)} %merge.1.rest_0_), channel_id=1, source_target_pairs={{0,6},{2,0},{4,2},{6,4},{8,14},{10,8},{12,10},{14,12},{16,22},{18,... | collective-permute-start | bytes 135176 | tf_op jit(solution)/shard_map/ppermute | solution.py:979
  83.0 7.4 %collective-permute-start.9 = (bf16[176,128]{1,0:T(8,128)(2,1)S(1)}, bf16[176,128]{1,0:T(8,128)(2,1)S(1)}, u32[]{:S(2)}, u32[]{:S(2)}) collective-permute-start(bf16[176,128]{1,0:T(8,128)(2,1)S(1)} %fold.2.rest_0_), channel_id=1, source_target_pairs={{0,8},{2,10},{4,12},{6,14},{8,16},{10,18},{12,20},{14,22},{16,24},... | collective-permute-start | bytes 135176 | tf_op jit(solution)/shard_map/ppermute | solution.py:979
  84.2 6.1 %collective-permute-start.10 = (bf16[176,128]{1,0:T(8,128)(2,1)S(1)}, bf16[176,128]{1,0:T(8,128)(2,1)S(1)}, u32[]{:S(2)}, u32[]{:S(2)}) collective-permute-start(bf16[176,128]{1,0:T(8,128)(2,1)S(1)} %fold.2.rest_0_), channel_id=1, source_target_pairs={{0,16},{2,18},{4,20},{6,22},{8,24},{10,26},{12,28},{14,30},{16,0},... | collective-permute-start | bytes 135176 | tf_op jit(solution)/shard_map/ppermute | solution.py:979
  86.9 4.0 %collective-permute-start.11 = (bf16[176,128]{1,0:T(8,128)(2,1)S(1)}, bf16[176,128]{1,0:T(8,128)(2,1)S(1)}, u32[]{:S(2)}, u32[]{:S(2)}) collective-permute-start(bf16[176,128]{1,0:T(8,128)(2,1)S(1)} %fold.2.rest_0_), channel_id=1, source_target_pairs={{0,24},{2,26},{4,28},{6,30},{8,0},{10,2},{12,4},{14,6},{16,8},{18,... | collective-permute-start | bytes 135176 | tf_op jit(solution)/shard_map/ppermute | solution.py:979
  87.5 4.5 %collective-permute-start.12 = (bf16[3,5120]{1,0:T(4,128)(2,1)S(1)}, bf16[3,5120]{1,0:T(4,128)(2,1)S(1)}, u32[]{:S(2)}, u32[]{:S(2)}) collective-permute-start(bf16[3,5120]{1,0:T(4,128)(2,1)S(1)} %get-tuple-element.181), channel_id=1, source_target_pairs={{1,0},{2,1},{3,2},{4,3},{5,4},{6,5},{7,6},{8,7},{9,8},{10,9},{11,1... | collective-permute-start | bytes 92168 | tf_op jit(solution)/shard_map/ppermute | solution.py:1047
  92.0 9.7 %collective-permute-start.13 = (bf16[176,128]{1,0:T(8,128)(2,1)S(1)}, bf16[176,128]{1,0:T(8,128)(2,1)S(1)}, u32[]{:S(2)}, u32[]{:S(2)}) collective-permute-start(bf16[176,128]{1,0:T(8,128)(2,1)S(1)} %fold.3.rest_0_), channel_id=1, source_target_pairs={{0,32},{1,225},{32,64},{33,1},{64,96},{65,33},{96,128},{97,65},{12... | collective-permute-start | bytes 135176 | tf_op jit(solution)/shard_map/ppermute | solution.py:992
  93.9 10.5 %collective-permute-start.14 = (bf16[176,128]{1,0:T(8,128)(2,1)S(1)}, bf16[176,128]{1,0:T(8,128)(2,1)S(1)}, u32[]{:S(2)}, u32[]{:S(2)}) collective-permute-start(bf16[176,128]{1,0:T(8,128)(2,1)S(1)} %fold.3.rest_0_), channel_id=1, source_target_pairs={{0,64},{1,193},{32,96},{33,225},{64,128},{65,1},{96,160},{97,33},{... | collective-permute-start | bytes 135176 | tf_op jit(solution)/shard_map/ppermute | solution.py:992
  97.2 7.5 %collective-permute-start.15 = (bf16[176,128]{1,0:T(8,128)(2,1)S(1)}, bf16[176,128]{1,0:T(8,128)(2,1)S(1)}, u32[]{:S(2)}, u32[]{:S(2)}) collective-permute-start(bf16[176,128]{1,0:T(8,128)(2,1)S(1)} %fold.3.rest_0_), channel_id=1, source_target_pairs={{0,96},{1,161},{32,128},{33,193},{64,160},{65,225},{96,192},{97,1}... | collective-permute-start | bytes 135176 | tf_op jit(solution)/shard_map/ppermute | solution.py:992
  100.9 8.0 %collective-permute-start.19 = (bf16[176,128]{1,0:T(8,128)(2,1)S(1)}, bf16[176,128]{1,0:T(8,128)(2,1)S(1)}, u32[]{:S(2)}, u32[]{:S(2)}) collective-permute-start(bf16[176,128]{1,0:T(8,128)(2,1)S(1)} %fold.3.rest_0_), channel_id=1, source_target_pairs={{0,128},{1,129},{32,160},{33,161},{64,192},{65,193},{96,224},{97,2... | collective-permute-start | bytes 135176 | tf_op jit(solution)/shard_map/ppermute | solution.py:992
  101.7 7.3 %collective-permute-start.16 = (bf16[176,128]{1,0:T(8,128)(2,1)S(1)}, bf16[176,128]{1,0:T(8,128)(2,1)S(1)}, u32[]{:S(2)}, u32[]{:S(2)}) collective-permute-start(bf16[176,128]{1,0:T(8,128)(2,1)S(1)} %collective-permute-done.13.rest_1_), channel_id=1, source_target_pairs={{0,1},{1,0},{2,3},{3,2},{4,5},{5,4},{6,7},{7,6},{8,9},{9,8},{10,11... | collective-permute-start | bytes 135176 | tf_op jit(solution)/shard_map/ppermute | solution.py:996
  104.4 4.6 %collective-permute-start.17 = (bf16[176,128]{1,0:T(8,128)(2,1)S(1)}, bf16[176,128]{1,0:T(8,128)(2,1)S(1)}, u32[]{:S(2)}, u32[]{:S(2)}) collective-permute-start(bf16[176,128]{1,0:T(8,128)(2,1)S(1)} %collective-permute-done.14.rest_2_), channel_id=1, source_target_pairs={{0,1},{1,0},{2,3},{3,2},{4,5},{5,4},{6,7},{7,6},{8,9},{9,8},{10,11... | collective-permute-start | bytes 135176 | tf_op jit(solution)/shard_map/ppermute | solution.py:996
  104.7 4.4 %collective-permute-start.18 = (bf16[176,128]{1,0:T(8,128)(2,1)S(1)}, bf16[176,128]{1,0:T(8,128)(2,1)S(1)}, u32[]{:S(2)}, u32[]{:S(2)}) collective-permute-start(bf16[176,128]{1,0:T(8,128)(2,1)S(1)} %collective-permute-done.15.rest_3_), channel_id=1, source_target_pairs={{0,1},{1,0},{2,3},{3,2},{4,5},{5,4},{6,7},{7,6},{8,9},{9,8},{10,11... | collective-permute-start | bytes 135176 | tf_op jit(solution)/shard_map/ppermute | solution.py:996
  105.0 1.3 %copy-start.1 = (f32[128,2560]{1,0:T(8,128)S(1)}, f32[128,2560]{1,0:T(8,128)}, u32[]{:S(2)}) copy-start(f32[128,2560]{1,0:T(8,128)} %copy-done) | copy-start | bytes 3932164

commit v8 on v7

--- a/solution.py
+++ b/solution.py
@@ -446,8 +446,7 @@
     far, rest = rest[: len(NEAR)], rest[len(NEAR) :]
     common_far, rest = rest[: len(COMMON)], rest[len(COMMON) :]
     mine_ref, send_ref, *rest = rest
-    near = [rest[i * len(NEAR) : (i + 1) * len(NEAR)] for i in range(HALF_GROUPS)]
-    rest = rest[HALF_GROUPS * len(NEAR) :]
+    near, rest = rest[: len(NEAR)], rest[len(NEAR) :]
     common, rest = rest[: len(COMMON)], rest[len(COMMON) :]
     left_ref, right_ref, tots_ref, sems, fetch_sems = rest
     first = start_all([(tots_h, tots_ref)], sems.at[STEPS])
@@ -457,9 +456,8 @@
         steps.append(
             start_all([(left_h.at[at], left_ref.at[at]), (right_h.at[at], right_ref.at[at])], sems.at[step])
         )
-    fetches = start_all(list(zip(common_far, common)), fetch_sems.at[HALF_GROUPS])
-    for jj in range(HALF_GROUPS):
-        fetches += fetch_group(core_ref[0] * HALF_GROUPS + jj, far, near[jj], fetch_sems.at[jj])
+    fetches = start_all(list(zip(common_far, common)), fetch_sems.at[1])
+    fetches += fetch_group(core_ref[0] * HALF_GROUPS, far, near, fetch_sems.at[0])
     wait_all(first)
     second = core_ref[0] == 1
     for i in range(HALF_PAIRS):
@@ -483,19 +481,19 @@
 
 def run_unpack(core, back, left, right, tots, far, common):
     half = (2, HALF_PAIRS, STATE, LANES)
-    out = [("V", half, BF16)] * 2 + NEAR * HALF_GROUPS + COMMON
+    out = [("V", half, BF16)] * 2 + NEAR + COMMON
     scratch = [
         pltpu.VMEM(half[1:], BF16),
         pltpu.VMEM(half[1:], BF16),
         pltpu.VMEM((2 * PAIRS, LANES), F32),
         DMA(STEPS + 1, 2),
-        DMA(HALF_GROUPS + 1, FETCHES),
+        DMA(2, FETCHES),
     ]
     specs = "svhhh" + "h" * (len(NEAR) + len(COMMON))
     outs = call(unpack_kernel, "unpack", out, specs, 3, scratch, mib=8)(
         core, back, left, right, tots, *far, *common
     )
-    at = 2 + HALF_GROUPS * len(NEAR)
+    at = 2 + len(NEAR)
     return outs[0], outs[1], outs[2:at], outs[at:]
 
 
@@ -667,27 +665,27 @@
         del rest[:count]
         return taken
 
-    sets = [take(len(NEAR)) for _ in range(HALF_GROUPS)]
+    sets = [take(len(NEAR))]
     before_ref, small_ref, raw_ref, skips_ref, _ = take(len(COMMON))
+    far = take(len(NEAR))
     half = 1 - core_ref[0] if theirs else core_ref[0]
-    fetches = []
     if theirs:
-        pre_own_ref, _, _ = take(3)
-        out_h, step_h, pre_ref, sum_ref, first_ref = take(5)
-        head_ref, out_ref, step_ref, win_ref, sems = rest
+        take(3)
+        out_h, pre_h, step_h, sum_ref, first_ref = take(5)
+        head_ref, = take(1)
+    else:
+        out_h, pre_h, step_h, sum_ref = take(4)
+        after = take(len(NEAR))
+    sets.append(take(len(NEAR)))
+    out_ref, pre_ref, step_ref, win_ref, sems = rest
+    arrivals = fetch_group(half * HALF_GROUPS + 1, far, sets[1], sems.at[2])
+    if theirs:
         own = core_ref[0]
-        head_ref[:, span(own, HALF_X)] = pre_own_ref[0:8, 0:HALF_X]
         size = HALF_GROUPS * STATE
-        for base in range(2):
-            at = HALF_X + base * size
-            head_ref[:, span(WIDTH_X // size + 2 * base + own, size)] = pre_own_ref[0:8, at : at + size]
+        pieces = [span(own, HALF_X)] + [span(WIDTH_X // size + 2 * base + own, size) for base in range(2)]
+        fetches = start_all([(pre_h.at[pl.ds(0, 8), at], head_ref.at[:, at]) for at in pieces], sems.at[3])
     else:
-        far = take(len(NEAR))
-        out_h, step_h, pre_ref, sum_ref = take(4)
-        after = [take(len(NEAR)) for _ in range(HALF_GROUPS)]
-        out_ref, step_ref, win_ref, sems = rest
-        for jj in range(HALF_GROUPS):
-            fetches += fetch_group((1 - half) * HALF_GROUPS + jj, far, after[jj], sems.at[2 + jj])
+        fetches = fetch_group((1 - half) * HALF_GROUPS, far, after, sems.at[3])
     last = iota((8, 2 * LANES), 0) == 7
     lower = (iota((T, T), 0) >= iota((T, T), 1)).astype(F32)
 
@@ -711,6 +709,8 @@
     for jj in range(HALF_GROUPS):
         j = half * HALF_GROUPS + jj
         x_ref, g_ref, y_ref, gx_ref, slope_ref, tok_ref, bc_ref, gbc_ref = sets[jj]
+        if jj:
+            wait_all(arrivals)
         b = bc_ref[:, 0:STATE]
         c = bc_ref[:, STATE:]
         grad_b = gbc_ref[:, 0:STATE]
@@ -766,6 +766,7 @@
                 near_at = pl.ds(jj * GROUP_X + (q // 4) * size, size)
                 far_at = span(2 * j + q // 4, size)
                 save(out_ref.at[:, near_at], out_h.at[:, far_at])
+                save(pre_ref.at[:, near_at], pre_h.at[:, far_at])
         for grad, base in ((grad_b, 0), (grad_c, 1)):
             at = HALF_X + (base * HALF_GROUPS + jj) * STATE
             tail = slice(GROUP_X + base * STATE, GROUP_X + (base + 1) * STATE)
@@ -776,6 +777,7 @@
             if theirs:
                 head_ref[:, far_at] = grad_pre[0:8]
             terms += tap_sums(grad_pre, 0)
+            save(pre_ref.at[:, pl.ds(at, STATE)], pre_h.at[:, far_at])
         heads = span(j, GROUP_HEADS)
         behind = exact_dot(seg_grad, lower)
         dt = small_ref[pl.ds(pl.multiple_of(ROW_DT + j * GROUP_HEADS, GROUP_HEADS), GROUP_HEADS), :]
@@ -791,68 +793,67 @@
     wait_all(saves)
 
 
-def run_leave(core, state, near, common, far, before_out):
-    theirs = before_out is not None
+def run_leave(core, state, near, common, far, done):
+    theirs = done is not None
     out = [
         ("h", (T, WIDTH_X), BF16),
+        ("h", (T, CHANNELS), F32),
         ("h", (HEADS, T), F32),
-        ("V", (T, HALF_X + HALF_B), F32),
         ("V", (HALF_GROUPS * SUM_GROUP, LANES), F32),
     ]
-    scratch = [
+    scratch = [pltpu.VMEM(shape, dtype) for _, shape, dtype in NEAR] + [
         pltpu.VMEM((T, HALF_X), BF16),
+        pltpu.VMEM((T, HALF_X + HALF_B), F32),
         pltpu.VMEM((HALF_GROUPS * GROUP_HEADS, T), F32),
         pltpu.VMEM((8 + T, GROUP_X), F32),
-        DMA(2 + HALF_GROUPS, FETCHES),
+        DMA(4, FETCHES),
     ]
     args = [core, state, *near, *common, *far]
     specs = "s" + ("v" if theirs else "V") + "V" * (len(near) + len(COMMON)) + "h" * len(far)
     aliases = {}
     if theirs:
-        done, pre_own = before_out
-        args += [pre_own]
-        aliases = {len(args) + i: i for i in range(2)}
+        aliases = {len(args) + i: i for i in range(3)}
         args += done
-        specs += "Vhh"
+        specs += "hhh"
         out += [("V", (TAPS - 1, CHANNELS), BF16)]
         scratch = [pltpu.VMEM((8, CHANNELS), F32)] + scratch
     else:
-        out += NEAR * HALF_GROUPS
+        out += NEAR
     kernel = functools.partial(leave_kernel, theirs)
-    outs = call(kernel, "leave", out, specs, 5, scratch, mib=8, aliases=aliases)(*args)
-    return outs[:2], outs[2], outs[3], outs[4:]
-
-
-def spread_kernel(core_ref, own_ref, theirs_ref, halo_ref, weight_ref, out_h, out_ref, win_ref, sems):
+    outs = call(kernel, "leave", out, specs, 5, scratch, mib=12, aliases=aliases)(*args)
+    return outs[:3], outs[3], outs[4:]
+
+
+def spread_kernel(pre_h, halo_ref, weight_ref, out_h, pre_ref, out_ref, win_ref, sems):
+    blocks = [pl.ds(i * GROUP_X, GROUP_X) for i in range(BLOCKS)]
+    loads = start_all([(pre_h.at[:, at], pre_ref.at[:, at]) for at in blocks], sems.at[0])
     saves = []
-    size = HALF_GROUPS * STATE
-    for side, pre_ref in enumerate((own_ref, theirs_ref)):
-        half = 1 - core_ref[0] if side else core_ref[0]
-        blocks = [(jj * GROUP_X, span(half * HALF_GROUPS + jj, GROUP_X), GROUP_X) for jj in range(HALF_GROUPS)]
-        blocks += [
-            (HALF_X + base * size, span(WIDTH_X // size + 2 * base + half, size), size) for base in range(2)
-        ]
-        for near, far, width in blocks:
-            win_ref[0:T, 0:width] = pre_ref[:, near : near + width]
-            win_ref[T : T + TAPS - 1, 0:width] = halo_ref[:, far].astype(F32)
-            weights = weight_ref[:, far]
-            base = side * (HALF_X + HALF_B) + near
-            for lo in range(0, width, LANES):
-                at = slice(lo, lo + LANES)
-                acc = weights[0:1, at] * win_ref[3 : 3 + T, at]
-                for k in range(1, TAPS):
-                    acc = acc + weights[k : k + 1, at] * win_ref[3 - k : 3 - k + T, at]
-                out_ref[:, base + lo : base + lo + LANES] = acc.astype(BF16)
-            copy = pltpu.make_async_copy(out_ref.at[:, pl.ds(base, width)], out_h.at[:, far], sems.at[len(saves)])
-            copy.start()
-            saves.append(copy)
+    for i, load in enumerate(loads):
+        load.wait()
+        cols = slice(i * GROUP_X, (i + 1) * GROUP_X)
+        win_ref[0:T, :] = pre_ref[:, cols]
+        win_ref[T : T + TAPS - 1, :] = halo_ref[:, cols].astype(F32)
+        weights = weight_ref[:, cols]
+        for lo in range(0, GROUP_X, LANES):
+            at = slice(lo, lo + LANES)
+            acc = weights[0:1, at] * win_ref[3 : 3 + T, at]
+            for k in range(1, TAPS):
+                acc = acc + weights[k : k + 1, at] * win_ref[3 - k : 3 - k + T, at]
+            out_ref[:, i * GROUP_X + lo : i * GROUP_X + lo + LANES] = acc.astype(BF16)
+        saves.append(pltpu.make_async_copy(out_ref.at[:, blocks[i]], out_h.at[:, blocks[i]], sems.at[1, i]))
+        saves[-1].start()
     wait_all(saves)
 
 
-def run_spread(core, own, theirs, halo, weight):
+def run_spread(pre, halo, weight):
     out = [("h", (T, CHANNELS), BF16)]
-    scratch = [pltpu.VMEM((T, CHANNELS), BF16), pltpu.VMEM((T + 8, GROUP_X), F32), DMA(8)]
-    return call(spread_kernel, "spread", out, "sVVvV", 3, scratch, mib=6)(core, own, theirs, halo, weight)[0]
+    scratch = [
+        pltpu.VMEM((T, CHANNELS), F32),
+        pltpu.VMEM((T, CHANNELS), BF16),
+        pltpu.VMEM((T + 8, GROUP_X), F32),
+        DMA(2, BLOCKS),
+    ]
+    return call(spread_kernel, "spread", out, "hvV", 3, scratch, mib=8)(pre, halo, weight)[0]
 
 
 CONV_ROWS = TAPS * (CHANNELS // LANES)
@@ -1034,22 +1035,20 @@
         core, back, left, right, tots, far, (before, small, raw, skips, conv_weight)
     )
     theirs = lax.ppermute(send, "core", swap)
-    half, pre_own, sum_own, near = run_leave(core, mine, near, common, far, None)
+    half, sum_own, near = run_leave(core, mine, near, common, far, None)
     sum_own_got = lax.ppermute(sum_own, "core", swap)
-    (out_tokens, grad_step), pre_theirs, sum_theirs, (first,) = run_leave(
-        core, theirs, near, common, (), (half, pre_own)
-    )
+    (out_tokens, pre, grad_step), sum_theirs, (first,) = run_leave(core, theirs, near, common, far, half)
     sum_theirs_got = lax.ppermute(sum_theirs, "core", swap)
+    after = lax.ppermute(first, CTX, [(i + 1, i) for i in range(devices - 1)])
     sums = run_merge(core, sum_own, sum_own_got, sum_theirs, sum_theirs_got)
     chip = lax.axis_index("chip")
     values = around(sums, "chip", chips, SIDE, lambda i, d: i // SIDE * SIDE + (i % SIDE + d) % SIDE)
-    sums, first = tie(run_fold(scalar(lax.rem(chip, SIDE)), values), first)
-    after = lax.ppermute(first, CTX, [(i + 1, i) for i in range(devices - 1)])
+    grad_tokens = run_spread(pre, after, common[4])
+    values, grad_tokens = tie(values, grad_tokens)
+    sums = run_fold(scalar(lax.rem(chip, SIDE)), values)
     values = around(sums, "chip", chips, chips // SIDE, lambda i, d: (i + d * SIDE) % chips)
-    sums, after = tie(run_fold(scalar(lax.div(chip, SIDE)), values), after)
+    sums = run_fold(scalar(lax.div(chip, SIDE)), values)
     values = around_by_sides(sums, sequences)
-    grad_tokens = run_spread(core, pre_own, pre_theirs, after, common[4])
-    values, grad_tokens = tie(values, grad_tokens)
     grad_conv, grad_decay, grad_skip = run_finish(core, scalar(lax.axis_index("dp")), values)
     return (
         out_tokens[None],

time: 112 us -> 114 us (1.018); the launches traced: 110 us -> 113 us
  waiting for transfers between devices: 23.5 us -> 28.6 us
  starting transfers between devices: 41.7 us -> 39.2 us
  Pallas kernels: 41.6 us -> 43.8 us
  local copies, waits for them, and re-layouts: 2.24 us -> 0.91 us
    ppermute x4, waiting for transfers between devices: 0.12 us -> 6.94 us  [hear(): return lax.ppermute(value, ('dp', 'core'), shifts(first, second))]
    ppermute x3, starting transfers between devices: 3.17 us -> 0.47 us  [around_by_sides(): swapped = [lax.ppermute(part, 'core', [(0, 1), (1, 0)]) for part in heard]]
    pallas_call x15, Pallas kernels: 41.6 us -> 43.8 us  [go(): run(*[pin(a, spaces[p]) if p in spaces else a for a, p in zip(args, specs...]
    unnamed x4 -> x0, local copies, waits for them, and re-layouts: 1.32 us -> none
    ppermute x1, starting transfers between devices: 2.8 us -> 4.07 us  [local(): after = lax.ppermute(first, CTX, [(i + 1, i) for i in range(devices - 1)])]
    ppermute x1, waiting for transfers between devices: 1.2 us -> 0.01 us  [local(): sum_theirs_got = lax.ppermute(sum_theirs, 'core', swap)]
    ppermute x6, starting transfers between devices: 9.1 us -> 7.92 us  [around(): lax.ppermute(value, axis, [(i, move(i, d)) for i in range(count)])]
  transfers between devices with their start and end apart: 22 -> 22, of which waited for: 11 -> 9; matrix products, arithmetic and copies ran while one was open for 0% -> 0% of each run, Pallas kernels for 29% -> 31%
where the time goes in v8:
time: 114 us; the launch traced here: 113 us
  Pallas kernels  43.8 us (38%)
  starting transfers between devices  39.2 us (34%)
  waiting for transfers between devices  28.6 us (25%)
    pallas_call x15, Pallas kernels, go(): run(*[pin(a, spaces[p]) if p in spaces else a for a, p in zip(args, specs...  43.8 us
    all_to_all x2, waiting for transfers between devices, all_to_all(): return lax.all_to_all(value, axis, 0, 0, tiled=True)  16.4 us
    all_to_all x2, starting transfers between devices, all_to_all(): return lax.all_to_all(value, axis, 0, 0, tiled=True)  13.4 us
    ppermute x4, starting transfers between devices, hear(): return lax.ppermute(value, ('dp', 'core'), shifts(first, second))  9.85 us
    ppermute x6, starting transfers between devices, around(): lax.ppermute(value, axis, [(i, move(i, d)) for i in range(count)])  7.92 us
    ppermute x4, waiting for transfers between devices, hear(): return lax.ppermute(value, ('dp', 'core'), shifts(first, second))  6.94 us
    ppermute x1, starting transfers between devices, local(): after = lax.ppermute(first, CTX, [(i + 1, i) for i in range(devices - 1)])  4.07 us
    ppermute x6, waiting for transfers between devices, around(): lax.ppermute(value, axis, [(i, move(i, d)) for i in range(count)])  3.4 us
  transfers between devices with their start and end apart: 22, of which 9 were waited for; matrix products, arithmetic and copies ran while one was open for 0% of the time, Pallas kernels for 31%

profile of v8, /device:TPU:2, one launch (start us, length us, event | category | flops | bytes accessed | tf_op | source)
XLA Modules:
  0.0 113.4 jit_solution(4183574292878679938)
XLA Ops:
  0.6 0.9 slice_bitcast_fusion
  1.5 1.9 %collective-permute-start = (bf16[3,5120]{1,0:T(4,128)(2,1)S(1)}, bf16[3,5120]{1,0:T(4,128)(2,1)S(1)}, u32[]{:S(2)}, u32[]{:S(2)}) collective-permute-start(bf16[3,5120]{1,0:T(4,128)(2,1)S(1)} %slice_bitcast_fusion), channel_id=1, source_target_pairs={{0,1},{1,2},{2,3},{3,4},{4,5},{5,6},{6,7},{7,8},{8,9},{9,10},{10,1... | collective-permute-start | bytes 92168 | tf_op jit(solution)/shard_map/ppermute | solution.py:1014
  3.5 4.2 %begin.1 = (f32[512,128]{1,0:T(8,128)}, f32[512,128]{1,0:T(8,128)S(1)}, f32[32,128]{1,0:T(8,128)S(1)}, bf16[128,4096]{1,0:T(8,128)(2,1)S(1)}, bf16[128,1024]{1,0...) custom-call(f32[64,128]{1,0:T(8,128)} %bitcast.28, ...), custom_call_target="tpu_custom_call" | custom-call | flops 4000000000 | bytes 14400000 | tf_op jit(solution)/shard_map/begin/pallas_call | solution.py:97
  7.7 1.2 %collective-permute-done.halo_ref = bf16[3,5120]{1,0:T(4,128)(2,1)S(1)} collective-permute-done((bf16[3,5120]{1,0:T(4,128)(2,1)S(1)}, bf16[3,5120]{1,0:T(4,128)(2,1)S(1)}, u32[]{:S(2)}, u32[]{:S(2)}) %collective-permute-start) | collective-permute-done | bytes 30752 | tf_op jit(solution)/shard_map/ppermute | solution.py:1014
  9.0 2.4 %enter.1 = (bf16[128,4096]{1,0:T(8,128)(2,1)}, bf16[128,1024]{1,0:T(8,128)(2,1)}, f32[8,5120]{1,0:T(8,128)}, bf16[128,4096]{1,0:T(8,128)(2,1)S(1)}, bf16[128,102...) custom-call(s32[1]{0:T(128)} %bitcast.core_ref, bf16[128,4096]{1,0:T(8,128)(2,1)S(1)} %get-tuple-element.78.x0_ref, ...), custom_call_target="tpu_custom_call" | custom-call | flops 3000000000 | bytes 10800000 | tf_op jit(solution)/shard_map/enter/pallas_call | solution.py:97
  11.4 0.5 collective-permute-start.1
  11.9 0.1 collective-permute-start.2
  12.0 1.6 %own.1.own_ref = bf16[2,16,128,128]{3,2,1,0:T(8,128)(2,1)S(1)} custom-call(s32[1]{0:T(128)} %bitcast.core_ref, bf16[128,4096]{1,0:T(8,128)(2,1)S(1)} %get-tuple-element.85.x_ref, bf16[128,1024]{1,0:T(8,128)(2,1)S(1)} %get-tuple-element.86.bc_ref, bf16[128,4096]{1,0:T(8,128)(2,1)S(1)} %get-tuple-element.82.g_ref, f32[512,128]{1,0:T(8,128)S(1)} %get-tuple-element.83.small_ref), custom_call_target="tpu_custom_call" | custom-call | flops 3000000000 | bytes 10800000 | tf_op jit(solution)/shard_map/own/pallas_call | solution.py:97
  13.6 0.6 collective-permute-done.2.other_ref
  14.2 0.0 collective-permute-done.1.got_ref
  14.2 1.4 %pack.1 = (bf16[16,272,128]{2,1,0:T(8,128)(2,1)}, bf16[16,128,128]{2,1,0:T(8,128)(2,1)}, bf16[16,128,128]{2,1,0:T(8,128)(2,1)}, f32[64,128]{1,0:T(8,128)}) custom-call(s32[1]{0:T(128)} %bitcast.core_ref, bf16[2,16,128,128]{3,2,1,0:T(8,128)(2,1)S(1)} %own.1.own_ref, bf16[2,16,128,128]{3,2,1,0:T(8,128)(2,1)S(1)} %collective-permute-done.1.got_ref, ...), custom_call_target="tpu_custom_call" | custom-call | flops 2000000000 | bytes 7200000 | tf_op jit(solution)/shard_map/pack/pallas_call | solution.py:97
  15.6 7.2 %all-to-all-start = ((bf16[16,272,128]{2,1,0:T(8,128)(2,1)}), bf16[16,272,128]{2,1,0:T(8,128)(2,1)S(1)}, u32[]{:S(2)}, u32[]{:S(2)}) async-start(bf16[16,272,128]{2,1,0:T(8,128)(2,1)} %get-tuple-element.89), calls=%async_computation | async-start | bytes 2228224 | tf_op jit(solution)/shard_map/all_to_all | solution.py:968
  22.9 5.6 %inner.1 = (f32[128,4096]{1,0:T(8,128)}, f32[128,1024]{1,0:T(8,128)}, f32[32,128]{1,0:T(8,128)}) custom-call(bf16[128,4096]{1,0:T(8,128)(2,1)} %get-tuple-element.90.x_h.rest_0_.rest_13_, bf16[128,1024]{1,0:T(8,128)(2,1)} %get-tuple-element.97.bc_h.rest_6_.rest_19_, bf16[128,4096]{1,0:T(8,128)(2,1)} %bitcast.22, f32[512,128]{1,0:T(8,128)} %get-tuple-element.91.small_h.rest_9_), custom_call_target="tpu_custom_call" | custom-call | flops 4000000000 | bytes 14400000 | tf_op jit(solution)/shard_map/inner/pallas_call | solution.py:97
  28.5 10.9 %all-to-all-done.in_ref = bf16[16,272,128]{2,1,0:T(8,128)(2,1)S(1)} async-done(((bf16[16,272,128]{2,1,0:T(8,128)(2,1)}), bf16[16,272,128]{2,1,0:T(8,128)(2,1)S(1)}, u32[]{:S(2)}, u32[]{:S(2)}) %all-to-all-start) | async-done | bytes 1114144 | tf_op jit(solution)/shard_map/all_to_all | solution.py:968
  39.3 1.3 %chain.1 = bf16[16,256,128]{2,1,0:T(8,128)(2,1)} custom-call(bf16[16,272,128]{2,1,0:T(8,128)(2,1)S(1)} %all-to-all-done.in_ref), custom_call_target="tpu_custom_call" | custom-call | flops 1000000000 | bytes 3600000 | tf_op jit(solution)/shard_map/chain/pallas_call | solution.py:97
  40.6 6.2 %all-to-all-start.1 = ((bf16[16,256,128]{2,1,0:T(8,128)(2,1)}), bf16[16,256,128]{2,1,0:T(8,128)(2,1)S(1)}, u32[]{:S(2)}, u32[]{:S(2)}) async-start(bf16[16,256,128]{2,1,0:T(8,128)(2,1)} %chain.1), calls=%async_computation.1 | async-start | bytes 2097152 | tf_op jit(solution)/shard_map/all_to_all | solution.py:968
  46.8 8.7 %slopes.1 = (f32[128,4096]{1,0:T(8,128)}, f32[128,5120]{1,0:T(8,128)}) custom-call(bf16[128,1024]{1,0:T(8,128)(2,1)} %get-tuple-element.97.bc_h.rest_6_.rest_19_, bf16[128,4096]{1,0:T(8,128)(2,1)} %bitcast.23, f32[512,128]{1,0:T(8,128)} %get-tuple-element.91.small_h.rest_9_, bf16[128,5120]{1,0:T(8,128)(2,1)} %bitcast.17, ...), custom_call_target="tpu_custom_call" | custom-call | flops 6000000000 | bytes 21600000 | tf_op jit(solution)/shard_map/slopes/pallas_call | solution.py:97
  55.5 5.6 %all-to-all-done.1.back_ref = bf16[16,256,128]{2,1,0:T(8,128)(2,1)S(1)} async-done(((bf16[16,256,128]{2,1,0:T(8,128)(2,1)}), bf16[16,256,128]{2,1,0:T(8,128)(2,1)S(1)}, u32[]{:S(2)}, u32[]{:S(2)}) %all-to-all-start.1) | async-done | bytes 1048608 | tf_op jit(solution)/shard_map/all_to_all | solution.py:968
  61.1 2.8 %unpack.1 = (bf16[2,16,128,128]{3,2,1,0:T(8,128)(2,1)S(1)}, bf16[2,16,128,128]{3,2,1,0:T(8,128)(2,1)S(1)}, bf16[128,1024]{1,0:T(8,128)(2,1)S(1)}, bf16[128,1024]...) custom-call(s32[1]{0:T(128)} %bitcast.core_ref, ...), custom_call_target="tpu_custom_call" | custom-call | flops 3000000000 | bytes 10800000 | tf_op jit(solution)/shard_map/unpack/pallas_call | solution.py:97
  63.9 0.3 collective-permute-start.3
  64.2 5.7 %leave.2 = (bf16[128,4096]{1,0:T(8,128)(2,1)}, f32[128,5120]{1,0:T(8,128)}, f32[64,128]{1,0:T(8,128)}, f32[128,128]{1,0:T(8,128)S(1)}, bf16[128,1024]{1,0:T(8,12...) custom-call(s32[1]{0:T(128)} %bitcast.core_ref, ...), custom_call_target="tpu_custom_call" | custom-call | flops 5000000000 | bytes 18000000 | tf_op jit(solution)/shard_map/leave/pallas_call | solution.py:97
  69.9 0.6 collective-permute-start.4
  70.4 0.0 collective-permute-done.3.state_ref
  70.4 4.7 %leave.3 = (bf16[128,4096]{1,0:T(8,128)(2,1)}, f32[128,5120]{1,0:T(8,128)}, f32[64,128]{1,0:T(8,128)}, f32[128,128]{1,0:T(8,128)S(1)}, bf16[3,5120]{1,0:T(4,128)(2,1)S(1)}) custom-call(s32[1]{0:T(128)} %bitcast.core_ref, ...), custom_call_target="tpu_custom_call", output_to_operand_aliasing={{0}: (23, {}), {1}: (24, {}), {2}: (25, {})} | custom-call | flops 5000000000 | bytes 18000000 | tf_op jit(solution)/shard_map/leave/pallas_call | solution.py:97
  75.2 0.1 collective-permute-start.5
  75.3 4.1 %collective-permute-start.9 = (bf16[3,5120]{1,0:T(4,128)(2,1)S(1)}, bf16[3,5120]{1,0:T(4,128)(2,1)S(1)}, u32[]{:S(2)}, u32[]{:S(2)}) collective-permute-start(bf16[3,5120]{1,0:T(4,128)(2,1)S(1)} %get-tuple-element.140), channel_id=1, source_target_pairs={{1,0},{2,1},{3,2},{4,3},{5,4},{6,5},{7,6},{8,7},{9,8},{10,9},{11,1... | collective-permute-start | bytes 92168 | tf_op jit(solution)/shard_map/ppermute | solution.py:1042
  79.4 0.0 collective-permute-done.4.own_got_ref
  79.4 0.0 collective-permute-done.5.theirs_got_ref
  79.4 0.6 merge.1.rest_0_
  80.0 0.0 collective-permute-start.6
  80.0 1.8 %collective-permute-start.7 = (bf16[176,128]{1,0:T(8,128)(2,1)S(1)}, bf16[176,128]{1,0:T(8,128)(2,1)S(1)}, u32[]{:S(2)}, u32[]{:S(2)}) collective-permute-start(bf16[176,128]{1,0:T(8,128)(2,1)S(1)} %merge.1.rest_0_), channel_id=1, source_target_pairs={{0,4},{2,6},{4,0},{6,2},{8,12},{10,14},{12,8},{14,10},{16,20},{18,... | collective-permute-start | bytes 135176 | tf_op jit(solution)/shard_map/ppermute | solution.py:980
  81.8 1.4 %collective-permute-start.8 = (bf16[176,128]{1,0:T(8,128)(2,1)S(1)}, bf16[176,128]{1,0:T(8,128)(2,1)S(1)}, u32[]{:S(2)}, u32[]{:S(2)}) collective-permute-start(bf16[176,128]{1,0:T(8,128)(2,1)S(1)} %merge.1.rest_0_), channel_id=1, source_target_pairs={{0,6},{2,0},{4,2},{6,4},{8,14},{10,8},{12,10},{14,12},{16,22},{18,... | collective-permute-start | bytes 135176 | tf_op jit(solution)/shard_map/ppermute | solution.py:980
  83.2 0.0 collective-permute-done.9.halo_ref
  83.2 4.0 %spread.1 = bf16[128,5120]{1,0:T(8,128)(2,1)} custom-call(f32[128,5120]{1,0:T(8,128)} %get-tuple-element.139.pre_h, bf16[3,5120]{1,0:T(4,128)(2,1)S(1)} %collective-permute-done.9.halo_ref, f32[4,5120]{1,0:T(4,128)S(1)} %get-tuple-element.124.rest_12_.weight_ref), custom_call_target="tpu_custom_call" | custom-call | flops 3000000000 | bytes 10800000 | tf_op jit(solution)/shard_map/spread/pallas_call | solution.py:97
  87.3 0.7 collective-permute-start.10
  88.0 3.3 %collective-permute-start.11 = (bf16[176,128]{1,0:T(8,128)(2,1)S(1)}, bf16[176,128]{1,0:T(8,128)(2,1)S(1)}, u32[]{:S(2)}, u32[]{:S(2)}) collective-permute-start(bf16[176,128]{1,0:T(8,128)(2,1)S(1)} %fold.2.rest_0_), channel_id=1, source_target_pairs={{0,16},{2,18},{4,20},{6,22},{8,24},{10,26},{12,28},{14,30},{16,0},... | collective-permute-start | bytes 135176 | tf_op jit(solution)/shard_map/ppermute | solution.py:980
  91.3 0.7 collective-permute-start.12
  92.0 1.6 %collective-permute-done.11.rest_2_ = bf16[176,128]{1,0:T(8,128)(2,1)S(1)} collective-permute-done((bf16[176,128]{1,0:T(8,128)(2,1)S(1)}, bf16[176,128]{1,0:T(8,128)(2,1)S(1)}, u32[]{:S(2)}, u32[]{:S(2)}) %collective-permute-start.11) | collective-permute-done | bytes 45088 | tf_op jit(solution)/shard_map/ppermute | solution.py:980
  93.6 1.8 %collective-permute-done.12.rest_3_ = bf16[176,128]{1,0:T(8,128)(2,1)S(1)} collective-permute-done((bf16[176,128]{1,0:T(8,128)(2,1)S(1)}, bf16[176,128]{1,0:T(8,128)(2,1)S(1)}, u32[]{:S(2)}, u32[]{:S(2)}) %collective-permute-start.12) | collective-permute-done | bytes 45088 | tf_op jit(solution)/shard_map/ppermute | solution.py:980
  95.4 2.0 %collective-permute-start.13 = (bf16[176,128]{1,0:T(8,128)(2,1)S(1)}, bf16[176,128]{1,0:T(8,128)(2,1)S(1)}, u32[]{:S(2)}, u32[]{:S(2)}) collective-permute-start(bf16[176,128]{1,0:T(8,128)(2,1)S(1)} %fold.3.rest_0_), channel_id=1, source_target_pairs={{0,32},{1,225},{32,64},{33,1},{64,96},{65,33},{96,128},{97,65},{12... | collective-permute-start | bytes 135176 | tf_op jit(solution)/shard_map/ppermute | solution.py:993
  97.4 3.3 %collective-permute-start.14 = (bf16[176,128]{1,0:T(8,128)(2,1)S(1)}, bf16[176,128]{1,0:T(8,128)(2,1)S(1)}, u32[]{:S(2)}, u32[]{:S(2)}) collective-permute-start(bf16[176,128]{1,0:T(8,128)(2,1)S(1)} %fold.3.rest_0_), channel_id=1, source_target_pairs={{0,64},{1,193},{32,96},{33,225},{64,128},{65,1},{96,160},{97,33},{... | collective-permute-start | bytes 135176 | tf_op jit(solution)/shard_map/ppermute | solution.py:993
  100.7 4.0 %collective-permute-start.15 = (bf16[176,128]{1,0:T(8,128)(2,1)S(1)}, bf16[176,128]{1,0:T(8,128)(2,1)S(1)}, u32[]{:S(2)}, u32[]{:S(2)}) collective-permute-start(bf16[176,128]{1,0:T(8,128)(2,1)S(1)} %fold.3.rest_0_), channel_id=1, source_target_pairs={{0,96},{1,161},{32,128},{33,193},{64,160},{65,225},{96,192},{97,1}... | collective-permute-start | bytes 135176 | tf_op jit(solution)/shard_map/ppermute | solution.py:993
  104.7 0.5 collective-permute-start.19
  105.2 0.1 collective-permute-done.14.rest_2_
  105.3 0.5 collective-permute-start.17
  105.8 2.5 %collective-permute-done.15.rest_3_ = bf16[176,128]{1,0:T(8,128)(2,1)S(1)} collective-permute-done((bf16[176,128]{1,0:T(8,128)(2,1)S(1)}, bf16[176,128]{1,0:T(8,128)(2,1)S(1)}, u32[]{:S(2)}, u32[]{:S(2)}) %collective-permute-start.15) | collective-permute-done | bytes 45088 | tf_op jit(solution)/shard_map/ppermute | solution.py:993
  108.2 4.4 %collective-permute-done.19.rest_7_ = bf16[176,128]{1,0:T(8,128)(2,1)S(1)} collective-permute-done((bf16[176,128]{1,0:T(8,128)(2,1)S(1)}, bf16[176,128]{1,0:T(8,128)(2,1)S(1)}, u32[]{:S(2)}, u32[]{:S(2)}) %collective-permute-start.19) | collective-permute-done | bytes 45088 | tf_op jit(solution)/shard_map/ppermute | solution.py:993
  112.7 0.7 finish.1
  (12 shorter events, 0.1 us)
Async XLA Ops:
  1.5 7.4 %collective-permute-start = (bf16[3,5120]{1,0:T(4,128)(2,1)S(1)}, bf16[3,5120]{1,0:T(4,128)(2,1)S(1)}, u32[]{:S(2)}, u32[]{:S(2)}) collective-permute-start(bf16[3,5120]{1,0:T(4,128)(2,1)S(1)} %slice_bitcast_fusion), channel_id=1, source_target_pairs={{0,1},{1,2},{2,3},{3,4},{4,5},{5,6},{6,7},{7,8},{8,9},{9,10},{10,1... | collective-permute-start | bytes 92168 | tf_op jit(solution)/shard_map/ppermute | solution.py:1014
  11.4 2.8 %collective-permute-start.1 = (bf16[2,16,128,128]{3,2,1,0:T(8,128)(2,1)S(1)}, bf16[2,16,128,128]{3,2,1,0:T(8,128)(2,1)S(1)}, u32[]{:S(2)}, u32[]{:S(2)}) collective-permute-start(bf16[2,16,128,128]{3,2,1,0:T(8,128)(2,1)S(1)} %get-tuple-element.87), channel_id=1, source_target_pairs={{0,1},{1,0},{2,3},{3,2},{4,5},{5,4},{6,7},{7,6},{8,9},{9,8},{10,11... | collective-permute-start | bytes 3145736 | tf_op jit(solution)/shard_map/ppermute | solution.py:1022
  11.9 2.3 %collective-permute-start.2 = (f32[32,128]{1,0:T(8,128)S(1)}, f32[32,128]{1,0:T(8,128)S(1)}, u32[]{:S(2)}, u32[]{:S(2)}) collective-permute-start(f32[32,128]{1,0:T(8,128)S(1)} %get-tuple-element.88.tot_ref), channel_id=1, source_target_pairs={{0,1},{1,0},{2,3},{3,2},{4,5},{5,4},{6,7},{7,6},{8,9},{9,8},{10,11... | collective-permute-start | bytes 49160 | tf_op jit(solution)/shard_map/ppermute | solution.py:1018
  15.6 23.7 %all-to-all-start = ((bf16[16,272,128]{2,1,0:T(8,128)(2,1)}), bf16[16,272,128]{2,1,0:T(8,128)(2,1)S(1)}, u32[]{:S(2)}, u32[]{:S(2)}) async-start(bf16[16,272,128]{2,1,0:T(8,128)(2,1)} %get-tuple-element.89), calls=%async_computation | async-start | bytes 2228224 | tf_op jit(solution)/shard_map/all_to_all | solution.py:968
  40.6 20.5 %all-to-all-start.1 = ((bf16[16,256,128]{2,1,0:T(8,128)(2,1)}), bf16[16,256,128]{2,1,0:T(8,128)(2,1)S(1)}, u32[]{:S(2)}, u32[]{:S(2)}) async-start(bf16[16,256,128]{2,1,0:T(8,128)(2,1)} %chain.1), calls=%async_computation.1 | async-start | bytes 2097152 | tf_op jit(solution)/shard_map/all_to_all | solution.py:968
  63.9 6.5 %collective-permute-start.3 = (bf16[2,16,128,128]{3,2,1,0:T(8,128)(2,1)S(1)}, bf16[2,16,128,128]{3,2,1,0:T(8,128)(2,1)S(1)}, u32[]{:S(2)}, u32[]{:S(2)}) collective-permute-start(bf16[2,16,128,128]{3,2,1,0:T(8,128)(2,1)S(1)} %get-tuple-element.110), channel_id=1, source_target_pairs={{0,1},{1,0},{2,3},{3,2},{4,5},{5,4},{6,7},{7,6},{8,9},{9,8},{10,11... | collective-permute-start | bytes 3145736 | tf_op jit(solution)/shard_map/ppermute | solution.py:1037
  69.9 9.5 %collective-permute-start.4 = (f32[128,128]{1,0:T(8,128)S(1)}, f32[128,128]{1,0:T(8,128)S(1)}, u32[]{:S(2)}, u32[]{:S(2)}) collective-permute-start(f32[128,128]{1,0:T(8,128)S(1)} %get-tuple-element.137.own_ref), channel_id=1, source_target_pairs={{0,1},{1,0},{2,3},{3,2},{4,5},{5,4},{6,7},{7,6},{8,9},{9,8},{10,11... | collective-permute-start | bytes 196616 | tf_op jit(solution)/shard_map/ppermute | solution.py:1039
  75.2 4.2 %collective-permute-start.5 = (f32[128,128]{1,0:T(8,128)S(1)}, f32[128,128]{1,0:T(8,128)S(1)}, u32[]{:S(2)}, u32[]{:S(2)}) collective-permute-start(f32[128,128]{1,0:T(8,128)S(1)} %get-tuple-element.138.theirs_ref), channel_id=1, source_target_pairs={{0,1},{1,0},{2,3},{3,2},{4,5},{5,4},{6,7},{7,6},{8,9},{9,8},{10,11... | collective-permute-start | bytes 196616 | tf_op jit(solution)/shard_map/ppermute | solution.py:1041
  75.3 7.9 %collective-permute-start.9 = (bf16[3,5120]{1,0:T(4,128)(2,1)S(1)}, bf16[3,5120]{1,0:T(4,128)(2,1)S(1)}, u32[]{:S(2)}, u32[]{:S(2)}) collective-permute-start(bf16[3,5120]{1,0:T(4,128)(2,1)S(1)} %get-tuple-element.140), channel_id=1, source_target_pairs={{1,0},{2,1},{3,2},{4,3},{5,4},{6,5},{7,6},{8,7},{9,8},{10,9},{11,1... | collective-permute-start | bytes 92168 | tf_op jit(solution)/shard_map/ppermute | solution.py:1042
  80.0 7.2 %collective-permute-start.6 = (bf16[176,128]{1,0:T(8,128)(2,1)S(1)}, bf16[176,128]{1,0:T(8,128)(2,1)S(1)}, u32[]{:S(2)}, u32[]{:S(2)}) collective-permute-start(bf16[176,128]{1,0:T(8,128)(2,1)S(1)} %merge.1.rest_0_), channel_id=1, source_target_pairs={{0,2},{2,4},{4,6},{6,0},{8,10},{10,12},{12,14},{14,8},{16,18},{18,... | collective-permute-start | bytes 135176 | tf_op jit(solution)/shard_map/ppermute | solution.py:980
  80.0 7.2 %collective-permute-start.7 = (bf16[176,128]{1,0:T(8,128)(2,1)S(1)}, bf16[176,128]{1,0:T(8,128)(2,1)S(1)}, u32[]{:S(2)}, u32[]{:S(2)}) collective-permute-start(bf16[176,128]{1,0:T(8,128)(2,1)S(1)} %merge.1.rest_0_), channel_id=1, source_target_pairs={{0,4},{2,6},{4,0},{6,2},{8,12},{10,14},{12,8},{14,10},{16,20},{18,... | collective-permute-start | bytes 135176 | tf_op jit(solution)/shard_map/ppermute | solution.py:980
  81.8 5.4 %collective-permute-start.8 = (bf16[176,128]{1,0:T(8,128)(2,1)S(1)}, bf16[176,128]{1,0:T(8,128)(2,1)S(1)}, u32[]{:S(2)}, u32[]{:S(2)}) collective-permute-start(bf16[176,128]{1,0:T(8,128)(2,1)S(1)} %merge.1.rest_0_), channel_id=1, source_target_pairs={{0,6},{2,0},{4,2},{6,4},{8,14},{10,8},{12,10},{14,12},{16,22},{18,... | collective-permute-start | bytes 135176 | tf_op jit(solution)/shard_map/ppermute | solution.py:980
  87.3 4.7 %collective-permute-start.10 = (bf16[176,128]{1,0:T(8,128)(2,1)S(1)}, bf16[176,128]{1,0:T(8,128)(2,1)S(1)}, u32[]{:S(2)}, u32[]{:S(2)}) collective-permute-start(bf16[176,128]{1,0:T(8,128)(2,1)S(1)} %fold.2.rest_0_), channel_id=1, source_target_pairs={{0,8},{2,10},{4,12},{6,14},{8,16},{10,18},{12,20},{14,22},{16,24},... | collective-permute-start | bytes 135176 | tf_op jit(solution)/shard_map/ppermute | solution.py:980
  88.0 5.6 %collective-permute-start.11 = (bf16[176,128]{1,0:T(8,128)(2,1)S(1)}, bf16[176,128]{1,0:T(8,128)(2,1)S(1)}, u32[]{:S(2)}, u32[]{:S(2)}) collective-permute-start(bf16[176,128]{1,0:T(8,128)(2,1)S(1)} %fold.2.rest_0_), channel_id=1, source_target_pairs={{0,16},{2,18},{4,20},{6,22},{8,24},{10,26},{12,28},{14,30},{16,0},... | collective-permute-start | bytes 135176 | tf_op jit(solution)/shard_map/ppermute | solution.py:980
  91.3 4.0 %collective-permute-start.12 = (bf16[176,128]{1,0:T(8,128)(2,1)S(1)}, bf16[176,128]{1,0:T(8,128)(2,1)S(1)}, u32[]{:S(2)}, u32[]{:S(2)}) collective-permute-start(bf16[176,128]{1,0:T(8,128)(2,1)S(1)} %fold.2.rest_0_), channel_id=1, source_target_pairs={{0,24},{2,26},{4,28},{6,30},{8,0},{10,2},{12,4},{14,6},{16,8},{18,... | collective-permute-start | bytes 135176 | tf_op jit(solution)/shard_map/ppermute | solution.py:980
  95.4 9.9 %collective-permute-start.13 = (bf16[176,128]{1,0:T(8,128)(2,1)S(1)}, bf16[176,128]{1,0:T(8,128)(2,1)S(1)}, u32[]{:S(2)}, u32[]{:S(2)}) collective-permute-start(bf16[176,128]{1,0:T(8,128)(2,1)S(1)} %fold.3.rest_0_), channel_id=1, source_target_pairs={{0,32},{1,225},{32,64},{33,1},{64,96},{65,33},{96,128},{97,65},{12... | collective-permute-start | bytes 135176 | tf_op jit(solution)/shard_map/ppermute | solution.py:993
  97.4 7.9 %collective-permute-start.14 = (bf16[176,128]{1,0:T(8,128)(2,1)S(1)}, bf16[176,128]{1,0:T(8,128)(2,1)S(1)}, u32[]{:S(2)}, u32[]{:S(2)}) collective-permute-start(bf16[176,128]{1,0:T(8,128)(2,1)S(1)} %fold.3.rest_0_), channel_id=1, source_target_pairs={{0,64},{1,193},{32,96},{33,225},{64,128},{65,1},{96,160},{97,33},{... | collective-permute-start | bytes 135176 | tf_op jit(solution)/shard_map/ppermute | solution.py:993
  100.7 7.6 %collective-permute-start.15 = (bf16[176,128]{1,0:T(8,128)(2,1)S(1)}, bf16[176,128]{1,0:T(8,128)(2,1)S(1)}, u32[]{:S(2)}, u32[]{:S(2)}) collective-permute-start(bf16[176,128]{1,0:T(8,128)(2,1)S(1)} %fold.3.rest_0_), channel_id=1, source_target_pairs={{0,96},{1,161},{32,128},{33,193},{64,160},{65,225},{96,192},{97,1}... | collective-permute-start | bytes 135176 | tf_op jit(solution)/shard_map/ppermute | solution.py:993
  104.7 8.0 %collective-permute-start.19 = (bf16[176,128]{1,0:T(8,128)(2,1)S(1)}, bf16[176,128]{1,0:T(8,128)(2,1)S(1)}, u32[]{:S(2)}, u32[]{:S(2)}) collective-permute-start(bf16[176,128]{1,0:T(8,128)(2,1)S(1)} %fold.3.rest_0_), channel_id=1, source_target_pairs={{0,128},{1,129},{32,160},{33,161},{64,192},{65,193},{96,224},{97,2... | collective-permute-start | bytes 135176 | tf_op jit(solution)/shard_map/ppermute | solution.py:993
  105.2 7.4 %collective-permute-start.16 = (bf16[176,128]{1,0:T(8,128)(2,1)S(1)}, bf16[176,128]{1,0:T(8,128)(2,1)S(1)}, u32[]{:S(2)}, u32[]{:S(2)}) collective-permute-start(bf16[176,128]{1,0:T(8,128)(2,1)S(1)} %collective-permute-done.13.rest_1_), channel_id=1, source_target_pairs={{0,1},{1,0},{2,3},{3,2},{4,5},{5,4},{6,7},{7,6},{8,9},{9,8},{10,11... | collective-permute-start | bytes 135176 | tf_op jit(solution)/shard_map/ppermute | solution.py:997
  105.3 7.4 %collective-permute-start.17 = (bf16[176,128]{1,0:T(8,128)(2,1)S(1)}, bf16[176,128]{1,0:T(8,128)(2,1)S(1)}, u32[]{:S(2)}, u32[]{:S(2)}) collective-permute-start(bf16[176,128]{1,0:T(8,128)(2,1)S(1)} %collective-permute-done.14.rest_2_), channel_id=1, source_target_pairs={{0,1},{1,0},{2,3},{3,2},{4,5},{5,4},{6,7},{7,6},{8,9},{9,8},{10,11... | collective-permute-start | bytes 135176 | tf_op jit(solution)/shard_map/ppermute | solution.py:997
  108.2 4.4 %collective-permute-start.18 = (bf16[176,128]{1,0:T(8,128)(2,1)S(1)}, bf16[176,128]{1,0:T(8,128)(2,1)S(1)}, u32[]{:S(2)}, u32[]{:S(2)}) collective-permute-start(bf16[176,128]{1,0:T(8,128)(2,1)S(1)} %collective-permute-done.15.rest_3_), channel_id=1, source_target_pairs={{0,1},{1,0},{2,3},{3,2},{4,5},{5,4},{6,7},{7,6},{8,9},{9,8},{10,11... | collective-permute-start | bytes 135176 | tf_op jit(solution)/shard_map/ppermute | solution.py:997

commit v9 on v7

--- a/solution.py
+++ b/solution.py
@@ -673,8 +673,8 @@
     fetches = []
     if theirs:
         pre_own_ref, _, _ = take(3)
-        out_h, step_h, pre_ref, sum_ref, first_ref = take(5)
-        head_ref, out_ref, step_ref, win_ref, sems = rest
+        out_h, step_h, pre_h, sum_ref, first_ref = take(5)
+        head_ref, pre_ref, out_ref, step_ref, win_ref, sems = rest
         own = core_ref[0]
         head_ref[:, span(own, HALF_X)] = pre_own_ref[0:8, 0:HALF_X]
         size = HALF_GROUPS * STATE
@@ -766,6 +766,8 @@
                 near_at = pl.ds(jj * GROUP_X + (q // 4) * size, size)
                 far_at = span(2 * j + q // 4, size)
                 save(out_ref.at[:, near_at], out_h.at[:, far_at])
+                if theirs:
+                    save(pre_ref.at[:, near_at], pre_h.at[:, near_at])
         for grad, base in ((grad_b, 0), (grad_c, 1)):
             at = HALF_X + (base * HALF_GROUPS + jj) * STATE
             tail = slice(GROUP_X + base * STATE, GROUP_X + (base + 1) * STATE)
@@ -775,6 +777,7 @@
             pre_ref[:, at : at + STATE] = grad_pre
             if theirs:
                 head_ref[:, far_at] = grad_pre[0:8]
+                save(pre_ref.at[:, pl.ds(at, STATE)], pre_h.at[:, pl.ds(at, STATE)])
             terms += tap_sums(grad_pre, 0)
         heads = span(j, GROUP_HEADS)
         behind = exact_dot(seg_grad, lower)
@@ -796,7 +799,7 @@
     out = [
         ("h", (T, WIDTH_X), BF16),
         ("h", (HEADS, T), F32),
-        ("V", (T, HALF_X + HALF_B), F32),
+        ("h" if theirs else "V", (T, HALF_X + HALF_B), F32),
         ("V", (HALF_GROUPS * SUM_GROUP, LANES), F32),
     ]
     scratch = [
@@ -815,7 +818,7 @@
         args += done
         specs += "Vhh"
         out += [("V", (TAPS - 1, CHANNELS), BF16)]
-        scratch = [pltpu.VMEM((8, CHANNELS), F32)] + scratch
+        scratch = [pltpu.VMEM((8, CHANNELS), F32), pltpu.VMEM((T, HALF_X + HALF_B), F32)] + scratch
     else:
         out += NEAR * HALF_GROUPS
     kernel = functools.partial(leave_kernel, theirs)
@@ -823,11 +826,14 @@
     return outs[:2], outs[2], outs[3], outs[4:]
 
 
-def spread_kernel(core_ref, own_ref, theirs_ref, halo_ref, weight_ref, out_h, out_ref, win_ref, sems):
+def spread_kernel(core_ref, own_ref, theirs_h, halo_ref, weight_ref, out_h, theirs_ref, out_ref, win_ref, sems):
+    load = start_all([(theirs_h, theirs_ref)], sems.at[pl.ds(8, 1)])
     saves = []
     size = HALF_GROUPS * STATE
     for side, pre_ref in enumerate((own_ref, theirs_ref)):
         half = 1 - core_ref[0] if side else core_ref[0]
+        if side:
+            wait_all(load)
         blocks = [(jj * GROUP_X, span(half * HALF_GROUPS + jj, GROUP_X), GROUP_X) for jj in range(HALF_GROUPS)]
         blocks += [
             (HALF_X + base * size, span(WIDTH_X // size + 2 * base + half, size), size) for base in range(2)
@@ -851,8 +857,13 @@
 
 def run_spread(core, own, theirs, halo, weight):
     out = [("h", (T, CHANNELS), BF16)]
-    scratch = [pltpu.VMEM((T, CHANNELS), BF16), pltpu.VMEM((T + 8, GROUP_X), F32), DMA(8)]
-    return call(spread_kernel, "spread", out, "sVVvV", 3, scratch, mib=6)(core, own, theirs, halo, weight)[0]
+    scratch = [
+        pltpu.VMEM((T, HALF_X + HALF_B), F32),
+        pltpu.VMEM((T, CHANNELS), BF16),
+        pltpu.VMEM((T + 8, GROUP_X), F32),
+        DMA(9),
+    ]
+    return call(spread_kernel, "spread", out, "sVhvV", 3, scratch, mib=8)(core, own, theirs, halo, weight)[0]
 
 
 CONV_ROWS = TAPS * (CHANNELS // LANES)
@@ -908,30 +919,7 @@
     return call(merge_kernel, "merge", out, "svvvv", 1, mib=4)(core, own, own_got, theirs, theirs_got)[0]
 
 
-def ring_sum(me_ref, hold_ref):
-    count = hold_ref.shape[0]
-    conv, thin = read_send(hold_ref[lax.rem(me_ref[0], count)])
-    for k in range(1, count):
-        more, little = read_send(hold_ref[lax.rem(me_ref[0] + count - k, count)])
-        conv, thin = conv + more, thin + little
-    return conv, thin
-
-
-def fold_kernel(me_ref, *rest):
-    *refs, out_ref, hold_ref = rest
-    for d, ref in enumerate(refs):
-        hold_ref[d] = ref[...]
-    write_send(out_ref, *ring_sum(me_ref, hold_ref))
-
-
-def run_fold(me, values):
-    out = [("v", (SEND_ROWS, LANES), BF16)]
-    scratch = [pltpu.VMEM((len(values), SEND_ROWS, LANES), BF16)]
-    return call(fold_kernel, "fold", out, "s" + "v" * len(values), 1, scratch, mib=4)(me, *values)[0]
-
-
-def finish_kernel(core_ref, me_ref, *rest):
-    *refs, conv_ref, decay_ref, skip_ref, hold_ref = rest
+def ring_sum(core_ref, me_ref, refs, hold_ref):
     count = len(refs)
     sides = (count - 1) // 2
     hold_ref[0] = refs[0][...]
@@ -941,7 +929,27 @@
         hold_ref[count - mine] = refs[sides + k][...]
     if count % 2 == 0:
         hold_ref[count // 2] = refs[count - 1][...]
-    conv, thin = ring_sum(me_ref, hold_ref)
+    conv, thin = read_send(hold_ref[lax.rem(me_ref[0], count)])
+    for k in range(1, count):
+        more, little = read_send(hold_ref[lax.rem(me_ref[0] + count - k, count)])
+        conv, thin = conv + more, thin + little
+    return conv, thin
+
+
+def fold_kernel(core_ref, me_ref, *rest):
+    *refs, out_ref, hold_ref = rest
+    write_send(out_ref, *ring_sum(core_ref, me_ref, refs, hold_ref))
+
+
+def run_fold(core, me, values):
+    out = [("v", (SEND_ROWS, LANES), BF16)]
+    scratch = [pltpu.VMEM((len(values), SEND_ROWS, LANES), BF16)]
+    return call(fold_kernel, "fold", out, "ss" + "v" * len(values), 1, scratch, mib=4)(core, me, *values)[0]
+
+
+def finish_kernel(core_ref, me_ref, *rest):
+    *refs, conv_ref, decay_ref, skip_ref, hold_ref = rest
+    conv, thin = ring_sum(core_ref, me_ref, refs, hold_ref)
     for i in range(CHANNELS // LANES):
         if i < PAIRS:
             row = CONV_GROUP * (i // GROUP_PAIRS) + TAPS * (i % GROUP_PAIRS)
@@ -974,25 +982,16 @@
 SIDE = 4
 
 
-def around(value, axis, count, ring, move):
-    return [value] + [
-        lax.ppermute(value, axis, [(i, move(i, d)) for i in range(count)]) for d in range(1, ring)
-    ]
-
-
-def around_by_sides(value, count):
-    def shifts(first, second):
-        return [
-            (2 * i + side, 2 * ((i + move) % count) + side)
-            for i in range(count)
-            for side, move in enumerate((first, second))
-        ]
-
+def around(value, axis, size, ring, move):
     def hear(first, second):
-        return lax.ppermute(value, ("dp", "core"), shifts(first, second))
-
-    middle = [hear(count // 2, count // 2)] if count % 2 == 0 else []
-    heard = [hear(k, -k) for k in range((count - 1) // 2, 0, -1)][::-1]
+        return lax.ppermute(
+            value,
+            (axis, "core"),
+            [(2 * i + side, 2 * move(i, d) + side) for i in range(size) for side, d in enumerate((first, second))],
+        )
+
+    middle = [hear(ring // 2, ring // 2)] if ring % 2 == 0 else []
+    heard = [hear(k, ring - k) for k in range(1, (ring - 1) // 2 + 1)]
     swapped = [lax.ppermute(part, "core", [(0, 1), (1, 0)]) for part in heard]
     return [value] + heard + swapped + middle
 
@@ -1040,17 +1039,23 @@
         core, theirs, near, common, (), (half, pre_own)
     )
     sum_theirs_got = lax.ppermute(sum_theirs, "core", swap)
+    after = lax.ppermute(first, CTX, [(i + 1, i) for i in range(devices - 1)])
     sums = run_merge(core, sum_own, sum_own_got, sum_theirs, sum_theirs_got)
-    chip = lax.axis_index("chip")
+    chip, sequence = lax.axis_index("chip"), lax.axis_index("dp")
+    rows = chips // SIDE
     values = around(sums, "chip", chips, SIDE, lambda i, d: i // SIDE * SIDE + (i % SIDE + d) % SIDE)
-    sums, first = tie(run_fold(scalar(lax.rem(chip, SIDE)), values), first)
-    after = lax.ppermute(first, CTX, [(i + 1, i) for i in range(devices - 1)])
-    values = around(sums, "chip", chips, chips // SIDE, lambda i, d: (i + d * SIDE) % chips)
-    sums, after = tie(run_fold(scalar(lax.div(chip, SIDE)), values), after)
-    values = around_by_sides(sums, sequences)
+    values, after = tie(values, after)
+    sums = run_fold(core, scalar(lax.rem(chip, SIDE)), values)
+    values = around(sums, "chip", chips, rows, lambda i, d: (i + d * SIDE) % chips)
     grad_tokens = run_spread(core, pre_own, pre_theirs, after, common[4])
     values, grad_tokens = tie(values, grad_tokens)
-    grad_conv, grad_decay, grad_skip = run_finish(core, scalar(lax.axis_index("dp")), values)
+    sums = run_fold(core, scalar(lax.div(chip, SIDE)), values)
+    near = 2 if sequences % 2 == 0 else 1
+    if near > 1:
+        values = around(sums, "dp", sequences, near, lambda i, d: i // 2 * 2 + (i % 2 + d) % 2)
+        sums = run_fold(core, scalar(lax.rem(sequence, near)), values)
+    values = around(sums, "dp", sequences, sequences // near, lambda i, d: (i + d * near) % sequences)
+    grad_conv, grad_decay, grad_skip = run_finish(core, scalar(lax.div(sequence, near)), values)
     return (
         out_tokens[None],
         grad_tokens[None],

time: 112 us -> 114 us (1.018)
  the two profiles are of different devices: /device:TPU:2 before, /device:TPU:9 now
where the time goes in v9:
time: 114 us
  Pallas kernels  41.9 us (37%)
  starting transfers between devices  41.4 us (36%)
  waiting for transfers between devices  28.8 us (25%)
    pallas_call x16, Pallas kernels, go(): run(*[pin(a, spaces[p]) if p in spaces else a for a, p in zip(args, specs...  41.9 us
    all_to_all x2, waiting for transfers between devices, all_to_all(): return lax.all_to_all(value, axis, 0, 0, tiled=True)  15.5 us
    all_to_all x2, starting transfers between devices, all_to_all(): return lax.all_to_all(value, axis, 0, 0, tiled=True)  11.9 us
    ppermute x7, starting transfers between devices, hear(): lax.ppermute(value, (axis, 'core'), [(2 * i + side, 2 * move(i, d) + side...  11.5 us
    ppermute x7, waiting for transfers between devices, hear(): lax.ppermute(value, (axis, 'core'), [(2 * i + side, 2 * move(i, d) + side...  8.43 us
    ppermute x3, starting transfers between devices, around(): swapped = [lax.ppermute(part, 'core', [(0, 1), (1, 0)]) for part in heard]  7.8 us
    ppermute x1, starting transfers between devices, local(): lax.ppermute(tokens[T - TAPS + 1:], CTX, [(i, i + 1) for i in range(devic...  3.77 us
    ppermute x1, waiting for transfers between devices, local(): after = lax.ppermute(first, CTX, [(i + 1, i) for i in range(devices - 1)])  3.39 us
  transfers between devices with their start and end apart: 19, of which 10 were waited for; matrix products, arithmetic and copies ran while one was open for 0% of the time, Pallas kernels for 28%

profile of v9, /device:TPU:9, one launch (start us, length us, event | category | flops | bytes accessed | tf_op | source)
XLA Modules:
  0.0 113.8 jit_solution(12393005677223480837)
XLA Ops:
  0.6 0.9 slice_bitcast_fusion
  1.5 3.8 %collective-permute-start = (bf16[3,5120]{1,0:T(4,128)(2,1)S(1)}, bf16[3,5120]{1,0:T(4,128)(2,1)S(1)}, u32[]{:S(2)}, u32[]{:S(2)}) collective-permute-start(bf16[3,5120]{1,0:T(4,128)(2,1)S(1)} %slice_bitcast_fusion), channel_id=1, source_target_pairs={{0,1},{1,2},{2,3},{3,4},{4,5},{5,6},{6,7},{7,8},{8,9},{9,10},{10,1... | collective-permute-start | bytes 92168 | tf_op jit(solution)/shard_map/ppermute | solution.py:1012
  5.3 4.2 %begin.1 = (f32[512,128]{1,0:T(8,128)}, f32[512,128]{1,0:T(8,128)S(1)}, f32[32,128]{1,0:T(8,128)S(1)}, bf16[128,4096]{1,0:T(8,128)(2,1)S(1)}, bf16[128,1024]{1,0...) custom-call(f32[64,128]{1,0:T(8,128)} %bitcast.26, ...), custom_call_target="tpu_custom_call" | custom-call | flops 4000000000 | bytes 14400000 | tf_op jit(solution)/shard_map/begin/pallas_call | solution.py:97
  9.6 2.4 %enter.1 = (bf16[128,4096]{1,0:T(8,128)(2,1)}, bf16[128,1024]{1,0:T(8,128)(2,1)}, f32[8,5120]{1,0:T(8,128)}, bf16[128,4096]{1,0:T(8,128)(2,1)S(1)}, bf16[128,102...) custom-call(s32[1]{0:T(128)} %bitcast.core_ref, bf16[128,4096]{1,0:T(8,128)(2,1)S(1)} %get-tuple-element.99.x0_ref, ...), custom_call_target="tpu_custom_call" | custom-call | flops 3000000000 | bytes 10800000 | tf_op jit(solution)/shard_map/enter/pallas_call | solution.py:97
  12.0 0.1 collective-permute-start.1
  12.1 0.5 collective-permute-start.2
  12.6 1.6 %own.1.own_ref = bf16[2,16,128,128]{3,2,1,0:T(8,128)(2,1)S(1)} custom-call(s32[1]{0:T(128)} %bitcast.core_ref, bf16[128,4096]{1,0:T(8,128)(2,1)S(1)} %get-tuple-element.106.x_ref, bf16[128,1024]{1,0:T(8,128)(2,1)S(1)} %get-tuple-element.107.bc_ref, bf16[128,4096]{1,0:T(8,128)(2,1)S(1)} %get-tuple-element.103.g_ref, f32[512,128]{1,0:T(8,128)S(1)} %get-tuple-element.104.small_ref), custom_call_target="tpu_custom_call" | custom-call | flops 3000000000 | bytes 10800000 | tf_op jit(solution)/shard_map/own/pallas_call | solution.py:97
  14.2 0.5 collective-permute-done.2.other_ref
  14.8 0.0 collective-permute-done.1.got_ref
  14.8 1.4 %pack.1 = (bf16[16,272,128]{2,1,0:T(8,128)(2,1)}, bf16[16,128,128]{2,1,0:T(8,128)(2,1)}, bf16[16,128,128]{2,1,0:T(8,128)(2,1)}, f32[64,128]{1,0:T(8,128)}) custom-call(s32[1]{0:T(128)} %bitcast.core_ref, bf16[2,16,128,128]{3,2,1,0:T(8,128)(2,1)S(1)} %own.1.own_ref, bf16[2,16,128,128]{3,2,1,0:T(8,128)(2,1)S(1)} %collective-permute-done.1.got_ref, ...), custom_call_target="tpu_custom_call" | custom-call | flops 2000000000 | bytes 7200000 | tf_op jit(solution)/shard_map/pack/pallas_call | solution.py:97
  16.2 6.5 %all-to-all-start = ((bf16[16,272,128]{2,1,0:T(8,128)(2,1)}), bf16[16,272,128]{2,1,0:T(8,128)(2,1)S(1)}, u32[]{:S(2)}, u32[]{:S(2)}) async-start(bf16[16,272,128]{2,1,0:T(8,128)(2,1)} %get-tuple-element.110), calls=%async_computation | async-start | bytes 2228224 | tf_op jit(solution)/shard_map/all_to_all | solution.py:975
  22.7 5.7 %inner.1 = (f32[128,4096]{1,0:T(8,128)}, f32[128,1024]{1,0:T(8,128)}, f32[32,128]{1,0:T(8,128)}) custom-call(bf16[128,4096]{1,0:T(8,128)(2,1)} %get-tuple-element.111.x_h.rest_0_.rest_21_, bf16[128,1024]{1,0:T(8,128)(2,1)} %get-tuple-element.118.bc_h.rest_6_.rest_27_, bf16[128,4096]{1,0:T(8,128)(2,1)} %bitcast.22, f32[512,128]{1,0:T(8,128)} %get-tuple-element.112.small_h.rest_9_), custom_call_target="tpu_custom_call" | custom-call | flops 4000000000 | bytes 14400000 | tf_op jit(solution)/shard_map/inner/pallas_call | solution.py:97
  28.4 10.2 %all-to-all-done.in_ref = bf16[16,272,128]{2,1,0:T(8,128)(2,1)S(1)} async-done(((bf16[16,272,128]{2,1,0:T(8,128)(2,1)}), bf16[16,272,128]{2,1,0:T(8,128)(2,1)S(1)}, u32[]{:S(2)}, u32[]{:S(2)}) %all-to-all-start) | async-done | bytes 1114144 | tf_op jit(solution)/shard_map/all_to_all | solution.py:975
  38.6 1.3 %chain.1 = bf16[16,256,128]{2,1,0:T(8,128)(2,1)} custom-call(bf16[16,272,128]{2,1,0:T(8,128)(2,1)S(1)} %all-to-all-done.in_ref), custom_call_target="tpu_custom_call" | custom-call | flops 1000000000 | bytes 3600000 | tf_op jit(solution)/shard_map/chain/pallas_call | solution.py:97
  39.9 5.3 %all-to-all-start.1 = ((bf16[16,256,128]{2,1,0:T(8,128)(2,1)}), bf16[16,256,128]{2,1,0:T(8,128)(2,1)S(1)}, u32[]{:S(2)}, u32[]{:S(2)}) async-start(bf16[16,256,128]{2,1,0:T(8,128)(2,1)} %chain.1), calls=%async_computation.1 | async-start | bytes 2097152 | tf_op jit(solution)/shard_map/all_to_all | solution.py:975
  45.2 8.7 %slopes.1 = (f32[128,4096]{1,0:T(8,128)}, f32[128,5120]{1,0:T(8,128)}) custom-call(bf16[128,1024]{1,0:T(8,128)(2,1)} %get-tuple-element.118.bc_h.rest_6_.rest_27_, bf16[128,4096]{1,0:T(8,128)(2,1)} %bitcast.23, f32[512,128]{1,0:T(8,128)} %get-tuple-element.112.small_h.rest_9_, bf16[128,5120]{1,0:T(8,128)(2,1)} %bitcast.18, ...), custom_call_target="tpu_custom_call" | custom-call | flops 6000000000 | bytes 21600000 | tf_op jit(solution)/shard_map/slopes/pallas_call | solution.py:97
  53.9 5.3 %all-to-all-done.1.back_ref = bf16[16,256,128]{2,1,0:T(8,128)(2,1)S(1)} async-done(((bf16[16,256,128]{2,1,0:T(8,128)(2,1)}), bf16[16,256,128]{2,1,0:T(8,128)(2,1)S(1)}, u32[]{:S(2)}, u32[]{:S(2)}) %all-to-all-start.1) | async-done | bytes 1048608 | tf_op jit(solution)/shard_map/all_to_all | solution.py:975
  59.2 3.8 %unpack.1 = (bf16[2,16,128,128]{3,2,1,0:T(8,128)(2,1)S(1)}, bf16[2,16,128,128]{3,2,1,0:T(8,128)(2,1)S(1)}, bf16[128,1024]{1,0:T(8,128)(2,1)S(1)}, bf16[128,1024]...) custom-call(s32[1]{0:T(128)} %bitcast.core_ref, ...), custom_call_target="tpu_custom_call" | custom-call | flops 3000000000 | bytes 10800000 | tf_op jit(solution)/shard_map/unpack/pallas_call | solution.py:97
  63.0 3.2 %collective-permute-start.3 = (bf16[2,16,128,128]{3,2,1,0:T(8,128)(2,1)S(1)}, bf16[2,16,128,128]{3,2,1,0:T(8,128)(2,1)S(1)}, u32[]{:S(2)}, u32[]{:S(2)}) collective-permute-start(bf16[2,16,128,128]{3,2,1,0:T(8,128)(2,1)S(1)} %get-tuple-element.131), channel_id=1, source_target_pairs={{0,1},{1,0},{2,3},{3,2},{4,5},{5,4},{6,7},{7,6},{8,9},{9,8},{10,11... | collective-permute-start | bytes 3145736 | tf_op jit(solution)/shard_map/ppermute | solution.py:1035
  66.3 4.2 %leave.2 = (bf16[128,4096]{1,0:T(8,128)(2,1)}, f32[64,128]{1,0:T(8,128)}, f32[128,2560]{1,0:T(8,128)S(1)}, f32[128,128]{1,0:T(8,128)S(1)}, bf16[128,1024]{1,0:T(...) custom-call(s32[1]{0:T(128)} %bitcast.core_ref, ...), custom_call_target="tpu_custom_call" | custom-call | flops 5000000000 | bytes 18000000 | tf_op jit(solution)/shard_map/leave/pallas_call | solution.py:97
  70.5 0.1 collective-permute-start.4
  70.6 0.0 collective-permute-done.3.state_ref
  70.6 4.2 %leave.3 = (bf16[128,4096]{1,0:T(8,128)(2,1)}, f32[64,128]{1,0:T(8,128)}, f32[128,2560]{1,0:T(8,128)}, f32[128,128]{1,0:T(8,128)S(1)}, bf16[3,5120]{1,0:T(4,128)(2,1)S(1)}) custom-call(s32[1]{0:T(128)} %bitcast.core_ref, bf16[2,16,128,128]{3,2,1,0:T(8,128)(2,1)S(1)} %collective-permute-done.3.state_ref, ...), custom_call_target="tpu_custom_call", output_to_operand_aliasing={{0}: (24, {}), {1}: (25, {})} | custom-call | flops 5000000000 | bytes 18000000 | tf_op jit(solution)/shard_map/leave/pallas_call | solution.py:97
  74.8 0.5 collective-permute-start.5
  75.4 0.0 collective-permute-done.4.own_got_ref
  75.4 0.9 collective-permute-done.5.theirs_got_ref
  76.3 0.6 merge.1.rest_0_
  76.8 1.2 %collective-permute-start.6 = (bf16[176,128]{1,0:T(8,128)(2,1)S(1)}, bf16[176,128]{1,0:T(8,128)(2,1)S(1)}, u32[]{:S(2)}, u32[]{:S(2)}) collective-permute-start(bf16[176,128]{1,0:T(8,128)(2,1)S(1)} %merge.1.rest_0_), channel_id=1, source_target_pairs={{0,2},{1,7},{2,4},{3,1},{4,6},{5,3},{6,0},{7,5},{8,10},{9,15},{10,... | collective-permute-start | bytes 135176 | tf_op jit(solution)/shard_map/ppermute | solution.py:987
  78.0 0.1 collective-permute-start.8
  78.1 1.6 %collective-permute-done.6.rest_1_ = bf16[176,128]{1,0:T(8,128)(2,1)S(1)} collective-permute-done((bf16[176,128]{1,0:T(8,128)(2,1)S(1)}, bf16[176,128]{1,0:T(8,128)(2,1)S(1)}, u32[]{:S(2)}, u32[]{:S(2)}) %collective-permute-start.6) | collective-permute-done | bytes 45088 | tf_op jit(solution)/shard_map/ppermute | solution.py:987
  79.7 1.5 %collective-permute-start.7 = (bf16[176,128]{1,0:T(8,128)(2,1)S(1)}, bf16[176,128]{1,0:T(8,128)(2,1)S(1)}, u32[]{:S(2)}, u32[]{:S(2)}) collective-permute-start(bf16[176,128]{1,0:T(8,128)(2,1)S(1)} %collective-permute-done.6.rest_1_), channel_id=1, source_target_pairs={{0,1},{1,0},{2,3},{3,2},{4,5},{5,4},{6,7},{7,6},{8,9},{9,8},{10,11... | collective-permute-start | bytes 135176 | tf_op jit(solution)/shard_map/ppermute | solution.py:995
  81.2 1.9 %collective-permute-start.9 = (bf16[3,5120]{1,0:T(4,128)(2,1)S(1)}, bf16[3,5120]{1,0:T(4,128)(2,1)S(1)}, u32[]{:S(2)}, u32[]{:S(2)}) collective-permute-start(bf16[3,5120]{1,0:T(4,128)(2,1)S(1)} %get-tuple-element.176), channel_id=1, source_target_pairs={{1,0},{2,1},{3,2},{4,3},{5,4},{6,5},{7,6},{8,7},{9,8},{10,9},{11,1... | collective-permute-start | bytes 92168 | tf_op jit(solution)/shard_map/ppermute | solution.py:1042
  83.2 3.4 %collective-permute-done.9.halo_ref = bf16[3,5120]{1,0:T(4,128)(2,1)S(1)} collective-permute-done((bf16[3,5120]{1,0:T(4,128)(2,1)S(1)}, bf16[3,5120]{1,0:T(4,128)(2,1)S(1)}, u32[]{:S(2)}, u32[]{:S(2)}) %collective-permute-start.9) | collective-permute-done | bytes 30752 | tf_op jit(solution)/shard_map/ppermute | solution.py:1042
  86.5 0.0 collective-permute-done.8.rest_3_
  86.5 0.0 collective-permute-done.7.rest_2_
  86.6 1.1 collective-permute-start.10
  87.7 0.6 collective-permute-start.12
  88.2 1.3 %collective-permute-done.10.rest_1_ = bf16[176,128]{1,0:T(8,128)(2,1)S(1)} collective-permute-done((bf16[176,128]{1,0:T(8,128)(2,1)S(1)}, bf16[176,128]{1,0:T(8,128)(2,1)S(1)}, u32[]{:S(2)}, u32[]{:S(2)}) %collective-permute-start.10) | collective-permute-done | bytes 45088 | tf_op jit(solution)/shard_map/ppermute | solution.py:987
  89.6 4.0 %collective-permute-start.11 = (bf16[176,128]{1,0:T(8,128)(2,1)S(1)}, bf16[176,128]{1,0:T(8,128)(2,1)S(1)}, u32[]{:S(2)}, u32[]{:S(2)}) collective-permute-start(bf16[176,128]{1,0:T(8,128)(2,1)S(1)} %collective-permute-done.10.rest_1_), channel_id=1, source_target_pairs={{0,1},{1,0},{2,3},{3,2},{4,5},{5,4},{6,7},{7,6},{8,9},{9,8},{10,11... | collective-permute-start | bytes 135176 | tf_op jit(solution)/shard_map/ppermute | solution.py:995
  93.6 3.0 %spread.1 = bf16[128,5120]{1,0:T(8,128)(2,1)} custom-call(s32[1]{0:T(128)} %bitcast.core_ref, f32[128,2560]{1,0:T(8,128)S(1)} %get-tuple-element.170.rest_21_.own_ref, f32[128,2560]{1,0:T(8,128)} %get-tuple-element.181.theirs_h, bf16[3,5120]{1,0:T(4,128)(2,1)S(1)} %collective-permute-done.9.halo_ref, f32[4,5120]{1,0:T(4,128)S(1)} %get-tuple-element.153.rest_20_.weight_ref), custom_call_target="tpu_custom_call" | custom-call | flops 3000000000 | bytes 10800000 | tf_op jit(solution)/shard_map/spread/pallas_call | solution.py:97
  96.7 1.7 %collective-permute-start.13 = (bf16[176,128]{1,0:T(8,128)(2,1)S(1)}, bf16[176,128]{1,0:T(8,128)(2,1)S(1)}, u32[]{:S(2)}, u32[]{:S(2)}) collective-permute-start(bf16[176,128]{1,0:T(8,128)(2,1)S(1)} %fold.4.rest_0_), channel_id=1, source_target_pairs={{0,32},{1,33},{32,0},{33,1},{64,96},{65,97},{96,64},{97,65},{128,1... | collective-permute-start | bytes 135176 | tf_op jit(solution)/shard_map/ppermute | solution.py:987
  98.4 1.9 %collective-permute-done.13.rest_1_ = bf16[176,128]{1,0:T(8,128)(2,1)S(1)} collective-permute-done((bf16[176,128]{1,0:T(8,128)(2,1)S(1)}, bf16[176,128]{1,0:T(8,128)(2,1)S(1)}, u32[]{:S(2)}, u32[]{:S(2)}) %collective-permute-start.13) | collective-permute-done | bytes 45088 | tf_op jit(solution)/shard_map/ppermute | solution.py:987
  100.3 5.9 %collective-permute-start.14 = (bf16[176,128]{1,0:T(8,128)(2,1)S(1)}, bf16[176,128]{1,0:T(8,128)(2,1)S(1)}, u32[]{:S(2)}, u32[]{:S(2)}) collective-permute-start(bf16[176,128]{1,0:T(8,128)(2,1)S(1)} %fold.5.rest_0_), channel_id=1, source_target_pairs={{0,64},{1,193},{32,96},{33,225},{64,128},{65,1},{96,160},{97,33},{... | collective-permute-start | bytes 135176 | tf_op jit(solution)/shard_map/ppermute | solution.py:987
  106.2 1.0 collective-permute-start.16
  107.2 0.1 collective-permute-done.14.rest_1_
  107.3 2.3 %collective-permute-start.15 = (bf16[176,128]{1,0:T(8,128)(2,1)S(1)}, bf16[176,128]{1,0:T(8,128)(2,1)S(1)}, u32[]{:S(2)}, u32[]{:S(2)}) collective-permute-start(bf16[176,128]{1,0:T(8,128)(2,1)S(1)} %collective-permute-done.14.rest_1_), channel_id=1, source_target_pairs={{0,1},{1,0},{2,3},{3,2},{4,5},{5,4},{6,7},{7,6},{8,9},{9,8},{10,11... | collective-permute-start | bytes 135176 | tf_op jit(solution)/shard_map/ppermute | solution.py:995
  109.6 3.5 %collective-permute-done.16.rest_3_ = bf16[176,128]{1,0:T(8,128)(2,1)S(1)} collective-permute-done((bf16[176,128]{1,0:T(8,128)(2,1)S(1)}, bf16[176,128]{1,0:T(8,128)(2,1)S(1)}, u32[]{:S(2)}, u32[]{:S(2)}) %collective-permute-start.16) | collective-permute-done | bytes 45088 | tf_op jit(solution)/shard_map/ppermute | solution.py:987
  113.1 0.7 finish.1
  (7 shorter events, 0.1 us)
Async XLA Ops:
  1.5 8.0 %collective-permute-start = (bf16[3,5120]{1,0:T(4,128)(2,1)S(1)}, bf16[3,5120]{1,0:T(4,128)(2,1)S(1)}, u32[]{:S(2)}, u32[]{:S(2)}) collective-permute-start(bf16[3,5120]{1,0:T(4,128)(2,1)S(1)} %slice_bitcast_fusion), channel_id=1, source_target_pairs={{0,1},{1,2},{2,3},{3,4},{4,5},{5,6},{6,7},{7,8},{8,9},{9,10},{10,1... | collective-permute-start | bytes 92168 | tf_op jit(solution)/shard_map/ppermute | solution.py:1012
  12.0 2.8 %collective-permute-start.1 = (bf16[2,16,128,128]{3,2,1,0:T(8,128)(2,1)S(1)}, bf16[2,16,128,128]{3,2,1,0:T(8,128)(2,1)S(1)}, u32[]{:S(2)}, u32[]{:S(2)}) collective-permute-start(bf16[2,16,128,128]{3,2,1,0:T(8,128)(2,1)S(1)} %get-tuple-element.108), channel_id=1, source_target_pairs={{0,1},{1,0},{2,3},{3,2},{4,5},{5,4},{6,7},{7,6},{8,9},{9,8},{10,11... | collective-permute-start | bytes 3145736 | tf_op jit(solution)/shard_map/ppermute | solution.py:1020
  12.1 2.7 %collective-permute-start.2 = (f32[32,128]{1,0:T(8,128)S(1)}, f32[32,128]{1,0:T(8,128)S(1)}, u32[]{:S(2)}, u32[]{:S(2)}) collective-permute-start(f32[32,128]{1,0:T(8,128)S(1)} %get-tuple-element.109.tot_ref), channel_id=1, source_target_pairs={{0,1},{1,0},{2,3},{3,2},{4,5},{5,4},{6,7},{7,6},{8,9},{9,8},{10,11... | collective-permute-start | bytes 49160 | tf_op jit(solution)/shard_map/ppermute | solution.py:1016
  16.2 22.4 %all-to-all-start = ((bf16[16,272,128]{2,1,0:T(8,128)(2,1)}), bf16[16,272,128]{2,1,0:T(8,128)(2,1)S(1)}, u32[]{:S(2)}, u32[]{:S(2)}) async-start(bf16[16,272,128]{2,1,0:T(8,128)(2,1)} %get-tuple-element.110), calls=%async_computation | async-start | bytes 2228224 | tf_op jit(solution)/shard_map/all_to_all | solution.py:975
  39.9 19.3 %all-to-all-start.1 = ((bf16[16,256,128]{2,1,0:T(8,128)(2,1)}), bf16[16,256,128]{2,1,0:T(8,128)(2,1)S(1)}, u32[]{:S(2)}, u32[]{:S(2)}) async-start(bf16[16,256,128]{2,1,0:T(8,128)(2,1)} %chain.1), calls=%async_computation.1 | async-start | bytes 2097152 | tf_op jit(solution)/shard_map/all_to_all | solution.py:975
  63.0 7.6 %collective-permute-start.3 = (bf16[2,16,128,128]{3,2,1,0:T(8,128)(2,1)S(1)}, bf16[2,16,128,128]{3,2,1,0:T(8,128)(2,1)S(1)}, u32[]{:S(2)}, u32[]{:S(2)}) collective-permute-start(bf16[2,16,128,128]{3,2,1,0:T(8,128)(2,1)S(1)} %get-tuple-element.131), channel_id=1, source_target_pairs={{0,1},{1,0},{2,3},{3,2},{4,5},{5,4},{6,7},{7,6},{8,9},{9,8},{10,11... | collective-permute-start | bytes 3145736 | tf_op jit(solution)/shard_map/ppermute | solution.py:1035
  70.5 4.9 %collective-permute-start.4 = (f32[128,128]{1,0:T(8,128)S(1)}, f32[128,128]{1,0:T(8,128)S(1)}, u32[]{:S(2)}, u32[]{:S(2)}) collective-permute-start(f32[128,128]{1,0:T(8,128)S(1)} %get-tuple-element.174.own_ref), channel_id=1, source_target_pairs={{0,1},{1,0},{2,3},{3,2},{4,5},{5,4},{6,7},{7,6},{8,9},{9,8},{10,11... | collective-permute-start | bytes 196616 | tf_op jit(solution)/shard_map/ppermute | solution.py:1037
  74.8 1.5 %collective-permute-start.5 = (f32[128,128]{1,0:T(8,128)S(1)}, f32[128,128]{1,0:T(8,128)S(1)}, u32[]{:S(2)}, u32[]{:S(2)}) collective-permute-start(f32[128,128]{1,0:T(8,128)S(1)} %get-tuple-element.175.theirs_ref), channel_id=1, source_target_pairs={{0,1},{1,0},{2,3},{3,2},{4,5},{5,4},{6,7},{7,6},{8,9},{9,8},{10,11... | collective-permute-start | bytes 196616 | tf_op jit(solution)/shard_map/ppermute | solution.py:1041
  76.8 2.9 %collective-permute-start.6 = (bf16[176,128]{1,0:T(8,128)(2,1)S(1)}, bf16[176,128]{1,0:T(8,128)(2,1)S(1)}, u32[]{:S(2)}, u32[]{:S(2)}) collective-permute-start(bf16[176,128]{1,0:T(8,128)(2,1)S(1)} %merge.1.rest_0_), channel_id=1, source_target_pairs={{0,2},{1,7},{2,4},{3,1},{4,6},{5,3},{6,0},{7,5},{8,10},{9,15},{10,... | collective-permute-start | bytes 135176 | tf_op jit(solution)/shard_map/ppermute | solution.py:987
  78.0 8.5 %collective-permute-start.8 = (bf16[176,128]{1,0:T(8,128)(2,1)S(1)}, bf16[176,128]{1,0:T(8,128)(2,1)S(1)}, u32[]{:S(2)}, u32[]{:S(2)}) collective-permute-start(bf16[176,128]{1,0:T(8,128)(2,1)S(1)} %merge.1.rest_0_), channel_id=1, source_target_pairs={{0,4},{1,5},{2,6},{3,7},{4,0},{5,1},{6,2},{7,3},{8,12},{9,13},{10,... | collective-permute-start | bytes 135176 | tf_op jit(solution)/shard_map/ppermute | solution.py:987
  79.7 6.8 %collective-permute-start.7 = (bf16[176,128]{1,0:T(8,128)(2,1)S(1)}, bf16[176,128]{1,0:T(8,128)(2,1)S(1)}, u32[]{:S(2)}, u32[]{:S(2)}) collective-permute-start(bf16[176,128]{1,0:T(8,128)(2,1)S(1)} %collective-permute-done.6.rest_1_), channel_id=1, source_target_pairs={{0,1},{1,0},{2,3},{3,2},{4,5},{5,4},{6,7},{7,6},{8,9},{9,8},{10,11... | collective-permute-start | bytes 135176 | tf_op jit(solution)/shard_map/ppermute | solution.py:995
  81.2 5.3 %collective-permute-start.9 = (bf16[3,5120]{1,0:T(4,128)(2,1)S(1)}, bf16[3,5120]{1,0:T(4,128)(2,1)S(1)}, u32[]{:S(2)}, u32[]{:S(2)}) collective-permute-start(bf16[3,5120]{1,0:T(4,128)(2,1)S(1)} %get-tuple-element.176), channel_id=1, source_target_pairs={{1,0},{2,1},{3,2},{4,3},{5,4},{6,5},{7,6},{8,7},{9,8},{10,9},{11,1... | collective-permute-start | bytes 92168 | tf_op jit(solution)/shard_map/ppermute | solution.py:1042
  86.6 3.0 %collective-permute-start.10 = (bf16[176,128]{1,0:T(8,128)(2,1)S(1)}, bf16[176,128]{1,0:T(8,128)(2,1)S(1)}, u32[]{:S(2)}, u32[]{:S(2)}) collective-permute-start(bf16[176,128]{1,0:T(8,128)(2,1)S(1)} %fold.3.rest_0_), channel_id=1, source_target_pairs={{0,8},{1,25},{2,10},{3,27},{4,12},{5,29},{6,14},{7,31},{8,16},{9,1... | collective-permute-start | bytes 135176 | tf_op jit(solution)/shard_map/ppermute | solution.py:987
  87.7 9.0 %collective-permute-start.12 = (bf16[176,128]{1,0:T(8,128)(2,1)S(1)}, bf16[176,128]{1,0:T(8,128)(2,1)S(1)}, u32[]{:S(2)}, u32[]{:S(2)}) collective-permute-start(bf16[176,128]{1,0:T(8,128)(2,1)S(1)} %fold.3.rest_0_), channel_id=1, source_target_pairs={{0,16},{1,17},{2,18},{3,19},{4,20},{5,21},{6,22},{7,23},{8,24},{9,... | collective-permute-start | bytes 135176 | tf_op jit(solution)/shard_map/ppermute | solution.py:987
  89.6 7.1 %collective-permute-start.11 = (bf16[176,128]{1,0:T(8,128)(2,1)S(1)}, bf16[176,128]{1,0:T(8,128)(2,1)S(1)}, u32[]{:S(2)}, u32[]{:S(2)}) collective-permute-start(bf16[176,128]{1,0:T(8,128)(2,1)S(1)} %collective-permute-done.10.rest_1_), channel_id=1, source_target_pairs={{0,1},{1,0},{2,3},{3,2},{4,5},{5,4},{6,7},{7,6},{8,9},{9,8},{10,11... | collective-permute-start | bytes 135176 | tf_op jit(solution)/shard_map/ppermute | solution.py:995
  96.7 3.6 %collective-permute-start.13 = (bf16[176,128]{1,0:T(8,128)(2,1)S(1)}, bf16[176,128]{1,0:T(8,128)(2,1)S(1)}, u32[]{:S(2)}, u32[]{:S(2)}) collective-permute-start(bf16[176,128]{1,0:T(8,128)(2,1)S(1)} %fold.4.rest_0_), channel_id=1, source_target_pairs={{0,32},{1,33},{32,0},{33,1},{64,96},{65,97},{96,64},{97,65},{128,1... | collective-permute-start | bytes 135176 | tf_op jit(solution)/shard_map/ppermute | solution.py:987
  100.3 7.1 %collective-permute-start.14 = (bf16[176,128]{1,0:T(8,128)(2,1)S(1)}, bf16[176,128]{1,0:T(8,128)(2,1)S(1)}, u32[]{:S(2)}, u32[]{:S(2)}) collective-permute-start(bf16[176,128]{1,0:T(8,128)(2,1)S(1)} %fold.5.rest_0_), channel_id=1, source_target_pairs={{0,64},{1,193},{32,96},{33,225},{64,128},{65,1},{96,160},{97,33},{... | collective-permute-start | bytes 135176 | tf_op jit(solution)/shard_map/ppermute | solution.py:987
  106.2 6.9 %collective-permute-start.16 = (bf16[176,128]{1,0:T(8,128)(2,1)S(1)}, bf16[176,128]{1,0:T(8,128)(2,1)S(1)}, u32[]{:S(2)}, u32[]{:S(2)}) collective-permute-start(bf16[176,128]{1,0:T(8,128)(2,1)S(1)} %fold.5.rest_0_), channel_id=1, source_target_pairs={{0,128},{1,129},{32,160},{33,161},{64,192},{65,193},{96,224},{97,2... | collective-permute-start | bytes 135176 | tf_op jit(solution)/shard_map/ppermute | solution.py:987
  107.3 5.8 %collective-permute-start.15 = (bf16[176,128]{1,0:T(8,128)(2,1)S(1)}, bf16[176,128]{1,0:T(8,128)(2,1)S(1)}, u32[]{:S(2)}, u32[]{:S(2)}) collective-permute-start(bf16[176,128]{1,0:T(8,128)(2,1)S(1)} %collective-permute-done.14.rest_1_), channel_id=1, source_target_pairs={{0,1},{1,0},{2,3},{3,2},{4,5},{5,4},{6,7},{7,6},{8,9},{9,8},{10,11... | collective-permute-start | bytes 135176 | tf_op jit(solution)/shard_map/ppermute | solution.py:995

commit v10 on v9

--- a/solution.py
+++ b/solution.py
@@ -1044,11 +1044,10 @@
     chip, sequence = lax.axis_index("chip"), lax.axis_index("dp")
     rows = chips // SIDE
     values = around(sums, "chip", chips, SIDE, lambda i, d: i // SIDE * SIDE + (i % SIDE + d) % SIDE)
-    values, after = tie(values, after)
+    grad_tokens = run_spread(core, pre_own, pre_theirs, after, common[4])
+    values, grad_tokens = tie(values, grad_tokens)
     sums = run_fold(core, scalar(lax.rem(chip, SIDE)), values)
     values = around(sums, "chip", chips, rows, lambda i, d: (i + d * SIDE) % chips)
-    grad_tokens = run_spread(core, pre_own, pre_theirs, after, common[4])
-    values, grad_tokens = tie(values, grad_tokens)
     sums = run_fold(core, scalar(lax.div(chip, SIDE)), values)
     near = 2 if sequences % 2 == 0 else 1
     if near > 1:

time: 114 us -> 111 us (0.974)
  the two profiles are of different devices: /device:TPU:9 before, /device:TPU:2 now
where the time goes in v10:
time: 111 us; the launch traced here: 110 us
  Pallas kernels  41.9 us (38%)
  starting transfers between devices  36.2 us (33%)
  waiting for transfers between devices  30.1 us (27%)
    pallas_call x16, Pallas kernels, go(): run(*[pin(a, spaces[p]) if p in spaces else a for a, p in zip(args, specs...  41.9 us
    all_to_all x2, waiting for transfers between devices, all_to_all(): return lax.all_to_all(value, axis, 0, 0, tiled=True)  16.4 us
    ppermute x7, starting transfers between devices, hear(): lax.ppermute(value, (axis, 'core'), [(2 * i + side, 2 * move(i, d) + side...  15.6 us
    all_to_all x2, starting transfers between devices, all_to_all(): return lax.all_to_all(value, axis, 0, 0, tiled=True)  13.4 us
    ppermute x7, waiting for transfers between devices, hear(): lax.ppermute(value, (axis, 'core'), [(2 * i + side, 2 * move(i, d) + side...  10.2 us
    ppermute x1, starting transfers between devices, local(): after = lax.ppermute(first, CTX, [(i + 1, i) for i in range(devices - 1)])  3.76 us
  transfers between devices with their start and end apart: 19, of which 11 were waited for; matrix products, arithmetic and copies ran while one was open for 0% of the time, Pallas kernels for 29%

profile of v10, /device:TPU:2, one launch (start us, length us, event | category | flops | bytes accessed | tf_op | source)
XLA Modules:
  0.0 109.9 jit_solution(6420337722333854483)
XLA Ops:
  0.6 0.9 slice_bitcast_fusion
  1.5 1.9 %collective-permute-start = (bf16[3,5120]{1,0:T(4,128)(2,1)S(1)}, bf16[3,5120]{1,0:T(4,128)(2,1)S(1)}, u32[]{:S(2)}, u32[]{:S(2)}) collective-permute-start(bf16[3,5120]{1,0:T(4,128)(2,1)S(1)} %slice_bitcast_fusion), channel_id=1, source_target_pairs={{0,1},{1,2},{2,3},{3,4},{4,5},{5,6},{6,7},{7,8},{8,9},{9,10},{10,1... | collective-permute-start | bytes 92168 | tf_op jit(solution)/shard_map/ppermute | solution.py:1012
  3.5 4.2 %begin.1 = (f32[512,128]{1,0:T(8,128)}, f32[512,128]{1,0:T(8,128)S(1)}, f32[32,128]{1,0:T(8,128)S(1)}, bf16[128,4096]{1,0:T(8,128)(2,1)S(1)}, bf16[128,1024]{1,0...) custom-call(f32[64,128]{1,0:T(8,128)} %bitcast.26, ...), custom_call_target="tpu_custom_call" | custom-call | flops 4000000000 | bytes 14400000 | tf_op jit(solution)/shard_map/begin/pallas_call | solution.py:97
  7.7 1.2 %collective-permute-done.halo_ref = bf16[3,5120]{1,0:T(4,128)(2,1)S(1)} collective-permute-done((bf16[3,5120]{1,0:T(4,128)(2,1)S(1)}, bf16[3,5120]{1,0:T(4,128)(2,1)S(1)}, u32[]{:S(2)}, u32[]{:S(2)}) %collective-permute-start) | collective-permute-done | bytes 30752 | tf_op jit(solution)/shard_map/ppermute | solution.py:1012
  9.0 2.4 %enter.1 = (bf16[128,4096]{1,0:T(8,128)(2,1)}, bf16[128,1024]{1,0:T(8,128)(2,1)}, f32[8,5120]{1,0:T(8,128)}, bf16[128,4096]{1,0:T(8,128)(2,1)S(1)}, bf16[128,102...) custom-call(s32[1]{0:T(128)} %bitcast.core_ref, bf16[128,4096]{1,0:T(8,128)(2,1)S(1)} %get-tuple-element.94.x0_ref, ...), custom_call_target="tpu_custom_call" | custom-call | flops 3000000000 | bytes 10800000 | tf_op jit(solution)/shard_map/enter/pallas_call | solution.py:97
  11.4 0.5 collective-permute-start.1
  11.9 0.1 collective-permute-start.2
  12.0 1.6 %own.1.own_ref = bf16[2,16,128,128]{3,2,1,0:T(8,128)(2,1)S(1)} custom-call(s32[1]{0:T(128)} %bitcast.core_ref, bf16[128,4096]{1,0:T(8,128)(2,1)S(1)} %get-tuple-element.101.x_ref, bf16[128,1024]{1,0:T(8,128)(2,1)S(1)} %get-tuple-element.102.bc_ref, bf16[128,4096]{1,0:T(8,128)(2,1)S(1)} %get-tuple-element.98.g_ref, f32[512,128]{1,0:T(8,128)S(1)} %get-tuple-element.99.small_ref), custom_call_target="tpu_custom_call" | custom-call | flops 3000000000 | bytes 10800000 | tf_op jit(solution)/shard_map/own/pallas_call | solution.py:97
  13.6 0.6 collective-permute-done.2.other_ref
  14.2 0.0 collective-permute-done.1.got_ref
  14.2 1.4 %pack.1 = (bf16[16,272,128]{2,1,0:T(8,128)(2,1)}, bf16[16,128,128]{2,1,0:T(8,128)(2,1)}, bf16[16,128,128]{2,1,0:T(8,128)(2,1)}, f32[64,128]{1,0:T(8,128)}) custom-call(s32[1]{0:T(128)} %bitcast.core_ref, bf16[2,16,128,128]{3,2,1,0:T(8,128)(2,1)S(1)} %own.1.own_ref, bf16[2,16,128,128]{3,2,1,0:T(8,128)(2,1)S(1)} %collective-permute-done.1.got_ref, ...), custom_call_target="tpu_custom_call" | custom-call | flops 2000000000 | bytes 7200000 | tf_op jit(solution)/shard_map/pack/pallas_call | solution.py:97
  15.6 7.2 %all-to-all-start = ((bf16[16,272,128]{2,1,0:T(8,128)(2,1)}), bf16[16,272,128]{2,1,0:T(8,128)(2,1)S(1)}, u32[]{:S(2)}, u32[]{:S(2)}) async-start(bf16[16,272,128]{2,1,0:T(8,128)(2,1)} %get-tuple-element.105), calls=%async_computation | async-start | bytes 2228224 | tf_op jit(solution)/shard_map/all_to_all | solution.py:975
  22.9 5.7 %inner.1 = (f32[128,4096]{1,0:T(8,128)}, f32[128,1024]{1,0:T(8,128)}, f32[32,128]{1,0:T(8,128)}) custom-call(bf16[128,4096]{1,0:T(8,128)(2,1)} %get-tuple-element.106.x_h.rest_0_.rest_21_, bf16[128,1024]{1,0:T(8,128)(2,1)} %get-tuple-element.113.bc_h.rest_6_.rest_27_, bf16[128,4096]{1,0:T(8,128)(2,1)} %bitcast.22, f32[512,128]{1,0:T(8,128)} %get-tuple-element.107.small_h.rest_9_), custom_call_target="tpu_custom_call" | custom-call | flops 4000000000 | bytes 14400000 | tf_op jit(solution)/shard_map/inner/pallas_call | solution.py:97
  28.5 10.8 %all-to-all-done.in_ref = bf16[16,272,128]{2,1,0:T(8,128)(2,1)S(1)} async-done(((bf16[16,272,128]{2,1,0:T(8,128)(2,1)}), bf16[16,272,128]{2,1,0:T(8,128)(2,1)S(1)}, u32[]{:S(2)}, u32[]{:S(2)}) %all-to-all-start) | async-done | bytes 1114144 | tf_op jit(solution)/shard_map/all_to_all | solution.py:975
  39.3 1.3 %chain.1 = bf16[16,256,128]{2,1,0:T(8,128)(2,1)} custom-call(bf16[16,272,128]{2,1,0:T(8,128)(2,1)S(1)} %all-to-all-done.in_ref), custom_call_target="tpu_custom_call" | custom-call | flops 1000000000 | bytes 3600000 | tf_op jit(solution)/shard_map/chain/pallas_call | solution.py:97
  40.6 6.2 %all-to-all-start.1 = ((bf16[16,256,128]{2,1,0:T(8,128)(2,1)}), bf16[16,256,128]{2,1,0:T(8,128)(2,1)S(1)}, u32[]{:S(2)}, u32[]{:S(2)}) async-start(bf16[16,256,128]{2,1,0:T(8,128)(2,1)} %chain.1), calls=%async_computation.1 | async-start | bytes 2097152 | tf_op jit(solution)/shard_map/all_to_all | solution.py:975
  46.8 8.7 %slopes.1 = (f32[128,4096]{1,0:T(8,128)}, f32[128,5120]{1,0:T(8,128)}) custom-call(bf16[128,1024]{1,0:T(8,128)(2,1)} %get-tuple-element.113.bc_h.rest_6_.rest_27_, bf16[128,4096]{1,0:T(8,128)(2,1)} %bitcast.23, f32[512,128]{1,0:T(8,128)} %get-tuple-element.107.small_h.rest_9_, bf16[128,5120]{1,0:T(8,128)(2,1)} %bitcast.18, ...), custom_call_target="tpu_custom_call" | custom-call | flops 6000000000 | bytes 21600000 | tf_op jit(solution)/shard_map/slopes/pallas_call | solution.py:97
  55.5 5.6 %all-to-all-done.1.back_ref = bf16[16,256,128]{2,1,0:T(8,128)(2,1)S(1)} async-done(((bf16[16,256,128]{2,1,0:T(8,128)(2,1)}), bf16[16,256,128]{2,1,0:T(8,128)(2,1)S(1)}, u32[]{:S(2)}, u32[]{:S(2)}) %all-to-all-start.1) | async-done | bytes 1048608 | tf_op jit(solution)/shard_map/all_to_all | solution.py:975
  61.1 3.8 %unpack.1 = (bf16[2,16,128,128]{3,2,1,0:T(8,128)(2,1)S(1)}, bf16[2,16,128,128]{3,2,1,0:T(8,128)(2,1)S(1)}, bf16[128,1024]{1,0:T(8,128)(2,1)S(1)}, bf16[128,1024]...) custom-call(s32[1]{0:T(128)} %bitcast.core_ref, ...), custom_call_target="tpu_custom_call" | custom-call | flops 3000000000 | bytes 10800000 | tf_op jit(solution)/shard_map/unpack/pallas_call | solution.py:97
  64.9 0.3 collective-permute-start.3
  65.2 4.2 %leave.2 = (bf16[128,4096]{1,0:T(8,128)(2,1)}, f32[64,128]{1,0:T(8,128)}, f32[128,2560]{1,0:T(8,128)S(1)}, f32[128,128]{1,0:T(8,128)S(1)}, bf16[128,1024]{1,0:T(...) custom-call(s32[1]{0:T(128)} %bitcast.core_ref, ...), custom_call_target="tpu_custom_call" | custom-call | flops 5000000000 | bytes 18000000 | tf_op jit(solution)/shard_map/leave/pallas_call | solution.py:97
  69.4 0.6 collective-permute-start.4
  70.0 0.0 collective-permute-done.3.state_ref
  70.0 4.2 %leave.3 = (bf16[128,4096]{1,0:T(8,128)(2,1)}, f32[64,128]{1,0:T(8,128)}, f32[128,2560]{1,0:T(8,128)}, f32[128,128]{1,0:T(8,128)S(1)}, bf16[3,5120]{1,0:T(4,128)(2,1)S(1)}) custom-call(s32[1]{0:T(128)} %bitcast.core_ref, bf16[2,16,128,128]{3,2,1,0:T(8,128)(2,1)S(1)} %collective-permute-done.3.state_ref, ...), custom_call_target="tpu_custom_call", output_to_operand_aliasing={{0}: (24, {}), {1}: (25, {})} | custom-call | flops 5000000000 | bytes 18000000 | tf_op jit(solution)/shard_map/leave/pallas_call | solution.py:97
  74.2 0.1 collective-permute-start.5
  74.3 0.0 collective-permute-done.4.own_got_ref
  74.3 1.2 %collective-permute-done.5.theirs_got_ref = f32[128,128]{1,0:T(8,128)S(1)} collective-permute-done((f32[128,128]{1,0:T(8,128)S(1)}, f32[128,128]{1,0:T(8,128)S(1)}, u32[]{:S(2)}, u32[]{:S(2)}) %collective-permute-start.5) | collective-permute-done | bytes 65568 | tf_op jit(solution)/shard_map/ppermute | solution.py:1041
  75.5 0.6 merge.1.rest_0_
  76.1 0.6 collective-permute-start.6
  76.7 3.8 %collective-permute-start.9 = (bf16[3,5120]{1,0:T(4,128)(2,1)S(1)}, bf16[3,5120]{1,0:T(4,128)(2,1)S(1)}, u32[]{:S(2)}, u32[]{:S(2)}) collective-permute-start(bf16[3,5120]{1,0:T(4,128)(2,1)S(1)} %get-tuple-element.172), channel_id=1, source_target_pairs={{1,0},{2,1},{3,2},{4,3},{5,4},{6,5},{7,6},{8,7},{9,8},{10,9},{11,1... | collective-permute-start | bytes 92168 | tf_op jit(solution)/shard_map/ppermute | solution.py:1042
  80.4 1.2 %collective-permute-start.8 = (bf16[176,128]{1,0:T(8,128)(2,1)S(1)}, bf16[176,128]{1,0:T(8,128)(2,1)S(1)}, u32[]{:S(2)}, u32[]{:S(2)}) collective-permute-start(bf16[176,128]{1,0:T(8,128)(2,1)S(1)} %merge.1.rest_0_), channel_id=1, source_target_pairs={{0,4},{1,5},{2,6},{3,7},{4,0},{5,1},{6,2},{7,3},{8,12},{9,13},{10,... | collective-permute-start | bytes 135176 | tf_op jit(solution)/shard_map/ppermute | solution.py:987
  81.7 0.0 collective-permute-done.6.rest_1_
  81.7 0.0 collective-permute-start.7
  81.7 0.4 collective-permute-done.9.halo_ref
  82.1 3.0 %spread.1 = bf16[128,5120]{1,0:T(8,128)(2,1)} custom-call(s32[1]{0:T(128)} %bitcast.core_ref, f32[128,2560]{1,0:T(8,128)S(1)} %get-tuple-element.165.rest_21_.own_ref, f32[128,2560]{1,0:T(8,128)} %get-tuple-element.171.theirs_h, bf16[3,5120]{1,0:T(4,128)(2,1)S(1)} %collective-permute-done.9.halo_ref, f32[4,5120]{1,0:T(4,128)S(1)} %get-tuple-element.148.rest_20_.weight_ref), custom_call_target="tpu_custom_call" | custom-call | flops 3000000000 | bytes 10800000 | tf_op jit(solution)/shard_map/spread/pallas_call | solution.py:97
  85.1 0.9 collective-permute-done.8.rest_3_
  86.1 0.0 collective-permute-done.7.rest_2_
  86.1 1.3 %collective-permute-start.10 = (bf16[176,128]{1,0:T(8,128)(2,1)S(1)}, bf16[176,128]{1,0:T(8,128)(2,1)S(1)}, u32[]{:S(2)}, u32[]{:S(2)}) collective-permute-start(bf16[176,128]{1,0:T(8,128)(2,1)S(1)} %fold.3.rest_0_), channel_id=1, source_target_pairs={{0,8},{1,25},{2,10},{3,27},{4,12},{5,29},{6,14},{7,31},{8,16},{9,1... | collective-permute-start | bytes 135176 | tf_op jit(solution)/shard_map/ppermute | solution.py:987
  87.4 1.7 %collective-permute-start.12 = (bf16[176,128]{1,0:T(8,128)(2,1)S(1)}, bf16[176,128]{1,0:T(8,128)(2,1)S(1)}, u32[]{:S(2)}, u32[]{:S(2)}) collective-permute-start(bf16[176,128]{1,0:T(8,128)(2,1)S(1)} %fold.3.rest_0_), channel_id=1, source_target_pairs={{0,16},{1,17},{2,18},{3,19},{4,20},{5,21},{6,22},{7,23},{8,24},{9,... | collective-permute-start | bytes 135176 | tf_op jit(solution)/shard_map/ppermute | solution.py:987
  89.1 1.5 %collective-permute-done.10.rest_1_ = bf16[176,128]{1,0:T(8,128)(2,1)S(1)} collective-permute-done((bf16[176,128]{1,0:T(8,128)(2,1)S(1)}, bf16[176,128]{1,0:T(8,128)(2,1)S(1)}, u32[]{:S(2)}, u32[]{:S(2)}) %collective-permute-start.10) | collective-permute-done | bytes 45088 | tf_op jit(solution)/shard_map/ppermute | solution.py:987
  90.6 0.0 collective-permute-start.11
  90.6 2.3 %collective-permute-done.12.rest_3_ = bf16[176,128]{1,0:T(8,128)(2,1)S(1)} collective-permute-done((bf16[176,128]{1,0:T(8,128)(2,1)S(1)}, bf16[176,128]{1,0:T(8,128)(2,1)S(1)}, u32[]{:S(2)}, u32[]{:S(2)}) %collective-permute-start.12) | collective-permute-done | bytes 45088 | tf_op jit(solution)/shard_map/ppermute | solution.py:987
  93.0 2.0 %collective-permute-start.13 = (bf16[176,128]{1,0:T(8,128)(2,1)S(1)}, bf16[176,128]{1,0:T(8,128)(2,1)S(1)}, u32[]{:S(2)}, u32[]{:S(2)}) collective-permute-start(bf16[176,128]{1,0:T(8,128)(2,1)S(1)} %fold.4.rest_0_), channel_id=1, source_target_pairs={{0,32},{1,33},{32,0},{33,1},{64,96},{65,97},{96,64},{97,65},{128,1... | collective-permute-start | bytes 135176 | tf_op jit(solution)/shard_map/ppermute | solution.py:987
  95.0 2.1 %collective-permute-done.13.rest_1_ = bf16[176,128]{1,0:T(8,128)(2,1)S(1)} collective-permute-done((bf16[176,128]{1,0:T(8,128)(2,1)S(1)}, bf16[176,128]{1,0:T(8,128)(2,1)S(1)}, u32[]{:S(2)}, u32[]{:S(2)}) %collective-permute-start.13) | collective-permute-done | bytes 45088 | tf_op jit(solution)/shard_map/ppermute | solution.py:987
  97.2 3.3 %collective-permute-start.14 = (bf16[176,128]{1,0:T(8,128)(2,1)S(1)}, bf16[176,128]{1,0:T(8,128)(2,1)S(1)}, u32[]{:S(2)}, u32[]{:S(2)}) collective-permute-start(bf16[176,128]{1,0:T(8,128)(2,1)S(1)} %fold.5.rest_0_), channel_id=1, source_target_pairs={{0,64},{1,193},{32,96},{33,225},{64,128},{65,1},{96,160},{97,33},{... | collective-permute-start | bytes 135176 | tf_op jit(solution)/shard_map/ppermute | solution.py:987
  100.5 5.4 %collective-permute-start.16 = (bf16[176,128]{1,0:T(8,128)(2,1)S(1)}, bf16[176,128]{1,0:T(8,128)(2,1)S(1)}, u32[]{:S(2)}, u32[]{:S(2)}) collective-permute-start(bf16[176,128]{1,0:T(8,128)(2,1)S(1)} %fold.5.rest_0_), channel_id=1, source_target_pairs={{0,128},{1,129},{32,160},{33,161},{64,192},{65,193},{96,224},{97,2... | collective-permute-start | bytes 135176 | tf_op jit(solution)/shard_map/ppermute | solution.py:987
  105.9 3.3 %collective-permute-done.16.rest_3_ = bf16[176,128]{1,0:T(8,128)(2,1)S(1)} collective-permute-done((bf16[176,128]{1,0:T(8,128)(2,1)S(1)}, bf16[176,128]{1,0:T(8,128)(2,1)S(1)}, u32[]{:S(2)}, u32[]{:S(2)}) %collective-permute-start.16) | collective-permute-done | bytes 45088 | tf_op jit(solution)/shard_map/ppermute | solution.py:987
  109.3 0.7 finish.1
  (7 shorter events, 0.1 us)
Async XLA Ops:
  1.5 7.4 %collective-permute-start = (bf16[3,5120]{1,0:T(4,128)(2,1)S(1)}, bf16[3,5120]{1,0:T(4,128)(2,1)S(1)}, u32[]{:S(2)}, u32[]{:S(2)}) collective-permute-start(bf16[3,5120]{1,0:T(4,128)(2,1)S(1)} %slice_bitcast_fusion), channel_id=1, source_target_pairs={{0,1},{1,2},{2,3},{3,4},{4,5},{5,6},{6,7},{7,8},{8,9},{9,10},{10,1... | collective-permute-start | bytes 92168 | tf_op jit(solution)/shard_map/ppermute | solution.py:1012
  11.4 2.8 %collective-permute-start.1 = (bf16[2,16,128,128]{3,2,1,0:T(8,128)(2,1)S(1)}, bf16[2,16,128,128]{3,2,1,0:T(8,128)(2,1)S(1)}, u32[]{:S(2)}, u32[]{:S(2)}) collective-permute-start(bf16[2,16,128,128]{3,2,1,0:T(8,128)(2,1)S(1)} %get-tuple-element.103), channel_id=1, source_target_pairs={{0,1},{1,0},{2,3},{3,2},{4,5},{5,4},{6,7},{7,6},{8,9},{9,8},{10,11... | collective-permute-start | bytes 3145736 | tf_op jit(solution)/shard_map/ppermute | solution.py:1020
  11.9 2.3 %collective-permute-start.2 = (f32[32,128]{1,0:T(8,128)S(1)}, f32[32,128]{1,0:T(8,128)S(1)}, u32[]{:S(2)}, u32[]{:S(2)}) collective-permute-start(f32[32,128]{1,0:T(8,128)S(1)} %get-tuple-element.104.tot_ref), channel_id=1, source_target_pairs={{0,1},{1,0},{2,3},{3,2},{4,5},{5,4},{6,7},{7,6},{8,9},{9,8},{10,11... | collective-permute-start | bytes 49160 | tf_op jit(solution)/shard_map/ppermute | solution.py:1016
  15.6 23.7 %all-to-all-start = ((bf16[16,272,128]{2,1,0:T(8,128)(2,1)}), bf16[16,272,128]{2,1,0:T(8,128)(2,1)S(1)}, u32[]{:S(2)}, u32[]{:S(2)}) async-start(bf16[16,272,128]{2,1,0:T(8,128)(2,1)} %get-tuple-element.105), calls=%async_computation | async-start | bytes 2228224 | tf_op jit(solution)/shard_map/all_to_all | solution.py:975
  40.6 20.5 %all-to-all-start.1 = ((bf16[16,256,128]{2,1,0:T(8,128)(2,1)}), bf16[16,256,128]{2,1,0:T(8,128)(2,1)S(1)}, u32[]{:S(2)}, u32[]{:S(2)}) async-start(bf16[16,256,128]{2,1,0:T(8,128)(2,1)} %chain.1), calls=%async_computation.1 | async-start | bytes 2097152 | tf_op jit(solution)/shard_map/all_to_all | solution.py:975
  64.9 5.1 %collective-permute-start.3 = (bf16[2,16,128,128]{3,2,1,0:T(8,128)(2,1)S(1)}, bf16[2,16,128,128]{3,2,1,0:T(8,128)(2,1)S(1)}, u32[]{:S(2)}, u32[]{:S(2)}) collective-permute-start(bf16[2,16,128,128]{3,2,1,0:T(8,128)(2,1)S(1)} %get-tuple-element.126), channel_id=1, source_target_pairs={{0,1},{1,0},{2,3},{3,2},{4,5},{5,4},{6,7},{7,6},{8,9},{9,8},{10,11... | collective-permute-start | bytes 3145736 | tf_op jit(solution)/shard_map/ppermute | solution.py:1035
  69.4 4.9 %collective-permute-start.4 = (f32[128,128]{1,0:T(8,128)S(1)}, f32[128,128]{1,0:T(8,128)S(1)}, u32[]{:S(2)}, u32[]{:S(2)}) collective-permute-start(f32[128,128]{1,0:T(8,128)S(1)} %get-tuple-element.169.own_ref), channel_id=1, source_target_pairs={{0,1},{1,0},{2,3},{3,2},{4,5},{5,4},{6,7},{7,6},{8,9},{9,8},{10,11... | collective-permute-start | bytes 196616 | tf_op jit(solution)/shard_map/ppermute | solution.py:1037
  74.2 1.3 %collective-permute-start.5 = (f32[128,128]{1,0:T(8,128)S(1)}, f32[128,128]{1,0:T(8,128)S(1)}, u32[]{:S(2)}, u32[]{:S(2)}) collective-permute-start(f32[128,128]{1,0:T(8,128)S(1)} %get-tuple-element.170.theirs_ref), channel_id=1, source_target_pairs={{0,1},{1,0},{2,3},{3,2},{4,5},{5,4},{6,7},{7,6},{8,9},{9,8},{10,11... | collective-permute-start | bytes 196616 | tf_op jit(solution)/shard_map/ppermute | solution.py:1041
  76.1 5.6 %collective-permute-start.6 = (bf16[176,128]{1,0:T(8,128)(2,1)S(1)}, bf16[176,128]{1,0:T(8,128)(2,1)S(1)}, u32[]{:S(2)}, u32[]{:S(2)}) collective-permute-start(bf16[176,128]{1,0:T(8,128)(2,1)S(1)} %merge.1.rest_0_), channel_id=1, source_target_pairs={{0,2},{1,7},{2,4},{3,1},{4,6},{5,3},{6,0},{7,5},{8,10},{9,15},{10,... | collective-permute-start | bytes 135176 | tf_op jit(solution)/shard_map/ppermute | solution.py:987
  76.7 5.4 %collective-permute-start.9 = (bf16[3,5120]{1,0:T(4,128)(2,1)S(1)}, bf16[3,5120]{1,0:T(4,128)(2,1)S(1)}, u32[]{:S(2)}, u32[]{:S(2)}) collective-permute-start(bf16[3,5120]{1,0:T(4,128)(2,1)S(1)} %get-tuple-element.172), channel_id=1, source_target_pairs={{1,0},{2,1},{3,2},{4,3},{5,4},{6,5},{7,6},{8,7},{9,8},{10,9},{11,1... | collective-permute-start | bytes 92168 | tf_op jit(solution)/shard_map/ppermute | solution.py:1042
  80.4 5.6 %collective-permute-start.8 = (bf16[176,128]{1,0:T(8,128)(2,1)S(1)}, bf16[176,128]{1,0:T(8,128)(2,1)S(1)}, u32[]{:S(2)}, u32[]{:S(2)}) collective-permute-start(bf16[176,128]{1,0:T(8,128)(2,1)S(1)} %merge.1.rest_0_), channel_id=1, source_target_pairs={{0,4},{1,5},{2,6},{3,7},{4,0},{5,1},{6,2},{7,3},{8,12},{9,13},{10,... | collective-permute-start | bytes 135176 | tf_op jit(solution)/shard_map/ppermute | solution.py:987
  81.7 4.4 %collective-permute-start.7 = (bf16[176,128]{1,0:T(8,128)(2,1)S(1)}, bf16[176,128]{1,0:T(8,128)(2,1)S(1)}, u32[]{:S(2)}, u32[]{:S(2)}) collective-permute-start(bf16[176,128]{1,0:T(8,128)(2,1)S(1)} %collective-permute-done.6.rest_1_), channel_id=1, source_target_pairs={{0,1},{1,0},{2,3},{3,2},{4,5},{5,4},{6,7},{7,6},{8,9},{9,8},{10,11... | collective-permute-start | bytes 135176 | tf_op jit(solution)/shard_map/ppermute | solution.py:995
  86.1 4.5 %collective-permute-start.10 = (bf16[176,128]{1,0:T(8,128)(2,1)S(1)}, bf16[176,128]{1,0:T(8,128)(2,1)S(1)}, u32[]{:S(2)}, u32[]{:S(2)}) collective-permute-start(bf16[176,128]{1,0:T(8,128)(2,1)S(1)} %fold.3.rest_0_), channel_id=1, source_target_pairs={{0,8},{1,25},{2,10},{3,27},{4,12},{5,29},{6,14},{7,31},{8,16},{9,1... | collective-permute-start | bytes 135176 | tf_op jit(solution)/shard_map/ppermute | solution.py:987
  87.4 5.6 %collective-permute-start.12 = (bf16[176,128]{1,0:T(8,128)(2,1)S(1)}, bf16[176,128]{1,0:T(8,128)(2,1)S(1)}, u32[]{:S(2)}, u32[]{:S(2)}) collective-permute-start(bf16[176,128]{1,0:T(8,128)(2,1)S(1)} %fold.3.rest_0_), channel_id=1, source_target_pairs={{0,16},{1,17},{2,18},{3,19},{4,20},{5,21},{6,22},{7,23},{8,24},{9,... | collective-permute-start | bytes 135176 | tf_op jit(solution)/shard_map/ppermute | solution.py:987
  90.6 2.3 %collective-permute-start.11 = (bf16[176,128]{1,0:T(8,128)(2,1)S(1)}, bf16[176,128]{1,0:T(8,128)(2,1)S(1)}, u32[]{:S(2)}, u32[]{:S(2)}) collective-permute-start(bf16[176,128]{1,0:T(8,128)(2,1)S(1)} %collective-permute-done.10.rest_1_), channel_id=1, source_target_pairs={{0,1},{1,0},{2,3},{3,2},{4,5},{5,4},{6,7},{7,6},{8,9},{9,8},{10,11... | collective-permute-start | bytes 135176 | tf_op jit(solution)/shard_map/ppermute | solution.py:995
  93.0 4.1 %collective-permute-start.13 = (bf16[176,128]{1,0:T(8,128)(2,1)S(1)}, bf16[176,128]{1,0:T(8,128)(2,1)S(1)}, u32[]{:S(2)}, u32[]{:S(2)}) collective-permute-start(bf16[176,128]{1,0:T(8,128)(2,1)S(1)} %fold.4.rest_0_), channel_id=1, source_target_pairs={{0,32},{1,33},{32,0},{33,1},{64,96},{65,97},{96,64},{97,65},{128,1... | collective-permute-start | bytes 135176 | tf_op jit(solution)/shard_map/ppermute | solution.py:987
  97.2 8.7 %collective-permute-start.14 = (bf16[176,128]{1,0:T(8,128)(2,1)S(1)}, bf16[176,128]{1,0:T(8,128)(2,1)S(1)}, u32[]{:S(2)}, u32[]{:S(2)}) collective-permute-start(bf16[176,128]{1,0:T(8,128)(2,1)S(1)} %fold.5.rest_0_), channel_id=1, source_target_pairs={{0,64},{1,193},{32,96},{33,225},{64,128},{65,1},{96,160},{97,33},{... | collective-permute-start | bytes 135176 | tf_op jit(solution)/shard_map/ppermute | solution.py:987
  100.5 8.7 %collective-permute-start.16 = (bf16[176,128]{1,0:T(8,128)(2,1)S(1)}, bf16[176,128]{1,0:T(8,128)(2,1)S(1)}, u32[]{:S(2)}, u32[]{:S(2)}) collective-permute-start(bf16[176,128]{1,0:T(8,128)(2,1)S(1)} %fold.5.rest_0_), channel_id=1, source_target_pairs={{0,128},{1,129},{32,160},{33,161},{64,192},{65,193},{96,224},{97,2... | collective-permute-start | bytes 135176 | tf_op jit(solution)/shard_map/ppermute | solution.py:987
  105.9 3.3 %collective-permute-start.15 = (bf16[176,128]{1,0:T(8,128)(2,1)S(1)}, bf16[176,128]{1,0:T(8,128)(2,1)S(1)}, u32[]{:S(2)}, u32[]{:S(2)}) collective-permute-start(bf16[176,128]{1,0:T(8,128)(2,1)S(1)} %collective-permute-done.14.rest_1_), channel_id=1, source_target_pairs={{0,1},{1,0},{2,3},{3,2},{4,5},{5,4},{6,7},{7,6},{8,9},{9,8},{10,11... | collective-permute-start | bytes 135176 | tf_op jit(solution)/shard_map/ppermute | solution.py:995

commit v11 on v10

--- a/solution.py
+++ b/solution.py
@@ -123,9 +123,10 @@
 
 def pre_conv(win_ref, weights, lo):
     cols = slice(lo, lo + LANES)
-    acc = weights[0:1, cols] * win_ref[5 : 5 + T, cols]
-    for k in range(1, TAPS):
-        acc = acc + weights[k : k + 1, cols] * win_ref[5 + k : 5 + k + T, cols]
+    rows = win_ref[0 : 8 + T, cols]
+    acc = weights[TAPS - 1 : TAPS, cols] * rows[8:]
+    for k in range(TAPS - 1):
+        acc = acc + weights[k : k + 1, cols] * pltpu.roll(rows, TAPS - 1 - k, 0)[8:]
     return acc
 
 
@@ -692,11 +693,9 @@
     lower = (iota((T, T), 0) >= iota((T, T), 1)).astype(F32)
 
     def tap_sums(grad_pre, lo):
-        width = grad_pre.shape[1]
-        return [
-            jnp.sum(grad_pre * win_ref[5 + k : 5 + k + T, lo : lo + width], axis=0, keepdims=True)
-            for k in range(TAPS)
-        ]
+        rows = win_ref[0 : 8 + T, lo : lo + grad_pre.shape[1]]
+        moved = [pltpu.roll(rows, TAPS - 1 - k, 0)[8:] for k in range(TAPS - 1)] + [rows[8:]]
+        return [jnp.sum(grad_pre * part, axis=0, keepdims=True) for part in moved]
 
     def by_rows(sums):
         return [s[:, lo : lo + LANES] for lo in range(0, sums[0].shape[1], LANES) for s in sums]
@@ -845,9 +844,10 @@
             base = side * (HALF_X + HALF_B) + near
             for lo in range(0, width, LANES):
                 at = slice(lo, lo + LANES)
-                acc = weights[0:1, at] * win_ref[3 : 3 + T, at]
-                for k in range(1, TAPS):
-                    acc = acc + weights[k : k + 1, at] * win_ref[3 - k : 3 - k + T, at]
+                rows = win_ref[:, at]
+                acc = weights[TAPS - 1 : TAPS, at] * rows[:T]
+                for k in range(TAPS - 1):
+                    acc = acc + weights[k : k + 1, at] * pltpu.roll(rows, T + 8 - (TAPS - 1 - k), 0)[:T]
                 out_ref[:, base + lo : base + lo + LANES] = acc.astype(BF16)
             copy = pltpu.make_async_copy(out_ref.at[:, pl.ds(base, width)], out_h.at[:, far], sems.at[len(saves)])
             copy.start()
@@ -1039,21 +1039,21 @@
         core, theirs, near, common, (), (half, pre_own)
     )
     sum_theirs_got = lax.ppermute(sum_theirs, "core", swap)
-    after = lax.ppermute(first, CTX, [(i + 1, i) for i in range(devices - 1)])
     sums = run_merge(core, sum_own, sum_own_got, sum_theirs, sum_theirs_got)
     chip, sequence = lax.axis_index("chip"), lax.axis_index("dp")
     rows = chips // SIDE
     values = around(sums, "chip", chips, SIDE, lambda i, d: i // SIDE * SIDE + (i % SIDE + d) % SIDE)
-    grad_tokens = run_spread(core, pre_own, pre_theirs, after, common[4])
-    values, grad_tokens = tie(values, grad_tokens)
     sums = run_fold(core, scalar(lax.rem(chip, SIDE)), values)
     values = around(sums, "chip", chips, rows, lambda i, d: (i + d * SIDE) % chips)
-    sums = run_fold(core, scalar(lax.div(chip, SIDE)), values)
+    sums, first = tie(run_fold(core, scalar(lax.div(chip, SIDE)), values), first)
+    after = lax.ppermute(first, CTX, [(i + 1, i) for i in range(devices - 1)])
     near = 2 if sequences % 2 == 0 else 1
     if near > 1:
         values = around(sums, "dp", sequences, near, lambda i, d: i // 2 * 2 + (i % 2 + d) % 2)
         sums = run_fold(core, scalar(lax.rem(sequence, near)), values)
     values = around(sums, "dp", sequences, sequences // near, lambda i, d: (i + d * near) % sequences)
+    grad_tokens = run_spread(core, pre_own, pre_theirs, after, common[4])
+    values, grad_tokens = tie(values, grad_tokens)
     grad_conv, grad_decay, grad_skip = run_finish(core, scalar(lax.div(sequence, near)), values)
     return (
         out_tokens[None],

time: 111 us -> 112 us (level)
  waiting for transfers between devices: 30.1 us -> 32.3 us
  Pallas kernels: 41.9 us -> 40.6 us
    ppermute x1, starting transfers between devices: 3.76 us -> 6.62 us  [local(): after = lax.ppermute(first, CTX, [(i + 1, i) for i in range(devices - 1)])]
    pallas_call x16, Pallas kernels: 41.9 us -> 40.6 us  [go(): run(*[pin(a, spaces[p]) if p in spaces else a for a, p in zip(args, specs...]
    ppermute x7, starting transfers between devices: 15.6 us -> 14.4 us  [hear(): lax.ppermute(value, (axis, 'core'), [(2 * i + side, 2 * move(i, d) + side...]
  transfers between devices with their start and end apart: 19 -> 19, of which waited for: 11 -> 12; matrix products, arithmetic and copies ran while one was open for 0% -> 0% of each run, Pallas kernels for 29% -> 27%
where the time goes in v11:
time: 112 us
  Pallas kernels  40.6 us (36%)
  starting transfers between devices  37.1 us (33%)
  waiting for transfers between devices  32.3 us (29%)
    pallas_call x16, Pallas kernels, go(): run(*[pin(a, spaces[p]) if p in spaces else a for a, p in zip(args, specs...  40.6 us
    all_to_all x2, waiting for transfers between devices, all_to_all(): return lax.all_to_all(value, axis, 0, 0, tiled=True)  16.6 us
    ppermute x7, starting transfers between devices, hear(): lax.ppermute(value, (axis, 'core'), [(2 * i + side, 2 * move(i, d) + side...  14.4 us
    all_to_all x2, starting transfers between devices, all_to_all(): return lax.all_to_all(value, axis, 0, 0, tiled=True)  12.6 us
    ppermute x7, waiting for transfers between devices, hear(): lax.ppermute(value, (axis, 'core'), [(2 * i + side, 2 * move(i, d) + side...  11.2 us
    ppermute x1, starting transfers between devices, local(): after = lax.ppermute(first, CTX, [(i + 1, i) for i in range(devices - 1)])  6.62 us
  transfers between devices with their start and end apart: 19, of which 12 were waited for; matrix products, arithmetic and copies ran while one was open for 0% of the time, Pallas kernels for 27%

profile of v11, /device:TPU:2, one launch (start us, length us, event | category | flops | bytes accessed | tf_op | source)
XLA Modules:
  0.0 111.8 jit_solution(12364402341575684520)
XLA Ops:
  0.6 0.9 slice_bitcast_fusion
  1.5 1.9 %collective-permute-start = (bf16[3,5120]{1,0:T(4,128)(2,1)S(1)}, bf16[3,5120]{1,0:T(4,128)(2,1)S(1)}, u32[]{:S(2)}, u32[]{:S(2)}) collective-permute-start(bf16[3,5120]{1,0:T(4,128)(2,1)S(1)} %slice_bitcast_fusion), channel_id=1, source_target_pairs={{0,1},{1,2},{2,3},{3,4},{4,5},{5,6},{6,7},{7,8},{8,9},{9,10},{10,1... | collective-permute-start | bytes 92168 | tf_op jit(solution)/shard_map/ppermute | solution.py:1012
  3.5 3.4 %begin.1 = (f32[512,128]{1,0:T(8,128)}, f32[512,128]{1,0:T(8,128)S(1)}, f32[32,128]{1,0:T(8,128)S(1)}, bf16[128,4096]{1,0:T(8,128)(2,1)S(1)}, bf16[128,1024]{1,0...) custom-call(f32[64,128]{1,0:T(8,128)} %bitcast.26, ...), custom_call_target="tpu_custom_call" | custom-call | flops 4000000000 | bytes 14400000 | tf_op jit(solution)/shard_map/begin/pallas_call | solution.py:97
  6.9 2.1 %collective-permute-done.halo_ref = bf16[3,5120]{1,0:T(4,128)(2,1)S(1)} collective-permute-done((bf16[3,5120]{1,0:T(4,128)(2,1)S(1)}, bf16[3,5120]{1,0:T(4,128)(2,1)S(1)}, u32[]{:S(2)}, u32[]{:S(2)}) %collective-permute-start) | collective-permute-done | bytes 30752 | tf_op jit(solution)/shard_map/ppermute | solution.py:1012
  9.0 2.4 %enter.1 = (bf16[128,4096]{1,0:T(8,128)(2,1)}, bf16[128,1024]{1,0:T(8,128)(2,1)}, f32[8,5120]{1,0:T(8,128)}, bf16[128,4096]{1,0:T(8,128)(2,1)S(1)}, bf16[128,102...) custom-call(s32[1]{0:T(128)} %bitcast.core_ref, bf16[128,4096]{1,0:T(8,128)(2,1)S(1)} %get-tuple-element.96.x0_ref, ...), custom_call_target="tpu_custom_call" | custom-call | flops 3000000000 | bytes 10800000 | tf_op jit(solution)/shard_map/enter/pallas_call | solution.py:97
  11.4 0.1 collective-permute-start.1
  11.5 0.5 collective-permute-start.2
  12.0 1.6 %own.1.own_ref = bf16[2,16,128,128]{3,2,1,0:T(8,128)(2,1)S(1)} custom-call(s32[1]{0:T(128)} %bitcast.core_ref, bf16[128,4096]{1,0:T(8,128)(2,1)S(1)} %get-tuple-element.103.x_ref, bf16[128,1024]{1,0:T(8,128)(2,1)S(1)} %get-tuple-element.104.bc_ref, bf16[128,4096]{1,0:T(8,128)(2,1)S(1)} %get-tuple-element.100.g_ref, f32[512,128]{1,0:T(8,128)S(1)} %get-tuple-element.101.small_ref), custom_call_target="tpu_custom_call" | custom-call | flops 3000000000 | bytes 10800000 | tf_op jit(solution)/shard_map/own/pallas_call | solution.py:97
  13.6 0.5 collective-permute-done.2.other_ref
  14.1 1.4 %pack.1 = (bf16[16,272,128]{2,1,0:T(8,128)(2,1)}, bf16[16,128,128]{2,1,0:T(8,128)(2,1)}, bf16[16,128,128]{2,1,0:T(8,128)(2,1)}, f32[64,128]{1,0:T(8,128)}) custom-call(s32[1]{0:T(128)} %bitcast.core_ref, bf16[2,16,128,128]{3,2,1,0:T(8,128)(2,1)S(1)} %own.1.own_ref, bf16[2,16,128,128]{3,2,1,0:T(8,128)(2,1)S(1)} %collective-permute-done.1.got_ref, ...), custom_call_target="tpu_custom_call" | custom-call | flops 2000000000 | bytes 7200000 | tf_op jit(solution)/shard_map/pack/pallas_call | solution.py:97
  15.6 6.4 %all-to-all-start = ((bf16[16,272,128]{2,1,0:T(8,128)(2,1)}), bf16[16,272,128]{2,1,0:T(8,128)(2,1)S(1)}, u32[]{:S(2)}, u32[]{:S(2)}) async-start(bf16[16,272,128]{2,1,0:T(8,128)(2,1)} %get-tuple-element.107), calls=%async_computation | async-start | bytes 2228224 | tf_op jit(solution)/shard_map/all_to_all | solution.py:975
  22.0 5.7 %inner.1 = (f32[128,4096]{1,0:T(8,128)}, f32[128,1024]{1,0:T(8,128)}, f32[32,128]{1,0:T(8,128)}) custom-call(bf16[128,4096]{1,0:T(8,128)(2,1)} %get-tuple-element.108.x_h.rest_0_.rest_21_, bf16[128,1024]{1,0:T(8,128)(2,1)} %get-tuple-element.115.bc_h.rest_6_.rest_27_, bf16[128,4096]{1,0:T(8,128)(2,1)} %bitcast.22, f32[512,128]{1,0:T(8,128)} %get-tuple-element.109.small_h.rest_9_), custom_call_target="tpu_custom_call" | custom-call | flops 4000000000 | bytes 14400000 | tf_op jit(solution)/shard_map/inner/pallas_call | solution.py:97
  27.6 10.8 %all-to-all-done.in_ref = bf16[16,272,128]{2,1,0:T(8,128)(2,1)S(1)} async-done(((bf16[16,272,128]{2,1,0:T(8,128)(2,1)}), bf16[16,272,128]{2,1,0:T(8,128)(2,1)S(1)}, u32[]{:S(2)}, u32[]{:S(2)}) %all-to-all-start) | async-done | bytes 1114144 | tf_op jit(solution)/shard_map/all_to_all | solution.py:975
  38.5 1.3 %chain.1 = bf16[16,256,128]{2,1,0:T(8,128)(2,1)} custom-call(bf16[16,272,128]{2,1,0:T(8,128)(2,1)S(1)} %all-to-all-done.in_ref), custom_call_target="tpu_custom_call" | custom-call | flops 1000000000 | bytes 3600000 | tf_op jit(solution)/shard_map/chain/pallas_call | solution.py:97
  39.7 6.2 %all-to-all-start.1 = ((bf16[16,256,128]{2,1,0:T(8,128)(2,1)}), bf16[16,256,128]{2,1,0:T(8,128)(2,1)S(1)}, u32[]{:S(2)}, u32[]{:S(2)}) async-start(bf16[16,256,128]{2,1,0:T(8,128)(2,1)} %chain.1), calls=%async_computation.1 | async-start | bytes 2097152 | tf_op jit(solution)/shard_map/all_to_all | solution.py:975
  45.9 8.5 %slopes.1 = (f32[128,4096]{1,0:T(8,128)}, f32[128,5120]{1,0:T(8,128)}) custom-call(bf16[128,1024]{1,0:T(8,128)(2,1)} %get-tuple-element.115.bc_h.rest_6_.rest_27_, bf16[128,4096]{1,0:T(8,128)(2,1)} %bitcast.23, f32[512,128]{1,0:T(8,128)} %get-tuple-element.109.small_h.rest_9_, bf16[128,5120]{1,0:T(8,128)(2,1)} %bitcast.18, ...), custom_call_target="tpu_custom_call" | custom-call | flops 6000000000 | bytes 21600000 | tf_op jit(solution)/shard_map/slopes/pallas_call | solution.py:97
  54.5 5.8 %all-to-all-done.1.back_ref = bf16[16,256,128]{2,1,0:T(8,128)(2,1)S(1)} async-done(((bf16[16,256,128]{2,1,0:T(8,128)(2,1)}), bf16[16,256,128]{2,1,0:T(8,128)(2,1)S(1)}, u32[]{:S(2)}, u32[]{:S(2)}) %all-to-all-start.1) | async-done | bytes 1048608 | tf_op jit(solution)/shard_map/all_to_all | solution.py:975
  60.2 3.8 %unpack.1 = (bf16[2,16,128,128]{3,2,1,0:T(8,128)(2,1)S(1)}, bf16[2,16,128,128]{3,2,1,0:T(8,128)(2,1)S(1)}, bf16[128,1024]{1,0:T(8,128)(2,1)S(1)}, bf16[128,1024]...) custom-call(s32[1]{0:T(128)} %bitcast.core_ref, ...), custom_call_target="tpu_custom_call" | custom-call | flops 3000000000 | bytes 10800000 | tf_op jit(solution)/shard_map/unpack/pallas_call | solution.py:97
  64.0 0.3 collective-permute-start.3
  64.3 4.2 %leave.2 = (bf16[128,4096]{1,0:T(8,128)(2,1)}, f32[64,128]{1,0:T(8,128)}, f32[128,2560]{1,0:T(8,128)S(1)}, f32[128,128]{1,0:T(8,128)S(1)}, bf16[128,1024]{1,0:T(...) custom-call(s32[1]{0:T(128)} %bitcast.core_ref, ...), custom_call_target="tpu_custom_call" | custom-call | flops 5000000000 | bytes 18000000 | tf_op jit(solution)/shard_map/leave/pallas_call | solution.py:97
  68.5 0.6 collective-permute-start.4
  69.1 0.0 collective-permute-done.3.state_ref
  69.1 4.2 %leave.3 = (bf16[128,4096]{1,0:T(8,128)(2,1)}, f32[64,128]{1,0:T(8,128)}, f32[128,2560]{1,0:T(8,128)}, f32[128,128]{1,0:T(8,128)S(1)}, bf16[3,5120]{1,0:T(4,128)(2,1)S(1)}) custom-call(s32[1]{0:T(128)} %bitcast.core_ref, bf16[2,16,128,128]{3,2,1,0:T(8,128)(2,1)S(1)} %collective-permute-done.3.state_ref, ...), custom_call_target="tpu_custom_call", output_to_operand_aliasing={{0}: (24, {}), {1}: (25, {})} | custom-call | flops 5000000000 | bytes 18000000 | tf_op jit(solution)/shard_map/leave/pallas_call | solution.py:97
  73.3 0.1 collective-permute-start.5
  73.4 0.0 collective-permute-done.4.own_got_ref
  73.4 1.2 %collective-permute-done.5.theirs_got_ref = f32[128,128]{1,0:T(8,128)S(1)} collective-permute-done((f32[128,128]{1,0:T(8,128)S(1)}, f32[128,128]{1,0:T(8,128)S(1)}, u32[]{:S(2)}, u32[]{:S(2)}) %collective-permute-start.5) | collective-permute-done | bytes 65568 | tf_op jit(solution)/shard_map/ppermute | solution.py:1041
  74.6 0.6 merge.1.rest_0_
  75.2 0.6 collective-permute-start.6
  75.8 2.2 %collective-permute-start.8 = (bf16[176,128]{1,0:T(8,128)(2,1)S(1)}, bf16[176,128]{1,0:T(8,128)(2,1)S(1)}, u32[]{:S(2)}, u32[]{:S(2)}) collective-permute-start(bf16[176,128]{1,0:T(8,128)(2,1)S(1)} %merge.1.rest_0_), channel_id=1, source_target_pairs={{0,4},{1,5},{2,6},{3,7},{4,0},{5,1},{6,2},{7,3},{8,12},{9,13},{10,... | collective-permute-start | bytes 135176 | tf_op jit(solution)/shard_map/ppermute | solution.py:987
  78.0 2.5 %collective-permute-done.6.rest_1_ = bf16[176,128]{1,0:T(8,128)(2,1)S(1)} collective-permute-done((bf16[176,128]{1,0:T(8,128)(2,1)S(1)}, bf16[176,128]{1,0:T(8,128)(2,1)S(1)}, u32[]{:S(2)}, u32[]{:S(2)}) %collective-permute-start.6) | collective-permute-done | bytes 45088 | tf_op jit(solution)/shard_map/ppermute | solution.py:987
  80.5 1.0 collective-permute-done.8.rest_3_
  81.4 0.3 collective-permute-done.7.rest_2_
  81.7 1.1 collective-permute-start.9
  82.8 3.5 %collective-permute-start.11 = (bf16[176,128]{1,0:T(8,128)(2,1)S(1)}, bf16[176,128]{1,0:T(8,128)(2,1)S(1)}, u32[]{:S(2)}, u32[]{:S(2)}) collective-permute-start(bf16[176,128]{1,0:T(8,128)(2,1)S(1)} %fold.3.rest_0_), channel_id=1, source_target_pairs={{0,16},{1,17},{2,18},{3,19},{4,20},{5,21},{6,22},{7,23},{8,24},{9,... | collective-permute-start | bytes 135176 | tf_op jit(solution)/shard_map/ppermute | solution.py:987
  86.3 0.0 collective-permute-start.10
  86.3 2.2 %collective-permute-done.11.rest_3_ = bf16[176,128]{1,0:T(8,128)(2,1)S(1)} collective-permute-done((bf16[176,128]{1,0:T(8,128)(2,1)S(1)}, bf16[176,128]{1,0:T(8,128)(2,1)S(1)}, u32[]{:S(2)}, u32[]{:S(2)}) %collective-permute-start.11) | collective-permute-done | bytes 45088 | tf_op jit(solution)/shard_map/ppermute | solution.py:987
  88.5 0.0 collective-permute-done.10.rest_2_
  88.6 2.1 %collective-permute-start.12 = (bf16[176,128]{1,0:T(8,128)(2,1)S(1)}, bf16[176,128]{1,0:T(8,128)(2,1)S(1)}, u32[]{:S(2)}, u32[]{:S(2)}) collective-permute-start(bf16[176,128]{1,0:T(8,128)(2,1)S(1)} %fold.4.rest_0_), channel_id=1, source_target_pairs={{0,32},{1,33},{32,0},{33,1},{64,96},{65,97},{96,64},{97,65},{128,1... | collective-permute-start | bytes 135176 | tf_op jit(solution)/shard_map/ppermute | solution.py:987
  90.7 2.0 %collective-permute-done.12.rest_1_ = bf16[176,128]{1,0:T(8,128)(2,1)S(1)} collective-permute-done((bf16[176,128]{1,0:T(8,128)(2,1)S(1)}, bf16[176,128]{1,0:T(8,128)(2,1)S(1)}, u32[]{:S(2)}, u32[]{:S(2)}) %collective-permute-start.12) | collective-permute-done | bytes 45088 | tf_op jit(solution)/shard_map/ppermute | solution.py:987
  92.8 3.7 %collective-permute-start.13 = (bf16[176,128]{1,0:T(8,128)(2,1)S(1)}, bf16[176,128]{1,0:T(8,128)(2,1)S(1)}, u32[]{:S(2)}, u32[]{:S(2)}) collective-permute-start(bf16[176,128]{1,0:T(8,128)(2,1)S(1)} %fold.5.rest_0_), channel_id=1, source_target_pairs={{0,64},{1,193},{32,96},{33,225},{64,128},{65,1},{96,160},{97,33},{... | collective-permute-start | bytes 135176 | tf_op jit(solution)/shard_map/ppermute | solution.py:987
  96.4 6.6 %collective-permute-start.16 = (bf16[3,5120]{1,0:T(4,128)(2,1)S(1)}, bf16[3,5120]{1,0:T(4,128)(2,1)S(1)}, u32[]{:S(2)}, u32[]{:S(2)}) collective-permute-start(bf16[3,5120]{1,0:T(4,128)(2,1)S(1)} %get-tuple-element.176), channel_id=1, source_target_pairs={{1,0},{2,1},{3,2},{4,3},{5,4},{6,5},{7,6},{8,7},{9,8},{10,9},{11,1... | collective-permute-start | bytes 92168 | tf_op jit(solution)/shard_map/ppermute | solution.py:1049
  103.1 1.3 %collective-permute-start.15 = (bf16[176,128]{1,0:T(8,128)(2,1)S(1)}, bf16[176,128]{1,0:T(8,128)(2,1)S(1)}, u32[]{:S(2)}, u32[]{:S(2)}) collective-permute-start(bf16[176,128]{1,0:T(8,128)(2,1)S(1)} %fold.5.rest_0_), channel_id=1, source_target_pairs={{0,128},{1,129},{32,160},{33,161},{64,192},{65,193},{96,224},{97,2... | collective-permute-start | bytes 135176 | tf_op jit(solution)/shard_map/ppermute | solution.py:987
  104.3 0.0 collective-permute-done.13.rest_1_
  104.3 0.0 collective-permute-start.14
  104.3 0.4 collective-permute-done.16.halo_ref
  104.7 2.8 %spread.1 = bf16[128,5120]{1,0:T(8,128)(2,1)} custom-call(s32[1]{0:T(128)} %bitcast.core_ref, f32[128,2560]{1,0:T(8,128)S(1)} %get-tuple-element.167.rest_21_.own_ref, f32[128,2560]{1,0:T(8,128)} %get-tuple-element.175.theirs_h, bf16[3,5120]{1,0:T(4,128)(2,1)S(1)} %collective-permute-done.16.halo_ref, f32[4,5120]{1,0:T(4,128)S(1)} %get-tuple-element.150.rest_20_.weight_ref), custom_call_target="tpu_custom_call" | custom-call | flops 3000000000 | bytes 10800000 | tf_op jit(solution)/shard_map/spread/pallas_call | solution.py:97
  107.5 3.6 %collective-permute-done.15.rest_3_ = bf16[176,128]{1,0:T(8,128)(2,1)S(1)} collective-permute-done((bf16[176,128]{1,0:T(8,128)(2,1)S(1)}, bf16[176,128]{1,0:T(8,128)(2,1)S(1)}, u32[]{:S(2)}, u32[]{:S(2)}) %collective-permute-start.15) | collective-permute-done | bytes 45088 | tf_op jit(solution)/shard_map/ppermute | solution.py:987
  111.1 0.7 finish.1
  (7 shorter events, 0.1 us)
Async XLA Ops:
  1.5 7.4 %collective-permute-start = (bf16[3,5120]{1,0:T(4,128)(2,1)S(1)}, bf16[3,5120]{1,0:T(4,128)(2,1)S(1)}, u32[]{:S(2)}, u32[]{:S(2)}) collective-permute-start(bf16[3,5120]{1,0:T(4,128)(2,1)S(1)} %slice_bitcast_fusion), channel_id=1, source_target_pairs={{0,1},{1,2},{2,3},{3,4},{4,5},{5,6},{6,7},{7,8},{8,9},{9,10},{10,1... | collective-permute-start | bytes 92168 | tf_op jit(solution)/shard_map/ppermute | solution.py:1012
  11.4 2.8 %collective-permute-start.1 = (bf16[2,16,128,128]{3,2,1,0:T(8,128)(2,1)S(1)}, bf16[2,16,128,128]{3,2,1,0:T(8,128)(2,1)S(1)}, u32[]{:S(2)}, u32[]{:S(2)}) collective-permute-start(bf16[2,16,128,128]{3,2,1,0:T(8,128)(2,1)S(1)} %get-tuple-element.105), channel_id=1, source_target_pairs={{0,1},{1,0},{2,3},{3,2},{4,5},{5,4},{6,7},{7,6},{8,9},{9,8},{10,11... | collective-permute-start | bytes 3145736 | tf_op jit(solution)/shard_map/ppermute | solution.py:1020
  11.5 2.7 %collective-permute-start.2 = (f32[32,128]{1,0:T(8,128)S(1)}, f32[32,128]{1,0:T(8,128)S(1)}, u32[]{:S(2)}, u32[]{:S(2)}) collective-permute-start(f32[32,128]{1,0:T(8,128)S(1)} %get-tuple-element.106.tot_ref), channel_id=1, source_target_pairs={{0,1},{1,0},{2,3},{3,2},{4,5},{5,4},{6,7},{7,6},{8,9},{9,8},{10,11... | collective-permute-start | bytes 49160 | tf_op jit(solution)/shard_map/ppermute | solution.py:1016
  15.6 22.9 %all-to-all-start = ((bf16[16,272,128]{2,1,0:T(8,128)(2,1)}), bf16[16,272,128]{2,1,0:T(8,128)(2,1)S(1)}, u32[]{:S(2)}, u32[]{:S(2)}) async-start(bf16[16,272,128]{2,1,0:T(8,128)(2,1)} %get-tuple-element.107), calls=%async_computation | async-start | bytes 2228224 | tf_op jit(solution)/shard_map/all_to_all | solution.py:975
  39.7 20.5 %all-to-all-start.1 = ((bf16[16,256,128]{2,1,0:T(8,128)(2,1)}), bf16[16,256,128]{2,1,0:T(8,128)(2,1)S(1)}, u32[]{:S(2)}, u32[]{:S(2)}) async-start(bf16[16,256,128]{2,1,0:T(8,128)(2,1)} %chain.1), calls=%async_computation.1 | async-start | bytes 2097152 | tf_op jit(solution)/shard_map/all_to_all | solution.py:975
  64.0 5.1 %collective-permute-start.3 = (bf16[2,16,128,128]{3,2,1,0:T(8,128)(2,1)S(1)}, bf16[2,16,128,128]{3,2,1,0:T(8,128)(2,1)S(1)}, u32[]{:S(2)}, u32[]{:S(2)}) collective-permute-start(bf16[2,16,128,128]{3,2,1,0:T(8,128)(2,1)S(1)} %get-tuple-element.128), channel_id=1, source_target_pairs={{0,1},{1,0},{2,3},{3,2},{4,5},{5,4},{6,7},{7,6},{8,9},{9,8},{10,11... | collective-permute-start | bytes 3145736 | tf_op jit(solution)/shard_map/ppermute | solution.py:1035
  68.5 4.9 %collective-permute-start.4 = (f32[128,128]{1,0:T(8,128)S(1)}, f32[128,128]{1,0:T(8,128)S(1)}, u32[]{:S(2)}, u32[]{:S(2)}) collective-permute-start(f32[128,128]{1,0:T(8,128)S(1)} %get-tuple-element.171.own_ref), channel_id=1, source_target_pairs={{0,1},{1,0},{2,3},{3,2},{4,5},{5,4},{6,7},{7,6},{8,9},{9,8},{10,11... | collective-permute-start | bytes 196616 | tf_op jit(solution)/shard_map/ppermute | solution.py:1037
  73.3 1.3 %collective-permute-start.5 = (f32[128,128]{1,0:T(8,128)S(1)}, f32[128,128]{1,0:T(8,128)S(1)}, u32[]{:S(2)}, u32[]{:S(2)}) collective-permute-start(f32[128,128]{1,0:T(8,128)S(1)} %get-tuple-element.172.theirs_ref), channel_id=1, source_target_pairs={{0,1},{1,0},{2,3},{3,2},{4,5},{5,4},{6,7},{7,6},{8,9},{9,8},{10,11... | collective-permute-start | bytes 196616 | tf_op jit(solution)/shard_map/ppermute | solution.py:1041
  75.2 5.3 %collective-permute-start.6 = (bf16[176,128]{1,0:T(8,128)(2,1)S(1)}, bf16[176,128]{1,0:T(8,128)(2,1)S(1)}, u32[]{:S(2)}, u32[]{:S(2)}) collective-permute-start(bf16[176,128]{1,0:T(8,128)(2,1)S(1)} %merge.1.rest_0_), channel_id=1, source_target_pairs={{0,2},{1,7},{2,4},{3,1},{4,6},{5,3},{6,0},{7,5},{8,10},{9,15},{10,... | collective-permute-start | bytes 135176 | tf_op jit(solution)/shard_map/ppermute | solution.py:987
  75.8 5.7 %collective-permute-start.8 = (bf16[176,128]{1,0:T(8,128)(2,1)S(1)}, bf16[176,128]{1,0:T(8,128)(2,1)S(1)}, u32[]{:S(2)}, u32[]{:S(2)}) collective-permute-start(bf16[176,128]{1,0:T(8,128)(2,1)S(1)} %merge.1.rest_0_), channel_id=1, source_target_pairs={{0,4},{1,5},{2,6},{3,7},{4,0},{5,1},{6,2},{7,3},{8,12},{9,13},{10,... | collective-permute-start | bytes 135176 | tf_op jit(solution)/shard_map/ppermute | solution.py:987
  80.5 1.2 %collective-permute-start.7 = (bf16[176,128]{1,0:T(8,128)(2,1)S(1)}, bf16[176,128]{1,0:T(8,128)(2,1)S(1)}, u32[]{:S(2)}, u32[]{:S(2)}) collective-permute-start(bf16[176,128]{1,0:T(8,128)(2,1)S(1)} %collective-permute-done.6.rest_1_), channel_id=1, source_target_pairs={{0,1},{1,0},{2,3},{3,2},{4,5},{5,4},{6,7},{7,6},{8,9},{9,8},{10,11... | collective-permute-start | bytes 135176 | tf_op jit(solution)/shard_map/ppermute | solution.py:995
  81.7 4.6 %collective-permute-start.9 = (bf16[176,128]{1,0:T(8,128)(2,1)S(1)}, bf16[176,128]{1,0:T(8,128)(2,1)S(1)}, u32[]{:S(2)}, u32[]{:S(2)}) collective-permute-start(bf16[176,128]{1,0:T(8,128)(2,1)S(1)} %fold.3.rest_0_), channel_id=1, source_target_pairs={{0,8},{1,25},{2,10},{3,27},{4,12},{5,29},{6,14},{7,31},{8,16},{9,1... | collective-permute-start | bytes 135176 | tf_op jit(solution)/shard_map/ppermute | solution.py:987
  82.8 5.7 %collective-permute-start.11 = (bf16[176,128]{1,0:T(8,128)(2,1)S(1)}, bf16[176,128]{1,0:T(8,128)(2,1)S(1)}, u32[]{:S(2)}, u32[]{:S(2)}) collective-permute-start(bf16[176,128]{1,0:T(8,128)(2,1)S(1)} %fold.3.rest_0_), channel_id=1, source_target_pairs={{0,16},{1,17},{2,18},{3,19},{4,20},{5,21},{6,22},{7,23},{8,24},{9,... | collective-permute-start | bytes 135176 | tf_op jit(solution)/shard_map/ppermute | solution.py:987
  86.3 2.2 %collective-permute-start.10 = (bf16[176,128]{1,0:T(8,128)(2,1)S(1)}, bf16[176,128]{1,0:T(8,128)(2,1)S(1)}, u32[]{:S(2)}, u32[]{:S(2)}) collective-permute-start(bf16[176,128]{1,0:T(8,128)(2,1)S(1)} %collective-permute-done.9.rest_1_), channel_id=1, source_target_pairs={{0,1},{1,0},{2,3},{3,2},{4,5},{5,4},{6,7},{7,6},{8,9},{9,8},{10,11... | collective-permute-start | bytes 135176 | tf_op jit(solution)/shard_map/ppermute | solution.py:995
  88.6 4.2 %collective-permute-start.12 = (bf16[176,128]{1,0:T(8,128)(2,1)S(1)}, bf16[176,128]{1,0:T(8,128)(2,1)S(1)}, u32[]{:S(2)}, u32[]{:S(2)}) collective-permute-start(bf16[176,128]{1,0:T(8,128)(2,1)S(1)} %fold.4.rest_0_), channel_id=1, source_target_pairs={{0,32},{1,33},{32,0},{33,1},{64,96},{65,97},{96,64},{97,65},{128,1... | collective-permute-start | bytes 135176 | tf_op jit(solution)/shard_map/ppermute | solution.py:987
  92.8 11.6 %collective-permute-start.13 = (bf16[176,128]{1,0:T(8,128)(2,1)S(1)}, bf16[176,128]{1,0:T(8,128)(2,1)S(1)}, u32[]{:S(2)}, u32[]{:S(2)}) collective-permute-start(bf16[176,128]{1,0:T(8,128)(2,1)S(1)} %fold.5.rest_0_), channel_id=1, source_target_pairs={{0,64},{1,193},{32,96},{33,225},{64,128},{65,1},{96,160},{97,33},{... | collective-permute-start | bytes 135176 | tf_op jit(solution)/shard_map/ppermute | solution.py:987
  96.4 8.3 %collective-permute-start.16 = (bf16[3,5120]{1,0:T(4,128)(2,1)S(1)}, bf16[3,5120]{1,0:T(4,128)(2,1)S(1)}, u32[]{:S(2)}, u32[]{:S(2)}) collective-permute-start(bf16[3,5120]{1,0:T(4,128)(2,1)S(1)} %get-tuple-element.176), channel_id=1, source_target_pairs={{1,0},{2,1},{3,2},{4,3},{5,4},{6,5},{7,6},{8,7},{9,8},{10,9},{11,1... | collective-permute-start | bytes 92168 | tf_op jit(solution)/shard_map/ppermute | solution.py:1049
  103.1 8.0 %collective-permute-start.15 = (bf16[176,128]{1,0:T(8,128)(2,1)S(1)}, bf16[176,128]{1,0:T(8,128)(2,1)S(1)}, u32[]{:S(2)}, u32[]{:S(2)}) collective-permute-start(bf16[176,128]{1,0:T(8,128)(2,1)S(1)} %fold.5.rest_0_), channel_id=1, source_target_pairs={{0,128},{1,129},{32,160},{33,161},{64,192},{65,193},{96,224},{97,2... | collective-permute-start | bytes 135176 | tf_op jit(solution)/shard_map/ppermute | solution.py:987
  104.3 6.8 %collective-permute-start.14 = (bf16[176,128]{1,0:T(8,128)(2,1)S(1)}, bf16[176,128]{1,0:T(8,128)(2,1)S(1)}, u32[]{:S(2)}, u32[]{:S(2)}) collective-permute-start(bf16[176,128]{1,0:T(8,128)(2,1)S(1)} %collective-permute-done.13.rest_1_), channel_id=1, source_target_pairs={{0,1},{1,0},{2,3},{3,2},{4,5},{5,4},{6,7},{7,6},{8,9},{9,8},{10,11... | collective-permute-start | bytes 135176 | tf_op jit(solution)/shard_map/ppermute | solution.py:995

commit v12 on v11

--- a/solution.py
+++ b/solution.py
@@ -825,8 +825,16 @@
     return outs[:2], outs[2], outs[3], outs[4:]
 
 
-def spread_kernel(core_ref, own_ref, theirs_h, halo_ref, weight_ref, out_h, theirs_ref, out_ref, win_ref, sems):
+def spread_kernel(core_ref, chip_ref, own_ref, theirs_h, swap_ref, near_ref, far_ref, weight_ref, out_h,
+                  theirs_ref, halo_ref, out_ref, win_ref, sems):
     load = start_all([(theirs_h, theirs_ref)], sems.at[pl.ds(8, 1)])
+    edge = lax.rem(chip_ref[0], SIDE) == SIDE - 1
+    last = (chip_ref[0] == chip_ref[1] - 1).astype(F32)
+    rows = jnp.where(edge, far_ref[SEND_ROWS:, :].astype(F32), near_ref[SEND_ROWS:, :].astype(F32)) * (1.0 - last)
+    for i in range(CHANNELS // LANES):
+        cols = slice(i * LANES, (i + 1) * LANES)
+        across = rows[i * (TAPS - 1) : (i + 1) * (TAPS - 1)]
+        halo_ref[0 : TAPS - 1, cols] = jnp.where(core_ref[0] == 0, swap_ref[:, cols].astype(F32), across)
     saves = []
     size = HALF_GROUPS * STATE
     for side, pre_ref in enumerate((own_ref, theirs_ref)):
@@ -839,7 +847,7 @@
         ]
         for near, far, width in blocks:
             win_ref[0:T, 0:width] = pre_ref[:, near : near + width]
-            win_ref[T : T + TAPS - 1, 0:width] = halo_ref[:, far].astype(F32)
+            win_ref[T : T + 8, 0:width] = halo_ref[:, far]
             weights = weight_ref[:, far]
             base = side * (HALF_X + HALF_B) + near
             for lo in range(0, width, LANES):
@@ -855,20 +863,24 @@
     wait_all(saves)
 
 
-def run_spread(core, own, theirs, halo, weight):
+def run_spread(core, chip, own, theirs, swapped, near, far, weight):
     out = [("h", (T, CHANNELS), BF16)]
     scratch = [
         pltpu.VMEM((T, HALF_X + HALF_B), F32),
+        pltpu.VMEM((8, CHANNELS), F32),
         pltpu.VMEM((T, CHANNELS), BF16),
         pltpu.VMEM((T + 8, GROUP_X), F32),
         DMA(9),
     ]
-    return call(spread_kernel, "spread", out, "sVhvV", 3, scratch, mib=8)(core, own, theirs, halo, weight)[0]
+    return call(spread_kernel, "spread", out, "ssVhvvvV", 3, scratch, mib=8)(
+        core, chip, own, theirs, swapped, near, far, weight
+    )[0]
 
 
 CONV_ROWS = TAPS * (CHANNELS // LANES)
 CONV_GROUP = CONV_ROWS // GROUPS
 SEND_ROWS = CONV_ROWS + 16
+PLUS_ROWS = SEND_ROWS + 128
 
 
 def write_send(out_ref, conv, thin):
@@ -884,7 +896,7 @@
     return wide[0:CONV_ROWS], wide[CONV_ROWS : CONV_ROWS + 1] + wide[CONV_ROWS + 1 : CONV_ROWS + 2]
 
 
-def merge_kernel(core_ref, own_ref, own_got_ref, theirs_ref, theirs_got_ref, out_ref):
+def merge_kernel(core_ref, own_ref, own_got_ref, theirs_ref, theirs_got_ref, swap_ref, out_ref, plus_ref):
     thin = jnp.zeros((8, LANES), F32)
     left = iota((8, LANES), 1) < HEAD_DIM
     count = HEADS // 2
@@ -912,14 +924,43 @@
         [jnp.where(first, parts[0], parts[1]), jnp.where(first, parts[1], parts[0])], axis=0
     )
     write_send(out_ref, conv, thin[0:1])
-
-
-def run_merge(core, own, own_got, theirs, theirs_got):
-    out = [("v", (SEND_ROWS, LANES), BF16)]
-    return call(merge_kernel, "merge", out, "svvvv", 1, mib=4)(core, own, own_got, theirs, theirs_got)[0]
-
-
-def ring_sum(core_ref, me_ref, refs, hold_ref):
+    plus_ref[0:SEND_ROWS, :] = out_ref[...]
+    rows = [swap_ref[:, i * LANES : (i + 1) * LANES].astype(F32) for i in range(CHANNELS // LANES)]
+    rows.append(jnp.zeros((PLUS_ROWS - SEND_ROWS - (TAPS - 1) * (CHANNELS // LANES), LANES), F32))
+    plus_ref[SEND_ROWS:PLUS_ROWS, :] = jnp.concatenate(rows, axis=0).astype(BF16)
+
+
+def run_merge(core, own, own_got, theirs, theirs_got, swapped):
+    out = [("v", (SEND_ROWS, LANES), BF16), ("v", (PLUS_ROWS, LANES), BF16)]
+    return call(merge_kernel, "merge", out, "svvvvv", 1, mib=4)(core, own, own_got, theirs, theirs_got, swapped)
+
+
+def ring_sum(me_ref, hold_ref):
+    count = hold_ref.shape[0]
+    conv, thin = read_send(hold_ref[lax.rem(me_ref[0], count)])
+    for k in range(1, count):
+        more, little = read_send(hold_ref[lax.rem(me_ref[0] + count - k, count)])
+        conv, thin = conv + more, thin + little
+    return conv, thin
+
+
+def fold_kernel(me_ref, *rest):
+    *refs, out_ref, plus_ref, hold_ref = rest
+    for d, ref in enumerate(refs):
+        hold_ref[d] = ref[0:SEND_ROWS, :]
+    write_send(out_ref, *ring_sum(me_ref, hold_ref))
+    plus_ref[0:SEND_ROWS, :] = out_ref[...]
+    plus_ref[SEND_ROWS:PLUS_ROWS, :] = refs[-1][SEND_ROWS:PLUS_ROWS, :]
+
+
+def run_fold(me, values):
+    out = [("v", (SEND_ROWS, LANES), BF16), ("v", (PLUS_ROWS, LANES), BF16)]
+    scratch = [pltpu.VMEM((len(values), SEND_ROWS, LANES), BF16)]
+    return call(fold_kernel, "fold", out, "s" + "v" * len(values), 1, scratch, mib=4)(me, *values)
+
+
+def finish_kernel(core_ref, me_ref, *rest):
+    *refs, conv_ref, decay_ref, skip_ref, hold_ref = rest
     count = len(refs)
     sides = (count - 1) // 2
     hold_ref[0] = refs[0][...]
@@ -929,27 +970,7 @@
         hold_ref[count - mine] = refs[sides + k][...]
     if count % 2 == 0:
         hold_ref[count // 2] = refs[count - 1][...]
-    conv, thin = read_send(hold_ref[lax.rem(me_ref[0], count)])
-    for k in range(1, count):
-        more, little = read_send(hold_ref[lax.rem(me_ref[0] + count - k, count)])
-        conv, thin = conv + more, thin + little
-    return conv, thin
-
-
-def fold_kernel(core_ref, me_ref, *rest):
-    *refs, out_ref, hold_ref = rest
-    write_send(out_ref, *ring_sum(core_ref, me_ref, refs, hold_ref))
-
-
-def run_fold(core, me, values):
-    out = [("v", (SEND_ROWS, LANES), BF16)]
-    scratch = [pltpu.VMEM((len(values), SEND_ROWS, LANES), BF16)]
-    return call(fold_kernel, "fold", out, "ss" + "v" * len(values), 1, scratch, mib=4)(core, me, *values)[0]
-
-
-def finish_kernel(core_ref, me_ref, *rest):
-    *refs, conv_ref, decay_ref, skip_ref, hold_ref = rest
-    conv, thin = ring_sum(core_ref, me_ref, refs, hold_ref)
+    conv, thin = ring_sum(me_ref, hold_ref)
     for i in range(CHANNELS // LANES):
         if i < PAIRS:
             row = CONV_GROUP * (i // GROUP_PAIRS) + TAPS * (i % GROUP_PAIRS)
@@ -982,7 +1003,14 @@
 SIDE = 4
 
 
-def around(value, axis, size, ring, move):
+def around(value, plus, axis, size, ring, move):
+    return [value] + [
+        lax.ppermute(plus if d == ring - 1 else value, axis, [(i, move(i, d)) for i in range(size)])
+        for d in range(1, ring)
+    ]
+
+
+def around_by_sides(value, axis, size, ring, move):
     def hear(first, second):
         return lax.ppermute(
             value,
@@ -1039,22 +1067,23 @@
         core, theirs, near, common, (), (half, pre_own)
     )
     sum_theirs_got = lax.ppermute(sum_theirs, "core", swap)
-    sums = run_merge(core, sum_own, sum_own_got, sum_theirs, sum_theirs_got)
+    first_got = lax.ppermute(first, "core", swap)
+    sums, plus = run_merge(core, sum_own, sum_own_got, sum_theirs, sum_theirs_got, first_got)
     chip, sequence = lax.axis_index("chip"), lax.axis_index("dp")
     rows = chips // SIDE
-    values = around(sums, "chip", chips, SIDE, lambda i, d: i // SIDE * SIDE + (i % SIDE + d) % SIDE)
-    sums = run_fold(core, scalar(lax.rem(chip, SIDE)), values)
-    values = around(sums, "chip", chips, rows, lambda i, d: (i + d * SIDE) % chips)
-    sums, first = tie(run_fold(core, scalar(lax.div(chip, SIDE)), values), first)
-    after = lax.ppermute(first, CTX, [(i + 1, i) for i in range(devices - 1)])
-    near = 2 if sequences % 2 == 0 else 1
-    if near > 1:
-        values = around(sums, "dp", sequences, near, lambda i, d: i // 2 * 2 + (i % 2 + d) % 2)
-        sums = run_fold(core, scalar(lax.rem(sequence, near)), values)
-    values = around(sums, "dp", sequences, sequences // near, lambda i, d: (i + d * near) % sequences)
-    grad_tokens = run_spread(core, pre_own, pre_theirs, after, common[4])
+    values = around(sums, plus, "chip", chips, SIDE, lambda i, d: i // SIDE * SIDE + (i % SIDE + d) % SIDE)
+    after_y = values[-1]
+    sums, plus = run_fold(scalar(lax.rem(chip, SIDE)), values)
+    after_x = plus
+    if rows > 1:
+        values = around(sums, plus, "chip", chips, rows, lambda i, d: (i + d * SIDE) % chips)
+        after_x = values[-1]
+        sums, _ = run_fold(scalar(lax.div(chip, SIDE)), values)
+    values = around_by_sides(sums, "dp", sequences, sequences, lambda i, d: (i + d) % sequences)
+    place = jnp.stack([chip.astype(jnp.int32), jnp.int32(chips)])
+    grad_tokens = run_spread(core, place, pre_own, pre_theirs, first_got, after_y, after_x, common[4])
     values, grad_tokens = tie(values, grad_tokens)
-    grad_conv, grad_decay, grad_skip = run_finish(core, scalar(lax.div(sequence, near)), values)
+    grad_conv, grad_decay, grad_skip = run_finish(core, scalar(sequence), values)
     return (
         out_tokens[None],
         grad_tokens[None],

time: 112 us -> 112 us (level)
  the two profiles are of different devices: /device:TPU:2 before, /device:TPU:1 now
where the time goes in v12:
time: 112 us
  Pallas kernels  41.7 us (37%)
  starting transfers between devices  41.3 us (37%)
  waiting for transfers between devices  26.9 us (24%)
    pallas_call x15, Pallas kernels, go(): run(*[pin(a, spaces[p]) if p in spaces else a for a, p in zip(args, specs...  41.7 us
    all_to_all x2, waiting for transfers between devices, all_to_all(): return lax.all_to_all(value, axis, 0, 0, tiled=True)  17.8 us
    ppermute x4, starting transfers between devices, hear(): lax.ppermute(value, (axis, 'core'), [(2 * i + side, 2 * move(i, d) + side...  11.7 us
    all_to_all x2, starting transfers between devices, all_to_all(): return lax.all_to_all(value, axis, 0, 0, tiled=True)  10.7 us
    ppermute x6, waiting for transfers between devices, around(): lax.ppermute(plus if d == ring - 1 else value, axis, [(i, move(i, d)) for...  7.49 us
    ppermute x3, starting transfers between devices, around_by_sides(): swapped = [lax.ppermute(part, 'core', [(0, 1), (1, 0)]) for part in heard]  4.97 us
    ppermute x1, starting transfers between devices, local(): lax.ppermute(tokens[T - TAPS + 1:], CTX, [(i, i + 1) for i in range(devic...  4.59 us
    ppermute x6, starting transfers between devices, around(): lax.ppermute(plus if d == ring - 1 else value, axis, [(i, move(i, d)) for...  4.52 us
  transfers between devices with their start and end apart: 22, of which 8 were waited for; matrix products, arithmetic and copies ran while one was open for 0% of the time, Pallas kernels for 28%

profile of v12, /device:TPU:1, one launch (start us, length us, event | category | flops | bytes accessed | tf_op | source)
XLA Modules:
  0.0 111.7 jit_solution(10593143325014468234)
XLA Ops:
  0.6 0.9 slice_bitcast_fusion
  1.5 4.6 %collective-permute-start = (bf16[3,5120]{1,0:T(4,128)(2,1)S(1)}, bf16[3,5120]{1,0:T(4,128)(2,1)S(1)}, u32[]{:S(2)}, u32[]{:S(2)}) collective-permute-start(bf16[3,5120]{1,0:T(4,128)(2,1)S(1)} %slice_bitcast_fusion), channel_id=1, source_target_pairs={{0,1},{1,2},{2,3},{3,4},{4,5},{5,6},{6,7},{7,8},{8,9},{9,10},{10,1... | collective-permute-start | bytes 92168 | tf_op jit(solution)/shard_map/ppermute | solution.py:1040
  6.2 3.4 %begin.1 = (f32[512,128]{1,0:T(8,128)}, f32[512,128]{1,0:T(8,128)S(1)}, f32[32,128]{1,0:T(8,128)S(1)}, bf16[128,4096]{1,0:T(8,128)(2,1)S(1)}, bf16[128,1024]{1,0...) custom-call(f32[64,128]{1,0:T(8,128)} %bitcast.26, ...), custom_call_target="tpu_custom_call" | custom-call | flops 4000000000 | bytes 14400000 | tf_op jit(solution)/shard_map/begin/pallas_call | solution.py:97
  9.5 0.0 collective-permute-done.halo_ref
  9.5 2.4 %enter.1 = (bf16[128,4096]{1,0:T(8,128)(2,1)}, bf16[128,1024]{1,0:T(8,128)(2,1)}, f32[8,5120]{1,0:T(8,128)}, bf16[128,4096]{1,0:T(8,128)(2,1)S(1)}, bf16[128,102...) custom-call(s32[1]{0:T(128)} %bitcast.core_ref, bf16[128,4096]{1,0:T(8,128)(2,1)S(1)} %get-tuple-element.103.x0_ref, ...), custom_call_target="tpu_custom_call" | custom-call | flops 3000000000 | bytes 10800000 | tf_op jit(solution)/shard_map/enter/pallas_call | solution.py:97
  12.0 0.1 collective-permute-start.1
  12.1 0.5 collective-permute-start.2
  12.6 1.6 %own.1.own_ref = bf16[2,16,128,128]{3,2,1,0:T(8,128)(2,1)S(1)} custom-call(s32[1]{0:T(128)} %bitcast.core_ref, bf16[128,4096]{1,0:T(8,128)(2,1)S(1)} %get-tuple-element.110.x_ref, bf16[128,1024]{1,0:T(8,128)(2,1)S(1)} %get-tuple-element.111.bc_ref, bf16[128,4096]{1,0:T(8,128)(2,1)S(1)} %get-tuple-element.107.g_ref, f32[512,128]{1,0:T(8,128)S(1)} %get-tuple-element.108.small_ref), custom_call_target="tpu_custom_call" | custom-call | flops 3000000000 | bytes 10800000 | tf_op jit(solution)/shard_map/own/pallas_call | solution.py:97
  14.2 0.5 collective-permute-done.2.other_ref
  14.7 1.4 %pack.1 = (bf16[16,272,128]{2,1,0:T(8,128)(2,1)}, bf16[16,128,128]{2,1,0:T(8,128)(2,1)}, bf16[16,128,128]{2,1,0:T(8,128)(2,1)}, f32[64,128]{1,0:T(8,128)}) custom-call(s32[1]{0:T(128)} %bitcast.core_ref, bf16[2,16,128,128]{3,2,1,0:T(8,128)(2,1)S(1)} %own.1.own_ref, bf16[2,16,128,128]{3,2,1,0:T(8,128)(2,1)S(1)} %collective-permute-done.1.got_ref, ...), custom_call_target="tpu_custom_call" | custom-call | flops 2000000000 | bytes 7200000 | tf_op jit(solution)/shard_map/pack/pallas_call | solution.py:97
  16.2 6.5 %all-to-all-start = ((bf16[16,272,128]{2,1,0:T(8,128)(2,1)}), bf16[16,272,128]{2,1,0:T(8,128)(2,1)S(1)}, u32[]{:S(2)}, u32[]{:S(2)}) async-start(bf16[16,272,128]{2,1,0:T(8,128)(2,1)} %get-tuple-element.114), calls=%async_computation | async-start | bytes 2228224 | tf_op jit(solution)/shard_map/all_to_all | solution.py:996
  22.6 5.6 %inner.1 = (f32[128,4096]{1,0:T(8,128)}, f32[128,1024]{1,0:T(8,128)}, f32[32,128]{1,0:T(8,128)}) custom-call(bf16[128,4096]{1,0:T(8,128)(2,1)} %get-tuple-element.115.x_h.rest_0_.rest_21_, bf16[128,1024]{1,0:T(8,128)(2,1)} %get-tuple-element.122.bc_h.rest_6_.rest_27_, bf16[128,4096]{1,0:T(8,128)(2,1)} %bitcast.22, f32[512,128]{1,0:T(8,128)} %get-tuple-element.116.small_h.rest_9_), custom_call_target="tpu_custom_call" | custom-call | flops 4000000000 | bytes 14400000 | tf_op jit(solution)/shard_map/inner/pallas_call | solution.py:97
  28.2 11.4 %all-to-all-done.in_ref = bf16[16,272,128]{2,1,0:T(8,128)(2,1)S(1)} async-done(((bf16[16,272,128]{2,1,0:T(8,128)(2,1)}), bf16[16,272,128]{2,1,0:T(8,128)(2,1)S(1)}, u32[]{:S(2)}, u32[]{:S(2)}) %all-to-all-start) | async-done | bytes 1114144 | tf_op jit(solution)/shard_map/all_to_all | solution.py:996
  39.6 1.3 %chain.1 = bf16[16,256,128]{2,1,0:T(8,128)(2,1)} custom-call(bf16[16,272,128]{2,1,0:T(8,128)(2,1)S(1)} %all-to-all-done.in_ref), custom_call_target="tpu_custom_call" | custom-call | flops 1000000000 | bytes 3600000 | tf_op jit(solution)/shard_map/chain/pallas_call | solution.py:97
  40.9 4.2 %all-to-all-start.1 = ((bf16[16,256,128]{2,1,0:T(8,128)(2,1)}), bf16[16,256,128]{2,1,0:T(8,128)(2,1)S(1)}, u32[]{:S(2)}, u32[]{:S(2)}) async-start(bf16[16,256,128]{2,1,0:T(8,128)(2,1)} %chain.1), calls=%async_computation.1 | async-start | bytes 2097152 | tf_op jit(solution)/shard_map/all_to_all | solution.py:996
  45.1 8.5 %slopes.1 = (f32[128,4096]{1,0:T(8,128)}, f32[128,5120]{1,0:T(8,128)}) custom-call(bf16[128,1024]{1,0:T(8,128)(2,1)} %get-tuple-element.122.bc_h.rest_6_.rest_27_, bf16[128,4096]{1,0:T(8,128)(2,1)} %bitcast.23, f32[512,128]{1,0:T(8,128)} %get-tuple-element.116.small_h.rest_9_, bf16[128,5120]{1,0:T(8,128)(2,1)} %bitcast.18, ...), custom_call_target="tpu_custom_call" | custom-call | flops 6000000000 | bytes 21600000 | tf_op jit(solution)/shard_map/slopes/pallas_call | solution.py:97
  53.6 6.4 %all-to-all-done.1.back_ref = bf16[16,256,128]{2,1,0:T(8,128)(2,1)S(1)} async-done(((bf16[16,256,128]{2,1,0:T(8,128)(2,1)}), bf16[16,256,128]{2,1,0:T(8,128)(2,1)S(1)}, u32[]{:S(2)}, u32[]{:S(2)}) %all-to-all-start.1) | async-done | bytes 1048608 | tf_op jit(solution)/shard_map/all_to_all | solution.py:996
  60.0 3.8 %unpack.1 = (bf16[2,16,128,128]{3,2,1,0:T(8,128)(2,1)S(1)}, bf16[2,16,128,128]{3,2,1,0:T(8,128)(2,1)S(1)}, bf16[128,1024]{1,0:T(8,128)(2,1)S(1)}, bf16[128,1024]...) custom-call(s32[1]{0:T(128)} %bitcast.core_ref, ...), custom_call_target="tpu_custom_call" | custom-call | flops 3000000000 | bytes 10800000 | tf_op jit(solution)/shard_map/unpack/pallas_call | solution.py:97
  63.9 3.4 %collective-permute-start.3 = (bf16[2,16,128,128]{3,2,1,0:T(8,128)(2,1)S(1)}, bf16[2,16,128,128]{3,2,1,0:T(8,128)(2,1)S(1)}, u32[]{:S(2)}, u32[]{:S(2)}) collective-permute-start(bf16[2,16,128,128]{3,2,1,0:T(8,128)(2,1)S(1)} %get-tuple-element.135), channel_id=1, source_target_pairs={{0,1},{1,0},{2,3},{3,2},{4,5},{5,4},{6,7},{7,6},{8,9},{9,8},{10,11... | collective-permute-start | bytes 3145736 | tf_op jit(solution)/shard_map/ppermute | solution.py:1063
  67.3 4.2 %leave.2 = (bf16[128,4096]{1,0:T(8,128)(2,1)}, f32[64,128]{1,0:T(8,128)}, f32[128,2560]{1,0:T(8,128)S(1)}, f32[128,128]{1,0:T(8,128)S(1)}, bf16[128,1024]{1,0:T(...) custom-call(s32[1]{0:T(128)} %bitcast.core_ref, ...), custom_call_target="tpu_custom_call" | custom-call | flops 5000000000 | bytes 18000000 | tf_op jit(solution)/shard_map/leave/pallas_call | solution.py:97
  71.5 0.1 collective-permute-start.4
  71.6 4.2 %leave.3 = (bf16[128,4096]{1,0:T(8,128)(2,1)}, f32[64,128]{1,0:T(8,128)}, f32[128,2560]{1,0:T(8,128)}, f32[128,128]{1,0:T(8,128)S(1)}, bf16[3,5120]{1,0:T(4,128)(2,1)S(1)}) custom-call(s32[1]{0:T(128)} %bitcast.core_ref, bf16[2,16,128,128]{3,2,1,0:T(8,128)(2,1)S(1)} %collective-permute-done.3.state_ref, ...), custom_call_target="tpu_custom_call", output_to_operand_aliasing={{0}: (24, {}), {1}: (25, {})} | custom-call | flops 5000000000 | bytes 18000000 | tf_op jit(solution)/shard_map/leave/pallas_call | solution.py:97
  75.8 0.6 collective-permute-start.5
  76.3 0.1 collective-permute-start.6
  76.4 1.1 collective-permute-done.6.swap_ref
  77.6 0.6 merge.1
  78.1 0.4 collective-permute-start.9
  78.6 1.0 collective-permute-start.7
  79.6 0.7 collective-permute-start.8
  80.3 2.4 %collective-permute-done.7.rest_1_ = bf16[176,128]{1,0:T(8,128)(2,1)S(1)} collective-permute-done((bf16[176,128]{1,0:T(8,128)(2,1)S(1)}, bf16[176,128]{1,0:T(8,128)(2,1)S(1)}, u32[]{:S(2)}, u32[]{:S(2)}) %collective-permute-start.7) | collective-permute-done | bytes 45088 | tf_op jit(solution)/shard_map/ppermute | solution.py:1008
  82.7 1.4 %collective-permute-done.8.rest_2_ = bf16[176,128]{1,0:T(8,128)(2,1)S(1)} collective-permute-done((bf16[176,128]{1,0:T(8,128)(2,1)S(1)}, bf16[176,128]{1,0:T(8,128)(2,1)S(1)}, u32[]{:S(2)}, u32[]{:S(2)}) %collective-permute-start.8) | collective-permute-done | bytes 45088 | tf_op jit(solution)/shard_map/ppermute | solution.py:1008
  84.1 0.1 fold.2
  84.1 1.1 collective-permute-start.12
  85.2 0.5 collective-permute-start.10
  85.7 0.8 collective-permute-start.11
  86.5 2.8 %collective-permute-done.10.rest_1_ = bf16[176,128]{1,0:T(8,128)(2,1)S(1)} collective-permute-done((bf16[176,128]{1,0:T(8,128)(2,1)S(1)}, bf16[176,128]{1,0:T(8,128)(2,1)S(1)}, u32[]{:S(2)}, u32[]{:S(2)}) %collective-permute-start.10) | collective-permute-done | bytes 45088 | tf_op jit(solution)/shard_map/ppermute | solution.py:1008
  89.3 0.9 collective-permute-done.11.rest_2_
  90.2 0.7 fold.3
  90.9 5.6 %collective-permute-start.13 = (bf16[176,128]{1,0:T(8,128)(2,1)S(1)}, bf16[176,128]{1,0:T(8,128)(2,1)S(1)}, u32[]{:S(2)}, u32[]{:S(2)}) collective-permute-start(bf16[176,128]{1,0:T(8,128)(2,1)S(1)} %get-tuple-element.189.rest_0_), channel_id=1, source_target_pairs={{0,32},{1,225},{32,64},{33,1},{64,96},{65,33},{96,128},{97,65},{12... | collective-permute-start | bytes 135176 | tf_op jit(solution)/shard_map/ppermute | solution.py:1015
  96.5 1.2 %collective-permute-start.14 = (bf16[176,128]{1,0:T(8,128)(2,1)S(1)}, bf16[176,128]{1,0:T(8,128)(2,1)S(1)}, u32[]{:S(2)}, u32[]{:S(2)}) collective-permute-start(bf16[176,128]{1,0:T(8,128)(2,1)S(1)} %get-tuple-element.189.rest_0_), channel_id=1, source_target_pairs={{0,64},{1,193},{32,96},{33,225},{64,128},{65,1},{96,160},{97,33},{... | collective-permute-start | bytes 135176 | tf_op jit(solution)/shard_map/ppermute | solution.py:1015
  97.6 0.5 collective-permute-start.15
  98.1 0.1 pad_add_fusion.chip_ref
  98.2 4.5 %collective-permute-start.19 = (bf16[176,128]{1,0:T(8,128)(2,1)S(1)}, bf16[176,128]{1,0:T(8,128)(2,1)S(1)}, u32[]{:S(2)}, u32[]{:S(2)}) collective-permute-start(bf16[176,128]{1,0:T(8,128)(2,1)S(1)} %get-tuple-element.189.rest_0_), channel_id=1, source_target_pairs={{0,128},{1,129},{32,160},{33,161},{64,192},{65,193},{96,224},{97,2... | collective-permute-start | bytes 135176 | tf_op jit(solution)/shard_map/ppermute | solution.py:1015
  102.7 1.5 %collective-permute-start.16 = (bf16[176,128]{1,0:T(8,128)(2,1)S(1)}, bf16[176,128]{1,0:T(8,128)(2,1)S(1)}, u32[]{:S(2)}, u32[]{:S(2)}) collective-permute-start(bf16[176,128]{1,0:T(8,128)(2,1)S(1)} %collective-permute-done.13.rest_1_), channel_id=1, source_target_pairs={{0,1},{1,0},{2,3},{3,2},{4,5},{5,4},{6,7},{7,6},{8,9},{9,8},{10,11... | collective-permute-start | bytes 135176 | tf_op jit(solution)/shard_map/ppermute | solution.py:1023
  104.2 0.1 collective-permute-start.17
  104.3 3.4 %collective-permute-start.18 = (bf16[176,128]{1,0:T(8,128)(2,1)S(1)}, bf16[176,128]{1,0:T(8,128)(2,1)S(1)}, u32[]{:S(2)}, u32[]{:S(2)}) collective-permute-start(bf16[176,128]{1,0:T(8,128)(2,1)S(1)} %collective-permute-done.15.rest_3_), channel_id=1, source_target_pairs={{0,1},{1,0},{2,3},{3,2},{4,5},{5,4},{6,7},{7,6},{8,9},{9,8},{10,11... | collective-permute-start | bytes 135176 | tf_op jit(solution)/shard_map/ppermute | solution.py:1023
  107.6 3.3 %spread.1 = bf16[128,5120]{1,0:T(8,128)(2,1)} custom-call(s32[1]{0:T(128)} %bitcast.core_ref, s32[2]{0:T(128)S(1)} %pad_add_fusion.chip_ref, f32[128,2560]{1,0:T(8,128)S(1)} %get-tuple-element.174.rest_21_.own_ref, f32[128,2560]{1,0:T(8,128)} %get-tuple-element.186.theirs_h, bf16[3,5120]{1,0:T(4,128)(2,1)S(1)} %collective-permute-done.6.swap_ref, ...), custom_call_target="tpu_custom_call" | custom-call | flops 3000000000 | bytes 10800000 | tf_op jit(solution)/shard_map/spread/pallas_call | solution.py:97
  111.0 0.7 finish.1
  (13 shorter events, 0.0 us)
Async XLA Ops:
  1.5 8.0 %collective-permute-start = (bf16[3,5120]{1,0:T(4,128)(2,1)S(1)}, bf16[3,5120]{1,0:T(4,128)(2,1)S(1)}, u32[]{:S(2)}, u32[]{:S(2)}) collective-permute-start(bf16[3,5120]{1,0:T(4,128)(2,1)S(1)} %slice_bitcast_fusion), channel_id=1, source_target_pairs={{0,1},{1,2},{2,3},{3,4},{4,5},{5,6},{6,7},{7,8},{8,9},{9,10},{10,1... | collective-permute-start | bytes 92168 | tf_op jit(solution)/shard_map/ppermute | solution.py:1040
  12.0 2.8 %collective-permute-start.1 = (bf16[2,16,128,128]{3,2,1,0:T(8,128)(2,1)S(1)}, bf16[2,16,128,128]{3,2,1,0:T(8,128)(2,1)S(1)}, u32[]{:S(2)}, u32[]{:S(2)}) collective-permute-start(bf16[2,16,128,128]{3,2,1,0:T(8,128)(2,1)S(1)} %get-tuple-element.112), channel_id=1, source_target_pairs={{0,1},{1,0},{2,3},{3,2},{4,5},{5,4},{6,7},{7,6},{8,9},{9,8},{10,11... | collective-permute-start | bytes 3145736 | tf_op jit(solution)/shard_map/ppermute | solution.py:1048
  12.1 2.7 %collective-permute-start.2 = (f32[32,128]{1,0:T(8,128)S(1)}, f32[32,128]{1,0:T(8,128)S(1)}, u32[]{:S(2)}, u32[]{:S(2)}) collective-permute-start(f32[32,128]{1,0:T(8,128)S(1)} %get-tuple-element.113.tot_ref), channel_id=1, source_target_pairs={{0,1},{1,0},{2,3},{3,2},{4,5},{5,4},{6,7},{7,6},{8,9},{9,8},{10,11... | collective-permute-start | bytes 49160 | tf_op jit(solution)/shard_map/ppermute | solution.py:1044
  16.2 23.5 %all-to-all-start = ((bf16[16,272,128]{2,1,0:T(8,128)(2,1)}), bf16[16,272,128]{2,1,0:T(8,128)(2,1)S(1)}, u32[]{:S(2)}, u32[]{:S(2)}) async-start(bf16[16,272,128]{2,1,0:T(8,128)(2,1)} %get-tuple-element.114), calls=%async_computation | async-start | bytes 2228224 | tf_op jit(solution)/shard_map/all_to_all | solution.py:996
  40.9 19.2 %all-to-all-start.1 = ((bf16[16,256,128]{2,1,0:T(8,128)(2,1)}), bf16[16,256,128]{2,1,0:T(8,128)(2,1)S(1)}, u32[]{:S(2)}, u32[]{:S(2)}) async-start(bf16[16,256,128]{2,1,0:T(8,128)(2,1)} %chain.1), calls=%async_computation.1 | async-start | bytes 2097152 | tf_op jit(solution)/shard_map/all_to_all | solution.py:996
  63.9 7.7 %collective-permute-start.3 = (bf16[2,16,128,128]{3,2,1,0:T(8,128)(2,1)S(1)}, bf16[2,16,128,128]{3,2,1,0:T(8,128)(2,1)S(1)}, u32[]{:S(2)}, u32[]{:S(2)}) collective-permute-start(bf16[2,16,128,128]{3,2,1,0:T(8,128)(2,1)S(1)} %get-tuple-element.135), channel_id=1, source_target_pairs={{0,1},{1,0},{2,3},{3,2},{4,5},{5,4},{6,7},{7,6},{8,9},{9,8},{10,11... | collective-permute-start | bytes 3145736 | tf_op jit(solution)/shard_map/ppermute | solution.py:1063
  71.5 5.0 %collective-permute-start.4 = (f32[128,128]{1,0:T(8,128)S(1)}, f32[128,128]{1,0:T(8,128)S(1)}, u32[]{:S(2)}, u32[]{:S(2)}) collective-permute-start(f32[128,128]{1,0:T(8,128)S(1)} %get-tuple-element.178.own_ref), channel_id=1, source_target_pairs={{0,1},{1,0},{2,3},{3,2},{4,5},{5,4},{6,7},{7,6},{8,9},{9,8},{10,11... | collective-permute-start | bytes 196616 | tf_op jit(solution)/shard_map/ppermute | solution.py:1065
  75.8 1.8 %collective-permute-start.5 = (f32[128,128]{1,0:T(8,128)S(1)}, f32[128,128]{1,0:T(8,128)S(1)}, u32[]{:S(2)}, u32[]{:S(2)}) collective-permute-start(f32[128,128]{1,0:T(8,128)S(1)} %get-tuple-element.179.theirs_ref), channel_id=1, source_target_pairs={{0,1},{1,0},{2,3},{3,2},{4,5},{5,4},{6,7},{7,6},{8,9},{9,8},{10,11... | collective-permute-start | bytes 196616 | tf_op jit(solution)/shard_map/ppermute | solution.py:1069
  76.3 1.2 %collective-permute-start.6 = (bf16[3,5120]{1,0:T(4,128)(2,1)S(1)}, bf16[3,5120]{1,0:T(4,128)(2,1)S(1)}, u32[]{:S(2)}, u32[]{:S(2)}) collective-permute-start(bf16[3,5120]{1,0:T(4,128)(2,1)S(1)} %get-tuple-element.180), channel_id=1, source_target_pairs={{0,1},{1,0},{2,3},{3,2},{4,5},{5,4},{6,7},{7,6},{8,9},{9,8},{10,11... | collective-permute-start | bytes 92168 | tf_op jit(solution)/shard_map/ppermute | solution.py:1070
  78.1 5.9 %collective-permute-start.9 = (bf16[304,128]{1,0:T(8,128)(2,1)S(1)}, bf16[304,128]{1,0:T(8,128)(2,1)S(1)}, u32[]{:S(2)}, u32[]{:S(2)}) collective-permute-start(bf16[304,128]{1,0:T(8,128)(2,1)S(1)} %get-tuple-element.182), channel_id=1, source_target_pairs={{0,6},{2,0},{4,2},{6,4},{8,14},{10,8},{12,10},{14,12},{16,22},{18,... | collective-permute-start | bytes 233480 | tf_op jit(solution)/shard_map/ppermute | solution.py:1008
  78.6 4.1 %collective-permute-start.7 = (bf16[176,128]{1,0:T(8,128)(2,1)S(1)}, bf16[176,128]{1,0:T(8,128)(2,1)S(1)}, u32[]{:S(2)}, u32[]{:S(2)}) collective-permute-start(bf16[176,128]{1,0:T(8,128)(2,1)S(1)} %get-tuple-element.181.rest_0_), channel_id=1, source_target_pairs={{0,2},{2,4},{4,6},{6,0},{8,10},{10,12},{12,14},{14,8},{16,18},{18,... | collective-permute-start | bytes 135176 | tf_op jit(solution)/shard_map/ppermute | solution.py:1008
  79.6 4.5 %collective-permute-start.8 = (bf16[176,128]{1,0:T(8,128)(2,1)S(1)}, bf16[176,128]{1,0:T(8,128)(2,1)S(1)}, u32[]{:S(2)}, u32[]{:S(2)}) collective-permute-start(bf16[176,128]{1,0:T(8,128)(2,1)S(1)} %get-tuple-element.181.rest_0_), channel_id=1, source_target_pairs={{0,4},{2,6},{4,0},{6,2},{8,12},{10,14},{12,8},{14,10},{16,20},{18,... | collective-permute-start | bytes 135176 | tf_op jit(solution)/shard_map/ppermute | solution.py:1008
  84.1 6.1 %collective-permute-start.12 = (bf16[304,128]{1,0:T(8,128)(2,1)S(1)}, bf16[304,128]{1,0:T(8,128)(2,1)S(1)}, u32[]{:S(2)}, u32[]{:S(2)}) collective-permute-start(bf16[304,128]{1,0:T(8,128)(2,1)S(1)} %get-tuple-element.184), channel_id=1, source_target_pairs={{0,24},{2,26},{4,28},{6,30},{8,0},{10,2},{12,4},{14,6},{16,8},{18,... | collective-permute-start | bytes 233480 | tf_op jit(solution)/shard_map/ppermute | solution.py:1008
  85.2 4.1 %collective-permute-start.10 = (bf16[176,128]{1,0:T(8,128)(2,1)S(1)}, bf16[176,128]{1,0:T(8,128)(2,1)S(1)}, u32[]{:S(2)}, u32[]{:S(2)}) collective-permute-start(bf16[176,128]{1,0:T(8,128)(2,1)S(1)} %get-tuple-element.183.rest_0_), channel_id=1, source_target_pairs={{0,8},{2,10},{4,12},{6,14},{8,16},{10,18},{12,20},{14,22},{16,24},... | collective-permute-start | bytes 135176 | tf_op jit(solution)/shard_map/ppermute | solution.py:1008
  85.7 4.5 %collective-permute-start.11 = (bf16[176,128]{1,0:T(8,128)(2,1)S(1)}, bf16[176,128]{1,0:T(8,128)(2,1)S(1)}, u32[]{:S(2)}, u32[]{:S(2)}) collective-permute-start(bf16[176,128]{1,0:T(8,128)(2,1)S(1)} %get-tuple-element.183.rest_0_), channel_id=1, source_target_pairs={{0,16},{2,18},{4,20},{6,22},{8,24},{10,26},{12,28},{14,30},{16,0},... | collective-permute-start | bytes 135176 | tf_op jit(solution)/shard_map/ppermute | solution.py:1008
  90.9 11.8 %collective-permute-start.13 = (bf16[176,128]{1,0:T(8,128)(2,1)S(1)}, bf16[176,128]{1,0:T(8,128)(2,1)S(1)}, u32[]{:S(2)}, u32[]{:S(2)}) collective-permute-start(bf16[176,128]{1,0:T(8,128)(2,1)S(1)} %get-tuple-element.189.rest_0_), channel_id=1, source_target_pairs={{0,32},{1,225},{32,64},{33,1},{64,96},{65,33},{96,128},{97,65},{12... | collective-permute-start | bytes 135176 | tf_op jit(solution)/shard_map/ppermute | solution.py:1015
  96.5 7.7 %collective-permute-start.14 = (bf16[176,128]{1,0:T(8,128)(2,1)S(1)}, bf16[176,128]{1,0:T(8,128)(2,1)S(1)}, u32[]{:S(2)}, u32[]{:S(2)}) collective-permute-start(bf16[176,128]{1,0:T(8,128)(2,1)S(1)} %get-tuple-element.189.rest_0_), channel_id=1, source_target_pairs={{0,64},{1,193},{32,96},{33,225},{64,128},{65,1},{96,160},{97,33},{... | collective-permute-start | bytes 135176 | tf_op jit(solution)/shard_map/ppermute | solution.py:1015
  97.6 6.6 %collective-permute-start.15 = (bf16[176,128]{1,0:T(8,128)(2,1)S(1)}, bf16[176,128]{1,0:T(8,128)(2,1)S(1)}, u32[]{:S(2)}, u32[]{:S(2)}) collective-permute-start(bf16[176,128]{1,0:T(8,128)(2,1)S(1)} %get-tuple-element.189.rest_0_), channel_id=1, source_target_pairs={{0,96},{1,161},{32,128},{33,193},{64,160},{65,225},{96,192},{97,1}... | collective-permute-start | bytes 135176 | tf_op jit(solution)/shard_map/ppermute | solution.py:1015
  98.2 12.7 %collective-permute-start.19 = (bf16[176,128]{1,0:T(8,128)(2,1)S(1)}, bf16[176,128]{1,0:T(8,128)(2,1)S(1)}, u32[]{:S(2)}, u32[]{:S(2)}) collective-permute-start(bf16[176,128]{1,0:T(8,128)(2,1)S(1)} %get-tuple-element.189.rest_0_), channel_id=1, source_target_pairs={{0,128},{1,129},{32,160},{33,161},{64,192},{65,193},{96,224},{97,2... | collective-permute-start | bytes 135176 | tf_op jit(solution)/shard_map/ppermute | solution.py:1015
  102.7 8.3 %collective-permute-start.16 = (bf16[176,128]{1,0:T(8,128)(2,1)S(1)}, bf16[176,128]{1,0:T(8,128)(2,1)S(1)}, u32[]{:S(2)}, u32[]{:S(2)}) collective-permute-start(bf16[176,128]{1,0:T(8,128)(2,1)S(1)} %collective-permute-done.13.rest_1_), channel_id=1, source_target_pairs={{0,1},{1,0},{2,3},{3,2},{4,5},{5,4},{6,7},{7,6},{8,9},{9,8},{10,11... | collective-permute-start | bytes 135176 | tf_op jit(solution)/shard_map/ppermute | solution.py:1023
  104.2 6.8 %collective-permute-start.17 = (bf16[176,128]{1,0:T(8,128)(2,1)S(1)}, bf16[176,128]{1,0:T(8,128)(2,1)S(1)}, u32[]{:S(2)}, u32[]{:S(2)}) collective-permute-start(bf16[176,128]{1,0:T(8,128)(2,1)S(1)} %collective-permute-done.14.rest_2_), channel_id=1, source_target_pairs={{0,1},{1,0},{2,3},{3,2},{4,5},{5,4},{6,7},{7,6},{8,9},{9,8},{10,11... | collective-permute-start | bytes 135176 | tf_op jit(solution)/shard_map/ppermute | solution.py:1023
  104.3 6.7 %collective-permute-start.18 = (bf16[176,128]{1,0:T(8,128)(2,1)S(1)}, bf16[176,128]{1,0:T(8,128)(2,1)S(1)}, u32[]{:S(2)}, u32[]{:S(2)}) collective-permute-start(bf16[176,128]{1,0:T(8,128)(2,1)S(1)} %collective-permute-done.15.rest_3_), channel_id=1, source_target_pairs={{0,1},{1,0},{2,3},{3,2},{4,5},{5,4},{6,7},{7,6},{8,9},{9,8},{10,11... | collective-permute-start | bytes 135176 | tf_op jit(solution)/shard_map/ppermute | solution.py:1023

commit v13 on v11

--- a/solution.py
+++ b/solution.py
@@ -1039,21 +1039,21 @@
         core, theirs, near, common, (), (half, pre_own)
     )
     sum_theirs_got = lax.ppermute(sum_theirs, "core", swap)
+    after = lax.ppermute(first, CTX, [(i + 1, i) for i in range(devices - 1)])
     sums = run_merge(core, sum_own, sum_own_got, sum_theirs, sum_theirs_got)
     chip, sequence = lax.axis_index("chip"), lax.axis_index("dp")
     rows = chips // SIDE
     values = around(sums, "chip", chips, SIDE, lambda i, d: i // SIDE * SIDE + (i % SIDE + d) % SIDE)
+    grad_tokens = run_spread(core, pre_own, pre_theirs, after, common[4])
+    values, grad_tokens = tie(values, grad_tokens)
     sums = run_fold(core, scalar(lax.rem(chip, SIDE)), values)
     values = around(sums, "chip", chips, rows, lambda i, d: (i + d * SIDE) % chips)
-    sums, first = tie(run_fold(core, scalar(lax.div(chip, SIDE)), values), first)
-    after = lax.ppermute(first, CTX, [(i + 1, i) for i in range(devices - 1)])
+    sums = run_fold(core, scalar(lax.div(chip, SIDE)), values)
     near = 2 if sequences % 2 == 0 else 1
     if near > 1:
         values = around(sums, "dp", sequences, near, lambda i, d: i // 2 * 2 + (i % 2 + d) % 2)
         sums = run_fold(core, scalar(lax.rem(sequence, near)), values)
     values = around(sums, "dp", sequences, sequences // near, lambda i, d: (i + d * near) % sequences)
-    grad_tokens = run_spread(core, pre_own, pre_theirs, after, common[4])
-    values, grad_tokens = tie(values, grad_tokens)
     grad_conv, grad_decay, grad_skip = run_finish(core, scalar(lax.div(sequence, near)), values)
     return (
         out_tokens[None],

time: 112 us -> 110 us (0.982)
  starting transfers between devices: 37.1 us -> 35 us
    ppermute x1, starting transfers between devices: 6.62 us -> 3.75 us  [local(): after = lax.ppermute(first, CTX, [(i + 1, i) for i in range(devices - 1)])]
  transfers between devices with their start and end apart: 19 -> 19, of which waited for: 12 -> 11; matrix products, arithmetic and copies ran while one was open for 0% -> 0% of each run, Pallas kernels for 27% -> 28%
where the time goes in v13:
time: 110 us; the launch traced here: 109 us
  Pallas kernels  40.7 us (37%)
  starting transfers between devices  35 us (32%)
  waiting for transfers between devices  31.5 us (29%)
    pallas_call x16, Pallas kernels, go(): run(*[pin(a, spaces[p]) if p in spaces else a for a, p in zip(args, specs...  40.7 us
    all_to_all x2, waiting for transfers between devices, all_to_all(): return lax.all_to_all(value, axis, 0, 0, tiled=True)  16.6 us
    ppermute x7, starting transfers between devices, hear(): lax.ppermute(value, (axis, 'core'), [(2 * i + side, 2 * move(i, d) + side...  15.1 us
    all_to_all x2, starting transfers between devices, all_to_all(): return lax.all_to_all(value, axis, 0, 0, tiled=True)  12.6 us
    ppermute x7, waiting for transfers between devices, hear(): lax.ppermute(value, (axis, 'core'), [(2 * i + side, 2 * move(i, d) + side...  10.7 us
    ppermute x1, starting transfers between devices, local(): after = lax.ppermute(first, CTX, [(i + 1, i) for i in range(devices - 1)])  3.75 us
  transfers between devices with their start and end apart: 19, of which 11 were waited for; matrix products, arithmetic and copies ran while one was open for 0% of the time, Pallas kernels for 28%

profile of v13, /device:TPU:2, one launch (start us, length us, event | category | flops | bytes accessed | tf_op | source)
XLA Modules:
  0.0 108.8 jit_solution(12548618029659354737)
XLA Ops:
  0.6 0.9 slice_bitcast_fusion
  1.5 1.9 %collective-permute-start = (bf16[3,5120]{1,0:T(4,128)(2,1)S(1)}, bf16[3,5120]{1,0:T(4,128)(2,1)S(1)}, u32[]{:S(2)}, u32[]{:S(2)}) collective-permute-start(bf16[3,5120]{1,0:T(4,128)(2,1)S(1)} %slice_bitcast_fusion), channel_id=1, source_target_pairs={{0,1},{1,2},{2,3},{3,4},{4,5},{5,6},{6,7},{7,8},{8,9},{9,10},{10,1... | collective-permute-start | bytes 92168 | tf_op jit(solution)/shard_map/ppermute | solution.py:1012
  3.5 3.4 %begin.1 = (f32[512,128]{1,0:T(8,128)}, f32[512,128]{1,0:T(8,128)S(1)}, f32[32,128]{1,0:T(8,128)S(1)}, bf16[128,4096]{1,0:T(8,128)(2,1)S(1)}, bf16[128,1024]{1,0...) custom-call(f32[64,128]{1,0:T(8,128)} %bitcast.26, ...), custom_call_target="tpu_custom_call" | custom-call | flops 4000000000 | bytes 14400000 | tf_op jit(solution)/shard_map/begin/pallas_call | solution.py:97
  6.9 2.1 %collective-permute-done.halo_ref = bf16[3,5120]{1,0:T(4,128)(2,1)S(1)} collective-permute-done((bf16[3,5120]{1,0:T(4,128)(2,1)S(1)}, bf16[3,5120]{1,0:T(4,128)(2,1)S(1)}, u32[]{:S(2)}, u32[]{:S(2)}) %collective-permute-start) | collective-permute-done | bytes 30752 | tf_op jit(solution)/shard_map/ppermute | solution.py:1012
  9.0 2.4 %enter.1 = (bf16[128,4096]{1,0:T(8,128)(2,1)}, bf16[128,1024]{1,0:T(8,128)(2,1)}, f32[8,5120]{1,0:T(8,128)}, bf16[128,4096]{1,0:T(8,128)(2,1)S(1)}, bf16[128,102...) custom-call(s32[1]{0:T(128)} %bitcast.core_ref, bf16[128,4096]{1,0:T(8,128)(2,1)S(1)} %get-tuple-element.94.x0_ref, ...), custom_call_target="tpu_custom_call" | custom-call | flops 3000000000 | bytes 10800000 | tf_op jit(solution)/shard_map/enter/pallas_call | solution.py:97
  11.4 0.1 collective-permute-start.1
  11.5 0.5 collective-permute-start.2
  12.0 1.6 %own.1.own_ref = bf16[2,16,128,128]{3,2,1,0:T(8,128)(2,1)S(1)} custom-call(s32[1]{0:T(128)} %bitcast.core_ref, bf16[128,4096]{1,0:T(8,128)(2,1)S(1)} %get-tuple-element.101.x_ref, bf16[128,1024]{1,0:T(8,128)(2,1)S(1)} %get-tuple-element.102.bc_ref, bf16[128,4096]{1,0:T(8,128)(2,1)S(1)} %get-tuple-element.98.g_ref, f32[512,128]{1,0:T(8,128)S(1)} %get-tuple-element.99.small_ref), custom_call_target="tpu_custom_call" | custom-call | flops 3000000000 | bytes 10800000 | tf_op jit(solution)/shard_map/own/pallas_call | solution.py:97
  13.6 0.5 collective-permute-done.2.other_ref
  14.1 1.4 %pack.1 = (bf16[16,272,128]{2,1,0:T(8,128)(2,1)}, bf16[16,128,128]{2,1,0:T(8,128)(2,1)}, bf16[16,128,128]{2,1,0:T(8,128)(2,1)}, f32[64,128]{1,0:T(8,128)}) custom-call(s32[1]{0:T(128)} %bitcast.core_ref, bf16[2,16,128,128]{3,2,1,0:T(8,128)(2,1)S(1)} %own.1.own_ref, bf16[2,16,128,128]{3,2,1,0:T(8,128)(2,1)S(1)} %collective-permute-done.1.got_ref, ...), custom_call_target="tpu_custom_call" | custom-call | flops 2000000000 | bytes 7200000 | tf_op jit(solution)/shard_map/pack/pallas_call | solution.py:97
  15.6 6.4 %all-to-all-start = ((bf16[16,272,128]{2,1,0:T(8,128)(2,1)}), bf16[16,272,128]{2,1,0:T(8,128)(2,1)S(1)}, u32[]{:S(2)}, u32[]{:S(2)}) async-start(bf16[16,272,128]{2,1,0:T(8,128)(2,1)} %get-tuple-element.105), calls=%async_computation | async-start | bytes 2228224 | tf_op jit(solution)/shard_map/all_to_all | solution.py:975
  22.0 5.7 %inner.1 = (f32[128,4096]{1,0:T(8,128)}, f32[128,1024]{1,0:T(8,128)}, f32[32,128]{1,0:T(8,128)}) custom-call(bf16[128,4096]{1,0:T(8,128)(2,1)} %get-tuple-element.106.x_h.rest_0_.rest_21_, bf16[128,1024]{1,0:T(8,128)(2,1)} %get-tuple-element.113.bc_h.rest_6_.rest_27_, bf16[128,4096]{1,0:T(8,128)(2,1)} %bitcast.22, f32[512,128]{1,0:T(8,128)} %get-tuple-element.107.small_h.rest_9_), custom_call_target="tpu_custom_call" | custom-call | flops 4000000000 | bytes 14400000 | tf_op jit(solution)/shard_map/inner/pallas_call | solution.py:97
  27.6 10.8 %all-to-all-done.in_ref = bf16[16,272,128]{2,1,0:T(8,128)(2,1)S(1)} async-done(((bf16[16,272,128]{2,1,0:T(8,128)(2,1)}), bf16[16,272,128]{2,1,0:T(8,128)(2,1)S(1)}, u32[]{:S(2)}, u32[]{:S(2)}) %all-to-all-start) | async-done | bytes 1114144 | tf_op jit(solution)/shard_map/all_to_all | solution.py:975
  38.5 1.3 %chain.1 = bf16[16,256,128]{2,1,0:T(8,128)(2,1)} custom-call(bf16[16,272,128]{2,1,0:T(8,128)(2,1)S(1)} %all-to-all-done.in_ref), custom_call_target="tpu_custom_call" | custom-call | flops 1000000000 | bytes 3600000 | tf_op jit(solution)/shard_map/chain/pallas_call | solution.py:97
  39.7 6.2 %all-to-all-start.1 = ((bf16[16,256,128]{2,1,0:T(8,128)(2,1)}), bf16[16,256,128]{2,1,0:T(8,128)(2,1)S(1)}, u32[]{:S(2)}, u32[]{:S(2)}) async-start(bf16[16,256,128]{2,1,0:T(8,128)(2,1)} %chain.1), calls=%async_computation.1 | async-start | bytes 2097152 | tf_op jit(solution)/shard_map/all_to_all | solution.py:975
  45.9 8.5 %slopes.1 = (f32[128,4096]{1,0:T(8,128)}, f32[128,5120]{1,0:T(8,128)}) custom-call(bf16[128,1024]{1,0:T(8,128)(2,1)} %get-tuple-element.113.bc_h.rest_6_.rest_27_, bf16[128,4096]{1,0:T(8,128)(2,1)} %bitcast.23, f32[512,128]{1,0:T(8,128)} %get-tuple-element.107.small_h.rest_9_, bf16[128,5120]{1,0:T(8,128)(2,1)} %bitcast.18, ...), custom_call_target="tpu_custom_call" | custom-call | flops 6000000000 | bytes 21600000 | tf_op jit(solution)/shard_map/slopes/pallas_call | solution.py:97
  54.5 5.8 %all-to-all-done.1.back_ref = bf16[16,256,128]{2,1,0:T(8,128)(2,1)S(1)} async-done(((bf16[16,256,128]{2,1,0:T(8,128)(2,1)}), bf16[16,256,128]{2,1,0:T(8,128)(2,1)S(1)}, u32[]{:S(2)}, u32[]{:S(2)}) %all-to-all-start.1) | async-done | bytes 1048608 | tf_op jit(solution)/shard_map/all_to_all | solution.py:975
  60.2 3.8 %unpack.1 = (bf16[2,16,128,128]{3,2,1,0:T(8,128)(2,1)S(1)}, bf16[2,16,128,128]{3,2,1,0:T(8,128)(2,1)S(1)}, bf16[128,1024]{1,0:T(8,128)(2,1)S(1)}, bf16[128,1024]...) custom-call(s32[1]{0:T(128)} %bitcast.core_ref, ...), custom_call_target="tpu_custom_call" | custom-call | flops 3000000000 | bytes 10800000 | tf_op jit(solution)/shard_map/unpack/pallas_call | solution.py:97
  64.0 0.3 collective-permute-start.3
  64.3 4.2 %leave.2 = (bf16[128,4096]{1,0:T(8,128)(2,1)}, f32[64,128]{1,0:T(8,128)}, f32[128,2560]{1,0:T(8,128)S(1)}, f32[128,128]{1,0:T(8,128)S(1)}, bf16[128,1024]{1,0:T(...) custom-call(s32[1]{0:T(128)} %bitcast.core_ref, ...), custom_call_target="tpu_custom_call" | custom-call | flops 5000000000 | bytes 18000000 | tf_op jit(solution)/shard_map/leave/pallas_call | solution.py:97
  68.5 0.6 collective-permute-start.4
  69.1 4.2 %leave.3 = (bf16[128,4096]{1,0:T(8,128)(2,1)}, f32[64,128]{1,0:T(8,128)}, f32[128,2560]{1,0:T(8,128)}, f32[128,128]{1,0:T(8,128)S(1)}, bf16[3,5120]{1,0:T(4,128)(2,1)S(1)}) custom-call(s32[1]{0:T(128)} %bitcast.core_ref, bf16[2,16,128,128]{3,2,1,0:T(8,128)(2,1)S(1)} %collective-permute-done.3.state_ref, ...), custom_call_target="tpu_custom_call", output_to_operand_aliasing={{0}: (24, {}), {1}: (25, {})} | custom-call | flops 5000000000 | bytes 18000000 | tf_op jit(solution)/shard_map/leave/pallas_call | solution.py:97
  73.3 0.1 collective-permute-start.5
  73.4 0.0 collective-permute-done.4.own_got_ref
  73.4 1.2 %collective-permute-done.5.theirs_got_ref = f32[128,128]{1,0:T(8,128)S(1)} collective-permute-done((f32[128,128]{1,0:T(8,128)S(1)}, f32[128,128]{1,0:T(8,128)S(1)}, u32[]{:S(2)}, u32[]{:S(2)}) %collective-permute-start.5) | collective-permute-done | bytes 65568 | tf_op jit(solution)/shard_map/ppermute | solution.py:1041
  74.7 0.6 merge.1.rest_0_
  75.2 0.6 collective-permute-start.6
  75.8 3.8 %collective-permute-start.9 = (bf16[3,5120]{1,0:T(4,128)(2,1)S(1)}, bf16[3,5120]{1,0:T(4,128)(2,1)S(1)}, u32[]{:S(2)}, u32[]{:S(2)}) collective-permute-start(bf16[3,5120]{1,0:T(4,128)(2,1)S(1)} %get-tuple-element.172), channel_id=1, source_target_pairs={{1,0},{2,1},{3,2},{4,3},{5,4},{6,5},{7,6},{8,7},{9,8},{10,9},{11,1... | collective-permute-start | bytes 92168 | tf_op jit(solution)/shard_map/ppermute | solution.py:1042
  79.5 1.2 %collective-permute-start.8 = (bf16[176,128]{1,0:T(8,128)(2,1)S(1)}, bf16[176,128]{1,0:T(8,128)(2,1)S(1)}, u32[]{:S(2)}, u32[]{:S(2)}) collective-permute-start(bf16[176,128]{1,0:T(8,128)(2,1)S(1)} %merge.1.rest_0_), channel_id=1, source_target_pairs={{0,4},{1,5},{2,6},{3,7},{4,0},{5,1},{6,2},{7,3},{8,12},{9,13},{10,... | collective-permute-start | bytes 135176 | tf_op jit(solution)/shard_map/ppermute | solution.py:987
  80.8 0.0 collective-permute-done.6.rest_1_
  80.8 0.0 collective-permute-start.7
  80.8 0.4 collective-permute-done.9.halo_ref
  81.2 2.8 %spread.1 = bf16[128,5120]{1,0:T(8,128)(2,1)} custom-call(s32[1]{0:T(128)} %bitcast.core_ref, f32[128,2560]{1,0:T(8,128)S(1)} %get-tuple-element.165.rest_21_.own_ref, f32[128,2560]{1,0:T(8,128)} %get-tuple-element.171.theirs_h, bf16[3,5120]{1,0:T(4,128)(2,1)S(1)} %collective-permute-done.9.halo_ref, f32[4,5120]{1,0:T(4,128)S(1)} %get-tuple-element.148.rest_20_.weight_ref), custom_call_target="tpu_custom_call" | custom-call | flops 3000000000 | bytes 10800000 | tf_op jit(solution)/shard_map/spread/pallas_call | solution.py:97
  84.0 1.2 %collective-permute-done.8.rest_3_ = bf16[176,128]{1,0:T(8,128)(2,1)S(1)} collective-permute-done((bf16[176,128]{1,0:T(8,128)(2,1)S(1)}, bf16[176,128]{1,0:T(8,128)(2,1)S(1)}, u32[]{:S(2)}, u32[]{:S(2)}) %collective-permute-start.8) | collective-permute-done | bytes 45088 | tf_op jit(solution)/shard_map/ppermute | solution.py:987
  85.2 1.1 collective-permute-start.10
  86.3 1.5 %collective-permute-start.12 = (bf16[176,128]{1,0:T(8,128)(2,1)S(1)}, bf16[176,128]{1,0:T(8,128)(2,1)S(1)}, u32[]{:S(2)}, u32[]{:S(2)}) collective-permute-start(bf16[176,128]{1,0:T(8,128)(2,1)S(1)} %fold.3.rest_0_), channel_id=1, source_target_pairs={{0,16},{1,17},{2,18},{3,19},{4,20},{5,21},{6,22},{7,23},{8,24},{9,... | collective-permute-start | bytes 135176 | tf_op jit(solution)/shard_map/ppermute | solution.py:987
  87.8 1.8 %collective-permute-done.10.rest_1_ = bf16[176,128]{1,0:T(8,128)(2,1)S(1)} collective-permute-done((bf16[176,128]{1,0:T(8,128)(2,1)S(1)}, bf16[176,128]{1,0:T(8,128)(2,1)S(1)}, u32[]{:S(2)}, u32[]{:S(2)}) %collective-permute-start.10) | collective-permute-done | bytes 45088 | tf_op jit(solution)/shard_map/ppermute | solution.py:987
  89.7 0.0 collective-permute-start.11
  89.7 2.2 %collective-permute-done.12.rest_3_ = bf16[176,128]{1,0:T(8,128)(2,1)S(1)} collective-permute-done((bf16[176,128]{1,0:T(8,128)(2,1)S(1)}, bf16[176,128]{1,0:T(8,128)(2,1)S(1)}, u32[]{:S(2)}, u32[]{:S(2)}) %collective-permute-start.12) | collective-permute-done | bytes 45088 | tf_op jit(solution)/shard_map/ppermute | solution.py:987
  91.8 0.0 collective-permute-done.11.rest_2_
  91.9 2.0 %collective-permute-start.13 = (bf16[176,128]{1,0:T(8,128)(2,1)S(1)}, bf16[176,128]{1,0:T(8,128)(2,1)S(1)}, u32[]{:S(2)}, u32[]{:S(2)}) collective-permute-start(bf16[176,128]{1,0:T(8,128)(2,1)S(1)} %fold.4.rest_0_), channel_id=1, source_target_pairs={{0,32},{1,33},{32,0},{33,1},{64,96},{65,97},{96,64},{97,65},{128,1... | collective-permute-start | bytes 135176 | tf_op jit(solution)/shard_map/ppermute | solution.py:987
  93.9 2.1 %collective-permute-done.13.rest_1_ = bf16[176,128]{1,0:T(8,128)(2,1)S(1)} collective-permute-done((bf16[176,128]{1,0:T(8,128)(2,1)S(1)}, bf16[176,128]{1,0:T(8,128)(2,1)S(1)}, u32[]{:S(2)}, u32[]{:S(2)}) %collective-permute-start.13) | collective-permute-done | bytes 45088 | tf_op jit(solution)/shard_map/ppermute | solution.py:987
  96.1 3.3 %collective-permute-start.14 = (bf16[176,128]{1,0:T(8,128)(2,1)S(1)}, bf16[176,128]{1,0:T(8,128)(2,1)S(1)}, u32[]{:S(2)}, u32[]{:S(2)}) collective-permute-start(bf16[176,128]{1,0:T(8,128)(2,1)S(1)} %fold.5.rest_0_), channel_id=1, source_target_pairs={{0,64},{1,193},{32,96},{33,225},{64,128},{65,1},{96,160},{97,33},{... | collective-permute-start | bytes 135176 | tf_op jit(solution)/shard_map/ppermute | solution.py:987
  99.4 5.4 %collective-permute-start.16 = (bf16[176,128]{1,0:T(8,128)(2,1)S(1)}, bf16[176,128]{1,0:T(8,128)(2,1)S(1)}, u32[]{:S(2)}, u32[]{:S(2)}) collective-permute-start(bf16[176,128]{1,0:T(8,128)(2,1)S(1)} %fold.5.rest_0_), channel_id=1, source_target_pairs={{0,128},{1,129},{32,160},{33,161},{64,192},{65,193},{96,224},{97,2... | collective-permute-start | bytes 135176 | tf_op jit(solution)/shard_map/ppermute | solution.py:987
  104.8 0.0 collective-permute-done.14.rest_1_
  104.8 0.0 collective-permute-start.15
  104.8 3.3 %collective-permute-done.16.rest_3_ = bf16[176,128]{1,0:T(8,128)(2,1)S(1)} collective-permute-done((bf16[176,128]{1,0:T(8,128)(2,1)S(1)}, bf16[176,128]{1,0:T(8,128)(2,1)S(1)}, u32[]{:S(2)}, u32[]{:S(2)}) %collective-permute-start.16) | collective-permute-done | bytes 45088 | tf_op jit(solution)/shard_map/ppermute | solution.py:987
  108.1 0.7 finish.1
  (7 shorter events, 0.1 us)
Async XLA Ops:
  1.5 7.4 %collective-permute-start = (bf16[3,5120]{1,0:T(4,128)(2,1)S(1)}, bf16[3,5120]{1,0:T(4,128)(2,1)S(1)}, u32[]{:S(2)}, u32[]{:S(2)}) collective-permute-start(bf16[3,5120]{1,0:T(4,128)(2,1)S(1)} %slice_bitcast_fusion), channel_id=1, source_target_pairs={{0,1},{1,2},{2,3},{3,4},{4,5},{5,6},{6,7},{7,8},{8,9},{9,10},{10,1... | collective-permute-start | bytes 92168 | tf_op jit(solution)/shard_map/ppermute | solution.py:1012
  11.4 2.8 %collective-permute-start.1 = (bf16[2,16,128,128]{3,2,1,0:T(8,128)(2,1)S(1)}, bf16[2,16,128,128]{3,2,1,0:T(8,128)(2,1)S(1)}, u32[]{:S(2)}, u32[]{:S(2)}) collective-permute-start(bf16[2,16,128,128]{3,2,1,0:T(8,128)(2,1)S(1)} %get-tuple-element.103), channel_id=1, source_target_pairs={{0,1},{1,0},{2,3},{3,2},{4,5},{5,4},{6,7},{7,6},{8,9},{9,8},{10,11... | collective-permute-start | bytes 3145736 | tf_op jit(solution)/shard_map/ppermute | solution.py:1020
  11.5 2.7 %collective-permute-start.2 = (f32[32,128]{1,0:T(8,128)S(1)}, f32[32,128]{1,0:T(8,128)S(1)}, u32[]{:S(2)}, u32[]{:S(2)}) collective-permute-start(f32[32,128]{1,0:T(8,128)S(1)} %get-tuple-element.104.tot_ref), channel_id=1, source_target_pairs={{0,1},{1,0},{2,3},{3,2},{4,5},{5,4},{6,7},{7,6},{8,9},{9,8},{10,11... | collective-permute-start | bytes 49160 | tf_op jit(solution)/shard_map/ppermute | solution.py:1016
  15.6 22.9 %all-to-all-start = ((bf16[16,272,128]{2,1,0:T(8,128)(2,1)}), bf16[16,272,128]{2,1,0:T(8,128)(2,1)S(1)}, u32[]{:S(2)}, u32[]{:S(2)}) async-start(bf16[16,272,128]{2,1,0:T(8,128)(2,1)} %get-tuple-element.105), calls=%async_computation | async-start | bytes 2228224 | tf_op jit(solution)/shard_map/all_to_all | solution.py:975
  39.7 20.5 %all-to-all-start.1 = ((bf16[16,256,128]{2,1,0:T(8,128)(2,1)}), bf16[16,256,128]{2,1,0:T(8,128)(2,1)S(1)}, u32[]{:S(2)}, u32[]{:S(2)}) async-start(bf16[16,256,128]{2,1,0:T(8,128)(2,1)} %chain.1), calls=%async_computation.1 | async-start | bytes 2097152 | tf_op jit(solution)/shard_map/all_to_all | solution.py:975
  64.0 5.1 %collective-permute-start.3 = (bf16[2,16,128,128]{3,2,1,0:T(8,128)(2,1)S(1)}, bf16[2,16,128,128]{3,2,1,0:T(8,128)(2,1)S(1)}, u32[]{:S(2)}, u32[]{:S(2)}) collective-permute-start(bf16[2,16,128,128]{3,2,1,0:T(8,128)(2,1)S(1)} %get-tuple-element.126), channel_id=1, source_target_pairs={{0,1},{1,0},{2,3},{3,2},{4,5},{5,4},{6,7},{7,6},{8,9},{9,8},{10,11... | collective-permute-start | bytes 3145736 | tf_op jit(solution)/shard_map/ppermute | solution.py:1035
  68.5 4.9 %collective-permute-start.4 = (f32[128,128]{1,0:T(8,128)S(1)}, f32[128,128]{1,0:T(8,128)S(1)}, u32[]{:S(2)}, u32[]{:S(2)}) collective-permute-start(f32[128,128]{1,0:T(8,128)S(1)} %get-tuple-element.169.own_ref), channel_id=1, source_target_pairs={{0,1},{1,0},{2,3},{3,2},{4,5},{5,4},{6,7},{7,6},{8,9},{9,8},{10,11... | collective-permute-start | bytes 196616 | tf_op jit(solution)/shard_map/ppermute | solution.py:1037
  73.3 1.3 %collective-permute-start.5 = (f32[128,128]{1,0:T(8,128)S(1)}, f32[128,128]{1,0:T(8,128)S(1)}, u32[]{:S(2)}, u32[]{:S(2)}) collective-permute-start(f32[128,128]{1,0:T(8,128)S(1)} %get-tuple-element.170.theirs_ref), channel_id=1, source_target_pairs={{0,1},{1,0},{2,3},{3,2},{4,5},{5,4},{6,7},{7,6},{8,9},{9,8},{10,11... | collective-permute-start | bytes 196616 | tf_op jit(solution)/shard_map/ppermute | solution.py:1041
  75.2 5.6 %collective-permute-start.6 = (bf16[176,128]{1,0:T(8,128)(2,1)S(1)}, bf16[176,128]{1,0:T(8,128)(2,1)S(1)}, u32[]{:S(2)}, u32[]{:S(2)}) collective-permute-start(bf16[176,128]{1,0:T(8,128)(2,1)S(1)} %merge.1.rest_0_), channel_id=1, source_target_pairs={{0,2},{1,7},{2,4},{3,1},{4,6},{5,3},{6,0},{7,5},{8,10},{9,15},{10,... | collective-permute-start | bytes 135176 | tf_op jit(solution)/shard_map/ppermute | solution.py:987
  75.8 5.4 %collective-permute-start.9 = (bf16[3,5120]{1,0:T(4,128)(2,1)S(1)}, bf16[3,5120]{1,0:T(4,128)(2,1)S(1)}, u32[]{:S(2)}, u32[]{:S(2)}) collective-permute-start(bf16[3,5120]{1,0:T(4,128)(2,1)S(1)} %get-tuple-element.172), channel_id=1, source_target_pairs={{1,0},{2,1},{3,2},{4,3},{5,4},{6,5},{7,6},{8,7},{9,8},{10,9},{11,1... | collective-permute-start | bytes 92168 | tf_op jit(solution)/shard_map/ppermute | solution.py:1042
  79.5 5.6 %collective-permute-start.8 = (bf16[176,128]{1,0:T(8,128)(2,1)S(1)}, bf16[176,128]{1,0:T(8,128)(2,1)S(1)}, u32[]{:S(2)}, u32[]{:S(2)}) collective-permute-start(bf16[176,128]{1,0:T(8,128)(2,1)S(1)} %merge.1.rest_0_), channel_id=1, source_target_pairs={{0,4},{1,5},{2,6},{3,7},{4,0},{5,1},{6,2},{7,3},{8,12},{9,13},{10,... | collective-permute-start | bytes 135176 | tf_op jit(solution)/shard_map/ppermute | solution.py:987
  80.8 4.4 %collective-permute-start.7 = (bf16[176,128]{1,0:T(8,128)(2,1)S(1)}, bf16[176,128]{1,0:T(8,128)(2,1)S(1)}, u32[]{:S(2)}, u32[]{:S(2)}) collective-permute-start(bf16[176,128]{1,0:T(8,128)(2,1)S(1)} %collective-permute-done.6.rest_1_), channel_id=1, source_target_pairs={{0,1},{1,0},{2,3},{3,2},{4,5},{5,4},{6,7},{7,6},{8,9},{9,8},{10,11... | collective-permute-start | bytes 135176 | tf_op jit(solution)/shard_map/ppermute | solution.py:995
  85.2 4.4 %collective-permute-start.10 = (bf16[176,128]{1,0:T(8,128)(2,1)S(1)}, bf16[176,128]{1,0:T(8,128)(2,1)S(1)}, u32[]{:S(2)}, u32[]{:S(2)}) collective-permute-start(bf16[176,128]{1,0:T(8,128)(2,1)S(1)} %fold.3.rest_0_), channel_id=1, source_target_pairs={{0,8},{1,25},{2,10},{3,27},{4,12},{5,29},{6,14},{7,31},{8,16},{9,1... | collective-permute-start | bytes 135176 | tf_op jit(solution)/shard_map/ppermute | solution.py:987
  86.3 5.6 %collective-permute-start.12 = (bf16[176,128]{1,0:T(8,128)(2,1)S(1)}, bf16[176,128]{1,0:T(8,128)(2,1)S(1)}, u32[]{:S(2)}, u32[]{:S(2)}) collective-permute-start(bf16[176,128]{1,0:T(8,128)(2,1)S(1)} %fold.3.rest_0_), channel_id=1, source_target_pairs={{0,16},{1,17},{2,18},{3,19},{4,20},{5,21},{6,22},{7,23},{8,24},{9,... | collective-permute-start | bytes 135176 | tf_op jit(solution)/shard_map/ppermute | solution.py:987
  89.7 2.2 %collective-permute-start.11 = (bf16[176,128]{1,0:T(8,128)(2,1)S(1)}, bf16[176,128]{1,0:T(8,128)(2,1)S(1)}, u32[]{:S(2)}, u32[]{:S(2)}) collective-permute-start(bf16[176,128]{1,0:T(8,128)(2,1)S(1)} %collective-permute-done.10.rest_1_), channel_id=1, source_target_pairs={{0,1},{1,0},{2,3},{3,2},{4,5},{5,4},{6,7},{7,6},{8,9},{9,8},{10,11... | collective-permute-start | bytes 135176 | tf_op jit(solution)/shard_map/ppermute | solution.py:995
  91.9 4.1 %collective-permute-start.13 = (bf16[176,128]{1,0:T(8,128)(2,1)S(1)}, bf16[176,128]{1,0:T(8,128)(2,1)S(1)}, u32[]{:S(2)}, u32[]{:S(2)}) collective-permute-start(bf16[176,128]{1,0:T(8,128)(2,1)S(1)} %fold.4.rest_0_), channel_id=1, source_target_pairs={{0,32},{1,33},{32,0},{33,1},{64,96},{65,97},{96,64},{97,65},{128,1... | collective-permute-start | bytes 135176 | tf_op jit(solution)/shard_map/ppermute | solution.py:987
  96.1 8.7 %collective-permute-start.14 = (bf16[176,128]{1,0:T(8,128)(2,1)S(1)}, bf16[176,128]{1,0:T(8,128)(2,1)S(1)}, u32[]{:S(2)}, u32[]{:S(2)}) collective-permute-start(bf16[176,128]{1,0:T(8,128)(2,1)S(1)} %fold.5.rest_0_), channel_id=1, source_target_pairs={{0,64},{1,193},{32,96},{33,225},{64,128},{65,1},{96,160},{97,33},{... | collective-permute-start | bytes 135176 | tf_op jit(solution)/shard_map/ppermute | solution.py:987
  99.4 8.7 %collective-permute-start.16 = (bf16[176,128]{1,0:T(8,128)(2,1)S(1)}, bf16[176,128]{1,0:T(8,128)(2,1)S(1)}, u32[]{:S(2)}, u32[]{:S(2)}) collective-permute-start(bf16[176,128]{1,0:T(8,128)(2,1)S(1)} %fold.5.rest_0_), channel_id=1, source_target_pairs={{0,128},{1,129},{32,160},{33,161},{64,192},{65,193},{96,224},{97,2... | collective-permute-start | bytes 135176 | tf_op jit(solution)/shard_map/ppermute | solution.py:987
  104.8 3.3 %collective-permute-start.15 = (bf16[176,128]{1,0:T(8,128)(2,1)S(1)}, bf16[176,128]{1,0:T(8,128)(2,1)S(1)}, u32[]{:S(2)}, u32[]{:S(2)}) collective-permute-start(bf16[176,128]{1,0:T(8,128)(2,1)S(1)} %collective-permute-done.14.rest_1_), channel_id=1, source_target_pairs={{0,1},{1,0},{2,3},{3,2},{4,5},{5,4},{6,7},{7,6},{8,9},{9,8},{10,11... | collective-permute-start | bytes 135176 | tf_op jit(solution)/shard_map/ppermute | solution.py:995

commit v14 on v13

--- a/solution.py
+++ b/solution.py
@@ -1049,7 +1049,7 @@
     sums = run_fold(core, scalar(lax.rem(chip, SIDE)), values)
     values = around(sums, "chip", chips, rows, lambda i, d: (i + d * SIDE) % chips)
     sums = run_fold(core, scalar(lax.div(chip, SIDE)), values)
-    near = 2 if sequences % 2 == 0 else 1
+    near = 1
     if near > 1:
         values = around(sums, "dp", sequences, near, lambda i, d: i // 2 * 2 + (i % 2 + d) % 2)
         sums = run_fold(core, scalar(lax.rem(sequence, near)), values)

time: 110 us -> 110 us (level)
    ppermute x3 -> x5, starting transfers between devices: 0.01 us -> 1.21 us  [around(): swapped = [lax.ppermute(part, 'core', [(0, 1), (1, 0)]) for part in heard]]
    ppermute x7 -> x8, starting transfers between devices: 15.1 us -> 14.2 us  [hear(): lax.ppermute(value, (axis, 'core'), [(2 * i + side, 2 * move(i, d) + side...]
    ppermute x7 -> x8, waiting for transfers between devices: 10.7 us -> 11.4 us  [hear(): lax.ppermute(value, (axis, 'core'), [(2 * i + side, 2 * move(i, d) + side...]
    pallas_call x16 -> x15, Pallas kernels: 40.7 us -> 40.7 us  [go(): run(*[pin(a, spaces[p]) if p in spaces else a for a, p in zip(args, specs...]
  transfers between devices with their start and end apart: 19 -> 22, of which waited for: 11 -> 11; matrix products, arithmetic and copies ran while one was open for 0% -> 0% of each run, Pallas kernels for 28% -> 28%
where the time goes in v14:
time: 110 us
  Pallas kernels  40.7 us (37%)
  starting transfers between devices  35.3 us (32%)
  waiting for transfers between devices  32.2 us (29%)
    pallas_call x15, Pallas kernels, go(): run(*[pin(a, spaces[p]) if p in spaces else a for a, p in zip(args, specs...  40.7 us
    all_to_all x2, waiting for transfers between devices, all_to_all(): return lax.all_to_all(value, axis, 0, 0, tiled=True)  16.6 us
    ppermute x8, starting transfers between devices, hear(): lax.ppermute(value, (axis, 'core'), [(2 * i + side, 2 * move(i, d) + side...  14.2 us
    all_to_all x2, starting transfers between devices, all_to_all(): return lax.all_to_all(value, axis, 0, 0, tiled=True)  12.6 us
    ppermute x8, waiting for transfers between devices, hear(): lax.ppermute(value, (axis, 'core'), [(2 * i + side, 2 * move(i, d) + side...  11.4 us
    ppermute x1, starting transfers between devices, local(): after = lax.ppermute(first, CTX, [(i + 1, i) for i in range(devices - 1)])  3.75 us
  transfers between devices with their start and end apart: 22, of which 11 were waited for; matrix products, arithmetic and copies ran while one was open for 0% of the time, Pallas kernels for 28%

profile of v14, /device:TPU:2, one launch (start us, length us, event | category | flops | bytes accessed | tf_op | source)
XLA Modules:
  0.0 109.9 jit_solution(15839996567466855762)
XLA Ops:
  0.6 0.9 slice_bitcast_fusion
  1.5 1.9 %collective-permute-start = (bf16[3,5120]{1,0:T(4,128)(2,1)S(1)}, bf16[3,5120]{1,0:T(4,128)(2,1)S(1)}, u32[]{:S(2)}, u32[]{:S(2)}) collective-permute-start(bf16[3,5120]{1,0:T(4,128)(2,1)S(1)} %slice_bitcast_fusion), channel_id=1, source_target_pairs={{0,1},{1,2},{2,3},{3,4},{4,5},{5,6},{6,7},{7,8},{8,9},{9,10},{10,1... | collective-permute-start | bytes 92168 | tf_op jit(solution)/shard_map/ppermute | solution.py:1012
  3.5 3.4 %begin.1 = (f32[512,128]{1,0:T(8,128)}, f32[512,128]{1,0:T(8,128)S(1)}, f32[32,128]{1,0:T(8,128)S(1)}, bf16[128,4096]{1,0:T(8,128)(2,1)S(1)}, bf16[128,1024]{1,0...) custom-call(f32[64,128]{1,0:T(8,128)} %bitcast.25, ...), custom_call_target="tpu_custom_call" | custom-call | flops 4000000000 | bytes 14400000 | tf_op jit(solution)/shard_map/begin/pallas_call | solution.py:97
  6.9 2.1 %collective-permute-done.halo_ref = bf16[3,5120]{1,0:T(4,128)(2,1)S(1)} collective-permute-done((bf16[3,5120]{1,0:T(4,128)(2,1)S(1)}, bf16[3,5120]{1,0:T(4,128)(2,1)S(1)}, u32[]{:S(2)}, u32[]{:S(2)}) %collective-permute-start) | collective-permute-done | bytes 30752 | tf_op jit(solution)/shard_map/ppermute | solution.py:1012
  9.0 2.4 %enter.1 = (bf16[128,4096]{1,0:T(8,128)(2,1)}, bf16[128,1024]{1,0:T(8,128)(2,1)}, f32[8,5120]{1,0:T(8,128)}, bf16[128,4096]{1,0:T(8,128)(2,1)S(1)}, bf16[128,102...) custom-call(s32[1]{0:T(128)} %bitcast.core_ref, bf16[128,4096]{1,0:T(8,128)(2,1)S(1)} %get-tuple-element.94.x0_ref, ...), custom_call_target="tpu_custom_call" | custom-call | flops 3000000000 | bytes 10800000 | tf_op jit(solution)/shard_map/enter/pallas_call | solution.py:97
  11.4 0.1 collective-permute-start.1
  11.5 0.5 collective-permute-start.2
  12.0 1.6 %own.1.own_ref = bf16[2,16,128,128]{3,2,1,0:T(8,128)(2,1)S(1)} custom-call(s32[1]{0:T(128)} %bitcast.core_ref, bf16[128,4096]{1,0:T(8,128)(2,1)S(1)} %get-tuple-element.101.x_ref, bf16[128,1024]{1,0:T(8,128)(2,1)S(1)} %get-tuple-element.102.bc_ref, bf16[128,4096]{1,0:T(8,128)(2,1)S(1)} %get-tuple-element.98.g_ref, f32[512,128]{1,0:T(8,128)S(1)} %get-tuple-element.99.small_ref), custom_call_target="tpu_custom_call" | custom-call | flops 3000000000 | bytes 10800000 | tf_op jit(solution)/shard_map/own/pallas_call | solution.py:97
  13.6 0.5 collective-permute-done.2.other_ref
  14.1 0.0 collective-permute-done.1.got_ref
  14.1 1.4 %pack.1 = (bf16[16,272,128]{2,1,0:T(8,128)(2,1)}, bf16[16,128,128]{2,1,0:T(8,128)(2,1)}, bf16[16,128,128]{2,1,0:T(8,128)(2,1)}, f32[64,128]{1,0:T(8,128)}) custom-call(s32[1]{0:T(128)} %bitcast.core_ref, bf16[2,16,128,128]{3,2,1,0:T(8,128)(2,1)S(1)} %own.1.own_ref, bf16[2,16,128,128]{3,2,1,0:T(8,128)(2,1)S(1)} %collective-permute-done.1.got_ref, ...), custom_call_target="tpu_custom_call" | custom-call | flops 2000000000 | bytes 7200000 | tf_op jit(solution)/shard_map/pack/pallas_call | solution.py:97
  15.6 6.4 %all-to-all-start = ((bf16[16,272,128]{2,1,0:T(8,128)(2,1)}), bf16[16,272,128]{2,1,0:T(8,128)(2,1)S(1)}, u32[]{:S(2)}, u32[]{:S(2)}) async-start(bf16[16,272,128]{2,1,0:T(8,128)(2,1)} %get-tuple-element.105), calls=%async_computation | async-start | bytes 2228224 | tf_op jit(solution)/shard_map/all_to_all | solution.py:975
  22.0 5.6 %inner.1 = (f32[128,4096]{1,0:T(8,128)}, f32[128,1024]{1,0:T(8,128)}, f32[32,128]{1,0:T(8,128)}) custom-call(bf16[128,4096]{1,0:T(8,128)(2,1)} %get-tuple-element.106.x_h.rest_0_.rest_21_, bf16[128,1024]{1,0:T(8,128)(2,1)} %get-tuple-element.113.bc_h.rest_6_.rest_27_, bf16[128,4096]{1,0:T(8,128)(2,1)} %bitcast.21, f32[512,128]{1,0:T(8,128)} %get-tuple-element.107.small_h.rest_9_), custom_call_target="tpu_custom_call" | custom-call | flops 4000000000 | bytes 14400000 | tf_op jit(solution)/shard_map/inner/pallas_call | solution.py:97
  27.6 10.8 %all-to-all-done.in_ref = bf16[16,272,128]{2,1,0:T(8,128)(2,1)S(1)} async-done(((bf16[16,272,128]{2,1,0:T(8,128)(2,1)}), bf16[16,272,128]{2,1,0:T(8,128)(2,1)S(1)}, u32[]{:S(2)}, u32[]{:S(2)}) %all-to-all-start) | async-done | bytes 1114144 | tf_op jit(solution)/shard_map/all_to_all | solution.py:975
  38.5 1.3 %chain.1 = bf16[16,256,128]{2,1,0:T(8,128)(2,1)} custom-call(bf16[16,272,128]{2,1,0:T(8,128)(2,1)S(1)} %all-to-all-done.in_ref), custom_call_target="tpu_custom_call" | custom-call | flops 1000000000 | bytes 3600000 | tf_op jit(solution)/shard_map/chain/pallas_call | solution.py:97
  39.7 6.2 %all-to-all-start.1 = ((bf16[16,256,128]{2,1,0:T(8,128)(2,1)}), bf16[16,256,128]{2,1,0:T(8,128)(2,1)S(1)}, u32[]{:S(2)}, u32[]{:S(2)}) async-start(bf16[16,256,128]{2,1,0:T(8,128)(2,1)} %chain.1), calls=%async_computation.1 | async-start | bytes 2097152 | tf_op jit(solution)/shard_map/all_to_all | solution.py:975
  45.9 8.6 %slopes.1 = (f32[128,4096]{1,0:T(8,128)}, f32[128,5120]{1,0:T(8,128)}) custom-call(bf16[128,1024]{1,0:T(8,128)(2,1)} %get-tuple-element.113.bc_h.rest_6_.rest_27_, bf16[128,4096]{1,0:T(8,128)(2,1)} %bitcast.22, f32[512,128]{1,0:T(8,128)} %get-tuple-element.107.small_h.rest_9_, bf16[128,5120]{1,0:T(8,128)(2,1)} %bitcast.17, ...), custom_call_target="tpu_custom_call" | custom-call | flops 6000000000 | bytes 21600000 | tf_op jit(solution)/shard_map/slopes/pallas_call | solution.py:97
  54.5 5.7 %all-to-all-done.1.back_ref = bf16[16,256,128]{2,1,0:T(8,128)(2,1)S(1)} async-done(((bf16[16,256,128]{2,1,0:T(8,128)(2,1)}), bf16[16,256,128]{2,1,0:T(8,128)(2,1)S(1)}, u32[]{:S(2)}, u32[]{:S(2)}) %all-to-all-start.1) | async-done | bytes 1048608 | tf_op jit(solution)/shard_map/all_to_all | solution.py:975
  60.2 3.8 %unpack.1 = (bf16[2,16,128,128]{3,2,1,0:T(8,128)(2,1)S(1)}, bf16[2,16,128,128]{3,2,1,0:T(8,128)(2,1)S(1)}, bf16[128,1024]{1,0:T(8,128)(2,1)S(1)}, bf16[128,1024]...) custom-call(s32[1]{0:T(128)} %bitcast.core_ref, ...), custom_call_target="tpu_custom_call" | custom-call | flops 3000000000 | bytes 10800000 | tf_op jit(solution)/shard_map/unpack/pallas_call | solution.py:97
  64.0 0.3 collective-permute-start.3
  64.3 4.2 %leave.2 = (bf16[128,4096]{1,0:T(8,128)(2,1)}, f32[64,128]{1,0:T(8,128)}, f32[128,2560]{1,0:T(8,128)S(1)}, f32[128,128]{1,0:T(8,128)S(1)}, bf16[128,1024]{1,0:T(...) custom-call(s32[1]{0:T(128)} %bitcast.core_ref, ...), custom_call_target="tpu_custom_call" | custom-call | flops 5000000000 | bytes 18000000 | tf_op jit(solution)/shard_map/leave/pallas_call | solution.py:97
  68.5 0.6 collective-permute-start.4
  69.1 0.0 collective-permute-done.3.state_ref
  69.1 4.2 %leave.3 = (bf16[128,4096]{1,0:T(8,128)(2,1)}, f32[64,128]{1,0:T(8,128)}, f32[128,2560]{1,0:T(8,128)}, f32[128,128]{1,0:T(8,128)S(1)}, bf16[3,5120]{1,0:T(4,128)(2,1)S(1)}) custom-call(s32[1]{0:T(128)} %bitcast.core_ref, bf16[2,16,128,128]{3,2,1,0:T(8,128)(2,1)S(1)} %collective-permute-done.3.state_ref, ...), custom_call_target="tpu_custom_call", output_to_operand_aliasing={{0}: (24, {}), {1}: (25, {})} | custom-call | flops 5000000000 | bytes 18000000 | tf_op jit(solution)/shard_map/leave/pallas_call | solution.py:97
  73.3 0.1 collective-permute-start.5
  73.4 1.2 %collective-permute-done.5.theirs_got_ref = f32[128,128]{1,0:T(8,128)S(1)} collective-permute-done((f32[128,128]{1,0:T(8,128)S(1)}, f32[128,128]{1,0:T(8,128)S(1)}, u32[]{:S(2)}, u32[]{:S(2)}) %collective-permute-start.5) | collective-permute-done | bytes 65568 | tf_op jit(solution)/shard_map/ppermute | solution.py:1041
  74.7 0.6 merge.1.rest_0_
  75.2 0.6 collective-permute-start.6
  75.8 3.8 %collective-permute-start.9 = (bf16[3,5120]{1,0:T(4,128)(2,1)S(1)}, bf16[3,5120]{1,0:T(4,128)(2,1)S(1)}, u32[]{:S(2)}, u32[]{:S(2)}) collective-permute-start(bf16[3,5120]{1,0:T(4,128)(2,1)S(1)} %get-tuple-element.172), channel_id=1, source_target_pairs={{1,0},{2,1},{3,2},{4,3},{5,4},{6,5},{7,6},{8,7},{9,8},{10,9},{11,1... | collective-permute-start | bytes 92168 | tf_op jit(solution)/shard_map/ppermute | solution.py:1042
  79.5 1.2 %collective-permute-start.8 = (bf16[176,128]{1,0:T(8,128)(2,1)S(1)}, bf16[176,128]{1,0:T(8,128)(2,1)S(1)}, u32[]{:S(2)}, u32[]{:S(2)}) collective-permute-start(bf16[176,128]{1,0:T(8,128)(2,1)S(1)} %merge.1.rest_0_), channel_id=1, source_target_pairs={{0,4},{1,5},{2,6},{3,7},{4,0},{5,1},{6,2},{7,3},{8,12},{9,13},{10,... | collective-permute-start | bytes 135176 | tf_op jit(solution)/shard_map/ppermute | solution.py:987
  80.8 0.0 collective-permute-done.6.rest_1_
  80.8 0.4 collective-permute-done.9.halo_ref
  81.2 2.8 %spread.1 = bf16[128,5120]{1,0:T(8,128)(2,1)} custom-call(s32[1]{0:T(128)} %bitcast.core_ref, f32[128,2560]{1,0:T(8,128)S(1)} %get-tuple-element.165.rest_21_.own_ref, f32[128,2560]{1,0:T(8,128)} %get-tuple-element.171.theirs_h, bf16[3,5120]{1,0:T(4,128)(2,1)S(1)} %collective-permute-done.9.halo_ref, f32[4,5120]{1,0:T(4,128)S(1)} %get-tuple-element.148.rest_20_.weight_ref), custom_call_target="tpu_custom_call" | custom-call | flops 3000000000 | bytes 10800000 | tf_op jit(solution)/shard_map/spread/pallas_call | solution.py:97
  84.0 1.2 %collective-permute-done.8.rest_3_ = bf16[176,128]{1,0:T(8,128)(2,1)S(1)} collective-permute-done((bf16[176,128]{1,0:T(8,128)(2,1)S(1)}, bf16[176,128]{1,0:T(8,128)(2,1)S(1)}, u32[]{:S(2)}, u32[]{:S(2)}) %collective-permute-start.8) | collective-permute-done | bytes 45088 | tf_op jit(solution)/shard_map/ppermute | solution.py:987
  85.2 1.1 collective-permute-start.10
  86.3 1.5 %collective-permute-start.12 = (bf16[176,128]{1,0:T(8,128)(2,1)S(1)}, bf16[176,128]{1,0:T(8,128)(2,1)S(1)}, u32[]{:S(2)}, u32[]{:S(2)}) collective-permute-start(bf16[176,128]{1,0:T(8,128)(2,1)S(1)} %fold.2.rest_0_), channel_id=1, source_target_pairs={{0,16},{1,17},{2,18},{3,19},{4,20},{5,21},{6,22},{7,23},{8,24},{9,... | collective-permute-start | bytes 135176 | tf_op jit(solution)/shard_map/ppermute | solution.py:987
  87.8 1.8 %collective-permute-done.10.rest_1_ = bf16[176,128]{1,0:T(8,128)(2,1)S(1)} collective-permute-done((bf16[176,128]{1,0:T(8,128)(2,1)S(1)}, bf16[176,128]{1,0:T(8,128)(2,1)S(1)}, u32[]{:S(2)}, u32[]{:S(2)}) %collective-permute-start.10) | collective-permute-done | bytes 45088 | tf_op jit(solution)/shard_map/ppermute | solution.py:987
  89.7 0.0 collective-permute-start.11
  89.7 2.2 %collective-permute-done.12.rest_3_ = bf16[176,128]{1,0:T(8,128)(2,1)S(1)} collective-permute-done((bf16[176,128]{1,0:T(8,128)(2,1)S(1)}, bf16[176,128]{1,0:T(8,128)(2,1)S(1)}, u32[]{:S(2)}, u32[]{:S(2)}) %collective-permute-start.12) | collective-permute-done | bytes 45088 | tf_op jit(solution)/shard_map/ppermute | solution.py:987
  91.9 2.0 %collective-permute-start.13 = (bf16[176,128]{1,0:T(8,128)(2,1)S(1)}, bf16[176,128]{1,0:T(8,128)(2,1)S(1)}, u32[]{:S(2)}, u32[]{:S(2)}) collective-permute-start(bf16[176,128]{1,0:T(8,128)(2,1)S(1)} %fold.3.rest_0_), channel_id=1, source_target_pairs={{0,32},{1,225},{32,64},{33,1},{64,96},{65,33},{96,128},{97,65},{12... | collective-permute-start | bytes 135176 | tf_op jit(solution)/shard_map/ppermute | solution.py:987
  93.9 3.3 %collective-permute-start.14 = (bf16[176,128]{1,0:T(8,128)(2,1)S(1)}, bf16[176,128]{1,0:T(8,128)(2,1)S(1)}, u32[]{:S(2)}, u32[]{:S(2)}) collective-permute-start(bf16[176,128]{1,0:T(8,128)(2,1)S(1)} %fold.3.rest_0_), channel_id=1, source_target_pairs={{0,64},{1,193},{32,96},{33,225},{64,128},{65,1},{96,160},{97,33},{... | collective-permute-start | bytes 135176 | tf_op jit(solution)/shard_map/ppermute | solution.py:987
  97.2 4.0 %collective-permute-start.15 = (bf16[176,128]{1,0:T(8,128)(2,1)S(1)}, bf16[176,128]{1,0:T(8,128)(2,1)S(1)}, u32[]{:S(2)}, u32[]{:S(2)}) collective-permute-start(bf16[176,128]{1,0:T(8,128)(2,1)S(1)} %fold.3.rest_0_), channel_id=1, source_target_pairs={{0,96},{1,161},{32,128},{33,193},{64,160},{65,225},{96,192},{97,1}... | collective-permute-start | bytes 135176 | tf_op jit(solution)/shard_map/ppermute | solution.py:987
  101.2 0.5 collective-permute-start.19
  101.7 1.1 %collective-permute-start.16 = (bf16[176,128]{1,0:T(8,128)(2,1)S(1)}, bf16[176,128]{1,0:T(8,128)(2,1)S(1)}, u32[]{:S(2)}, u32[]{:S(2)}) collective-permute-start(bf16[176,128]{1,0:T(8,128)(2,1)S(1)} %collective-permute-done.13.rest_1_), channel_id=1, source_target_pairs={{0,1},{1,0},{2,3},{3,2},{4,5},{5,4},{6,7},{7,6},{8,9},{9,8},{10,11... | collective-permute-start | bytes 135176 | tf_op jit(solution)/shard_map/ppermute | solution.py:995
  102.9 0.1 collective-permute-start.17
  102.9 1.7 %collective-permute-done.15.rest_3_ = bf16[176,128]{1,0:T(8,128)(2,1)S(1)} collective-permute-done((bf16[176,128]{1,0:T(8,128)(2,1)S(1)}, bf16[176,128]{1,0:T(8,128)(2,1)S(1)}, u32[]{:S(2)}, u32[]{:S(2)}) %collective-permute-start.15) | collective-permute-done | bytes 45088 | tf_op jit(solution)/shard_map/ppermute | solution.py:987
  104.6 4.5 %collective-permute-done.19.rest_7_ = bf16[176,128]{1,0:T(8,128)(2,1)S(1)} collective-permute-done((bf16[176,128]{1,0:T(8,128)(2,1)S(1)}, bf16[176,128]{1,0:T(8,128)(2,1)S(1)}, u32[]{:S(2)}, u32[]{:S(2)}) %collective-permute-start.19) | collective-permute-done | bytes 45088 | tf_op jit(solution)/shard_map/ppermute | solution.py:987
  109.2 0.7 finish.1
  (12 shorter events, 0.1 us)
Async XLA Ops:
  1.5 7.4 %collective-permute-start = (bf16[3,5120]{1,0:T(4,128)(2,1)S(1)}, bf16[3,5120]{1,0:T(4,128)(2,1)S(1)}, u32[]{:S(2)}, u32[]{:S(2)}) collective-permute-start(bf16[3,5120]{1,0:T(4,128)(2,1)S(1)} %slice_bitcast_fusion), channel_id=1, source_target_pairs={{0,1},{1,2},{2,3},{3,4},{4,5},{5,6},{6,7},{7,8},{8,9},{9,10},{10,1... | collective-permute-start | bytes 92168 | tf_op jit(solution)/shard_map/ppermute | solution.py:1012
  11.4 2.8 %collective-permute-start.1 = (bf16[2,16,128,128]{3,2,1,0:T(8,128)(2,1)S(1)}, bf16[2,16,128,128]{3,2,1,0:T(8,128)(2,1)S(1)}, u32[]{:S(2)}, u32[]{:S(2)}) collective-permute-start(bf16[2,16,128,128]{3,2,1,0:T(8,128)(2,1)S(1)} %get-tuple-element.103), channel_id=1, source_target_pairs={{0,1},{1,0},{2,3},{3,2},{4,5},{5,4},{6,7},{7,6},{8,9},{9,8},{10,11... | collective-permute-start | bytes 3145736 | tf_op jit(solution)/shard_map/ppermute | solution.py:1020
  11.5 2.7 %collective-permute-start.2 = (f32[32,128]{1,0:T(8,128)S(1)}, f32[32,128]{1,0:T(8,128)S(1)}, u32[]{:S(2)}, u32[]{:S(2)}) collective-permute-start(f32[32,128]{1,0:T(8,128)S(1)} %get-tuple-element.104.tot_ref), channel_id=1, source_target_pairs={{0,1},{1,0},{2,3},{3,2},{4,5},{5,4},{6,7},{7,6},{8,9},{9,8},{10,11... | collective-permute-start | bytes 49160 | tf_op jit(solution)/shard_map/ppermute | solution.py:1016
  15.6 22.9 %all-to-all-start = ((bf16[16,272,128]{2,1,0:T(8,128)(2,1)}), bf16[16,272,128]{2,1,0:T(8,128)(2,1)S(1)}, u32[]{:S(2)}, u32[]{:S(2)}) async-start(bf16[16,272,128]{2,1,0:T(8,128)(2,1)} %get-tuple-element.105), calls=%async_computation | async-start | bytes 2228224 | tf_op jit(solution)/shard_map/all_to_all | solution.py:975
  39.7 20.5 %all-to-all-start.1 = ((bf16[16,256,128]{2,1,0:T(8,128)(2,1)}), bf16[16,256,128]{2,1,0:T(8,128)(2,1)S(1)}, u32[]{:S(2)}, u32[]{:S(2)}) async-start(bf16[16,256,128]{2,1,0:T(8,128)(2,1)} %chain.1), calls=%async_computation.1 | async-start | bytes 2097152 | tf_op jit(solution)/shard_map/all_to_all | solution.py:975
  64.0 5.1 %collective-permute-start.3 = (bf16[2,16,128,128]{3,2,1,0:T(8,128)(2,1)S(1)}, bf16[2,16,128,128]{3,2,1,0:T(8,128)(2,1)S(1)}, u32[]{:S(2)}, u32[]{:S(2)}) collective-permute-start(bf16[2,16,128,128]{3,2,1,0:T(8,128)(2,1)S(1)} %get-tuple-element.126), channel_id=1, source_target_pairs={{0,1},{1,0},{2,3},{3,2},{4,5},{5,4},{6,7},{7,6},{8,9},{9,8},{10,11... | collective-permute-start | bytes 3145736 | tf_op jit(solution)/shard_map/ppermute | solution.py:1035
  68.5 4.9 %collective-permute-start.4 = (f32[128,128]{1,0:T(8,128)S(1)}, f32[128,128]{1,0:T(8,128)S(1)}, u32[]{:S(2)}, u32[]{:S(2)}) collective-permute-start(f32[128,128]{1,0:T(8,128)S(1)} %get-tuple-element.169.own_ref), channel_id=1, source_target_pairs={{0,1},{1,0},{2,3},{3,2},{4,5},{5,4},{6,7},{7,6},{8,9},{9,8},{10,11... | collective-permute-start | bytes 196616 | tf_op jit(solution)/shard_map/ppermute | solution.py:1037
  73.3 1.3 %collective-permute-start.5 = (f32[128,128]{1,0:T(8,128)S(1)}, f32[128,128]{1,0:T(8,128)S(1)}, u32[]{:S(2)}, u32[]{:S(2)}) collective-permute-start(f32[128,128]{1,0:T(8,128)S(1)} %get-tuple-element.170.theirs_ref), channel_id=1, source_target_pairs={{0,1},{1,0},{2,3},{3,2},{4,5},{5,4},{6,7},{7,6},{8,9},{9,8},{10,11... | collective-permute-start | bytes 196616 | tf_op jit(solution)/shard_map/ppermute | solution.py:1041
  75.2 5.6 %collective-permute-start.6 = (bf16[176,128]{1,0:T(8,128)(2,1)S(1)}, bf16[176,128]{1,0:T(8,128)(2,1)S(1)}, u32[]{:S(2)}, u32[]{:S(2)}) collective-permute-start(bf16[176,128]{1,0:T(8,128)(2,1)S(1)} %merge.1.rest_0_), channel_id=1, source_target_pairs={{0,2},{1,7},{2,4},{3,1},{4,6},{5,3},{6,0},{7,5},{8,10},{9,15},{10,... | collective-permute-start | bytes 135176 | tf_op jit(solution)/shard_map/ppermute | solution.py:987
  75.8 5.4 %collective-permute-start.9 = (bf16[3,5120]{1,0:T(4,128)(2,1)S(1)}, bf16[3,5120]{1,0:T(4,128)(2,1)S(1)}, u32[]{:S(2)}, u32[]{:S(2)}) collective-permute-start(bf16[3,5120]{1,0:T(4,128)(2,1)S(1)} %get-tuple-element.172), channel_id=1, source_target_pairs={{1,0},{2,1},{3,2},{4,3},{5,4},{6,5},{7,6},{8,7},{9,8},{10,9},{11,1... | collective-permute-start | bytes 92168 | tf_op jit(solution)/shard_map/ppermute | solution.py:1042
  79.5 5.6 %collective-permute-start.8 = (bf16[176,128]{1,0:T(8,128)(2,1)S(1)}, bf16[176,128]{1,0:T(8,128)(2,1)S(1)}, u32[]{:S(2)}, u32[]{:S(2)}) collective-permute-start(bf16[176,128]{1,0:T(8,128)(2,1)S(1)} %merge.1.rest_0_), channel_id=1, source_target_pairs={{0,4},{1,5},{2,6},{3,7},{4,0},{5,1},{6,2},{7,3},{8,12},{9,13},{10,... | collective-permute-start | bytes 135176 | tf_op jit(solution)/shard_map/ppermute | solution.py:987
  80.8 4.4 %collective-permute-start.7 = (bf16[176,128]{1,0:T(8,128)(2,1)S(1)}, bf16[176,128]{1,0:T(8,128)(2,1)S(1)}, u32[]{:S(2)}, u32[]{:S(2)}) collective-permute-start(bf16[176,128]{1,0:T(8,128)(2,1)S(1)} %collective-permute-done.6.rest_1_), channel_id=1, source_target_pairs={{0,1},{1,0},{2,3},{3,2},{4,5},{5,4},{6,7},{7,6},{8,9},{9,8},{10,11... | collective-permute-start | bytes 135176 | tf_op jit(solution)/shard_map/ppermute | solution.py:995
  85.2 4.4 %collective-permute-start.10 = (bf16[176,128]{1,0:T(8,128)(2,1)S(1)}, bf16[176,128]{1,0:T(8,128)(2,1)S(1)}, u32[]{:S(2)}, u32[]{:S(2)}) collective-permute-start(bf16[176,128]{1,0:T(8,128)(2,1)S(1)} %fold.2.rest_0_), channel_id=1, source_target_pairs={{0,8},{1,25},{2,10},{3,27},{4,12},{5,29},{6,14},{7,31},{8,16},{9,1... | collective-permute-start | bytes 135176 | tf_op jit(solution)/shard_map/ppermute | solution.py:987
  86.3 5.6 %collective-permute-start.12 = (bf16[176,128]{1,0:T(8,128)(2,1)S(1)}, bf16[176,128]{1,0:T(8,128)(2,1)S(1)}, u32[]{:S(2)}, u32[]{:S(2)}) collective-permute-start(bf16[176,128]{1,0:T(8,128)(2,1)S(1)} %fold.2.rest_0_), channel_id=1, source_target_pairs={{0,16},{1,17},{2,18},{3,19},{4,20},{5,21},{6,22},{7,23},{8,24},{9,... | collective-permute-start | bytes 135176 | tf_op jit(solution)/shard_map/ppermute | solution.py:987
  89.7 2.2 %collective-permute-start.11 = (bf16[176,128]{1,0:T(8,128)(2,1)S(1)}, bf16[176,128]{1,0:T(8,128)(2,1)S(1)}, u32[]{:S(2)}, u32[]{:S(2)}) collective-permute-start(bf16[176,128]{1,0:T(8,128)(2,1)S(1)} %collective-permute-done.10.rest_1_), channel_id=1, source_target_pairs={{0,1},{1,0},{2,3},{3,2},{4,5},{5,4},{6,7},{7,6},{8,9},{9,8},{10,11... | collective-permute-start | bytes 135176 | tf_op jit(solution)/shard_map/ppermute | solution.py:995
  91.9 9.9 %collective-permute-start.13 = (bf16[176,128]{1,0:T(8,128)(2,1)S(1)}, bf16[176,128]{1,0:T(8,128)(2,1)S(1)}, u32[]{:S(2)}, u32[]{:S(2)}) collective-permute-start(bf16[176,128]{1,0:T(8,128)(2,1)S(1)} %fold.3.rest_0_), channel_id=1, source_target_pairs={{0,32},{1,225},{32,64},{33,1},{64,96},{65,33},{96,128},{97,65},{12... | collective-permute-start | bytes 135176 | tf_op jit(solution)/shard_map/ppermute | solution.py:987
  93.9 9.0 %collective-permute-start.14 = (bf16[176,128]{1,0:T(8,128)(2,1)S(1)}, bf16[176,128]{1,0:T(8,128)(2,1)S(1)}, u32[]{:S(2)}, u32[]{:S(2)}) collective-permute-start(bf16[176,128]{1,0:T(8,128)(2,1)S(1)} %fold.3.rest_0_), channel_id=1, source_target_pairs={{0,64},{1,193},{32,96},{33,225},{64,128},{65,1},{96,160},{97,33},{... | collective-permute-start | bytes 135176 | tf_op jit(solution)/shard_map/ppermute | solution.py:987
  97.2 7.5 %collective-permute-start.15 = (bf16[176,128]{1,0:T(8,128)(2,1)S(1)}, bf16[176,128]{1,0:T(8,128)(2,1)S(1)}, u32[]{:S(2)}, u32[]{:S(2)}) collective-permute-start(bf16[176,128]{1,0:T(8,128)(2,1)S(1)} %fold.3.rest_0_), channel_id=1, source_target_pairs={{0,96},{1,161},{32,128},{33,193},{64,160},{65,225},{96,192},{97,1}... | collective-permute-start | bytes 135176 | tf_op jit(solution)/shard_map/ppermute | solution.py:987
  101.2 8.0 %collective-permute-start.19 = (bf16[176,128]{1,0:T(8,128)(2,1)S(1)}, bf16[176,128]{1,0:T(8,128)(2,1)S(1)}, u32[]{:S(2)}, u32[]{:S(2)}) collective-permute-start(bf16[176,128]{1,0:T(8,128)(2,1)S(1)} %fold.3.rest_0_), channel_id=1, source_target_pairs={{0,128},{1,129},{32,160},{33,161},{64,192},{65,193},{96,224},{97,2... | collective-permute-start | bytes 135176 | tf_op jit(solution)/shard_map/ppermute | solution.py:987
  101.7 7.4 %collective-permute-start.16 = (bf16[176,128]{1,0:T(8,128)(2,1)S(1)}, bf16[176,128]{1,0:T(8,128)(2,1)S(1)}, u32[]{:S(2)}, u32[]{:S(2)}) collective-permute-start(bf16[176,128]{1,0:T(8,128)(2,1)S(1)} %collective-permute-done.13.rest_1_), channel_id=1, source_target_pairs={{0,1},{1,0},{2,3},{3,2},{4,5},{5,4},{6,7},{7,6},{8,9},{9,8},{10,11... | collective-permute-start | bytes 135176 | tf_op jit(solution)/shard_map/ppermute | solution.py:995
  102.9 6.3 %collective-permute-start.17 = (bf16[176,128]{1,0:T(8,128)(2,1)S(1)}, bf16[176,128]{1,0:T(8,128)(2,1)S(1)}, u32[]{:S(2)}, u32[]{:S(2)}) collective-permute-start(bf16[176,128]{1,0:T(8,128)(2,1)S(1)} %collective-permute-done.14.rest_2_), channel_id=1, source_target_pairs={{0,1},{1,0},{2,3},{3,2},{4,5},{5,4},{6,7},{7,6},{8,9},{9,8},{10,11... | collective-permute-start | bytes 135176 | tf_op jit(solution)/shard_map/ppermute | solution.py:995
  104.6 4.5 %collective-permute-start.18 = (bf16[176,128]{1,0:T(8,128)(2,1)S(1)}, bf16[176,128]{1,0:T(8,128)(2,1)S(1)}, u32[]{:S(2)}, u32[]{:S(2)}) collective-permute-start(bf16[176,128]{1,0:T(8,128)(2,1)S(1)} %collective-permute-done.15.rest_3_), channel_id=1, source_target_pairs={{0,1},{1,0},{2,3},{3,2},{4,5},{5,4},{6,7},{7,6},{8,9},{9,8},{10,11... | collective-permute-start | bytes 135176 | tf_op jit(solution)/shard_map/ppermute | solution.py:995
